TPU v7x, 32 devices: a whole 2x2x4 slice. The times are simulated.
32 devices in a mesh: dp: 16 (over z, y, core), mp: 2 (over x).
Axes of the slice: x: 2, y: 2, z: 4, core: 2. Of those that a mesh axis runs over, the one named last changes fastest.
Arguments:
- tokens: bfloat16 [32, 1024, 768], P('dp', 'mp'), may hold values from -6 to 6
- memory: bfloat16 [32, 1024, 768], P('dp', 'mp'), may hold values from -6 to 6
- doc_lengths: int32 [32, 3], P('dp'), may hold values from 1 to 895, as said below
- mem_lengths: int32 [32], P('dp'), may hold values from 513 to 1024
- norm_gains: float32 [3, 768], replicated, may hold values from 0.1 to 1.9
- rel_table: float32 [32, 12], replicated, may hold values from -4 to 4
- self_proj: bfloat16 [3, 768, 768], P(None, 'dp', 'mp'), may hold values from -0.109375 to 0.109375
- self_out: bfloat16 [768, 768], P('mp', 'dp'), may hold values from -1.75 to 1.75
- cross_proj: bfloat16 [3, 768, 768], P(None, 'dp', 'mp'), may hold values from -0.109375 to 0.109375
- cross_out: bfloat16 [768, 768], P('mp', 'dp'), may hold values from -1.75 to 1.75
- ffn_proj: bfloat16 [2, 768, 2048], P(None, 'dp', 'mp'), may hold values from -0.21875 to 0.21875
- ffn_out: bfloat16 [2048, 768], P('mp', 'dp'), may hold values from -0.125 to 0.125
- cotangent: bfloat16 [32, 1024, 768], P('dp', 'mp'), may hold values from -6 to 6
Outputs:
- output: float32 [32, 1024, 768], P('dp', 'mp')
- grad_tokens: float32 [32, 1024, 768], P('dp', 'mp')
- grad_memory: float32 [32, 1024, 768], P('dp', 'mp')
- grad_gains: float32 [3, 768], replicated
- bias_table_gradient: float32 [32, 12], replicated
- grad_self_proj: float32 [3, 768, 768], P(None, 'dp', 'mp')
- grad_self_out: float32 [768, 768], P('mp', 'dp')
- grad_cross_proj: float32 [3, 768, 768], P(None, 'dp', 'mp')
- grad_cross_out: float32 [768, 768], P('mp', 'dp')
- grad_ffn_proj: float32 [2, 768, 2048], P(None, 'dp', 'mp')
- grad_ffn_out: float32 [2048, 768], P('mp', 'dp')
Inputs may be any that keep to these rules, and one draw needn't show every extreme that they name: `doc_lengths`: each row holds three documents in this order followed by one or more padding slots; the second document covers slots 1024 // 4 to 767.
All inputs are finite; a program needn't handle non-finite values.
Results may differ from a plain program's by a relative error of at most 0.028.
The roundings to bfloat16 on the way count: a program that leaves them out, or rounds other values in their place, can miss the bound.
Values may be sent and summed in bfloat16 or wider, within the bound.
No kernel may reach another device: no remote copies, remote signals or barrier semaphores. Data moves between devices by JAX's collectives and lax.ppermute only.
A program may use at most 512 MiB of HBM per device.

v0:
```python
import jax
import jax.numpy as jnp
import numpy as np
from jax import lax
from jax.sharding import PartitionSpec as P

DH = 64
NB = 32
REACH = 128
ROW = 1024
MEM = 1024
MICRO = 2


epsilon = 1e-06
masked_score = -1000000000.0


def for_sending(shard):
    return jax.tree.map(lambda a: a.astype(jnp.bfloat16) if a.dtype == jnp.float32 else a, shard)


def bucket_table(length, buckets, reach):
    offsets = np.arange(length)
    exact_part = buckets // 2
    scaled = (
        np.log(np.maximum(offsets, 1) / exact_part)
        / np.log(reach / exact_part)
        * (buckets - exact_part)
    )
    far_bucket = np.minimum(exact_part + np.floor(scaled).astype(np.int64), buckets - 1)
    return np.where(offsets < exact_part, offsets, far_bucket).astype(np.int32)


def segment_ids(doc_lengths, length):
    bounds = jnp.cumsum(doc_lengths, axis=-1)
    slots = jnp.arange(length, dtype=jnp.int32)
    return jnp.sum((slots[None, :, None] >= bounds[:, None, :]).astype(jnp.int32), axis=-1)


def norm_forward(values, gain):
    inverse = lax.rsqrt(jnp.mean(values * values, axis=-1, keepdims=True) + epsilon)
    return (values * inverse * gain, inverse)


def norm_backward(values, inverse, gain, upstream):
    weighted = upstream * gain
    inner_mean = jnp.mean(weighted * values, axis=-1, keepdims=True)
    grad_values = inverse * weighted - values * inverse * inverse * inverse * inner_mean
    grad_gain = jnp.sum(upstream * values * inverse, axis=(0, 1))
    return (grad_values, grad_gain)


def whole_rows(values):
    return lax.all_gather(values, "mp", axis=1, tiled=True)


def own_share(values):
    return lax.psum_scatter(values, "mp", scatter_dimension=1, tiled=True)


def back_whole(values):
    return lax.all_gather(values, "mp", axis=1, tiled=True)


def back_share(values):
    return lax.psum_scatter(values, "mp", scatter_dimension=1, tiled=True)


def cross_share(values):
    return jax.tree.map(
        lambda part: part.astype(jnp.float32),
        lax.psum_scatter(for_sending(values), "mp", scatter_dimension=1, tiled=True),
    )


def score_block(query_block, key_heads, first_row, key_count, extra_fn, mask_fn):
    scores = jnp.einsum(
        "qhe,khe->hqk", query_block, key_heads[:key_count], preferred_element_type=jnp.float32
    )
    scores = scores + extra_fn(first_row, key_count)
    return jnp.where(mask_fn(first_row, key_count)[None], scores, masked_score)


def attention_forward_pass(query_matrix, key_heads, values, parts):
    extra_fn, mask_fn, table_fn, table_init, key_limit = parts
    block_rows = min(512, query_matrix.shape[0])
    mixed_blocks = []
    total_blocks = []
    for block_index in range(query_matrix.shape[0] // block_rows):
        first_row = block_index * block_rows
        key_count = key_limit(first_row)
        query_block = query_matrix[first_row : first_row + block_rows]
        scores = score_block(query_block, key_heads, first_row, key_count, extra_fn, mask_fn)
        top_score = jnp.max(scores, axis=-1, keepdims=True)
        exponent_terms = jnp.exp(scores - top_score)
        row_total = jnp.sum(exponent_terms, axis=-1, keepdims=True)
        weights = (exponent_terms / row_total).astype(jnp.bfloat16)
        mixed_out = jnp.einsum(
            "hqk,khe->qhe", weights, values[:key_count], preferred_element_type=jnp.float32
        )
        mixed_blocks.append(mixed_out.astype(jnp.bfloat16))
        total_blocks.append(top_score + jnp.log(row_total))
    return (jnp.concatenate(mixed_blocks, axis=0), jnp.stack(total_blocks))


def attend_backward(query_matrix, key_heads, values, log_total, grad_mixed, parts):
    extra_fn, mask_fn, table_fn, table_init, key_limit = parts
    block_rows = min(512, query_matrix.shape[0])
    grad_keys = jnp.zeros(key_heads.shape, jnp.float32)
    grad_values = jnp.zeros(key_heads.shape, jnp.float32)
    bias_table_gradient = table_init
    query_grads = []
    for block_index in range(query_matrix.shape[0] // block_rows):
        first_row = block_index * block_rows
        key_count = key_limit(first_row)
        query_block = query_matrix[first_row : first_row + block_rows]
        grad_block = grad_mixed[first_row : first_row + block_rows]
        scores = score_block(query_block, key_heads, first_row, key_count, extra_fn, mask_fn)
        probs = jnp.exp(scores - log_total[block_index])
        weights = probs.astype(jnp.bfloat16)
        grad_weights = jnp.einsum(
            "qhe,khe->hqk", grad_block, values[:key_count], preferred_element_type=jnp.float32
        )
        inner_sum = jnp.sum(probs * grad_weights, axis=-1, keepdims=True)
        score_gradient = (probs * (grad_weights - inner_sum)).astype(jnp.bfloat16)
        grad_query = jnp.einsum(
            "hqk,khe->qhe",
            score_gradient,
            key_heads[:key_count],
            preferred_element_type=jnp.float32,
        )
        grad_keys = grad_keys.at[:key_count].add(
            jnp.einsum(
                "hqk,qhe->khe", score_gradient, query_block, preferred_element_type=jnp.float32
            )
        )
        grad_values = grad_values.at[:key_count].add(
            jnp.einsum("hqk,qhe->khe", weights, grad_block, preferred_element_type=jnp.float32)
        )
        bias_table_gradient = bias_table_gradient + table_fn(first_row, key_count, score_gradient)
        query_grads.append(grad_query.astype(jnp.bfloat16))
    return (
        jnp.concatenate(query_grads, axis=0),
        grad_keys.astype(jnp.bfloat16),
        grad_values.astype(jnp.bfloat16),
        bias_table_gradient,
    )


def rows_forward(query_all, key_all, value_all, row_data, parts_fn):

    def one_row(row_args):
        query_matrix, key_heads, values, datum = row_args
        return attention_forward_pass(
            query_matrix, key_heads, values, parts_fn(datum, query_matrix.shape[0])
        )

    return lax.map(one_row, (query_all, key_all, value_all, row_data))


def rows_backward(query_all, key_all, value_all, total_all, grad_all, row_data, parts_fn):

    def one_row(row_args):
        query_matrix, key_heads, values, log_total, grad_mixed, datum = row_args
        return attend_backward(
            query_matrix,
            key_heads,
            values,
            log_total,
            grad_mixed,
            parts_fn(datum, query_matrix.shape[0]),
        )

    return lax.map(one_row, (query_all, key_all, value_all, total_all, grad_all, row_data))


def cross_parts(valid_row, length):

    def extra_fn(first_row, key_count):
        return jnp.zeros((), jnp.float32)

    def mask_fn(first_row, key_count):
        return valid_row[None, :key_count]

    def table_fn(first_row, key_count, score_gradient):
        return jnp.zeros((1,), jnp.float32)

    def key_limit(first_row):
        return valid_row.shape[0]

    return (extra_fn, mask_fn, table_fn, jnp.zeros((1,), jnp.float32), key_limit)


def split_heads(values):
    return values.reshape(values.shape[:-1] + (values.shape[-1] // DH, DH))


def join_heads(values):
    return values.reshape(values.shape[:-2] + (values.shape[-2] * values.shape[-1],))


def layer_pass(
    weights,
    resid_in,
    memory_part,
    cot_part,
    doc_rows,
    mem_rows,
    norm_gains,
    table_heads,
    first_slot_index,
    movers,
):
    gather_fn, share_fn, backward_gather_function, back_share_fn, cross_fn = movers
    proj_self, out_self, proj_cross, out_cross, proj_ffn, out_ffn = weights
    local_len = resid_in.shape[1]
    head_count = table_heads.shape[1]
    bucket_numpy = bucket_table(ROW, NB, REACH)
    bucket_dist = jnp.asarray(bucket_numpy)
    onehot_dist = (bucket_dist[:, None] == jnp.arange(NB, dtype=jnp.int32)[None, :]).astype(
        jnp.float32
    )
    dist_heads = jnp.dot(onehot_dist, table_heads, precision=lax.Precision.HIGHEST).T
    key_slots = jnp.arange(ROW, dtype=jnp.int32)

    def self_parts(segment_row, length):
        block_rows = min(512, length)

        def key_limit(first_row):
            return min(ROW, first_row + block_rows)

        def offsets_at(first_row, key_count):
            query_at = first_row + jnp.arange(block_rows, dtype=jnp.int32)
            return jnp.maximum(query_at[:, None] - key_slots[None, :key_count], 0)

        def extra_fn(first_row, key_count):
            return jnp.take(dist_heads, offsets_at(first_row, key_count), axis=1)

        def mask_fn(first_row, key_count):
            query_at = first_row + jnp.arange(block_rows, dtype=jnp.int32)
            query_seg = segment_row[first_row : first_row + block_rows]
            return (query_seg[:, None] == segment_row[None, :key_count]) & (
                key_slots[None, :key_count] <= query_at[:, None]
            )

        def table_fn(first_row, key_count, score_gradient):
            span = block_rows + key_count
            padded = jnp.pad(score_gradient, ((0, 0), (0, 0), (block_rows, 0)))
            flat = padded.reshape(head_count, block_rows * span)
            flat = jnp.pad(flat, ((0, 0), (0, block_rows)))
            skewed = flat.reshape(head_count, block_rows, span + 1)
            diagonals = jnp.sum(skewed, axis=1, dtype=jnp.float32)
            distance = np.clip(first_row + block_rows - np.arange(span + 1), 0, ROW - 1)
            onehot_diag = jnp.asarray(
                (bucket_numpy[distance][:, None] == np.arange(NB)[None, :]).astype(np.float32)
            )
            return jnp.dot(onehot_diag.T, diagonals.T, precision=lax.Precision.HIGHEST)

        return (extra_fn, mask_fn, table_fn, jnp.zeros((NB, head_count), jnp.float32), key_limit)

    segments = segment_ids(doc_rows, ROW)
    pad_local = (
        lax.dynamic_slice_in_dim(segments, first_slot_index, local_len, 1) == doc_rows.shape[-1]
    )
    mem_valid = jnp.arange(MEM, dtype=jnp.int32)[None, :] < mem_rows[:, None]
    normed_one, inverse_one = norm_forward(resid_in, norm_gains[0])
    gathered_one = gather_fn(normed_one.astype(jnp.bfloat16))
    qkv_self = jnp.einsum(
        "rld,sdc->srlc", gathered_one, proj_self, preferred_element_type=jnp.float32
    ).astype(jnp.bfloat16)
    heads_self = split_heads(qkv_self)
    mixed_self, total_self = rows_forward(
        heads_self[0], heads_self[1], heads_self[2], segments, self_parts
    )
    flattened_self_rows = join_heads(mixed_self)
    resid_two = resid_in + share_fn(
        jnp.einsum("rlc,cd->rld", flattened_self_rows, out_self, preferred_element_type=jnp.float32)
    )
    normed_two, inverse_two = norm_forward(resid_two, norm_gains[1])
    gathered_two = gather_fn(normed_two.astype(jnp.bfloat16))
    memory_all = gather_fn(memory_part)
    query_cross = jnp.einsum(
        "rld,dc->rlc", gathered_two, proj_cross[0], preferred_element_type=jnp.float32
    ).astype(jnp.bfloat16)
    kv_cross = jnp.einsum(
        "rmd,sdc->srmc", memory_all, proj_cross[1:], preferred_element_type=jnp.float32
    ).astype(jnp.bfloat16)
    heads_query = split_heads(query_cross)
    heads_kv = split_heads(kv_cross)
    mixed_cross, total_cross = rows_forward(
        heads_query, heads_kv[0], heads_kv[1], mem_valid, cross_parts
    )
    flat_cross = join_heads(mixed_cross)
    resid_three = resid_two + share_fn(
        jnp.einsum("rlc,cd->rld", flat_cross, out_cross, preferred_element_type=jnp.float32)
    )
    normed_three, inverse_three = norm_forward(resid_three, norm_gains[2])
    gathered_three = gather_fn(normed_three.astype(jnp.bfloat16))
    gate_up = jnp.einsum(
        "rld,sdf->srlf", gathered_three, proj_ffn, preferred_element_type=jnp.float32
    )
    activated, gelu_pull = jax.vjp(
        lambda gate_in: jax.nn.gelu(gate_in, approximate=True), gate_up[0]
    )
    hidden = (activated * gate_up[1]).astype(jnp.bfloat16)
    resid_four = resid_three + share_fn(
        jnp.einsum("rlf,fd->rld", hidden, out_ffn, preferred_element_type=jnp.float32)
    )
    output = jnp.where(pad_local[..., None], 0.0, resid_four)
    grad_four = jnp.where(pad_local[..., None], 0.0, cot_part.astype(jnp.float32))
    grad_branch = backward_gather_function(grad_four.astype(jnp.bfloat16))
    grad_out_ffn = jnp.einsum(
        "rlf,rld->fd", hidden, grad_branch, preferred_element_type=jnp.float32
    )
    grad_hidden = jnp.einsum(
        "rld,fd->rlf", grad_branch, out_ffn, preferred_element_type=jnp.float32
    )
    grad_gate = gelu_pull(grad_hidden * gate_up[1])[0].astype(jnp.bfloat16)
    grad_upward = (grad_hidden * activated).astype(jnp.bfloat16)
    grad_gate_up = jnp.stack([grad_gate, grad_upward])
    grad_proj_ffn = jnp.einsum(
        "rld,srlf->sdf", gathered_three, grad_gate_up, preferred_element_type=jnp.float32
    )
    grad_normed = back_share_fn(
        jnp.einsum("srlf,sdf->rld", grad_gate_up, proj_ffn, preferred_element_type=jnp.float32)
    )
    grad_resid, gain_three = norm_backward(resid_three, inverse_three, norm_gains[2], grad_normed)
    grad_three = grad_four + grad_resid
    grad_branch = backward_gather_function(grad_three.astype(jnp.bfloat16))
    grad_out_cross = jnp.einsum(
        "rlc,rld->cd", flat_cross, grad_branch, preferred_element_type=jnp.float32
    )
    grad_mixed = split_heads(
        jnp.einsum(
            "rld,cd->rlc", grad_branch, out_cross, preferred_element_type=jnp.float32
        ).astype(jnp.bfloat16)
    )
    grad_query, grad_keys, grad_values, unused_table = rows_backward(
        heads_query, heads_kv[0], heads_kv[1], total_cross, grad_mixed, mem_valid, cross_parts
    )
    grad_query = join_heads(grad_query)
    grad_keys = join_heads(grad_keys)
    grad_values = join_heads(grad_values)
    grad_proj_cross = jnp.stack(
        [
            jnp.einsum("rld,rlc->dc", gathered_two, grad_query, preferred_element_type=jnp.float32),
            jnp.einsum("rmd,rmc->dc", memory_all, grad_keys, preferred_element_type=jnp.float32),
            jnp.einsum("rmd,rmc->dc", memory_all, grad_values, preferred_element_type=jnp.float32),
        ]
    )
    query_term = jnp.einsum(
        "rlc,dc->rld", grad_query, proj_cross[0], preferred_element_type=jnp.float32
    )
    memory_term = jnp.einsum(
        "rmc,dc->rmd", grad_keys, proj_cross[1], preferred_element_type=jnp.float32
    ) + jnp.einsum("rmc,dc->rmd", grad_values, proj_cross[2], preferred_element_type=jnp.float32)
    grad_normed, grad_memory = cross_fn((query_term, memory_term))
    grad_resid, gain_two = norm_backward(resid_two, inverse_two, norm_gains[1], grad_normed)
    grad_two = grad_three + grad_resid
    grad_branch = backward_gather_function(grad_two.astype(jnp.bfloat16))
    grad_out_self = jnp.einsum(
        "rlc,rld->cd", flattened_self_rows, grad_branch, preferred_element_type=jnp.float32
    )
    grad_mixed = split_heads(
        jnp.einsum("rld,cd->rlc", grad_branch, out_self, preferred_element_type=jnp.float32).astype(
            jnp.bfloat16
        )
    )
    grad_query, grad_keys, grad_values, table_rows = rows_backward(
        heads_self[0], heads_self[1], heads_self[2], total_self, grad_mixed, segments, self_parts
    )
    grad_qkv = jnp.stack([join_heads(grad_query), join_heads(grad_keys), join_heads(grad_values)])
    grad_proj_self = jnp.einsum(
        "rld,srlc->sdc", gathered_one, grad_qkv, preferred_element_type=jnp.float32
    )
    grad_normed = back_share_fn(
        jnp.einsum("srlc,sdc->rld", grad_qkv, proj_self, preferred_element_type=jnp.float32)
    )
    grad_resid, gain_one = norm_backward(resid_in, inverse_one, norm_gains[0], grad_normed)
    grad_tokens = grad_two + grad_resid
    gains = jnp.stack([gain_one, gain_two, gain_three])
    table_sum = jnp.sum(table_rows, axis=0)
    step_grads = (
        grad_proj_self,
        grad_out_self,
        grad_proj_cross,
        grad_out_cross,
        grad_proj_ffn,
        grad_out_ffn,
    )
    return (output, grad_tokens, grad_memory, gains, table_sum, step_grads)


def per_device(
    tokens,
    memory,
    doc_lengths,
    mem_lengths,
    norm_gains,
    rel_table,
    self_proj,
    self_out,
    cross_proj,
    cross_out,
    ffn_proj,
    ffn_out,
    cotangent,
):
    mp_index = lax.axis_index("mp")
    micro_rows = tokens.shape[0] // MICRO
    local_len = tokens.shape[1]
    head_count = self_proj.shape[2] // DH
    head_first = mp_index * head_count
    table_local = lax.dynamic_slice_in_dim(rel_table, mp_index * head_count, head_count, 1)
    movers = (whole_rows, own_share, back_whole, back_share, cross_share)
    weight_sums = None
    gain_sum = jnp.zeros(norm_gains.shape, jnp.float32)
    table_sum = jnp.zeros((NB, head_count), jnp.float32)
    output_parts = []
    token_grads = []
    memory_grads = []
    for micro_step in range(MICRO):
        current = (
            lax.all_gather(self_proj, "dp", axis=1, tiled=True),
            lax.all_gather(self_out, "dp", axis=1, tiled=True),
            lax.all_gather(cross_proj, "dp", axis=1, tiled=True),
            lax.all_gather(cross_out, "dp", axis=1, tiled=True),
            lax.all_gather(ffn_proj, "dp", axis=1, tiled=True),
            lax.all_gather(ffn_out, "dp", axis=1, tiled=True),
        )
        row_first = micro_step * micro_rows
        row_last = row_first + micro_rows
        out_part, tok_part, mem_part, gains, table_part, step_grads = layer_pass(
            current,
            tokens[row_first:row_last].astype(jnp.float32),
            memory[row_first:row_last],
            cotangent[row_first:row_last],
            doc_lengths[row_first:row_last],
            mem_lengths[row_first:row_last],
            norm_gains,
            table_local,
            mp_index * local_len,
            movers,
        )
        output_parts.append(out_part)
        token_grads.append(tok_part)
        memory_grads.append(mem_part)
        gain_sum = gain_sum + gains
        table_sum = table_sum + table_part
        if weight_sums is None:
            weight_sums = step_grads
        else:
            weight_sums = tuple(
                (earlier + latest for earlier, latest in zip(weight_sums, step_grads))
            )
    output = jnp.concatenate(output_parts, axis=0)
    grad_tokens = jnp.concatenate(token_grads, axis=0)
    grad_memory = jnp.concatenate(memory_grads, axis=0)
    sum_proj_self, sum_out_self, sum_proj_cross, sum_out_cross, sum_proj_ffn, sum_out_ffn = (
        weight_sums
    )
    shard_grads = (
        lax.psum_scatter(sum_proj_self, "dp", scatter_dimension=1, tiled=True),
        lax.psum_scatter(sum_out_self, "dp", scatter_dimension=1, tiled=True),
        lax.psum_scatter(sum_proj_cross, "dp", scatter_dimension=1, tiled=True),
        lax.psum_scatter(sum_out_cross, "dp", scatter_dimension=1, tiled=True),
        lax.psum_scatter(sum_proj_ffn, "dp", scatter_dimension=1, tiled=True),
        lax.psum_scatter(sum_out_ffn, "dp", scatter_dimension=1, tiled=True),
    )
    full_table = lax.dynamic_update_slice(
        jnp.zeros(rel_table.shape, jnp.float32), table_sum, (jnp.int32(0), head_first)
    )
    grad_gains, bias_table_gradient = lax.psum((gain_sum, full_table), ("dp", "mp"))
    return (
        output,
        grad_tokens,
        grad_memory,
        grad_gains,
        bias_table_gradient,
        shard_grads[0],
        shard_grads[1],
        shard_grads[2],
        shard_grads[3],
        shard_grads[4],
        shard_grads[5],
    )


def solution(mesh):
    placed = (
        P("dp", "mp", None),
        P("dp", "mp", None),
        P("dp", None),
        P("dp"),
        P(),
        P(),
        P(None, "dp", "mp"),
        P("mp", "dp"),
        P(None, "dp", "mp"),
        P("mp", "dp"),
        P(None, "dp", "mp"),
        P("mp", "dp"),
        P("dp", "mp", None),
    )
    return jax.shard_map(
        per_device,
        mesh=mesh,
        in_specs=placed,
        out_specs=(
            P("dp", "mp", None),
            P("dp", "mp", None),
            P("dp", "mp", None),
            P(),
            P(),
            P(None, "dp", "mp"),
            P("mp", "dp"),
            P(None, "dp", "mp"),
            P("mp", "dp"),
            P(None, "dp", "mp"),
            P("mp", "dp"),
        ),
        check_vma=False,
    )
```

profile of v0, /device:TPU:0, one launch (start us, length us, event | category | flops | bytes accessed | tf_op | source)
XLA Modules:
  0.0 5103.3 jit_solution(16592781680325807666)
XLA Ops:
  19.7 1719.2 %gather_fusion.1 = f32[524288,6]{1,0:T(8,128)} fusion(f32[6,1024]{0,1:T(8,128)S(1)} %fusion.346, s32[524288]{0:T(1024)S(1)} %broadcast_clamp_fusion), kind=kCustom, calls=%fused_computation.1.clone | custom fusion | bytes 27262976 | tf_op jit(solution)/shard_map/while/body/eval_jaxpr/jit(_take)/gather | solution.py:238
  1739.0 141.7 %copy.210 = f32[512,1024,6]{1,0,2:T(8,128)} copy(f32[512,1024,6]{2,1,0:T(8,128)} %bitcast.20) | data formatting | bytes 25165824 | tf_op jit(solution)/shard_map/while/body/eval_jaxpr/jit(_take)/gather | solution.py:238
  1882.7 859.9 %gather_fusion = f32[262144,6]{1,0:T(8,128)} fusion(f32[6,1024]{0,1:T(8,128)S(1)} %fusion.346, s32[262144]{0:T(1024)S(1)} %broadcast_clamp_fusion.1), kind=kCustom, calls=%fused_computation.clone | custom fusion | bytes 13631488 | tf_op jit(solution)/shard_map/while/body/eval_jaxpr/jit(_take)/gather | solution.py:238
  2742.7 72.1 %copy.152 = f32[512,512,6]{0,1,2:T(8,128)} copy(f32[512,512,6]{2,1,0:T(8,128)} %bitcast.13) | data formatting | bytes 12582912 | tf_op jit(solution)/shard_map/while/body/eval_jaxpr/jit(_take)/gather | solution.py:238
  2913.5 46.1 reduce-scatter.19.cloned.1.call-done
  2989.9 41.8 all-gather.23.cloned.1.call-done
  3088.7 41.5 reduce-scatter.21.cloned.1.call-done
  3236.0 28.2 all-gather.29.cloned.1.call-done
  3293.6 42.1 all-gather.33.cloned.1.call-done
  3351.1 29.5 reduce-scatter.27.cloned.1.call-done
  3383.5 43.2 reduce-scatter.31.cloned.1.call-done
  3549.2 43.2 reduce-scatter.23.cloned.1.call-done
  3592.5 46.3 reduce-scatter.29.cloned.1.call-done
  3646.4 26.7 all-gather.51.cloned.1.call-done
  4134.3 29.9 copy.219
  4190.1 341.8 %while.42 = (u32[]{:T(128)}, f32[1,6,786944]{2,1,0:T(8,128)}, f32[4721664]{0:T(1024)}, u32[]{}, f32[]{:T(128)}, /*index=5*/u32[]{}, u32[]{}, u32[]{}) while((u32[]{:T(128)}, f32[1,6,786944]{2,1,0:T(8,128)}, f32[4721664]{0:T(1024)}, u32[]{}, f32[]{:T(128)}, /*index=5*/u32[]{}, u32[]{}, u32[]{}) %tuple.274), condition=%wide.cond, body=%wide.body.sunk | while | flops 9 | bytes 12591297
  4190.6 30.0 dynamic-slice_reduce_fusion.4
  4247.7 30.0 dynamic-slice_reduce_fusion.4
  4304.8 30.0 dynamic-slice_reduce_fusion.4
  4361.7 30.0 dynamic-slice_reduce_fusion.4
  4418.8 30.0 dynamic-slice_reduce_fusion.4
  4475.7 30.0 dynamic-slice_reduce_fusion.4
  4532.0 31.3 reshape.1658
  4611.9 341.6 %while.43 = (u32[]{:T(128)}, f32[1,6,786944]{2,1,0:T(8,128)}, f32[4721664]{0:T(1024)}, u32[]{}, f32[]{:T(128)}, /*index=5*/u32[]{}, u32[]{}, u32[]{}) while((u32[]{:T(128)}, f32[1,6,786944]{2,1,0:T(8,128)}, f32[4721664]{0:T(1024)}, u32[]{}, f32[]{:T(128)}, /*index=5*/u32[]{}, u32[]{}, u32[]{}) %tuple.277), condition=%wide.cond.1, body=%wide.body.1.sunk | while | flops 9 | bytes 12591297
  4612.6 30.0 dynamic-slice_reduce_fusion.5
  4669.5 30.0 dynamic-slice_reduce_fusion.5
  4726.4 30.0 dynamic-slice_reduce_fusion.5
  4783.3 30.0 dynamic-slice_reduce_fusion.5
  4840.2 30.0 dynamic-slice_reduce_fusion.5
  4897.2 30.0 dynamic-slice_reduce_fusion.5
  4953.5 31.4 reshape.1660
  5046.1 40.6 all-reduce.14
  (858 shorter events, 1409.9 us)
Async XLA Ops:
  7.2 2835.8 %all-gather.35.cloned.1.call-start = ((), (), s32[]{:S(2)}) async-start(), calls=%async_computation.29 | async-start | bytes 2359296 | tf_op jit(solution)/shard_map/all_gather | solution.py:55
  14.0 2829.0 %all-gather.21.cloned.1.call-start = ((), (), s32[]{:S(2)}) async-start(), calls=%async_computation.19 | async-start | bytes 1880064 | tf_op jit(solution)/shard_map/all_gather | solution.py:425
  14.8 2858.2 %all-gather.19.cloned.1.call-start = ((), (), s32[]{:S(2)}) async-start(), calls=%async_computation.18 | async-start | bytes 2359296 | tf_op jit(solution)/shard_map/all_gather | solution.py:55
  15.5 2898.1 %reduce-scatter.25.cloned.1.call-start = ((), (), s32[]{:S(2)}) async-start(), calls=%async_computation.30 | async-start | bytes 4718592 | tf_op jit(solution)/shard_map/reduce_scatter | solution.py:59
  2872.8 86.9 %reduce-scatter.19.cloned.1.call-start = ((), (), s32[]{:S(2)}) async-start(), calls=%async_computation.20 | async-start | bytes 4718592 | tf_op jit(solution)/shard_map/reduce_scatter | solution.py:59
  2905.6 126.1 %all-gather.23.cloned.1.call-start = ((), (), s32[]{:S(2)}) async-start(), calls=%async_computation.21 | async-start | bytes 1880064 | tf_op jit(solution)/shard_map/all_gather | solution.py:427
  2906.3 153.6 %all-gather.27.cloned.1.call-start = ((), (), s32[]{:S(2)}) async-start(), calls=%async_computation.23 | async-start | bytes 2359296 | tf_op jit(solution)/shard_map/all_gather | solution.py:55
  2965.2 165.0 %reduce-scatter.21.cloned.1.call-start = ((), (), s32[]{:S(2)}) async-start(), calls=%async_computation.24 | async-start | bytes 4718592 | tf_op jit(solution)/shard_map/reduce_scatter | solution.py:59
  3087.3 101.1 %all-gather.39.cloned.1.call-start = ((), (), s32[]{:S(2)}) async-start(), calls=%async_computation.32 | async-start | bytes 2359296 | tf_op jit(solution)/shard_map/all_gather | solution.py:55
  3088.0 148.0 %all-gather.31.cloned.1.call-start = ((), (), s32[]{:S(2)}) async-start(), calls=%async_computation.26 | async-start | bytes 3342336 | tf_op jit(solution)/shard_map/all_gather | solution.py:429
  3088.6 175.6 %all-gather.29.cloned.1.call-start = ((), (), s32[]{:S(2)}) async-start(), calls=%async_computation.25 | async-start | bytes 2359296 | tf_op jit(solution)/shard_map/all_gather | solution.py:55
  3134.6 158.9 %all-gather.43.cloned.1.call-start = ((), (), s32[]{:S(2)}) async-start(), calls=%async_computation.36 | async-start | bytes 2359296 | tf_op jit(solution)/shard_map/all_gather | solution.py:63
  3137.7 197.9 %all-gather.33.cloned.1.call-start = ((), (), s32[]{:S(2)}) async-start(), calls=%async_computation.27 | async-start | bytes 1671168 | tf_op jit(solution)/shard_map/all_gather | solution.py:430
  3138.3 242.4 %reduce-scatter.27.cloned.1.call-start = ((), (), s32[]{:S(2)}) async-start(), calls=%async_computation.33 | async-start | bytes 4718592 | tf_op jit(solution)/shard_map/reduce_scatter | solution.py:59
  3215.7 211.0 %reduce-scatter.31.cloned.1.call-start = ((), (), s32[]{:S(2)}) async-start(), calls=%async_computation.37 | async-start | bytes 4718592 | tf_op jit(solution)/shard_map/reduce_scatter | solution.py:67
  3351.1 107.3 %all-gather.41.cloned.1.call-start = ((), (), s32[]{:S(2)}) async-start(), calls=%async_computation.34 | async-start | bytes 2359296 | tf_op jit(solution)/shard_map/all_gather | solution.py:55
  3431.8 114.4 %reduce-scatter.37.cloned.1.call-start = ((), (), s32[]{:S(2)}) async-start(), calls=%async_computation.43 | async-start | bytes 4718592 | tf_op jit(solution)/shard_map/reduce_scatter | solution.py:67
  3502.7 89.7 %reduce-scatter.23.cloned.1.call-start = ((), (), s32[]{:S(2)}) async-start(), calls=%async_computation.28 | async-start | bytes 4718592 | tf_op jit(solution)/shard_map/reduce_scatter | solution.py:59
  3511.1 127.6 %reduce-scatter.29.cloned.1.call-start = ((), (), s32[]{:S(2)}) async-start(), calls=%async_computation.35 | async-start | bytes 4718592 | tf_op jit(solution)/shard_map/reduce_scatter | solution.py:59
  3519.7 153.4 %all-gather.51.cloned.1.call-start = ((), (), s32[]{:S(2)}) async-start(), calls=%async_computation.44 | async-start | bytes 2359296 | tf_op jit(solution)/shard_map/all_gather | solution.py:63
  3646.3 151.5 %reduce-scatter.39.cloned.1.call-start = ((), (), s32[]{:S(2)}) async-start(), calls=%async_computation.45 | async-start | bytes 2359296 | tf_op jit(solution)/shard_map/reduce_scatter | solution.py:73
  3786.1 104.0 %all-gather.47.cloned.1.call-start = ((), (), s32[]{:S(2)}) async-start(), calls=%async_computation.40 | async-start | bytes 2359296 | tf_op jit(solution)/shard_map/all_gather | solution.py:63
  3820.6 109.2 %all-gather.53.cloned.1.call-start = ((), (), s32[]{:S(2)}) async-start(), calls=%async_computation.46 | async-start | bytes 2359296 | tf_op jit(solution)/shard_map/all_gather | solution.py:63
  3852.0 214.6 %reduce-scatter.43.cloned.1.call-start = ((), (), s32[]{:S(2)}) async-start(), calls=%async_computation.48 | async-start | bytes 2359296 | tf_op jit(solution)/shard_map/reduce_scatter | solution.py:73
  3867.5 199.0 %reduce-scatter.45.cloned.1.call-start = ((), (), s32[]{:S(2)}) async-start(), calls=%async_computation.49 | async-start | bytes 2359296 | tf_op jit(solution)/shard_map/reduce_scatter | solution.py:73
  3889.8 1149.3 %all-reduce.18.cloned.1.call-start = ((), (), s32[]{:S(2)}) async-start(), calls=%async_computation.54 | async-start | bytes 22020096
  4016.7 1026.1 %reduce-scatter.35.cloned.1.call-start = ((), (), s32[]{:S(2)}) async-start(), calls=%async_computation.41 | async-start | bytes 4718592 | tf_op jit(solution)/shard_map/reduce_scatter | solution.py:67
  4023.1 1019.8 %reduce-scatter.41.cloned.1.call-start = ((), (), s32[]{:S(2)}) async-start(), calls=%async_computation.47 | async-start | bytes 4718592 | tf_op jit(solution)/shard_map/reduce_scatter | solution.py:67
  4029.8 1063.6 %reduce-scatter.53.cloned.1.call-start = ((), (), s32[]{:S(2)}) async-start(), calls=%async_computation.53 | async-start | bytes 3342336 | tf_op jit(solution)/shard_map/reduce_scatter | solution.py:469
  4043.0 1050.4 %reduce-scatter.51.cloned.1.call-start = ((), (), s32[]{:S(2)}) async-start(), calls=%async_computation.52 | async-start | bytes 1253376 | tf_op jit(solution)/shard_map/reduce_scatter | solution.py:467
  4053.8 1039.6 %reduce-scatter.49.cloned.1.call-start = ((), (), s32[]{:S(2)}) async-start(), calls=%async_computation.51 | async-start | bytes 3760128 | tf_op jit(solution)/shard_map/reduce_scatter | solution.py:466
  4064.8 1031.5 %reduce-scatter.47.cloned.1.call-start = ((), (), s32[]{:S(2)}) async-start(), calls=%async_computation.50 | async-start | bytes 1253376 | tf_op jit(solution)/shard_map/reduce_scatter | solution.py:465
  (246 other events, 4937.8 us)
Sparse Core Ops, SparseCore 0:
  14.1 29.8 all-gather.34
  46.4 40.3 all-gather.20
  2872.9 40.6 reduce-scatter.24
  2916.3 43.3 reduce-scatter.18
  2961.6 27.2 all-gather.24
  2991.2 40.4 all-gather.22
  3086.8 43.3 reduce-scatter.20
  3131.7 27.1 all-gather.36
  3161.1 27.1 all-gather.38
  3190.8 45.2 all-gather.30
  3266.3 27.1 all-gather.42
  3295.9 39.6 all-gather.32
  3338.4 42.2 reduce-scatter.26
  3383.3 43.3 reduce-scatter.30
  3431.2 27.1 all-gather.40
  3460.0 27.1 all-gather.48
  3502.9 43.3 reduce-scatter.36
  3549.1 43.3 reduce-scatter.22
  3595.4 43.3 reduce-scatter.28
  3645.8 27.2 all-gather.50
  3675.1 27.2 all-gather.44
  3740.0 26.2 reduce-scatter.38
  3820.7 27.2 all-gather.46
  3852.1 27.2 all-gather.52
  3909.9 26.1 reduce-scatter.44
  4016.9 209.1 all-reduce.17
  4228.3 43.4 reduce-scatter.34
  4273.9 43.3 reduce-scatter.40
  4321.8 66.2 reduce-scatter.52
  4392.2 56.9 reduce-scatter.50
  4453.5 67.2 reduce-scatter.48
  5037.5 58.6 reduce-scatter.46
  (5 shorter events, 130.1 us)
where the time goes:
time: 5140 us; the launch traced here: 5100 us
  local copies, waits for them, and re-layouts  3770 us (73%)
  waiting for transfers between devices  601 us (12%)
  matrix products  415 us (8%)
  other arithmetic  203 us (4%)
  blocking collectives  89.3 us (2%)
    gather x4, local copies, waits for them, and re-layouts, extra_fn(): return jnp.take(dist_heads, offsets_at(first_row, key_count), axis=1)  2790 us
    unnamed x537, local copies, waits for them, and re-layouts  827 us
    reduce_scatter x6, waiting for transfers between devices, own_share(): return lax.psum_scatter(values, 'mp', scatter_dimension=1, tiled=True)  214 us
    all_gather x8, waiting for transfers between devices, whole_rows(): return lax.all_gather(values, 'mp', axis=1, tiled=True)  123 us
    convert_element_type x4, local copies, waits for them, and re-layouts, table_fn(): diagonals = jnp.sum(skewed, axis=1, dtype=jnp.float32)  108 us
  transfers between devices with their start and end apart: 37, of which 21 were waited for; matrix products, arithmetic and copies ran while one was open for 84% of the time, Pallas kernels for 0%

commit v1 on v0

v1 whole, which is shorter than its diff:
```python
import functools
import jax
import jax.numpy as jnp
import numpy as np
from jax import lax
from jax.experimental import pallas as pl
from jax.experimental.pallas import tpu as pltpu
from jax.sharding import PartitionSpec as P

DH = 64
NB = 32
REACH = 128
ROW = 1024
LANES = 128
QB = 256
masked_score = -1000000000.0
BF = jnp.bfloat16
F32 = jnp.float32
VMEM_LIMIT = 56 * 1024 * 1024


def dot_t(a, b):
    return lax.dot_general(a, b, (((1,), (1,)), ((), ())), preferred_element_type=F32)


def dot_n(a, b):
    return lax.dot_general(a, b, (((1,), (0,)), ((), ())), preferred_element_type=F32)


def dot_tn(a, b):
    return lax.dot_general(a, b, (((0,), (0,)), ((), ())), preferred_element_type=F32)


def split_three(x):
    top = x.astype(BF)
    rest = x - top.astype(F32)
    mid = rest.astype(BF)
    low = (rest - mid.astype(F32)).astype(BF)
    return top.astype(F32), mid.astype(F32), low.astype(F32)


def place_three(x, slot, other):
    top, mid, low = split_three(x)
    return jnp.where(slot == 4, top, jnp.where(slot == 5, mid, jnp.where(slot == 6, low, other)))


def lane_slots(shape):
    lane = lax.broadcasted_iota(jnp.int32, shape, 1)
    return lane, lane % DH


def make_extras(bounds_ref, causal, extra_q, extra_k):
    shape = extra_q.shape
    _, slot = lane_slots(shape)
    rows = lax.broadcasted_iota(jnp.int32, shape, 0)
    if causal:
        first = bounds_ref[0]
        second = first + bounds_ref[1]
        third = second + bounds_ref[2]
        seg = (
            (rows >= first).astype(jnp.int32)
            + (rows >= second).astype(jnp.int32)
            + (rows >= third).astype(jnp.int32)
        )
        own = jnp.where(slot == seg, 1.0, 0.0)
        barred = jnp.where((slot < 4) & (slot != seg), masked_score, 0.0)
    else:
        own = jnp.where(slot == 0, 1.0, 0.0)
        barred = jnp.where((slot == 0) & (rows >= bounds_ref[0]), masked_score, 0.0)
    extra_q[...] = jnp.where(slot == 7, 1.0, own).astype(BF)
    extra_k[...] = jnp.where((slot >= 4) & (slot <= 6), 1.0, barred).astype(BF)


def band_square(band_ref, head):
    wide = jnp.broadcast_to(band_ref[head : head + 1, :], (LANES, 3 * LANES))
    rolled = pltpu.roll(wide, 0, 1, stride=1, stride_axis=0)
    return rolled[:, LANES : 2 * LANES], rolled[:, :LANES]


def forward_kernel(causal, bounds_ref, band_ref, q_ref, k_ref, v_ref, o_ref, qa_ref, extra_q, extra_k):
    length = q_ref.shape[0]

    @pl.when(pl.program_id(0) == 0)
    def _():
        make_extras(bounds_ref, causal, extra_q, extra_k)

    lane, slot = lane_slots((QB, LANES))
    full_lane, _ = lane_slots((length, LANES))
    values = v_ref[...]
    kept = []
    for head in range(2):
        mine = (full_lane < DH) == (head == 0)
        mine_block = (lane < DH) == (head == 0)
        keys = jnp.where(mine, k_ref[...], extra_k[...])
        if causal:
            near, side = band_square(band_ref, head)
            near_only = jnp.full((LANES, LANES), masked_score, F32)
        for block in range(length // QB):
            first = block * QB
            count = first + QB if causal else length
            queries = jnp.where(mine_block, q_ref[first : first + QB, :], extra_q[first : first + QB, :])
            scores = dot_t(queries, keys[:count])
            if causal:
                corner = jnp.concatenate([side, jnp.zeros((LANES, LANES), F32)], axis=0)
                left = jnp.concatenate([near, side], axis=0)
                right = jnp.concatenate([near_only, near], axis=0)
                pieces = []
                if block > 0:
                    if first > LANES:
                        pieces.append(scores[:, : first - LANES])
                    pieces.append(scores[:, first - LANES : first] + corner)
                pieces.append(scores[:, first : first + LANES] + left)
                pieces.append(scores[:, first + LANES :] + right)
                scores = jnp.concatenate(pieces, axis=1)
            top = jnp.max(scores, axis=1, keepdims=True)
            terms = jnp.exp(scores - top)
            total = jnp.sum(terms, axis=1, keepdims=True)
            probs = (terms * (1.0 / total)).astype(BF)
            mixed = dot_n(probs, values[:count])
            if head == 0:
                kept.append(mixed)
            else:
                o_ref[first : first + QB, :] = jnp.where(lane < DH, kept[block], mixed).astype(BF)
            minus_log = -(top + jnp.log(total))
            spare = place_three(minus_log, slot, queries.astype(F32))
            qa_ref[head, first : first + QB, :] = jnp.where(mine_block, queries, spare.astype(BF))


def backward_kernel(causal, bounds_ref, band_ref, qa_ref, k_ref, v_ref, g_ref, o_ref,
                    grad_ref, bias_ref, extra_q, extra_k, dk_acc, dv_acc, near_acc, side_acc):
    length = k_ref.shape[0]

    @pl.when(pl.program_id(0) == 0)
    def _():
        make_extras(bounds_ref, causal, extra_q, extra_k)

    lane, slot = lane_slots((QB, LANES))
    full_lane, full_slot = lane_slots((length, LANES))
    spare_v = jnp.where((full_slot >= 4) & (full_slot <= 6), 1.0, 0.0).astype(BF)
    for head in range(2):
        mine = (full_lane < DH) == (head == 0)
        mine_block = (lane < DH) == (head == 0)
        keys = jnp.where(mine, k_ref[...], extra_k[...])
        values = jnp.where(mine, v_ref[...], spare_v)
        if causal:
            near, side = band_square(band_ref, head)
            near, side = near.T, side.T
            near_only = jnp.full((LANES, LANES), masked_score, F32)
            near_acc[...] = jnp.zeros_like(near_acc)
            side_acc[...] = jnp.zeros_like(side_acc)
        dk_acc[...] = jnp.zeros_like(dk_acc)
        dv_acc[...] = jnp.zeros_like(dv_acc)
        for block in range(length // QB):
            first = block * QB
            count = first + QB if causal else length
            span = slice(first, first + QB)
            queries = qa_ref[head, span, :]
            upstream = g_ref[span, :]
            inner = jnp.sum(
                jnp.where(mine_block, upstream.astype(F32) * o_ref[span, :].astype(F32), 0.0), axis=1, keepdims=True
            )
            spare = place_three(-inner, slot, jnp.zeros((QB, LANES), F32))
            grads = jnp.where(mine_block, upstream, spare.astype(BF))
            scores = dot_t(keys[:count], queries)
            if causal:
                corner = jnp.concatenate([side, jnp.zeros((LANES, LANES), F32)], axis=1)
                upper = jnp.concatenate([near, side], axis=1)
                lower = jnp.concatenate([near_only, near], axis=1)
                pieces = []
                if block > 0:
                    if first > LANES:
                        pieces.append(scores[: first - LANES])
                    pieces.append(scores[first - LANES : first] + corner)
                pieces.append(scores[first : first + LANES] + upper)
                pieces.append(scores[first + LANES :] + lower)
                scores = jnp.concatenate(pieces, axis=0)
            probs = jnp.exp(scores)
            lifted = dot_t(values[:count], grads)
            score_grads = (probs * lifted).astype(BF)
            dv_acc[:count, :] += dot_n(probs.astype(BF), grads)
            dk_acc[:count, :] += dot_n(score_grads, queries)
            dq = dot_tn(score_grads, keys[:count])
            if causal:
                near_acc[...] += score_grads[first : first + LANES, :LANES].astype(F32)
                near_acc[...] += score_grads[first + LANES :, LANES:].astype(F32)
                side_acc[...] += score_grads[first : first + LANES, LANES:].astype(F32)
                if block > 0:
                    side_acc[...] += score_grads[first - LANES : first, :LANES].astype(F32)
            if head == 0:
                grad_ref[0, span, :] = dq.astype(BF)
            else:
                grad_ref[0, span, :] = jnp.where(lane < DH, grad_ref[0, span, :], dq.astype(BF))
        if head == 0:
            grad_ref[1] = dk_acc[...].astype(BF)
            grad_ref[2] = dv_acc[...].astype(BF)
        else:
            grad_ref[1] = jnp.where(full_lane < DH, grad_ref[1], dk_acc[...].astype(BF))
            grad_ref[2] = jnp.where(full_lane < DH, grad_ref[2], dv_acc[...].astype(BF))
        if causal:
            square = jnp.concatenate([side_acc[...], near_acc[...]], axis=0)
            wide = jnp.concatenate([square, jnp.zeros((2 * LANES, 2 * LANES), F32)], axis=1)
            half = LANES
            while half:
                wide = wide[:half] + pltpu.roll(wide[half:], 3 * LANES - half, 1)
                half //= 2
            diag = wide[:, 2 * LANES :]
            ones_column = jnp.where((full_lane % DH == 7) & ~mine, dk_acc[...], 0.0)
            whole = jnp.sum(ones_column, axis=0, keepdims=True)
            bias_ref[0, head : head + 1, :] = diag
            bias_ref[0, 2 + head : 3 + head, :] = whole


def attention_forward(causal, bounds, band, q, k, v, cols):
    rows = q[0].shape[0]
    pairs = cols // LANES

    def spec(offset):
        return pl.BlockSpec((rows, LANES), lambda p: (0, p + offset))

    n = rows * rows * pairs * 2
    return pl.pallas_call(
        functools.partial(forward_kernel, causal),
        grid=(pairs,),
        in_specs=[
            pl.BlockSpec(memory_space=pltpu.SMEM),
            pl.BlockSpec((None, 2, 3 * LANES), lambda p: (p, 0, 0)),
            spec(q[1]), spec(k[1]), spec(v[1]),
        ],
        out_specs=[
            pl.BlockSpec((rows, LANES), lambda p: (0, p)),
            pl.BlockSpec((2, rows, LANES), lambda p: (p, 0, 0)),
        ],
        out_shape=[
            jax.ShapeDtypeStruct((rows, cols), BF),
            jax.ShapeDtypeStruct((2 * pairs, rows, LANES), BF),
        ],
        scratch_shapes=[pltpu.VMEM((rows, LANES), BF), pltpu.VMEM((rows, LANES), BF)],
        compiler_params=pltpu.CompilerParams(vmem_limit_bytes=VMEM_LIMIT, dimension_semantics=("arbitrary",)),
        cost_estimate=pl.CostEstimate(flops=n * 256 * 4 // (2 if causal else 1), bytes_accessed=rows * cols * 16, transcendentals=n),
        name="attention_forward",
    )(bounds, band, q[0], k[0], v[0])


def attention_backward(causal, bounds, band, qa, k, v, g, o, cols):
    rows = qa.shape[1]
    pairs = cols // LANES

    def spec(offset):
        return pl.BlockSpec((rows, LANES), lambda p: (0, p + offset))

    n = rows * rows * pairs * 2
    return pl.pallas_call(
        functools.partial(backward_kernel, causal),
        grid=(pairs,),
        in_specs=[
            pl.BlockSpec(memory_space=pltpu.SMEM),
            pl.BlockSpec((None, 2, 3 * LANES), lambda p: (p, 0, 0)),
            pl.BlockSpec((2, rows, LANES), lambda p: (p, 0, 0)),
            spec(k[1]), spec(v[1]), spec(0), spec(0),
        ],
        out_specs=[
            pl.BlockSpec((3, rows, LANES), lambda p: (0, 0, p)),
            pl.BlockSpec((1, 8, LANES), lambda p: (p, 0, 0)),
        ],
        out_shape=[
            jax.ShapeDtypeStruct((3, rows, cols), BF),
            jax.ShapeDtypeStruct((pairs, 8, LANES), F32),
        ],
        scratch_shapes=[
            pltpu.VMEM((rows, LANES), BF), pltpu.VMEM((rows, LANES), BF),
            pltpu.VMEM((rows, LANES), F32), pltpu.VMEM((rows, LANES), F32),
            pltpu.VMEM((LANES, LANES), F32), pltpu.VMEM((LANES, LANES), F32),
        ],
        compiler_params=pltpu.CompilerParams(vmem_limit_bytes=VMEM_LIMIT, dimension_semantics=("arbitrary",)),
        cost_estimate=pl.CostEstimate(flops=n * 256 * 10 // (2 if causal else 1), bytes_accessed=rows * cols * 20, transcendentals=n),
        name="attention_backward",
    )(bounds, band, qa, k[0], v[0], g, o)


def bucket_table(length, buckets, reach):
    offsets = np.arange(length)
    exact_part = buckets // 2
    scaled = np.log(np.maximum(offsets, 1) / exact_part) / np.log(reach / exact_part) * (buckets - exact_part)
    far_bucket = np.minimum(exact_part + np.floor(scaled).astype(np.int64), buckets - 1)
    return np.where(offsets < exact_part, offsets, far_bucket).astype(np.int32)


def bias_band(rel_table):
    distance = LANES - np.arange(3 * LANES)
    buckets = bucket_table(LANES + 1, NB, REACH)
    onehot = np.zeros((3 * LANES, NB), np.float32)
    shift = np.zeros((3 * LANES,), np.float32)
    for at, far in enumerate(distance):
        if 0 <= far < LANES:
            onehot[at, buckets[far]] = 1.0
        elif -LANES < far < 0:
            shift[at] = masked_score
    relative = rel_table - rel_table[NB - 1 :]
    band = jnp.dot(jnp.asarray(onehot), relative, precision=lax.Precision.HIGHEST) + shift[:, None]
    return band.T.reshape(-1, 2, 3 * LANES)


def table_gradient(sums):
    buckets = bucket_table(LANES, NB, REACH)
    near = (buckets[:, None] == np.arange(NB)[None, :]) & (buckets[:, None] < NB - 1)
    diag = sums[:, 0:2].reshape(-1, LANES)
    whole = jnp.sum(sums[:, 2:4].reshape(-1, LANES), axis=-1)
    table = jnp.dot(diag, jnp.asarray(near.astype(np.float32)), precision=lax.Precision.HIGHEST)
    last = whole - jnp.sum(table, axis=-1)
    table = table + last[:, None] * jnp.asarray((np.arange(NB) == NB - 1).astype(np.float32))
    return table.T


epsilon = 1e-06


def norm_forward(values, gain):
    inverse = lax.rsqrt(jnp.mean(values * values, axis=-1, keepdims=True) + epsilon)
    return (values * inverse * gain).astype(BF), inverse


def norm_backward(values, inverse, gain, upstream):
    weighted = upstream * gain
    inner_mean = jnp.mean(weighted * values, axis=-1, keepdims=True)
    grad_values = inverse * weighted - values * inverse * inverse * inverse * inner_mean
    return grad_values, jnp.sum(upstream * values * inverse, axis=0)


def mm(a, b, dims, kind=F32):
    return lax.dot_general(a, b, ((dims[0], dims[1]), ((), ())), preferred_element_type=F32).astype(kind)


def nn(a, b, kind=F32):
    return mm(a, b, ((1,), (0,)), kind)


def nt(a, b, kind=F32):
    return mm(a, b, ((1,), (1,)), kind)


def tn(a, b, kind=F32):
    return mm(a, b, ((0,), (0,)), kind)


def whole_row(pair_rows, me, size):
    kept = lax.dynamic_index_in_dim(pair_rows, me, 0, False)
    sent = lax.dynamic_index_in_dim(pair_rows, 1 - me, 0, False)
    came = lax.ppermute(sent, "mp", [(0, 1), (1, 0)])
    return jnp.where(me == 0, jnp.concatenate([kept, came]), jnp.concatenate([came, kept]))


def row_halves(row, me):
    halves = row.reshape(2, row.shape[0] // 2, row.shape[1])
    kept = lax.dynamic_index_in_dim(halves, me, 0, False)
    sent = lax.dynamic_index_in_dim(halves, 1 - me, 0, False)
    came = lax.ppermute(sent.astype(BF), "mp", [(0, 1), (1, 0)]).astype(F32)
    return jnp.where(me == 0, jnp.stack([kept, came]), jnp.stack([came, kept]))


def gather_weights(shard):
    n, rows, cols = shard.shape
    pieces = lax.all_gather(shard, ("dp", "mp"), axis=0)
    dp = lax.axis_size("dp")
    mp = lax.axis_size("mp")
    pieces = pieces.reshape(dp, mp, n, rows, cols).transpose(2, 0, 3, 1, 4)
    return pieces.reshape(n, dp * rows, mp * cols)


def scatter_grads(grads):
    dp = lax.axis_size("dp")
    mp = lax.axis_size("mp")
    n, rows, cols = grads.shape
    pieces = grads.astype(BF).reshape(n, dp, rows // dp, mp, cols // mp).transpose(1, 3, 0, 2, 4)
    pieces = pieces.reshape(dp * mp, n, rows // dp, cols // mp)
    return lax.psum_scatter(pieces, ("dp", "mp"), scatter_dimension=0, tiled=True)[0].astype(F32)


def per_device(
    tokens,
    memory,
    doc_lengths,
    mem_lengths,
    norm_gains,
    rel_table,
    self_proj,
    self_out,
    cross_proj,
    cross_out,
    ffn_proj,
    ffn_out,
    cotangent,
):
    me = lax.axis_index("mp")
    width = tokens.shape[2]
    docs = lax.dynamic_index_in_dim(doc_lengths, me, 0, False)
    mem_length = lax.dynamic_slice_in_dim(mem_lengths, me, 1, 0)
    band = bias_band(rel_table)

    w_self = gather_weights(self_proj)
    w_mid = gather_weights(jnp.concatenate([self_out.T[None], cross_proj, cross_out.T[None]]))
    w_ffn = gather_weights(jnp.concatenate([ffn_proj, ffn_out.T[None]]))

    resid_in = whole_row(tokens, me, None).astype(F32)
    memory_row = whole_row(memory, me, None)
    cot_row = whole_row(cotangent, me, None)
    padding = (jnp.arange(ROW, dtype=jnp.int32) >= jnp.sum(docs))[:, None]

    normed_one, inverse_one = norm_forward(resid_in, norm_gains[0])
    qkv = jnp.concatenate([nn(normed_one, w_self[s], BF) for s in range(3)], axis=1)
    mixed_self, qa_self = attention_forward(True, docs, band, (qkv, 0), (qkv, 6), (qkv, 12), width)
    resid_two = resid_in + nt(mixed_self, w_mid[0])
    normed_two, inverse_two = norm_forward(resid_two, norm_gains[1])
    query_cross = nn(normed_two, w_mid[1], BF)
    key_cross = nn(memory_row, w_mid[2], BF)
    value_cross = nn(memory_row, w_mid[3], BF)
    mixed_cross, qa_cross = attention_forward(
        False, mem_length, band, (query_cross, 0), (key_cross, 0), (value_cross, 0), width
    )
    resid_three = resid_two + nt(mixed_cross, w_mid[4])
    normed_three, inverse_three = norm_forward(resid_three, norm_gains[2])
    gate = nn(normed_three, w_ffn[0])
    up = nn(normed_three, w_ffn[1])
    activated, gelu_pull = jax.vjp(lambda x: jax.nn.gelu(x, approximate=True), gate)
    hidden = (activated * up).astype(BF)
    output = jnp.where(padding, 0.0, resid_three + nt(hidden, w_ffn[2]))
    output = row_halves(output, me)

    grad_four = jnp.where(padding, 0.0, cot_row.astype(F32))
    branch = grad_four.astype(BF)
    grad_ffn_out = tn(branch, hidden, BF)
    grad_hidden = nn(branch, w_ffn[2])
    grad_gate = gelu_pull(grad_hidden * up)[0].astype(BF)
    grad_up = (grad_hidden * activated).astype(BF)
    ffn_grads = scatter_grads(
        jnp.stack([tn(normed_three, grad_gate, BF), tn(normed_three, grad_up, BF), grad_ffn_out])
    )
    upstream = nt(grad_gate, w_ffn[0]) + nt(grad_up, w_ffn[1])
    grad_resid, gain_three = norm_backward(resid_three, inverse_three, norm_gains[2], upstream)
    grad_three = grad_four + grad_resid

    branch = grad_three.astype(BF)
    grad_cross_out = tn(branch, mixed_cross, BF)
    grad_mixed = nn(branch, w_mid[4], BF)
    grads_cross, _ = attention_backward(
        False, mem_length, band, qa_cross, (key_cross, 0), (value_cross, 0), grad_mixed, mixed_cross, width
    )
    grad_memory = row_halves(nt(grads_cross[1], w_mid[2]) + nt(grads_cross[2], w_mid[3]), me)
    upstream = nt(grads_cross[0], w_mid[1])
    grad_resid, gain_two = norm_backward(resid_two, inverse_two, norm_gains[1], upstream)
    grad_two = grad_three + grad_resid

    branch = grad_two.astype(BF)
    grad_self_out = tn(branch, mixed_self, BF)
    mid_grads = scatter_grads(
        jnp.stack(
            [
                grad_self_out,
                tn(normed_two, grads_cross[0], BF),
                tn(memory_row, grads_cross[1], BF),
                tn(memory_row, grads_cross[2], BF),
                grad_cross_out,
            ]
        )
    )
    grad_mixed = nn(branch, w_mid[0], BF)
    grads_self, sums = attention_backward(
        True, docs, band, qa_self, (qkv, 6), (qkv, 12), grad_mixed, mixed_self, width
    )
    self_grads = scatter_grads(jnp.stack([tn(normed_one, grads_self[s], BF) for s in range(3)]))
    upstream = sum(nt(grads_self[s], w_self[s]) for s in range(3))
    grad_resid, gain_one = norm_backward(resid_in, inverse_one, norm_gains[0], upstream)
    grad_tokens = row_halves(grad_two + grad_resid, me)
    grad_gains, table = lax.psum(
        (jnp.stack([gain_one, gain_two, gain_three]), table_gradient(sums)), ("dp", "mp")
    )
    return (
        output,
        grad_tokens,
        grad_memory,
        grad_gains,
        table,
        self_grads,
        mid_grads[0].T,
        mid_grads[1:4],
        mid_grads[4].T,
        ffn_grads[:2],
        ffn_grads[2].T,
    )


def solution(mesh):
    rows = P("dp", "mp", None)
    proj = P(None, "dp", "mp")
    out = P("mp", "dp")
    return jax.shard_map(
        per_device,
        mesh=mesh,
        in_specs=(rows, rows, P("dp", None), P("dp"), P(), P(), proj, out, proj, out, proj, out, rows),
        out_specs=(rows, rows, rows, P(), P(), proj, out, proj, out, proj, out),
        check_vma=False,
    )
```

time: 5140 us -> 809 us (0.16)
  local copies, waits for them, and re-layouts: 3770 us -> 144 us
  waiting for transfers between devices: 601 us -> 219 us
  matrix products: 415 us -> 152 us
  other arithmetic: 203 us -> 56.6 us
  Pallas kernels: 0 us -> 132 us
    gather x4 -> x0, local copies, waits for them, and re-layouts: 2790 us -> none  [extra_fn(): return jnp.take(dist_heads, offsets_at(first_row, key_count), axis=1)]
    unnamed x537 -> x137, local copies, waits for them, and re-layouts: 827 us -> 15.4 us
    dot_general x99 -> x35, matrix products: 415 us -> 152 us  [the longest x33 152 us: mm(): lax.dot_general(a, b, ((dims[0], dims[1]), ((), ())), preferred_element_t...]
    all_gather x18 -> x3, waiting for transfers between devices: 294 us -> 86.8 us  [gather_weights(): pieces = lax.all_gather(shard, ('dp', 'mp'), axis=0)]
    reduce_scatter x18 -> x3, waiting for transfers between devices: 301 us -> 120 us  [scatter_grads(): lax.psum_scatter(pieces, ('dp', 'mp'), scatter_dimension=0, tiled=True)[0]]
    pallas_call x0 -> x4, Pallas kernels: none -> 132 us  [the longest x2 67.1 us: attention_backward(): pl.pallas_call(functools.partial(backward_kernel, causal), grid=(pairs,),...]
    convert_element_type x4 -> x3, local copies, waits for them, and re-layouts: 108 us -> 2.92 us  [row_halves(): came = lax.ppermute(sent.astype(BF), 'mp', [(0, 1), (1, 0)]).astype(F32)]
    convert_element_type x14 -> x4, other arithmetic: 93.8 us -> 5.12 us  [the longest x3 3.59 us: scatter_grads(): lax.psum_scatter(pieces, ('dp', 'mp'), scatter_dimension=0, tiled=True)[0]]
  transfers between devices with their start and end apart: 37 -> 12, of which waited for: 21 -> 5; matrix products, arithmetic and copies ran while one was open for 84% -> 33% of each run, Pallas kernels for 0% -> 8%
where the time goes in v1:
time: 809 us; the launch traced here: 803 us
  waiting for transfers between devices  219 us (27%)
  matrix products  152 us (19%)
  local copies, waits for them, and re-layouts  144 us (18%)
  Pallas kernels  132 us (16%)
  blocking collectives  75.3 us (9%)
  other arithmetic  56.6 us (7%)
  between operations  15.7 us (2%)
  starting transfers between devices  8.43 us (1%)
    dot_general x33, matrix products, mm(): lax.dot_general(a, b, ((dims[0], dims[1]), ((), ())), preferred_element_t...  152 us
    reduce_scatter x3, waiting for transfers between devices, scatter_grads(): lax.psum_scatter(pieces, ('dp', 'mp'), scatter_dimension=0, tiled=True)[0]  120 us
    all_gather x3, waiting for transfers between devices, gather_weights(): pieces = lax.all_gather(shard, ('dp', 'mp'), axis=0)  86.8 us
    psum x1, blocking collectives, per_device(): lax.psum((jnp.stack([gain_one, gain_two, gain_three]), table_gradient(sum...  75.3 us
    pallas_call x2, Pallas kernels, attention_backward(): pl.pallas_call(functools.partial(backward_kernel, causal), grid=(pairs,),...  67.1 us
    pallas_call x2, Pallas kernels, attention_forward(): pl.pallas_call(functools.partial(forward_kernel, causal), grid=(pairs,),...  64.7 us
    reshape x3, local copies, waits for them, and re-layouts, gather_weights(): pieces = pieces.reshape(dp, mp, n, rows, cols).transpose(2, 0, 3, 1, 4)  31.5 us
    transpose x2, other arithmetic, scatter_grads(): grads.astype(BF).reshape(n, dp, rows // dp, mp, cols // mp)  26.5 us
  transfers between devices with their start and end apart: 12, of which 5 were waited for; matrix products, arithmetic and copies ran while one was open for 33% of the time, Pallas kernels for 8%

profile of v1, /device:TPU:0, one launch (start us, length us, event | category | flops | bytes accessed | tf_op | source)
XLA Modules:
  0.0 803.1 jit_solution(9252332312061156343)
XLA Ops:
  25.3 11.1 %collective-permute-done = bf16[512,768]{1,0:T(8,128)(2,1)S(1)} collective-permute-done((bf16[512,768]{1,0:T(8,128)(2,1)}, bf16[512,768]{1,0:T(8,128)(2,1)S(1)}, u32[]{:S(2)}, u32[]{:S(2)}) %collective-permute-start) | collective-permute-done | bytes 786464 | tf_op jit(solution)/shard_map/ppermute | solution.py:348
  37.0 44.9 %all-gather.7.cloned.1.call-done = bf16[96,48,384]{2,1,0:T(8,128)(2,1)} async-done(((bf16[3,48,384]{2,1,0:T(8,128)(2,1)}), bf16[96,48,384]{2,1,0:T(8,128)(2,1)}) %all-gather.7.cloned.1.call-update) | async-done | bytes 3538960 | tf_op jit(solution)/shard_map/all_gather | solution.py:362
  98.2 29.2 %attention_forward.2 = (bf16[1024,768]{1,0:T(8,128)(2,1)}, bf16[12,1024,128]{2,1,0:T(8,128)(2,1)}) custom-call(s32[3]{0:T(128)} %get-tuple-element.61.bounds_ref, f32[6,2,384]{2,1,0:T(2,128)} %reshape.171.band_ref, bf16[1024,2304]{1,0:T(8,128)(2,1)} %pad_maximum_fusion.q_ref.k_ref.v_ref, bf16[1024,2304]{1,0:T(8,128)(2,1)} %pad_maximum_fusion.q_ref.k_ref.v_ref, ...), custom_call_target="tpu_custom_call" | custom-call | flops 6442450944 | bytes 12582912 | tf_op jit(solution)/shard_map/attention_forward/pallas_call | solution.py:221
  127.4 24.3 %all-gather.9.cloned.1.call-done = bf16[160,48,384]{2,1,0:T(8,128)(2,1)} async-done(((bf16[5,48,384]{2,1,0:T(8,128)(2,1)}), bf16[160,48,384]{2,1,0:T(8,128)(2,1)}) %all-gather.9.cloned.1.call-update) | async-done | bytes 5898256 | tf_op jit(solution)/shard_map/all_gather | solution.py:362
  151.7 9.0 %copy.70 = bf16[16,2,5,48,384]{4,1,3,0,2:T(2,128)(2,1)S(1)} copy(bf16[16,2,5,48,384]{4,3,2,1,0:T(8,128)(2,1)} %bitcast.215) | data formatting | bytes 11796480 | tf_op jit(solution)/shard_map/reshape | solution.py:365
  178.7 35.6 %attention_forward.3 = (bf16[1024,768]{1,0:T(8,128)(2,1)}, bf16[12,1024,128]{2,1,0:T(8,128)(2,1)}) custom-call(s32[1]{0:T(128)} %dynamic_slice.48.bounds_ref, f32[6,2,384]{2,1,0:T(2,128)} %reshape.171.band_ref, bf16[1024,768]{1,0:T(8,128)(2,1)} %convolution_convert_fusion.7.q_ref, bf16[1024,768]{1,0:T(8,128)(2,1)} %convolution_convert_fusion.6.k_ref, ...), custom_call_target="tpu_custom_call" | custom-call | flops 12884901888 | bytes 12582912 | tf_op jit(solution)/shard_map/attention_forward/pallas_call | solution.py:221
  218.7 17.6 %all-gather.11.cloned.1.call-done = bf16[96,48,1024]{2,1,0:T(8,128)(2,1)} async-done(((bf16[3,48,1024]{2,1,0:T(8,128)(2,1)}), bf16[96,48,1024]{2,1,0:T(8,128)(2,1)}) %all-gather.11.cloned.1.call-update) | async-done | bytes 9437200 | tf_op jit(solution)/shard_map/all_gather | solution.py:362
  236.3 17.6 %copy.69 = bf16[16,2,3,48,1024]{4,1,3,0,2:T(2,128)(2,1)S(1)} copy(bf16[16,2,3,48,1024]{4,3,2,1,0:T(8,128)(2,1)} %bitcast.213) | data formatting | bytes 18874368 | tf_op jit(solution)/shard_map/reshape | solution.py:365
  253.9 9.8 %fusion.93 = (bf16[1,16,48,2,1024]{4,3,2,1,0:T(2,128)(2,1)S(1)}, bf16[1,16,48,2,1024]{4,3,2,1,0:T(2,128)(2,1)S(1)}, bf16[1,16,48,2,1024]{4,3,2,1,0:T(2,128)(2,1)S(1)}) fusion(bf16[3,16,48,2,1024]{4,3,2,1,0:T(2,128)(2,1)S(1)} %bitcast.201), kind=kLoop, calls=%fused_computation.168 | loop fusion | bytes 18874368 | tf_op jit(solution)/shard_map/slice | solution.py:425
  265.0 5.7 fusion.98
  272.9 5.7 fusion.97
  278.6 18.0 %multiply_convert_fusion = (bf16[1024,2048]{1,0:T(8,128)(2,1)}, bf16[1024,2048]{1,0:T(8,128)(2,1)}, bf16[1024,2048]{1,0:T(8,128)(2,1)}) fusion(f32[1024,2048]{1,0:T(8,128)} %fusion.97, f32[1024,2048]{1,0:T(8,128)} %fusion.98, bf16[768,2048]{1,0:T(8,128)(2,1)S(1)} %bitcast.229, pred[1024]{0:T(1024)(128)(4,1)S(1)} %iota_compare_fusion, ...), kind=kOutput, calls=%fused_computation.11 | convolution fusion | flops 3285188608 | bytes 34079744 | tf_op jit(solution)/shard_map/dot_general | solution.py:330
  296.6 6.4 fusion.99
  313.5 38.6 %attention_backward.2 = (bf16[3,1024,768]{2,1,0:T(8,128)(2,1)}, f32[6,8,128]{2,1,0:T(8,128)}) custom-call(s32[1]{0:T(128)} %dynamic_slice.48.bounds_ref, f32[6,2,384]{2,1,0:T(2,128)} %reshape.171.band_ref, bf16[12,1024,128]{2,1,0:T(8,128)(2,1)} %get-tuple-element.20.qa_ref, bf16[1024,768]{1,0:T(8,128)(2,1)} %convolution_convert_fusion.6.k_ref, ...), custom_call_target="tpu_custom_call" | custom-call | flops 32212254720 | bytes 15728640 | tf_op jit(solution)/shard_map/attention_backward/pallas_call | solution.py:252
  359.3 28.5 %attention_backward.3 = (bf16[3,1024,768]{2,1,0:T(8,128)(2,1)}, f32[6,8,128]{2,1,0:T(8,128)}) custom-call(s32[3]{0:T(128)} %get-tuple-element.61.bounds_ref, f32[6,2,384]{2,1,0:T(2,128)} %reshape.171.band_ref, bf16[12,1024,128]{2,1,0:T(8,128)(2,1)} %get-tuple-element.22.qa_ref, bf16[1024,2304]{1,0:T(8,128)(2,1)} %pad_maximum_fusion.q_ref.k_ref.v_ref, ...), custom_call_target="tpu_custom_call" | custom-call | flops 16106127360 | bytes 15728640 | tf_op jit(solution)/shard_map/attention_backward/pallas_call | solution.py:252
  395.4 5.0 fusion.47
  404.0 5.1 fusion.50
  412.6 8.3 %maximum_bitcast_fusion.1 = bf16[16,2,3,48,384]{4,1,3,0,2:T(2,128)(2,1)S(1)} fusion(bf16[1,16,48,2,384]{4,3,2,1,0:T(2,128)(2,1)} %stack.117, bf16[1,16,48,2,384]{4,3,2,1,0:T(2,128)(2,1)} %stack.116, bf16[1,16,48,2,384]{4,3,2,1,0:T(2,128)(2,1)} %stack.115), kind=kLoop, calls=%fused_computation.23 | loop fusion | flops 3538944 | bytes 7077888 | tf_op jit(solution)/shard_map/transpose | solution.py:373
  431.6 5.0 fusion.41
  448.8 4.9 fusion.53
  457.2 4.9 convolution_convert_fusion.12
  476.0 7.8 convolution_convert_fusion.2
  483.8 6.4 stack.125
  490.1 7.8 convolution_convert_fusion.1
  497.9 6.2 stack.126
  504.1 8.5 %convolution_convert_fusion = bf16[768,2048]{1,0:T(8,128)(2,1)} fusion(bf16[1024,2048]{1,0:T(8,128)(2,1)} %get-tuple-element.38, pred[1024]{0:T(1024)(128)(4,1)S(1)} %iota_compare_fusion, bf16[512,768]{1,0:T(8,128)(2,1)} %collective-permute-done.3, bf16[512,768]{1,0:T(8,128)(2,1)} %get-tuple-element.50, pred[]{:T(512)S(6)} %eq.2), kind=kOutput, calls=%fused_computation.25 | convolution fusion | flops 3232235520 | bytes 8913921 | tf_op jit(solution)/shard_map/dot_general | solution.py:330
  512.6 6.1 stack.127
  518.8 18.2 %maximum_bitcast_fusion = bf16[16,2,3,48,1024]{4,1,3,0,2:T(2,128)(2,1)} fusion(bf16[1,16,48,2,1024]{4,3,2,1,0:T(2,128)(2,1)} %stack.127, bf16[1,16,48,2,1024]{4,3,2,1,0:T(2,128)(2,1)} %stack.126, bf16[1,16,48,2,1024]{4,3,2,1,0:T(2,128)(2,1)} %stack.125), kind=kLoop, calls=%fused_computation.2 | loop fusion | flops 9437184 | bytes 18874368 | tf_op jit(solution)/shard_map/transpose | solution.py:373
  537.0 10.8 %copy.51 = bf16[16,2,3,48,1024]{4,3,2,1,0:T(8,128)(2,1)} copy(bf16[16,2,3,48,1024]{4,1,3,0,2:T(2,128)(2,1)} %maximum_bitcast_fusion) | data formatting | bytes 18874368 | tf_op jit(solution)/shard_map/transpose | solution.py:373
  547.9 6.6 add_select_fusion
  581.5 75.3 %all-reduce = (f32[3,768]{1,0:T(4,128)}, f32[32,12]{0,1:T(8,128)}) all-reduce(f32[3,768]{1,0:T(4,128)S(1)} %pad_maximum_fusion.3, f32[32,12]{0,1:T(8,128)S(1)} %bitcast_add_fusion), channel_id=1, replica_groups=mesh['dp'=16,'mp'=2] {'dp','mp'}, use_global_device_ids=true, to_apply=%region_10.11 | all-reduce | flops 2688 | bytes 21504 | tf_op jit(solution)/shard_map/psum | solution.py:473
  673.4 120.0 %reduce-scatter.8.cloned.1.call-done = bf16[1,3,48,1024]{3,2,1,0:T(8,128)(2,1)} async-done(((bf16[32,3,48,1024]{3,2,1,0:T(8,128)(2,1)}), bf16[1,3,48,1024]{3,2,1,0:T(8,128)(2,1)}) %reduce-scatter.8.cloned.1.call-update) | async-done | bytes 294928 | tf_op jit(solution)/shard_map/reduce_scatter | solution.py:375
  (249 shorter events, 178.6 us)
Async XLA Ops:
  7.2 9.8 %copy-start.29 = (bf16[2,512,768]{2,1,0:T(8,128)(2,1)S(1)}, bf16[2,512,768]{2,1,0:T(8,128)(2,1)}, u32[]{:S(2)}) copy-start(bf16[2,512,768]{2,1,0:T(8,128)(2,1)} %param.18) | copy-start | bytes 4718596
  7.2 74.7 %all-gather.7.cloned.1.call-start = ((), (), s32[]{:S(2)}) async-start(), calls=%async_computation.6 | async-start | bytes 3649536 | tf_op jit(solution)/shard_map/all_gather | solution.py:362
  7.9 143.8 %all-gather.9.cloned.1.call-start = ((), (), s32[]{:S(2)}) async-start(), calls=%async_computation.7 | async-start | bytes 6082560 | tf_op jit(solution)/shard_map/all_gather | solution.py:362
  9.6 226.6 %all-gather.11.cloned.1.call-start = ((), (), s32[]{:S(2)}) async-start(), calls=%async_computation.8 | async-start | bytes 9732096 | tf_op jit(solution)/shard_map/all_gather | solution.py:362
  11.4 658.0 %reduce-scatter.4.cloned.1.call-start = ((), (), s32[]{:S(2)}) async-start(), calls=%async_computation.3 | async-start | bytes 3649536 | tf_op jit(solution)/shard_map/reduce_scatter | solution.py:375
  13.9 151.3 %copy-start.9 = (bf16[512,768]{1,0:T(8,128)(2,1)}, bf16[512,768]{1,0:T(8,128)(2,1)S(1)}, u32[]{:S(2)}) copy-start(bf16[512,768]{1,0:T(8,128)(2,1)S(1)} %get-tuple-element.55) | copy-start | bytes 2359300
  14.0 8.3 %copy-start.55 = (s32[2,3]{1,0:T(2,128)S(1)}, s32[2,3]{1,0:T(2,128)}, u32[]{:S(2)}) copy-start(s32[2,3]{1,0:T(2,128)} %param.19) | copy-start | bytes 76
  14.0 9.4 %copy-start.46 = (f32[32,12]{0,1:T(8,128)S(1)}, f32[32,12]{0,1:T(8,128)}, u32[]{:S(2)}) copy-start(f32[32,12]{0,1:T(8,128)} %param.22) | copy-start | bytes 4612
  14.0 9.6 %copy-start.44 = (f32[384,32]{1,0:T(8,128)S(1)}, f32[384,32]{1,0:T(8,128)}, u32[]{:S(2)}) copy-start(f32[384,32]{1,0:T(8,128)} %constant.76.clone) | copy-start | bytes 147460
  14.0 9.6 %copy-start.53 = (f32[384]{0:T(512)S(1)}, f32[384]{0:T(512)}, u32[]{:S(2)}) copy-start(f32[384]{0:T(512)} %constant.85) | copy-start | bytes 4612
  14.0 11.2 %copy-start.51 = (f32[3,768]{1,0:T(4,128)S(1)}, f32[3,768]{1,0:T(4,128)}, u32[]{:S(2)}) copy-start(f32[3,768]{1,0:T(4,128)} %param.21) | copy-start | bytes 27652
  14.0 22.4 %collective-permute-start = (bf16[512,768]{1,0:T(8,128)(2,1)}, bf16[512,768]{1,0:T(8,128)(2,1)S(1)}, u32[]{:S(2)}, u32[]{:S(2)}) collective-permute-start(bf16[512,768]{1,0:T(8,128)(2,1)} %get-tuple-element.54), channel_id=1, source_target_pairs={{0,1},{1,0},{2,3},{3,2},{4,5},{5,4},{6,7},{7,6},{8,9},{9,8},{10,11... | collective-permute-start | bytes 2359304 | tf_op jit(solution)/shard_map/ppermute | solution.py:348
  18.2 152.5 %collective-permute-start.1 = (bf16[512,768]{1,0:T(8,128)(2,1)}, bf16[512,768]{1,0:T(8,128)(2,1)}, u32[]{:S(2)}, u32[]{:S(2)}) collective-permute-start(bf16[512,768]{1,0:T(8,128)(2,1)} %get-tuple-element.53), channel_id=1, source_target_pairs={{0,1},{1,0},{2,3},{3,2},{4,5},{5,4},{6,7},{7,6},{8,9},{9,8},{10,11... | collective-permute-start | bytes 2359304 | tf_op jit(solution)/shard_map/ppermute | solution.py:348
  19.6 259.0 %collective-permute-start.3 = (bf16[512,768]{1,0:T(8,128)(2,1)}, bf16[512,768]{1,0:T(8,128)(2,1)}, u32[]{:S(2)}, u32[]{:S(2)}) collective-permute-start(bf16[512,768]{1,0:T(8,128)(2,1)} %get-tuple-element.51), channel_id=1, source_target_pairs={{0,1},{1,0},{2,3},{3,2},{4,5},{5,4},{6,7},{7,6},{8,9},{9,8},{10,11... | collective-permute-start | bytes 2359304 | tf_op jit(solution)/shard_map/ppermute | solution.py:348
  25.3 68.9 %copy-start.49 = (f32[768]{0:T(1024)}, f32[768]{0:T(1024)S(1)}, u32[]{:S(2)}) copy-start(f32[768]{0:T(1024)S(1)} %get-tuple-element.32) | copy-start | bytes 9220
  36.4 50.4 %copy-start.20 = (bf16[512,768]{1,0:T(8,128)(2,1)}, bf16[512,768]{1,0:T(8,128)(2,1)S(1)}, u32[]{:S(2)}) copy-start(bf16[512,768]{1,0:T(8,128)(2,1)S(1)} %collective-permute-done) | copy-start | bytes 2359300
  37.0 57.2 %copy-start.47 = (f32[1024]{0:T(1024)}, f32[1024]{0:T(1024)S(1)}, u32[]{:S(2)}) copy-start(f32[1024]{0:T(1024)S(1)} %add_rsqrt_fusion.2) | copy-start | bytes 12292
  167.0 47.2 %copy-start.2 = (f32[1024,768]{1,0:T(8,128)}, f32[1024,768]{1,0:T(8,128)S(1)}, u32[]{:S(2)}) copy-start(f32[1024,768]{1,0:T(8,128)S(1)} %get-tuple-element.63) | copy-start | bytes 9437188
  167.2 47.0 %copy-start.18 = (bf16[96,8,2,384]{3,1,2,0:T(8,128)(2,1)}, bf16[96,8,2,384]{3,1,2,0:T(8,128)(2,1)S(1)}, u32[]{:S(2)}) copy-start(bf16[96,8,2,384]{3,1,2,0:T(8,128)(2,1)S(1)} %copy.62) | copy-start | bytes 3538948
  313.5 38.6 %copy-start.3 = (f32[1024,768]{1,0:T(8,128)S(1)}, f32[1024,768]{1,0:T(8,128)}, u32[]{:S(2)}) copy-start(f32[1024,768]{1,0:T(8,128)} %copy-done.2) | copy-start | bytes 9437188
  313.5 38.6 %copy-start.42 = (bf16[96,8,2,384]{3,1,2,0:T(8,128)(2,1)S(1)}, bf16[96,8,2,384]{3,1,2,0:T(8,128)(2,1)}, u32[]{:S(2)}) copy-start(bf16[96,8,2,384]{3,1,2,0:T(8,128)(2,1)} %copy-done.41) | copy-start | bytes 3538948
  359.3 28.5 %copy-start.10 = (bf16[512,768]{1,0:T(8,128)(2,1)S(1)}, bf16[512,768]{1,0:T(8,128)(2,1)}, u32[]{:S(2)}) copy-start(bf16[512,768]{1,0:T(8,128)(2,1)} %copy-done.9) | copy-start | bytes 2359300
  359.3 28.5 %copy-start.23 = (bf16[512,768]{1,0:T(8,128)(2,1)S(1)}, bf16[512,768]{1,0:T(8,128)(2,1)}, u32[]{:S(2)}) copy-start(bf16[512,768]{1,0:T(8,128)(2,1)} %copy-done.20) | copy-start | bytes 2359300
  359.3 28.5 %copy-start.48 = (f32[1024]{0:T(1024)S(1)}, f32[1024]{0:T(1024)}, u32[]{:S(2)}) copy-start(f32[1024]{0:T(1024)} %copy-done.47) | copy-start | bytes 12292
  359.3 28.5 %copy-start.50 = (f32[768]{0:T(1024)S(1)}, f32[768]{0:T(1024)}, u32[]{:S(2)}) copy-start(f32[768]{0:T(1024)} %copy-done.49) | copy-start | bytes 9220
  423.2 247.9 %reduce-scatter.6.cloned.1.call-start = ((), (), s32[]{:S(2)}) async-start(), calls=%async_computation.4 | async-start | bytes 6082560 | tf_op jit(solution)/shard_map/reduce_scatter | solution.py:375
  475.9 317.5 %reduce-scatter.8.cloned.1.call-start = ((), (), s32[]{:S(2)}) async-start(), calls=%async_computation.5 | async-start | bytes 9732096 | tf_op jit(solution)/shard_map/reduce_scatter | solution.py:375
  547.9 10.7 %copy-start.52 = (f32[6,8,128]{2,1,0:T(8,128)S(1)}, f32[6,8,128]{2,1,0:T(8,128)}, u32[]{:S(2)}) copy-start(f32[6,8,128]{2,1,0:T(8,128)} %get-tuple-element.24) | copy-start | bytes 73732
  557.2 102.8 %collective-permute-start.2 = (bf16[512,768]{1,0:T(8,128)(2,1)}, bf16[512,768]{1,0:T(8,128)(2,1)}, u32[]{:S(2)}, u32[]{:S(2)}) collective-permute-start(bf16[512,768]{1,0:T(8,128)(2,1)} %fusion.71), channel_id=1, source_target_pairs={{0,1},{1,0},{2,3},{3,2},{4,5},{5,4},{6,7},{7,6},{8,9},{9,8},{10,11... | collective-permute-start | bytes 2359304 | tf_op jit(solution)/shard_map/ppermute | solution.py:356
  566.2 96.9 %collective-permute-start.5 = (bf16[512,768]{1,0:T(8,128)(2,1)}, bf16[512,768]{1,0:T(8,128)(2,1)}, u32[]{:S(2)}, u32[]{:S(2)}) collective-permute-start(bf16[512,768]{1,0:T(8,128)(2,1)} %fusion.73), channel_id=1, source_target_pairs={{0,1},{1,0},{2,3},{3,2},{4,5},{5,4},{6,7},{7,6},{8,9},{9,8},{10,11... | collective-permute-start | bytes 2359304 | tf_op jit(solution)/shard_map/ppermute | solution.py:356
  577.4 80.9 %copy-start.7 = (f32[1024,768]{1,0:T(8,128)S(1)}, f32[1024,768]{1,0:T(8,128)}, u32[]{:S(2)}) copy-start(f32[1024,768]{1,0:T(8,128)} %copy-done.6) | copy-start | bytes 9437188
  580.0 86.2 %collective-permute-start.4 = (bf16[512,768]{1,0:T(8,128)(2,1)}, bf16[512,768]{1,0:T(8,128)(2,1)}, u32[]{:S(2)}, u32[]{:S(2)}) collective-permute-start(bf16[512,768]{1,0:T(8,128)(2,1)} %fusion.72), channel_id=1, source_target_pairs={{0,1},{1,0},{2,3},{3,2},{4,5},{5,4},{6,7},{7,6},{8,9},{9,8},{10,11... | collective-permute-start | bytes 2359304 | tf_op jit(solution)/shard_map/ppermute | solution.py:356
  (41 other events, 155.7 us)
Sparse Core Ops, SparseCore 0:
  10.9 70.8 all-gather.6
  85.4 66.2 all-gather.8
  155.2 81.0 all-gather.10
  423.3 101.5 reduce-scatter.3
  530.4 122.5 reduce-scatter.5
  658.7 134.5 reduce-scatter.7

commit v2 on v1

--- a/solution.py
+++ b/solution.py
@@ -126,8 +126,8 @@
             qa_ref[head, first : first + QB, :] = jnp.where(mine_block, queries, spare.astype(BF))
 
 
-def backward_kernel(causal, bounds_ref, band_ref, qa_ref, k_ref, v_ref, g_ref, o_ref,
-                    grad_ref, bias_ref, extra_q, extra_k, dk_acc, dv_acc, near_acc, side_acc):
+def backward_kernel(causal, extra, bounds_ref, band_ref, qa_ref, k_ref, v_ref, g_ref, o_ref, *rest):
+    grad_ref, bias_ref, extra_q, extra_k, dk_acc, dv_acc, near_acc, side_acc = rest[extra:]
     length = k_ref.shape[0]
 
     @pl.when(pl.program_id(0) == 0)
@@ -241,31 +241,31 @@
     )(bounds, band, q[0], k[0], v[0])
 
 
-def attention_backward(causal, bounds, band, qa, k, v, g, o, cols):
+def attention_backward(causal, bounds, band, qa, k, v, g, o, cols, start=0, stop=None, into=None):
     rows = qa.shape[1]
-    pairs = cols // LANES
+    pairs = (cols // LANES if stop is None else stop) - start
 
     def spec(offset):
-        return pl.BlockSpec((rows, LANES), lambda p: (0, p + offset))
+        return pl.BlockSpec((rows, LANES), lambda p: (0, p + offset + start))
 
     n = rows * rows * pairs * 2
+    shape = jax.ShapeDtypeStruct((3, rows, cols), BF)
+    extra = [] if into is None else [into]
     return pl.pallas_call(
-        functools.partial(backward_kernel, causal),
+        functools.partial(backward_kernel, causal, len(extra)),
         grid=(pairs,),
         in_specs=[
             pl.BlockSpec(memory_space=pltpu.SMEM),
-            pl.BlockSpec((None, 2, 3 * LANES), lambda p: (p, 0, 0)),
-            pl.BlockSpec((2, rows, LANES), lambda p: (p, 0, 0)),
+            pl.BlockSpec((None, 2, 3 * LANES), lambda p: (p + start, 0, 0)),
+            pl.BlockSpec((2, rows, LANES), lambda p: (p + start, 0, 0)),
             spec(k[1]), spec(v[1]), spec(0), spec(0),
-        ],
+        ] + [pl.BlockSpec(memory_space=pl.ANY)] * len(extra),
         out_specs=[
-            pl.BlockSpec((3, rows, LANES), lambda p: (0, 0, p)),
+            pl.BlockSpec((3, rows, LANES), lambda p: (0, 0, p + start)),
             pl.BlockSpec((1, 8, LANES), lambda p: (p, 0, 0)),
         ],
-        out_shape=[
-            jax.ShapeDtypeStruct((3, rows, cols), BF),
-            jax.ShapeDtypeStruct((pairs, 8, LANES), F32),
-        ],
+        out_shape=[shape, jax.ShapeDtypeStruct((pairs, 8, LANES), F32)],
+        input_output_aliases={7: 0} if extra else {},
         scratch_shapes=[
             pltpu.VMEM((rows, LANES), BF), pltpu.VMEM((rows, LANES), BF),
             pltpu.VMEM((rows, LANES), F32), pltpu.VMEM((rows, LANES), F32),
@@ -274,7 +274,7 @@
         compiler_params=pltpu.CompilerParams(vmem_limit_bytes=VMEM_LIMIT, dimension_semantics=("arbitrary",)),
         cost_estimate=pl.CostEstimate(flops=n * 256 * 10 // (2 if causal else 1), bytes_accessed=rows * cols * 20, transcendentals=n),
         name="attention_backward",
-    )(bounds, band, qa, k[0], v[0], g, o)
+    )(bounds, band, qa, k[0], v[0], g, o, *extra)
 
 
 def bucket_table(length, buckets, reach):
@@ -310,69 +310,621 @@
     table = table + last[:, None] * jnp.asarray((np.arange(NB) == NB - 1).astype(np.float32))
     return table.T
 
-
 epsilon = 1e-06
-
-
-def norm_forward(values, gain):
+TB = 256
+
+
+def rms(values, gain):
     inverse = lax.rsqrt(jnp.mean(values * values, axis=-1, keepdims=True) + epsilon)
     return (values * inverse * gain).astype(BF), inverse
 
 
-def norm_backward(values, inverse, gain, upstream):
+def rms_back(values, inverse, gain, upstream):
     weighted = upstream * gain
     inner_mean = jnp.mean(weighted * values, axis=-1, keepdims=True)
-    grad_values = inverse * weighted - values * inverse * inverse * inverse * inner_mean
-    return grad_values, jnp.sum(upstream * values * inverse, axis=0)
-
-
-def mm(a, b, dims, kind=F32):
-    return lax.dot_general(a, b, ((dims[0], dims[1]), ((), ())), preferred_element_type=F32).astype(kind)
-
-
-def nn(a, b, kind=F32):
-    return mm(a, b, ((1,), (0,)), kind)
-
-
-def nt(a, b, kind=F32):
-    return mm(a, b, ((1,), (1,)), kind)
-
-
-def tn(a, b, kind=F32):
-    return mm(a, b, ((0,), (0,)), kind)
-
-
-def whole_row(pair_rows, me, size):
-    kept = lax.dynamic_index_in_dim(pair_rows, me, 0, False)
-    sent = lax.dynamic_index_in_dim(pair_rows, 1 - me, 0, False)
-    came = lax.ppermute(sent, "mp", [(0, 1), (1, 0)])
-    return jnp.where(me == 0, jnp.concatenate([kept, came]), jnp.concatenate([came, kept]))
-
-
-def row_halves(row, me):
-    halves = row.reshape(2, row.shape[0] // 2, row.shape[1])
-    kept = lax.dynamic_index_in_dim(halves, me, 0, False)
-    sent = lax.dynamic_index_in_dim(halves, 1 - me, 0, False)
-    came = lax.ppermute(sent.astype(BF), "mp", [(0, 1), (1, 0)]).astype(F32)
-    return jnp.where(me == 0, jnp.stack([kept, came]), jnp.stack([came, kept]))
-
-
-def gather_weights(shard):
+    grad_values = inverse * weighted - values * (inverse * inverse * inverse * inner_mean)
+    return grad_values, jnp.sum(upstream * values * inverse, axis=0, keepdims=True)
+
+
+def params():
+    return pltpu.CompilerParams(vmem_limit_bytes=VMEM_LIMIT, dimension_semantics=("arbitrary",))
+
+
+def held(shape):
+    zeros = (0,) * len(shape)
+    return pl.BlockSpec(shape, lambda s: zeros, pipeline_mode=pl.Buffered(1))
+
+
+def tokens_block(*lead):
+    zeros = (0,) * len(lead)
+
+    def spec(blocks, width):
+        return pl.BlockSpec(lead + (TB, width), lambda s: zeros + (jnp.minimum(s, blocks - 1), 0))
+
+    return spec
+
+
+def cost(flops, moved):
+    return pl.CostEstimate(flops=flops, bytes_accessed=moved, transcendentals=0)
+
+
+def piece_places():
+    return [(y, x, z0, c) for c in range(2) for z0 in range(2) for y in range(2) for x in range(2)]
+
+
+def relative_copies(ids_ref, pieces, place, sem):
+    mine = ids_ref[0]
+    count, rows, _ = pieces[0].shape[1:]
+
+    def copy(flip):
+        for piece, (y, x, z0, c) in zip(pieces, piece_places()):
+            for z1 in range(2):
+                block = jnp.bitwise_xor(mine, 8 * z1 + 4 * z0 + 2 * y + c)
+                span = pl.ds(pl.multiple_of(block * rows, 16), rows)
+                for n in range(count):
+                    pltpu.make_async_copy(piece.at[z1, n], place(n, span, x ^ flip), sem).start()
+
+    @pl.when(ids_ref[1] == 0)
+    def _():
+        copy(0)
+
+    @pl.when(ids_ref[1] == 1)
+    def _():
+        copy(1)
+
+
+def natural_place(w_ref, cols):
+    return lambda n, span, x: w_ref.at[n, span, x * cols : (x + 1) * cols]
+
+
+def plain_copies(w_in, w_ref, sem):
+    dp, mp, count, rows, cols = w_in.shape
+    for block in range(dp):
+        for x in range(mp):
+            for n in range(count):
+                target = w_ref.at[n, block * rows : (block + 1) * rows, x * cols : (x + 1) * cols]
+                pltpu.make_async_copy(w_in.at[block, x, n], target, sem).start()
+
+
+def project_kernel(pieces, ids_ref, gain_ref, x_ref, *refs):
+    w_in = refs[:pieces]
+    normed_ref, out_ref, w_ref, sem = refs[pieces:]
+
+    @pl.when(pl.program_id(0) == 0)
+    def _():
+        if pieces == 1:
+            whole = pltpu.make_async_copy(w_in[0], w_ref, sem)
+            whole.start()
+        else:
+            relative_copies(ids_ref, w_in, natural_place(w_ref, w_in[0].shape[-1]), sem)
+        pltpu.make_async_copy(w_ref, w_ref, sem).wait()
+
+    normed, _ = rms(x_ref[...].astype(F32), gain_ref[...])
+    normed_ref[...] = normed
+    width = x_ref.shape[1]
+    for s in range(3):
+        out_ref[:, s * width : (s + 1) * width] = dot_n(normed, w_ref[s]).astype(BF)
+
+
+def project(ids, gain, x, pieces):
+    rows, width = x.shape
+    blocks = rows // TB
+    spec = tokens_block()
+    full = (3, width, width)
+    shape = jax.ShapeDtypeStruct
+    return pl.pallas_call(
+        functools.partial(project_kernel, len(pieces)),
+        grid=(blocks,),
+        in_specs=[pl.BlockSpec(memory_space=pltpu.SMEM), held((1, width)), spec(blocks, width)]
+        + [pl.BlockSpec(memory_space=pl.ANY)] * len(pieces),
+        out_specs=[spec(blocks, width), spec(blocks, 3 * width), held(full)],
+        out_shape=[shape((rows, width), BF), shape((rows, 3 * width), BF), shape(full, BF)],
+        scratch_shapes=[pltpu.SemaphoreType.DMA],
+        compiler_params=params(),
+        cost_estimate=cost(6 * rows * width * width, 10 * rows * width + 6 * width * width),
+        name="project",
+    )(ids, gain, x, *pieces)
+
+
+def middle_kernel(gain_ref, x_ref, mixed_ref, memory_ref, w_in, resid_ref, normed_ref, q_ref, k_ref, v_ref, w_ref, sem):
+    @pl.when(pl.program_id(0) == 0)
+    def _():
+        if len(w_in.shape) == 3:
+            pltpu.make_async_copy(w_in, w_ref, sem).start()
+        else:
+            plain_copies(w_in, w_ref, sem)
+        pltpu.make_async_copy(w_ref, w_ref, sem).wait()
+
+    resid = x_ref[...].astype(F32) + dot_t(mixed_ref[...], w_ref[0])
+    resid_ref[...] = resid
+    normed, _ = rms(resid, gain_ref[...])
+    normed_ref[...] = normed
+    q_ref[...] = dot_n(normed, w_ref[1]).astype(BF)
+    memory = memory_ref[...]
+    k_ref[...] = dot_n(memory, w_ref[2]).astype(BF)
+    v_ref[...] = dot_n(memory, w_ref[3]).astype(BF)
+
+
+def middle(gain, x, mixed, memory, w):
+    rows, width = x.shape
+    blocks = rows // TB
+    spec = tokens_block()(blocks, width)
+    full = (5, width, width)
+    return pl.pallas_call(
+        middle_kernel,
+        grid=(blocks,),
+        in_specs=[held((1, width)), spec, spec, spec, pl.BlockSpec(memory_space=pl.ANY)],
+        out_specs=[spec] * 5 + [held(full)],
+        out_shape=[jax.ShapeDtypeStruct((rows, width), F32)] + [jax.ShapeDtypeStruct((rows, width), BF)] * 4
+        + [jax.ShapeDtypeStruct(full, BF)],
+        scratch_shapes=[pltpu.SemaphoreType.DMA],
+        compiler_params=params(),
+        cost_estimate=cost(8 * rows * width * width, 20 * rows * width + 10 * width * width),
+        name="middle",
+    )(gain, x, mixed, memory, w)
+
+
+def feed_kernel(blocks, pieces, ids_ref, docs_ref, gain_ref, resid_ref, mixed_ref, cot_ref, wo_ref, *refs):
+    w_in = refs[:pieces]
+    (out_ref, out_low_ref, grad_ref, gmix_ref, gain_grad_ref, wgrad_ref,
+     w_ref, normed_t, branch_t, hidden_s, gate_s, up_s, sem) = refs[pieces:]
+    step = pl.program_id(0)
+    width = resid_ref.shape[1]
+
+    def weight(which, x):
+        return w_ref[x, which]
+
+    @pl.when(step == 0)
+    def _():
+        if pieces == 1:
+            pltpu.make_async_copy(w_in[0], w_ref, sem).start()
+        else:
+            relative_copies(ids_ref, w_in, lambda n, span, x: w_ref.at[x, n, span], sem)
+        gain_grad_ref[...] = jnp.zeros_like(gain_grad_ref)
+        pltpu.make_async_copy(w_ref, w_ref, sem).wait()
+
+    @pl.when(step < blocks)
+    def _():
+        first = pl.multiple_of(step * TB, TB)
+        span = pl.ds(first, TB)
+        resid = resid_ref[...] + dot_t(mixed_ref[...], wo_ref[...])
+        normed, inverse = rms(resid, gain_ref[...])
+        slots = first + lax.broadcasted_iota(jnp.int32, (TB, 1), 0)
+        padding = slots >= docs_ref[0] + docs_ref[1] + docs_ref[2]
+        grad_four = jnp.where(padding, 0.0, cot_ref[...].astype(F32))
+        branch = grad_four.astype(BF)
+        normed_t[:, span] = normed.T
+        branch_t[:, span] = branch.T
+        total = resid
+        upstream = jnp.zeros((TB, width), F32)
+        for x in range(2):
+            gate = dot_n(normed, weight(0, x))
+            up = dot_n(normed, weight(1, x))
+            lifted = dot_n(branch, weight(2, x))
+            square = gate * gate
+            inner = jnp.tanh(gate * (0.7978845608028654 + 0.035677408136300125 * square))
+            half_up = 0.5 + 0.5 * inner
+            activated = gate * half_up
+            slope = half_up + (0.5 * gate) * (1.0 - inner * inner) * (
+                0.7978845608028654 + 0.10703222440890037 * square
+            )
+            hidden = (activated * up).astype(BF)
+            gate_grad = (lifted * up * slope).astype(BF)
+            up_grad = (lifted * activated).astype(BF)
+            hidden_s[x, span, :] = hidden
+            gate_s[x, span, :] = gate_grad
+            up_s[x, span, :] = up_grad
+            total = total + dot_t(hidden, weight(2, x))
+            upstream = upstream + dot_t(gate_grad, weight(0, x)) + dot_t(up_grad, weight(1, x))
+        output = jnp.where(padding, 0.0, total)
+        out_ref[...] = output
+        out_low_ref[...] = output.astype(BF)
+        grad_resid, gain_grad = rms_back(resid, inverse, gain_ref[...], upstream)
+        grad = grad_four + grad_resid
+        grad_ref[...] = grad
+        grad_low = grad.astype(BF)
+        gain_grad_ref[...] += gain_grad
+        gmix_ref[...] = dot_n(grad_low, wo_ref[...]).astype(BF)
+
+    for which, (left, right) in enumerate(((normed_t, gate_s), (normed_t, up_s), (branch_t, hidden_s))):
+        for x in range(2):
+
+            @pl.when(step == blocks + 2 * which + x)
+            def _():
+                wgrad = dot_n(left[...], right[x]).astype(BF)
+                wgrad_ref[...] = wgrad.reshape(wgrad_ref.shape)
+
+
+def feed(ids, docs, gain, resid, mixed, cot, wo, pieces, parts):
+    rows, width = resid.shape
+    half = pieces[0].shape[-1]
+    depth = width // parts
+    blocks = rows // TB
+    spec = tokens_block()(blocks, width)
+    shape = jax.ShapeDtypeStruct
+
+    def wgrad_at(s):
+        at = jnp.maximum(s - blocks, 0)
+        return (0, at % 2, at // 2, 0, 0)
+
+    return pl.pallas_call(
+        functools.partial(feed_kernel, blocks, len(pieces)),
+        grid=(blocks + 6,),
+        in_specs=[
+            pl.BlockSpec(memory_space=pltpu.SMEM), pl.BlockSpec(memory_space=pltpu.SMEM),
+            held((1, width)), spec, spec, spec, held(wo.shape),
+        ] + [pl.BlockSpec(memory_space=pl.ANY)] * len(pieces),
+        out_specs=[spec, spec, spec, spec, held((1, width)), pl.BlockSpec((parts, None, None, depth, half), wgrad_at)],
+        out_shape=[
+            shape((rows, width), F32),
+            shape((rows, width), BF),
+            shape((rows, width), F32),
+            shape((rows, width), BF),
+            shape((1, width), F32),
+            shape((parts, 2, 3, depth, half), BF),
+        ],
+        scratch_shapes=[pltpu.VMEM((2, 3, width, half), BF)] + [pltpu.VMEM((width, rows), BF)] * 2
+        + [pltpu.VMEM((2, rows, half), BF)] * 3 + [pltpu.SemaphoreType.DMA],
+        compiler_params=params(),
+        cost_estimate=cost(36 * rows * width * half, 24 * rows * width + 24 * width * half),
+        name="feed",
+    )(ids, docs, gain, resid, mixed, cot, wo, *pieces)
+
+
+def pack_blocks(ids_ref, full_ref, keep_ref, send_ref):
+    mine = ids_ref[0]
+    x_at = ids_ref[1]
+    n, rows, cols = keep_ref.shape[-3:]
+
+    def copy(flip):
+        for target, part in ((keep_ref, 0), (send_ref, 1)):
+            for y in range(2):
+                for z0 in range(2):
+                    for z1 in range(2):
+                        block = jnp.bitwise_xor(mine, 8 * z1 + 4 * z0 + 2 * y + part)
+                        span = pl.ds(pl.multiple_of(block * rows, 16), rows)
+                        for x in range(2):
+                            first = cols * (x ^ flip)
+                            target[y, x, z0, z1] = full_ref[:, span, first : first + cols]
+
+    @pl.when(x_at == 0)
+    def _():
+        copy(0)
+
+    @pl.when(x_at == 1)
+    def _():
+        copy(1)
+
+
+def packed_shapes(n, width):
+    return jax.ShapeDtypeStruct((2, 2, 2, 2, n, width // 16, width // 2), BF)
+
+
+def cross_back_kernel(blocks, packed, ids_ref, gain_ref, d_ref, resid_ref, normed_ref, memory_ref, grad_ref,
+                      mixed_cross_ref, mixed_self_ref, w_ref, *outs):
+    (grad_two_ref, gmix_ref, gmem_ref, gmem_low_ref, gain_grad_ref) = outs[:5]
+    rest = outs[5:]
+    if packed:
+        keep_ref, send_ref, full = rest[0], rest[1], rest[-1]
+        rest = rest[2:-1]
+    else:
+        full = rest[0]
+        rest = rest[1:]
+    lefts, rights = rest
+    step = pl.program_id(0)
+
+    @pl.when(step == 0)
+    def _():
+        gain_grad_ref[...] = jnp.zeros_like(gain_grad_ref)
+
+    @pl.when(step < blocks)
+    def _():
+        span = pl.ds(pl.multiple_of(step * TB, TB), TB)
+        resid = resid_ref[...]
+        inverse = lax.rsqrt(jnp.mean(resid * resid, axis=-1, keepdims=True) + epsilon)
+        grad_resid, gain_grad = rms_back(resid, inverse, gain_ref[...], dot_t(d_ref[0], w_ref[1]))
+        gain_grad_ref[...] += gain_grad
+        grad_three = grad_ref[...]
+        grad_two = grad_three + grad_resid
+        grad_two_ref[...] = grad_two
+        branch = grad_two.astype(BF)
+        gmix_ref[...] = dot_n(branch, w_ref[0]).astype(BF)
+        gmem = dot_t(d_ref[1], w_ref[2]) + dot_t(d_ref[2], w_ref[3])
+        gmem_ref[...] = gmem
+        gmem_low_ref[...] = gmem.astype(BF)
+        lefts[0, :, span] = branch.T
+        lefts[1, :, span] = normed_ref[...].T
+        lefts[2, :, span] = memory_ref[...].T
+        lefts[3, :, span] = grad_three.astype(BF).T
+        rights[0, span, :] = mixed_self_ref[...]
+        rights[1, span, :] = d_ref[0]
+        rights[2, span, :] = d_ref[1]
+        rights[3, span, :] = d_ref[2]
+        rights[4, span, :] = mixed_cross_ref[...]
+
+    for n, left in enumerate((0, 1, 2, 2, 3)):
+
+        @pl.when(step == blocks + n)
+        def _():
+            full[n] = dot_n(lefts[left], rights[n]).astype(BF)
+
+    if packed:
+
+        @pl.when(step == blocks + 4)
+        def _():
+            pack_blocks(ids_ref, full, keep_ref, send_ref)
+
+
+def cross_back(packed, ids, gain, d, resid, normed, memory, grad, mixed_cross, mixed_self, w):
+    rows, width = resid.shape
+    blocks = rows // TB
+    spec = tokens_block()(blocks, width)
+    shape = jax.ShapeDtypeStruct
+    full = shape((5, width, width), BF)
+    if packed:
+        extra = [packed_shapes(5, width)] * 2
+        scratch = [pltpu.VMEM(full.shape, BF)]
+    else:
+        extra = [full]
+        scratch = []
+    return pl.pallas_call(
+        functools.partial(cross_back_kernel, blocks, packed),
+        grid=(blocks + 5,),
+        in_specs=[
+            pl.BlockSpec(memory_space=pltpu.SMEM), held((1, width)), tokens_block(3)(blocks, width),
+            spec, spec, spec, spec, spec, spec, held(w.shape),
+        ],
+        out_specs=[spec, spec, spec, spec, held((1, width))] + [held(e.shape) for e in extra],
+        out_shape=[shape((rows, width), F32), shape((rows, width), BF), shape((rows, width), F32),
+                   shape((rows, width), BF), shape((1, width), F32)] + extra,
+        scratch_shapes=[pltpu.VMEM((4, width, rows), BF), pltpu.VMEM((5, rows, width), BF)] + scratch,
+        compiler_params=params(),
+        cost_estimate=cost(18 * rows * width * width, 36 * rows * width + 20 * width * width),
+        name="cross_back",
+    )(ids, gain, d, resid, normed, memory, grad, mixed_cross, mixed_self, w)
+
+
+def self_weights_kernel(packed, ids_ref, d_ref, normed_ref, *rest):
+    if packed:
+        keep_ref, send_ref, left, full = rest
+    else:
+        full, left = rest
+    step = pl.program_id(0)
+
+    @pl.when(step == 0)
+    def _():
+        left[...] = normed_ref[...].T
+
+    full[step] = dot_n(left[...], d_ref[...]).astype(BF)
+    if packed:
+
+        @pl.when(step == 2)
+        def _():
+            pack_blocks(ids_ref, full, keep_ref, send_ref)
+
+
+def self_weights(packed, ids, d, normed):
+    rows, width = normed.shape
+    full = jax.ShapeDtypeStruct((3, width, width), BF)
+    if packed:
+        outs = [packed_shapes(3, width)] * 2
+        scratch = [pltpu.VMEM(full.shape, BF)]
+    else:
+        outs = [full]
+        scratch = []
+    return pl.pallas_call(
+        functools.partial(self_weights_kernel, packed),
+        grid=(3,),
+        in_specs=[
+            pl.BlockSpec(memory_space=pltpu.SMEM),
+            pl.BlockSpec((None, rows, width), lambda s: (s, 0, 0)),
+            held((rows, width)),
+        ],
+        out_specs=[held(o.shape) for o in outs],
+        out_shape=outs,
+        scratch_shapes=[pltpu.VMEM((width, rows), BF)] + scratch,
+        compiler_params=params(),
+        cost_estimate=cost(6 * rows * width * width, 8 * rows * width + 6 * width * width),
+        name="self_weights",
+    )(ids, d, normed)
+
+
+def self_back_kernel(gain_ref, d_ref, x_ref, grad_ref, w_ref, out_ref, low_ref, gain_grad_ref):
+    @pl.when(pl.program_id(0) == 0)
+    def _():
+        gain_grad_ref[...] = jnp.zeros_like(gain_grad_ref)
+
+    values = x_ref[...].astype(F32)
+    inverse = lax.rsqrt(jnp.mean(values * values, axis=-1, keepdims=True) + epsilon)
+    upstream = dot_t(d_ref[0], w_ref[0]) + dot_t(d_ref[1], w_ref[1]) + dot_t(d_ref[2], w_ref[2])
+    grad_values, gain_grad = rms_back(values, inverse, gain_ref[...], upstream)
+    gain_grad_ref[...] += gain_grad
+    grad = grad_ref[...] + grad_values
+    out_ref[...] = grad
+    low_ref[...] = grad.astype(BF)
+
+
+def self_back(gain, d, x, grad, w):
+    rows, width = x.shape
+    blocks = rows // TB
+    spec = tokens_block()(blocks, width)
+    shape = jax.ShapeDtypeStruct
+    return pl.pallas_call(
+        self_back_kernel,
+        grid=(blocks,),
+        in_specs=[held((1, width)), tokens_block(3)(blocks, width), spec, spec, held(w.shape)],
+        out_specs=[spec, spec, held((1, width))],
+        out_shape=[shape((rows, width), F32), shape((rows, width), BF), shape((1, width), F32)],
+        compiler_params=params(),
+        cost_estimate=cost(6 * rows * width * width, 20 * rows * width + 6 * width * width),
+        name="self_back",
+    )(gain, d, x, grad, w)
+
+
+def flip_bit(values, bit):
+    size = lax.axis_size("dp")
+    return lax.ppermute(values, "dp", [(i, i ^ (1 << bit)) for i in range(size)])
+
+
+def flip_mp(values):
+    return lax.ppermute(values, "mp", [(0, 1), (1, 0)])
+
+
+def after(values, *others):
+    return lax.optimization_barrier((values, others))[0]
+
+
+class Gather:
+    def __init__(self, shard):
+        self.shard = shard
+
+    def first(self):
+        self.state = (flip_bit(self.shard, 3),)
+
+    def second(self):
+        self.low = jnp.stack([self.shard, self.state[0]])
+        self.state = (flip_bit(self.low, 2),)
+
+    def third(self):
+        (high,) = self.state
+        self.near = (self.low, high)
+        self.state = (flip_mp(self.low), flip_bit(high, 1), flip_bit(self.low, 0), flip_bit(high, 0))
+
+    def fourth(self):
+        low, high = self.near
+        low_x, high_y, low_c, high_c = self.state
+        self.near = (low, low_x, high, high_y, low_c, high_c)
+        self.state = (
+            flip_bit(low, 1), flip_bit(low_x, 1), flip_mp(high), flip_mp(high_y),
+            flip_bit(low_x, 0), flip_bit(high_y, 0),
+        )
+
+    def pieces(self):
+        low, low_x, high, high_y, low_c, high_c = self.near
+        low_y, low_xy, high_x, high_xy, low_x_c, high_y_c = self.state
+        return [
+            low, low_x, low_y, low_xy, high, high_x, high_y, high_xy,
+            low_c, low_x_c, flip_bit(low_y, 0), flip_bit(low_xy, 0),
+            high_c, flip_bit(high_x, 0), high_y_c, flip_bit(high_xy, 0),
+        ]
+
+
+class Scatter:
+    def __init__(self, keep, send):
+        self.keep = keep
+        self.send = send
+
+    def own(self, y, x, z0):
+        return self.keep[y, x, z0].astype(F32) + self.came[y, x, z0].astype(F32)
+
+    def first(self):
+        self.state = (flip_bit(self.send, 0),)
+
+    def second(self):
+        (self.came,) = self.state
+
+        def both(*parts):
+            return jnp.stack([p.astype(BF) for p in parts])
+
+        self.state = (
+            flip_bit(both(self.own(1, 0, 0), self.own(1, 1, 0)), 1),
+            flip_mp(both(self.own(0, 1, 1), self.own(1, 1, 1))),
+        )
+
+    def third(self):
+        low_y, high_x = self.state
+        self.kept = (low_y, high_x)
+        self.state = (
+            flip_mp((self.own(0, 1, 0) + low_y[1].astype(F32)).astype(BF)),
+            flip_bit((self.own(1, 0, 1) + high_x[1].astype(F32)).astype(BF), 1),
+        )
+
+    def fourth(self):
+        low_y, high_x = self.kept
+        low_x, high_y = self.state
+        high = self.own(0, 0, 1) + high_x[0].astype(F32) + high_y.astype(F32)
+        self.kept = self.own(0, 0, 0) + low_y[0].astype(F32) + low_x.astype(F32)
+        self.state = (flip_bit(high.astype(BF), 2),)
+
+    def fifth(self):
+        self.kept = self.kept + self.state[0].astype(F32)
+        self.state = (flip_bit(self.kept[1].astype(BF), 3),)
+
+    def total(self):
+        return self.kept[0] + self.state[0].astype(F32)
+
+
+def hold(value, *steps):
+    value, states = lax.optimization_barrier((value, [s.state for s in steps]))
+    for step, state in zip(steps, states):
+        step.state = state
+    return value
+
+
+def gather_plain(shard):
+    pieces = lax.all_gather(shard, ("dp", "mp"), axis=0)
+    return pieces.reshape((lax.axis_size("dp"), lax.axis_size("mp")) + shard.shape)
+
+
+def gather_whole(shard):
     n, rows, cols = shard.shape
-    pieces = lax.all_gather(shard, ("dp", "mp"), axis=0)
-    dp = lax.axis_size("dp")
-    mp = lax.axis_size("mp")
-    pieces = pieces.reshape(dp, mp, n, rows, cols).transpose(2, 0, 3, 1, 4)
-    return pieces.reshape(n, dp * rows, mp * cols)
-
-
-def scatter_grads(grads):
+    pieces = gather_plain(shard)
+    dp, mp = pieces.shape[:2]
+    return pieces.transpose(2, 0, 3, 1, 4).reshape(n, dp * rows, mp * cols)
+
+
+def scatter_plain(pieces):
+    flat = pieces.reshape((-1,) + pieces.shape[2:])
+    return lax.psum_scatter(flat, ("dp", "mp"), scatter_dimension=0, tiled=True)[0].astype(F32)
+
+
+def scatter_whole(grads):
     dp = lax.axis_size("dp")
     mp = lax.axis_size("mp")
     n, rows, cols = grads.shape
-    pieces = grads.astype(BF).reshape(n, dp, rows // dp, mp, cols // mp).transpose(1, 3, 0, 2, 4)
-    pieces = pieces.reshape(dp * mp, n, rows // dp, cols // mp)
-    return lax.psum_scatter(pieces, ("dp", "mp"), scatter_dimension=0, tiled=True)[0].astype(F32)
+    return scatter_plain(grads.reshape(n, dp, rows // dp, mp, cols // mp).transpose(1, 3, 0, 2, 4))
+
+
+class Sum:
+    def __init__(self, values):
+        self.held = values
+        self.state = None
+
+    def flip(self, bit):
+        if self.state is not None:
+            self.held = self.held + self.state
+        self.state = flip_bit(self.held, bit)
+
+    @property
+    def values(self):
+        return self.held if self.state is None else self.held + self.state
+
+
+class Swap:
+    def __init__(self, sent):
+        self.state = flip_mp(sent)
+
+
+def other_row(pair_rows, me):
+    return lax.dynamic_index_in_dim(pair_rows, 1 - me, 0, False)
+
+
+def whole_row(pair_rows, swap, me):
+    kept = lax.dynamic_index_in_dim(pair_rows, me, 0, False)
+    came = swap.state
+    return jnp.where(me == 0, jnp.concatenate([kept, came]), jnp.concatenate([came, kept]))
+
+
+def other_half(low, me):
+    half = low.shape[0] // 2
+    return lax.dynamic_slice_in_dim(low, (1 - me) * half, half, 0)
+
+
+def row_halves(row, swap, me):
+    half = row.shape[0] // 2
+    kept = lax.dynamic_slice_in_dim(row, me * half, half, 0)
+    came = swap.state.astype(F32)
+    return jnp.where(me == 0, jnp.stack([kept, came]), jnp.stack([came, kept]))
 
 
 def per_device(
@@ -391,94 +943,136 @@
     cotangent,
 ):
     me = lax.axis_index("mp")
+    dp = lax.axis_size("dp")
     width = tokens.shape[2]
+    packed = dp == 16 and lax.axis_size("mp") == 2
+    ids = jnp.stack([lax.axis_index("dp"), me]).astype(jnp.int32)
     docs = lax.dynamic_index_in_dim(doc_lengths, me, 0, False)
     mem_length = lax.dynamic_slice_in_dim(mem_lengths, me, 1, 0)
     band = bias_band(rel_table)
-
-    w_self = gather_weights(self_proj)
-    w_mid = gather_weights(jnp.concatenate([self_out.T[None], cross_proj, cross_out.T[None]]))
-    w_ffn = gather_weights(jnp.concatenate([ffn_proj, ffn_out.T[None]]))
-
-    resid_in = whole_row(tokens, me, None).astype(F32)
-    memory_row = whole_row(memory, me, None)
-    cot_row = whole_row(cotangent, me, None)
-    padding = (jnp.arange(ROW, dtype=jnp.int32) >= jnp.sum(docs))[:, None]
-
-    normed_one, inverse_one = norm_forward(resid_in, norm_gains[0])
-    qkv = jnp.concatenate([nn(normed_one, w_self[s], BF) for s in range(3)], axis=1)
+    gains = [norm_gains[i : i + 1] for i in range(3)]
+
+    shard_mid = jnp.concatenate([self_out.T[None], cross_proj, cross_out.T[None]])
+    shard_ffn = jnp.concatenate([ffn_proj, ffn_out.T[None]])
+    token_swap = Swap(other_row(tokens, me))
+    if packed:
+        w_mid = gather_plain(shard_mid)
+        w_one = Gather(self_proj)
+        w_one.first()
+        w_one.second()
+        hold((), w_one, token_swap)
+        w_one.third()
+        hold((), w_one)
+        w_one.fourth()
+        hold((), w_one)
+        w_self = w_one.pieces()
+        w_self, shard_ffn, memory, cotangent = lax.optimization_barrier((w_self, shard_ffn, memory, cotangent))
+        w_two = Gather(shard_ffn)
+        w_two.first()
+    else:
+        w_self = [gather_whole(self_proj)]
+        w_mid = gather_whole(shard_mid)
+        w_ffn = gather_whole(shard_ffn)
+        w_ffn = [w_ffn.reshape(3, width, 2, -1).transpose(2, 0, 1, 3)]
+    memory_swap = Swap(other_row(memory, me))
+    x = whole_row(tokens, token_swap, me)
+    normed_one, qkv, w_self = project(ids, gains[0], x, w_self)
+    if packed:
+        qkv = hold(qkv, w_two, memory_swap)
+        w_two.second()
+    cot_swap = Swap(other_row(cotangent, me))
     mixed_self, qa_self = attention_forward(True, docs, band, (qkv, 0), (qkv, 6), (qkv, 12), width)
-    resid_two = resid_in + nt(mixed_self, w_mid[0])
-    normed_two, inverse_two = norm_forward(resid_two, norm_gains[1])
-    query_cross = nn(normed_two, w_mid[1], BF)
-    key_cross = nn(memory_row, w_mid[2], BF)
-    value_cross = nn(memory_row, w_mid[3], BF)
+    if packed:
+        mixed_self = hold(mixed_self, w_two, cot_swap)
+        w_two.third()
+    memory_row = whole_row(memory, memory_swap, me)
+    resid_two, normed_two, q_cross, k_cross, v_cross, w_mid = middle(gains[1], x, mixed_self, memory_row, w_mid)
+    if packed:
+        q_cross = hold(q_cross, w_two)
+        w_two.fourth()
     mixed_cross, qa_cross = attention_forward(
-        False, mem_length, band, (query_cross, 0), (key_cross, 0), (value_cross, 0), width
+        False, mem_length, band, (q_cross, 0), (k_cross, 0), (v_cross, 0), width
     )
-    resid_three = resid_two + nt(mixed_cross, w_mid[4])
-    normed_three, inverse_three = norm_forward(resid_three, norm_gains[2])
-    gate = nn(normed_three, w_ffn[0])
-    up = nn(normed_three, w_ffn[1])
-    activated, gelu_pull = jax.vjp(lambda x: jax.nn.gelu(x, approximate=True), gate)
-    hidden = (activated * up).astype(BF)
-    output = jnp.where(padding, 0.0, resid_three + nt(hidden, w_ffn[2]))
-    output = row_halves(output, me)
-
-    grad_four = jnp.where(padding, 0.0, cot_row.astype(F32))
-    branch = grad_four.astype(BF)
-    grad_ffn_out = tn(branch, hidden, BF)
-    grad_hidden = nn(branch, w_ffn[2])
-    grad_gate = gelu_pull(grad_hidden * up)[0].astype(BF)
-    grad_up = (grad_hidden * activated).astype(BF)
-    ffn_grads = scatter_grads(
-        jnp.stack([tn(normed_three, grad_gate, BF), tn(normed_three, grad_up, BF), grad_ffn_out])
+    if packed:
+        mixed_cross = hold(mixed_cross, w_two)
+        w_ffn = w_two.pieces()
+    cot_row = whole_row(cotangent, cot_swap, me)
+    output, output_low, grad_three, grad_mixed, gain_three, ffn_grads = feed(
+        ids, docs, gains[2], resid_two, mixed_cross, cot_row, w_mid[4], w_ffn, dp if packed else 1
     )
-    upstream = nt(grad_gate, w_ffn[0]) + nt(grad_up, w_ffn[1])
-    grad_resid, gain_three = norm_backward(resid_three, inverse_three, norm_gains[2], upstream)
-    grad_three = grad_four + grad_resid
-
-    branch = grad_three.astype(BF)
-    grad_cross_out = tn(branch, mixed_cross, BF)
-    grad_mixed = nn(branch, w_mid[4], BF)
+    output_swap = Swap(other_half(output_low, me))
+    if packed:
+        ffn_grads = scatter_plain(ffn_grads)
+    else:
+        ffn_grads = scatter_whole(ffn_grads[0].transpose(1, 2, 0, 3).reshape(3, width, -1))
     grads_cross, _ = attention_backward(
-        False, mem_length, band, qa_cross, (key_cross, 0), (value_cross, 0), grad_mixed, mixed_cross, width
+        False, mem_length, band, qa_cross, (k_cross, 0), (v_cross, 0), grad_mixed, mixed_cross, width
     )
-    grad_memory = row_halves(nt(grads_cross[1], w_mid[2]) + nt(grads_cross[2], w_mid[3]), me)
-    upstream = nt(grads_cross[0], w_mid[1])
-    grad_resid, gain_two = norm_backward(resid_two, inverse_two, norm_gains[1], upstream)
-    grad_two = grad_three + grad_resid
-
-    branch = grad_two.astype(BF)
-    grad_self_out = tn(branch, mixed_self, BF)
-    mid_grads = scatter_grads(
-        jnp.stack(
-            [
-                grad_self_out,
-                tn(normed_two, grads_cross[0], BF),
-                tn(memory_row, grads_cross[1], BF),
-                tn(memory_row, grads_cross[2], BF),
-                grad_cross_out,
-            ]
-        )
+    grads_cross = hold(grads_cross, output_swap)
+    grad_two, grad_mixed, gmem, gmem_low, gain_two, *mid_grads = cross_back(
+        packed, ids, gains[1], grads_cross, resid_two, normed_two, memory_row, grad_three, mixed_cross, mixed_self, w_mid
     )
-    grad_mixed = nn(branch, w_mid[0], BF)
+    memory_swap = Swap(other_half(gmem_low, me))
+    if packed:
+        mid = Scatter(*mid_grads)
+        mid.first()
+    pairs = width // LANES
     grads_self, sums = attention_backward(
-        True, docs, band, qa_self, (qkv, 6), (qkv, 12), grad_mixed, mixed_self, width
+        True, docs, band, qa_self, (qkv, 6), (qkv, 12), grad_mixed, mixed_self, width, 0, pairs // 2
     )
-    self_grads = scatter_grads(jnp.stack([tn(normed_one, grads_self[s], BF) for s in range(3)]))
-    upstream = sum(nt(grads_self[s], w_self[s]) for s in range(3))
-    grad_resid, gain_one = norm_backward(resid_in, inverse_one, norm_gains[0], upstream)
-    grad_tokens = row_halves(grad_two + grad_resid, me)
-    grad_gains, table = lax.psum(
-        (jnp.stack([gain_one, gain_two, gain_three]), table_gradient(sums)), ("dp", "mp")
+    if packed:
+        grads_self = hold(grads_self, mid, memory_swap)
+        mid.second()
+    grads_self, more_sums = attention_backward(
+        True, docs, band, qa_self, (qkv, 6), (qkv, 12), grad_mixed, mixed_self, width, pairs // 2, pairs, grads_self
     )
+    sums = jnp.concatenate([sums, more_sums])
+    table = table_gradient(sums).reshape(1, -1)
+    if packed:
+        grads_self, table = hold((grads_self, table), mid)
+        mid.third()
+    self_grads = self_weights(packed, ids, grads_self, normed_one)
+    if packed:
+        self_grads = hold(self_grads, mid)
+        mid.fourth()
+        last = Scatter(*self_grads)
+        last.first()
+    grad_x, grad_x_low, gain_one = self_back(gains[0], grads_self, x, grad_two, w_self)
+    if packed:
+        grad_x_low, gain_one = hold((grad_x_low, gain_one), mid, last)
+        mid.fifth()
+        last.second()
+    token_swap = Swap(other_half(grad_x_low, me))
+    pad = width - table.shape[1]
+    small = Sum(jnp.concatenate([gain_one, gain_two, gain_three, jnp.pad(table, ((0, 0), (0, pad)))]))
+    if packed:
+        small.flip(0)
+        hold((), mid, last, small)
+        last.third()
+        small.flip(1)
+        hold((), last, small)
+        last.fourth()
+        small.flip(2)
+        hold((), last, small)
+        last.fifth()
+        small.flip(3)
+        hold((), last, small)
+        mid_grads = mid.total()
+        self_grads = last.total()
+        small = small.values + flip_mp(small.values)
+    else:
+        mid_grads = scatter_whole(mid_grads[0])
+        self_grads = scatter_whole(self_grads[0])
+        small = lax.psum(small.values, ("dp", "mp"))
+    output = row_halves(output, output_swap, me)
+    grad_memory = row_halves(gmem, memory_swap, me)
+    grad_tokens = row_halves(grad_x, token_swap, me)
     return (
         output,
         grad_tokens,
         grad_memory,
-        grad_gains,
-        table,
+        small[:3],
+        small[3, : NB * rel_table.shape[1]].reshape(rel_table.shape),
         self_grads,
         mid_grads[0].T,
         mid_grads[1:4],

time: 809 us -> 478 us (0.59)
  matrix products: 152 us -> 0.62 us
  waiting for transfers between devices: 219 us -> 92.3 us
  Pallas kernels: 132 us -> 258 us
  local copies, waits for them, and re-layouts: 144 us -> 23.8 us
  blocking collectives: 75.3 us -> 0 us
  starting transfers between devices: 8.43 us -> 51.2 us
  other arithmetic: 56.6 us -> 26.7 us
    dot_general x33 -> x0, matrix products: 152 us -> none  [mm(): lax.dot_general(a, b, ((dims[0], dims[1]), ((), ())), preferred_element_t...]
    pallas_call x2 -> x9, Pallas kernels: 67.1 us -> 193 us  [the longest x3 68.8 us: attention_backward(): pl.pallas_call(functools.partial(backward_kernel, causal, len(extra)), gr...]
    reduce_scatter x3 -> x1, waiting for transfers between devices: 120 us -> 0.01 us  [scatter_plain(): lax.psum_scatter(flat, ('dp', 'mp'), scatter_dimension=0, tiled=True)[0]]
    all_gather x3 -> x1, waiting for transfers between devices: 86.8 us -> 0.01 us  [gather_plain(): pieces = lax.all_gather(shard, ('dp', 'mp'), axis=0)]
    ppermute x6 -> x57, waiting for transfers between devices: 11.1 us -> 92.3 us  [the longest x40 58.1 us: flip_bit(): return lax.ppermute(values, 'dp', [(i, i ^ 1 << bit) for i in range(size)])]
    psum x1 -> x0, blocking collectives: 75.3 us -> none  [per_device(): lax.psum((jnp.stack([gain_one, gain_two, gain_three]), table_gradient(sum...]
    another operation x15 -> x4, local copies, waits for them, and re-layouts: 48.5 us -> 4.85 us  [the longest x3 4.75 us: row_halves(): return jnp.where(me == 0, jnp.stack([kept, came]), jnp.stack([came, kept]))]
    ppermute x6 -> x57, starting transfers between devices: 8.19 us -> 51.2 us  [the longest x40 31 us: flip_bit(): return lax.ppermute(values, 'dp', [(i, i ^ 1 << bit) for i in range(size)])]
  transfers between devices with their start and end apart: 12 -> 59, of which waited for: 5 -> 20; matrix products, arithmetic and copies ran while one was open for 33% -> 9% of each run, Pallas kernels for 8% -> 43%
where the time goes in v2:
time: 478 us; the launch traced here: 468 us
  Pallas kernels  258 us (54%)
  waiting for transfers between devices  92.3 us (19%)
  starting transfers between devices  51.2 us (11%)
  other arithmetic  26.7 us (6%)
  local copies, waits for them, and re-layouts  23.8 us (5%)
  between operations  15.3 us (3%)
    pallas_call x3, Pallas kernels, attention_backward(): pl.pallas_call(functools.partial(backward_kernel, causal, len(extra)), gr...  68.8 us
    pallas_call x2, Pallas kernels, attention_forward(): pl.pallas_call(functools.partial(forward_kernel, causal), grid=(pairs,),...  64.8 us
    ppermute x40, waiting for transfers between devices, flip_bit(): return lax.ppermute(values, 'dp', [(i, i ^ 1 << bit) for i in range(size)])  58.1 us
    pallas_call x1, Pallas kernels, feed(): pl.pallas_call(functools.partial(feed_kernel, blocks, len(pieces)), grid=...  56.7 us
    ppermute x17, waiting for transfers between devices, flip_mp(): return lax.ppermute(values, 'mp', [(0, 1), (1, 0)])  34.1 us
    ppermute x40, starting transfers between devices, flip_bit(): return lax.ppermute(values, 'dp', [(i, i ^ 1 << bit) for i in range(size)])  31 us
    pallas_call x1, Pallas kernels, cross_back(): pl.pallas_call(functools.partial(cross_back_kernel, blocks, packed), grid...  26.1 us
    ppermute x17, starting transfers between devices, flip_mp(): return lax.ppermute(values, 'mp', [(0, 1), (1, 0)])  20.1 us
  transfers between devices with their start and end apart: 59, of which 20 were waited for; matrix products, arithmetic and copies ran while one was open for 9% of the time, Pallas kernels for 43%

profile of v2, /device:TPU:0, one launch (start us, length us, event | category | flops | bytes accessed | tf_op | source)
XLA Modules:
  0.0 468.2 jit_solution(10705318508692486124)
XLA Ops:
  10.7 3.0 collective-permute-start.2
  13.7 2.6 collective-permute-start
  16.2 5.2 %collective-permute-done = bf16[3,48,384]{2,1,0:T(8,128)(2,1)S(1)} collective-permute-done((bf16[3,48,384]{2,1,0:T(8,128)(2,1)S(1)}, bf16[3,48,384]{2,1,0:T(8,128)(2,1)S(1)}, u32[]{:S(2)}, u32[]{:S(2)}) %collective-permute-start) | collective-permute-done | bytes 110624 | tf_op jit(solution)/shard_map/ppermute | solution.py:766
  24.3 4.7 %collective-permute-done.1.refs_4_ = bf16[2,3,48,384]{3,2,1,0:T(8,128)(2,1)S(1)} collective-permute-done((bf16[2,3,48,384]{3,2,1,0:T(8,128)(2,1)S(1)}, bf16[2,3,48,384]{3,2,1,0:T(8,128)(2,1)S(1)}, u32[]{:S(2)}, u32[]{:S(2)}) %collective-permute-start.1) | collective-permute-done | bytes 221216 | tf_op jit(solution)/shard_map/ppermute | solution.py:766
  29.0 4.4 collective-permute-done.2
  37.4 4.3 collective-permute-done.4.refs_6_
  45.5 4.9 %collective-permute-done.8.refs_3_ = bf16[2,3,48,384]{3,2,1,0:T(8,128)(2,1)S(1)} collective-permute-done((bf16[2,3,48,384]{3,2,1,0:T(8,128)(2,1)S(1)}, bf16[2,3,48,384]{3,2,1,0:T(8,128)(2,1)S(1)}, u32[]{:S(2)}, u32[]{:S(2)}) %collective-permute-start.8) | collective-permute-done | bytes 221216 | tf_op jit(solution)/shard_map/ppermute | solution.py:766
  50.4 3.1 collective-permute-done.10.refs_7_
  61.5 3.1 maximum_select_fusion.3.x_ref
  64.6 2.7 collective-permute-start.17
  68.1 9.3 %project.1 = (bf16[1024,768]{1,0:T(8,128)(2,1)}, bf16[1024,2304]{1,0:T(8,128)(2,1)}, bf16[3,768,768]{2,1,0:T(8,128)(2,1)}) custom-call(s32[2]{0:T(128)} %pad_add_fusion.ids_ref, f32[1,768]{1,0:T(1,128)} %get-tuple-element.293.gain_ref, bf16[1024,768]{1,0:T(8,128)(2,1)} %maximum_select_fusion.3.x_ref, bf16[2,3,48,384]{3,2,1,0:T(8,128)(2,1)} %copy-done.15, ...), custom_call_target="tpu_custom_call" | custom-call | flops 3623878656 | bytes 11403264 | tf_op jit(solution)/shard_map/project/pallas_call | solution.py:415
  77.4 10.3 %collective-permute-done.17 = bf16[3,48,1024]{2,1,0:T(8,128)(2,1)S(1)} collective-permute-done((bf16[3,48,1024]{2,1,0:T(8,128)(2,1)S(1)}, bf16[3,48,1024]{2,1,0:T(8,128)(2,1)S(1)}, u32[]{:S(2)}, u32[]{:S(2)}) %collective-permute-start.17) | collective-permute-done | bytes 294944 | tf_op jit(solution)/shard_map/ppermute | solution.py:766
  92.6 29.2 %attention_forward.2 = (bf16[1024,768]{1,0:T(8,128)(2,1)}, bf16[12,1024,128]{2,1,0:T(8,128)(2,1)}) custom-call(s32[3]{0:T(128)} %fusion.26.bounds_ref.docs_ref, f32[6,2,384]{2,1,0:T(2,128)} %reshape.334.band_ref, bf16[1024,2304]{1,0:T(8,128)(2,1)} %get-tuple-element.155.q_ref.k_ref.v_ref, bf16[1024,2304]{1,0:T(8,128)(2,1)} %get-tuple-element.155.q_ref.k_ref.v_ref, ...), custom_call_target="tpu_custom_call" | custom-call | flops 6442450944 | bytes 12582912 | tf_op jit(solution)/shard_map/attention_forward/pallas_call | solution.py:221
  123.4 3.1 maximum_select_fusion.4.memory_ref
  126.6 13.6 %middle.1 = (f32[1024,768]{1,0:T(8,128)}, bf16[1024,768]{1,0:T(8,128)(2,1)}, bf16[1024,768]{1,0:T(8,128)(2,1)}, bf16[1024,768]{1,0:T(8,128)(2,1)}, bf16[1024,768...) custom-call(f32[1,768]{1,0:T(1,128)} %get-tuple-element.294.gain_ref, bf16[1024,768]{1,0:T(8,128)(2,1)} %maximum_select_fusion.3.x_ref, ...), custom_call_target="tpu_custom_call" | custom-call | flops 4831838208 | bytes 21626880 | tf_op jit(solution)/shard_map/middle/pallas_call | solution.py:453
  143.1 35.6 %attention_forward.3 = (bf16[1024,768]{1,0:T(8,128)(2,1)}, bf16[12,1024,128]{2,1,0:T(8,128)(2,1)}) custom-call(s32[1]{0:T(128)} %dynamic_slice.50.bounds_ref, f32[6,2,384]{2,1,0:T(2,128)} %reshape.334.band_ref, bf16[1024,768]{1,0:T(8,128)(2,1)} %get-tuple-element.164.q_ref, bf16[1024,768]{1,0:T(8,128)(2,1)} %get-tuple-element.165.k_ref, ...), custom_call_target="tpu_custom_call" | custom-call | flops 12884901888 | bytes 12582912 | tf_op jit(solution)/shard_map/attention_forward/pallas_call | solution.py:221
  184.6 56.7 %feed.1 = (f32[1024,768]{1,0:T(8,128)}, bf16[1024,768]{1,0:T(8,128)(2,1)}, f32[1024,768]{1,0:T(8,128)}, bf16[1024,768]{1,0:T(8,128)(2,1)}, f32[1,768]{1,0:T(1,128)}, /*index=5*/bf16[16,2,3,48,1024]{4,3,2,1,0:T(8,128)(2,1)}) custom-call(s32[2]{0:T(128)} %pad_add_fusion.ids_ref, s32[3]{0:T(128)} %fusion.26.bounds_ref.docs_ref, ...), custom_call_target="tpu_custom_call" | custom-call | flops 28991029248 | bytes 37748736 | tf_op jit(solution)/shard_map/feed/pallas_call | solution.py:550
  243.8 37.9 %attention_backward.3 = (bf16[3,1024,768]{2,1,0:T(8,128)(2,1)}, f32[6,8,128]{2,1,0:T(8,128)}) custom-call(s32[1]{0:T(128)} %dynamic_slice.50.bounds_ref, f32[6,2,384]{2,1,0:T(2,128)} %reshape.334.band_ref, bf16[12,1024,128]{2,1,0:T(8,128)(2,1)} %get-tuple-element.182.qa_ref, bf16[1024,768]{1,0:T(8,128)(2,1)} %get-tuple-element.165.k_ref, ...), custom_call_target="tpu_custom_call" | custom-call | flops 32212254720 | bytes 15728640 | tf_op jit(solution)/shard_map/attention_backward/pallas_call | solution.py:254
  281.7 26.1 %cross_back.1 = (f32[1024,768]{1,0:T(8,128)}, bf16[1024,768]{1,0:T(8,128)(2,1)}, f32[1024,768]{1,0:T(8,128)}, bf16[1024,768]{1,0:T(8,128)(2,1)}, f32[1,768]{1,0:...) custom-call(s32[2]{0:T(128)} %pad_add_fusion.ids_ref, ...), custom_call_target="tpu_custom_call" | custom-call | flops 10871635968 | bytes 40108032 | tf_op jit(solution)/shard_map/cross_back/pallas_call | solution.py:670
  309.6 15.7 %attention_backward.4 = (bf16[3,1024,768]{2,1,0:T(8,128)(2,1)}, f32[3,8,128]{2,1,0:T(8,128)}) custom-call(s32[3]{0:T(128)} %fusion.26.bounds_ref.docs_ref, f32[6,2,384]{2,1,0:T(2,128)} %reshape.334.band_ref, bf16[12,1024,128]{2,1,0:T(8,128)(2,1)} %get-tuple-element.187.qa_ref, bf16[1024,2304]{1,0:T(8,128)(2,1)} %get-tuple-element.155.q_ref.k_ref.v_ref, ...), custom_call_target="tpu_custom_call" | custom-call | flops 8053063680 | bytes 15728640 | tf_op jit(solution)/shard_map/attention_backward/pallas_call | solution.py:254
  326.0 11.5 %collective-permute-done.37 = bf16[512,768]{1,0:T(8,128)(2,1)S(1)} collective-permute-done((bf16[512,768]{1,0:T(8,128)(2,1)S(1)}, bf16[512,768]{1,0:T(8,128)(2,1)S(1)}, u32[]{:S(2)}, u32[]{:S(2)}) %collective-permute-start.37) | collective-permute-done | bytes 786464 | tf_op jit(solution)/shard_map/ppermute | solution.py:770
  343.4 15.2 %attention_backward.5 = (bf16[3,1024,768]{2,1,0:T(8,128)(2,1)}, f32[3,8,128]{2,1,0:T(8,128)}) custom-call(s32[3]{0:T(128)} %fusion.26.bounds_ref.docs_ref, f32[6,2,384]{2,1,0:T(2,128)} %reshape.334.band_ref, bf16[12,1024,128]{2,1,0:T(8,128)(2,1)} %get-tuple-element.187.qa_ref, ...), custom_call_target="tpu_custom_call", output_to_operand_aliasing={{0}: (7, {})} | custom-call | flops 8053063680 | bytes 15728640 | tf_op jit(solution)/shard_map/attention_backward/pallas_call | solution.py:254
  360.1 7.2 %collective-permute-done.38 = bf16[2,2,5,48,384]{4,3,2,1,0:T(8,128)(2,1)} collective-permute-done((bf16[2,2,5,48,384]{4,3,2,1,0:T(8,128)(2,1)}, bf16[2,2,5,48,384]{4,3,2,1,0:T(8,128)(2,1)}, u32[]{:S(2)}, u32[]{:S(2)}) %collective-permute-start.38) | collective-permute-done | bytes 737312 | tf_op jit(solution)/shard_map/ppermute | solution.py:766
  372.5 9.1 %self_weights.1 = (bf16[2,2,2,2,3,48,384]{6,5,4,3,2,1,0:T(8,128)(2,1)}, bf16[2,2,2,2,3,48,384]{6,5,4,3,2,1,0:T(8,128)(2,1)}) custom-call(s32[2]{0:T(128)} %pad_add_fusion.ids_ref, bf16[3,1024,768]{2,1,0:T(8,128)(2,1)} %get-tuple-element.201.d_ref, bf16[1024,768]{1,0:T(8,128)(2,1)} %get-tuple-element.208.normed_ref), custom_call_target="tpu_custom_call" | custom-call | flops 3623878656 | bytes 9830400 | tf_op jit(solution)/shard_map/self_weights/pallas_call | solution.py:715
  384.4 3.0 maximum_select_fusion
  389.4 10.0 %self_back.1 = (f32[1024,768]{1,0:T(8,128)}, bf16[1024,768]{1,0:T(8,128)(2,1)}, f32[1,768]{1,0:T(1,128)}) custom-call(f32[1,768]{1,0:T(1,128)} %get-tuple-element.293.gain_ref, bf16[3,1024,768]{2,1,0:T(8,128)(2,1)} %get-tuple-element.201.d_ref, bf16[1024,768]{1,0:T(8,128)(2,1)} %maximum_select_fusion.3.x_ref, f32[1024,768]{1,0:T(8,128)} %get-tuple-element.202.grad_ref, ...), custom_call_target="tpu_custom_call" | custom-call | flops 3623878656 | bytes 19267584 | tf_op jit(solution)/shard_map/self_back/pallas_call | solution.py:752
  409.0 7.6 %collective-permute-done.45 = bf16[5,48,384]{2,1,0:T(8,128)(2,1)S(1)} collective-permute-done((bf16[5,48,384]{2,1,0:T(8,128)(2,1)S(1)}, bf16[5,48,384]{2,1,0:T(8,128)(2,1)S(1)}, u32[]{:S(2)}, u32[]{:S(2)}) %collective-permute-start.45) | collective-permute-done | bytes 184352 | tf_op jit(solution)/shard_map/ppermute | solution.py:766
  421.1 3.0 collective-permute-done.50
  424.1 12.3 %collective-permute-done.49 = bf16[2,3,48,384]{3,2,1,0:T(8,128)(2,1)S(1)} collective-permute-done((bf16[2,3,48,384]{3,2,1,0:T(8,128)(2,1)S(1)}, bf16[2,3,48,384]{3,2,1,0:T(8,128)(2,1)S(1)}, u32[]{:S(2)}, u32[]{:S(2)}) %collective-permute-start.49) | collective-permute-done | bytes 221216 | tf_op jit(solution)/shard_map/ppermute | solution.py:770
  440.2 4.0 collective-permute-done.52
  444.2 2.9 collective-permute-start.55
  449.8 4.1 collective-permute-done.54
  (264 shorter events, 87.7 us)
Async XLA Ops:
  7.2 119.4 %all-gather.3.cloned.1.call-start = ((), (), s32[]{:S(2)}) async-start(), calls=%async_computation.2 | async-start | bytes 6082560 | tf_op jit(solution)/shard_map/all_gather | solution.py:865
  8.9 449.5 %reduce-scatter.2.cloned.1.call-start = ((), (), s32[]{:S(2)}) async-start(), calls=%async_computation.1 | async-start | bytes 9732096 | tf_op jit(solution)/shard_map/reduce_scatter | solution.py:878
  10.7 22.8 %collective-permute-start.2 = (bf16[512,768]{1,0:T(8,128)(2,1)S(1)}, bf16[512,768]{1,0:T(8,128)(2,1)}, u32[]{:S(2)}, u32[]{:S(2)}) collective-permute-start(bf16[512,768]{1,0:T(8,128)(2,1)S(1)} %get-tuple-element.287), channel_id=1, source_target_pairs={{0,1},{1,0},{2,3},{3,2},{4,5},{5,4},{6,7},{7,6},{8,9},{9,8},{10,11... | collective-permute-start | bytes 2359304 | tf_op jit(solution)/shard_map/ppermute | solution.py:770
  22.2 21.4 %collective-permute-start.7 = (bf16[2,3,48,384]{3,2,1,0:T(8,128)(2,1)S(1)}, bf16[2,3,48,384]{3,2,1,0:T(8,128)(2,1)S(1)}, u32[]{:S(2)}, u32[]{:S(2)}) collective-permute-start(bf16[2,3,48,384]{3,2,1,0:T(8,128)(2,1)S(1)} %pad_maximum_fusion.6.refs_0_), channel_id=1, source_target_pairs={{0,4},{2,6},{4,0},{6,2},{8,12},{10,14},{12,8},{14,10},{16,20},{18,... | collective-permute-start | bytes 663560 | tf_op jit(solution)/shard_map/ppermute | solution.py:766
  23.7 12.0 %collective-permute-start.5 = (bf16[2,3,48,384]{3,2,1,0:T(8,128)(2,1)S(1)}, bf16[2,3,48,384]{3,2,1,0:T(8,128)(2,1)S(1)}, u32[]{:S(2)}, u32[]{:S(2)}) collective-permute-start(bf16[2,3,48,384]{3,2,1,0:T(8,128)(2,1)S(1)} %pad_maximum_fusion.6.refs_0_), channel_id=1, source_target_pairs={{0,2},{2,0},{4,6},{6,4},{8,10},{10,8},{12,14},{14,12},{16,18},{18,... | collective-permute-start | bytes 663560 | tf_op jit(solution)/shard_map/ppermute | solution.py:766
  23.7 13.6 %collective-permute-start.3 = (bf16[2,3,48,384]{3,2,1,0:T(8,128)(2,1)S(1)}, bf16[2,3,48,384]{3,2,1,0:T(8,128)(2,1)S(1)}, u32[]{:S(2)}, u32[]{:S(2)}) collective-permute-start(bf16[2,3,48,384]{3,2,1,0:T(8,128)(2,1)S(1)} %pad_maximum_fusion.6.refs_0_), channel_id=1, source_target_pairs={{0,1},{1,0},{2,3},{3,2},{4,5},{5,4},{6,7},{7,6},{8,9},{9,8},{10,11... | collective-permute-start | bytes 663560 | tf_op jit(solution)/shard_map/ppermute | solution.py:770
  57.6 31.2 %collective-permute-start.18 = (bf16[512,768]{1,0:T(8,128)(2,1)}, bf16[512,768]{1,0:T(8,128)(2,1)}, u32[]{:S(2)}, u32[]{:S(2)}) collective-permute-start(bf16[512,768]{1,0:T(8,128)(2,1)} %get-tuple-element.285), channel_id=1, source_target_pairs={{0,1},{1,0},{2,3},{3,2},{4,5},{5,4},{6,7},{7,6},{8,9},{9,8},{10,11... | collective-permute-start | bytes 2359304 | tf_op jit(solution)/shard_map/ppermute | solution.py:770
  64.6 23.0 %collective-permute-start.17 = (bf16[3,48,1024]{2,1,0:T(8,128)(2,1)S(1)}, bf16[3,48,1024]{2,1,0:T(8,128)(2,1)S(1)}, u32[]{:S(2)}, u32[]{:S(2)}) collective-permute-start(bf16[3,48,1024]{2,1,0:T(8,128)(2,1)S(1)} %pad_maximum_fusion.5), channel_id=1, source_target_pairs={{0,16},{2,18},{4,20},{6,22},{8,24},{10,26},{12,28},{14,30},{16,0},... | collective-permute-start | bytes 884744 | tf_op jit(solution)/shard_map/ppermute | solution.py:766
  67.4 54.3 %collective-permute-start.20 = (bf16[512,768]{1,0:T(8,128)(2,1)S(1)}, bf16[512,768]{1,0:T(8,128)(2,1)S(1)}, u32[]{:S(2)}, u32[]{:S(2)}) collective-permute-start(bf16[512,768]{1,0:T(8,128)(2,1)S(1)} %get-tuple-element.283), channel_id=1, source_target_pairs={{0,1},{1,0},{2,3},{3,2},{4,5},{5,4},{6,7},{7,6},{8,9},{9,8},{10,11... | collective-permute-start | bytes 2359304 | tf_op jit(solution)/shard_map/ppermute | solution.py:770
  89.0 53.1 %collective-permute-start.25 = (bf16[2,3,48,1024]{3,2,1,0:T(8,128)(2,1)S(1)}, bf16[2,3,48,1024]{3,2,1,0:T(8,128)(2,1)}, u32[]{:S(2)}, u32[]{:S(2)}) collective-permute-start(bf16[2,3,48,1024]{3,2,1,0:T(8,128)(2,1)S(1)} %pad_maximum_fusion.2.refs_0_), channel_id=1, source_target_pairs={{0,4},{2,6},{4,0},{6,2},{8,12},{10,14},{12,8},{14,10},{16,20},{18,... | collective-permute-start | bytes 1769480 | tf_op jit(solution)/shard_map/ppermute | solution.py:766
  90.1 50.1 %collective-permute-start.23 = (bf16[2,3,48,1024]{3,2,1,0:T(8,128)(2,1)S(1)}, bf16[2,3,48,1024]{3,2,1,0:T(8,128)(2,1)}, u32[]{:S(2)}, u32[]{:S(2)}) collective-permute-start(bf16[2,3,48,1024]{3,2,1,0:T(8,128)(2,1)S(1)} %pad_maximum_fusion.2.refs_0_), channel_id=1, source_target_pairs={{0,2},{2,0},{4,6},{6,4},{8,10},{10,8},{12,14},{14,12},{16,18},{18,... | collective-permute-start | bytes 1769480 | tf_op jit(solution)/shard_map/ppermute | solution.py:766
  90.1 50.7 %collective-permute-start.21 = (bf16[2,3,48,1024]{3,2,1,0:T(8,128)(2,1)S(1)}, bf16[2,3,48,1024]{3,2,1,0:T(8,128)(2,1)}, u32[]{:S(2)}, u32[]{:S(2)}) collective-permute-start(bf16[2,3,48,1024]{3,2,1,0:T(8,128)(2,1)S(1)} %pad_maximum_fusion.2.refs_0_), channel_id=1, source_target_pairs={{0,1},{1,0},{2,3},{3,2},{4,5},{5,4},{6,7},{7,6},{8,9},{9,8},{10,11... | collective-permute-start | bytes 1769480 | tf_op jit(solution)/shard_map/ppermute | solution.py:770
  91.0 30.8 %collective-permute-start.19 = (bf16[2,3,48,1024]{3,2,1,0:T(8,128)(2,1)S(1)}, bf16[2,3,48,1024]{3,2,1,0:T(8,128)(2,1)}, u32[]{:S(2)}, u32[]{:S(2)}) collective-permute-start(bf16[2,3,48,1024]{3,2,1,0:T(8,128)(2,1)S(1)} %pad_maximum_fusion.2.refs_0_), channel_id=1, source_target_pairs={{0,8},{2,10},{4,12},{6,14},{8,0},{10,2},{12,4},{14,6},{16,24},{18,... | collective-permute-start | bytes 1769480 | tf_op jit(solution)/shard_map/ppermute | solution.py:766
  121.8 19.0 %collective-permute-start.24 = (bf16[2,3,48,1024]{3,2,1,0:T(8,128)(2,1)}, bf16[2,3,48,1024]{3,2,1,0:T(8,128)(2,1)}, u32[]{:S(2)}, u32[]{:S(2)}) collective-permute-start(bf16[2,3,48,1024]{3,2,1,0:T(8,128)(2,1)} %collective-permute-done.19.refs_4_), channel_id=1, source_target_pairs={{0,2},{2,0},{4,6},{6,4},{8,10},{10,8},{12,14},{14,12},{16,18},{18,... | collective-permute-start | bytes 1769480 | tf_op jit(solution)/shard_map/ppermute | solution.py:766
  121.9 18.9 %collective-permute-start.22 = (bf16[2,3,48,1024]{3,2,1,0:T(8,128)(2,1)}, bf16[2,3,48,1024]{3,2,1,0:T(8,128)(2,1)}, u32[]{:S(2)}, u32[]{:S(2)}) collective-permute-start(bf16[2,3,48,1024]{3,2,1,0:T(8,128)(2,1)} %collective-permute-done.19.refs_4_), channel_id=1, source_target_pairs={{0,4},{2,6},{4,0},{6,2},{8,12},{10,14},{12,8},{14,10},{16,20},{18,... | collective-permute-start | bytes 1769480 | tf_op jit(solution)/shard_map/ppermute | solution.py:766
  140.2 38.5 %collective-permute-start.27 = (bf16[2,3,48,1024]{3,2,1,0:T(8,128)(2,1)}, bf16[2,3,48,1024]{3,2,1,0:T(8,128)(2,1)S(1)}, u32[]{:S(2)}, u32[]{:S(2)}) collective-permute-start(bf16[2,3,48,1024]{3,2,1,0:T(8,128)(2,1)} %collective-permute-done.19.refs_4_), channel_id=1, source_target_pairs={{0,1},{1,0},{2,3},{3,2},{4,5},{5,4},{6,7},{7,6},{8,9},{9,8},{10,11... | collective-permute-start | bytes 1769480 | tf_op jit(solution)/shard_map/ppermute | solution.py:770
  140.8 37.9 %collective-permute-start.29 = (bf16[2,3,48,1024]{3,2,1,0:T(8,128)(2,1)}, bf16[2,3,48,1024]{3,2,1,0:T(8,128)(2,1)S(1)}, u32[]{:S(2)}, u32[]{:S(2)}) collective-permute-start(bf16[2,3,48,1024]{3,2,1,0:T(8,128)(2,1)} %collective-permute-done.21.refs_1_), channel_id=1, source_target_pairs={{0,2},{2,0},{4,6},{6,4},{8,10},{10,8},{12,14},{14,12},{16,18},{18,... | collective-permute-start | bytes 1769480 | tf_op jit(solution)/shard_map/ppermute | solution.py:766
  140.9 37.9 %collective-permute-start.26 = (bf16[2,3,48,1024]{3,2,1,0:T(8,128)(2,1)}, bf16[2,3,48,1024]{3,2,1,0:T(8,128)(2,1)}, u32[]{:S(2)}, u32[]{:S(2)}) collective-permute-start(bf16[2,3,48,1024]{3,2,1,0:T(8,128)(2,1)} %collective-permute-done.21.refs_1_), channel_id=1, source_target_pairs={{0,4},{2,6},{4,0},{6,2},{8,12},{10,14},{12,8},{14,10},{16,20},{18,... | collective-permute-start | bytes 1769480 | tf_op jit(solution)/shard_map/ppermute | solution.py:766
  141.9 36.8 %collective-permute-start.30 = (bf16[2,3,48,1024]{3,2,1,0:T(8,128)(2,1)}, bf16[2,3,48,1024]{3,2,1,0:T(8,128)(2,1)S(1)}, u32[]{:S(2)}, u32[]{:S(2)}) collective-permute-start(bf16[2,3,48,1024]{3,2,1,0:T(8,128)(2,1)} %collective-permute-done.22.refs_6_), channel_id=1, source_target_pairs={{0,2},{2,0},{4,6},{6,4},{8,10},{10,8},{12,14},{14,12},{16,18},{18,... | collective-permute-start | bytes 1769480 | tf_op jit(solution)/shard_map/ppermute | solution.py:766
  142.1 36.7 %collective-permute-start.28 = (bf16[2,3,48,1024]{3,2,1,0:T(8,128)(2,1)}, bf16[2,3,48,1024]{3,2,1,0:T(8,128)(2,1)S(1)}, u32[]{:S(2)}, u32[]{:S(2)}) collective-permute-start(bf16[2,3,48,1024]{3,2,1,0:T(8,128)(2,1)} %collective-permute-done.22.refs_6_), channel_id=1, source_target_pairs={{0,1},{1,0},{2,3},{3,2},{4,5},{5,4},{6,7},{7,6},{8,9},{9,8},{10,11... | collective-permute-start | bytes 1769480 | tf_op jit(solution)/shard_map/ppermute | solution.py:770
  242.7 39.0 %collective-permute-start.35 = (bf16[512,768]{1,0:T(8,128)(2,1)S(1)}, bf16[512,768]{1,0:T(8,128)(2,1)S(1)}, u32[]{:S(2)}, u32[]{:S(2)}) collective-permute-start(bf16[512,768]{1,0:T(8,128)(2,1)S(1)} %constant_dynamic-slice_fusion.2), channel_id=1, source_target_pairs={{0,1},{1,0},{2,3},{3,2},{4,5},{5,4},{6,7},{7,6},{8,9},{9,8},{10,11... | collective-permute-start | bytes 2359304 | tf_op jit(solution)/shard_map/ppermute | solution.py:770
  307.8 29.7 %collective-permute-start.36 = (bf16[2,2,2,2,5,48,384]{6,5,4,3,2,1,0:T(8,128)(2,1)}, bf16[2,2,2,2,5,48,384]{6,5,4,3,2,1,0:T(8,128)(2,1)}, u32[]{:S(2)}, u32[]{:S(2)}) collective-permute-start(bf16[2,2,2,2,5,48,384]{6,5,4,3,2,1,0:T(8,128)(2,1)} %get-tuple-element.193), channel_id=1, source_target_pairs={{0,2},{2,0},{4,6},{6,4},{8,10},{10,8},{12,14},{14,12},{16,18},{18,... | collective-permute-start | bytes 8847368 | tf_op jit(solution)/shard_map/ppermute | solution.py:766
  309.1 28.4 %collective-permute-start.37 = (bf16[512,768]{1,0:T(8,128)(2,1)S(1)}, bf16[512,768]{1,0:T(8,128)(2,1)S(1)}, u32[]{:S(2)}, u32[]{:S(2)}) collective-permute-start(bf16[512,768]{1,0:T(8,128)(2,1)S(1)} %constant_dynamic-slice_fusion.1), channel_id=1, source_target_pairs={{0,1},{1,0},{2,3},{3,2},{4,5},{5,4},{6,7},{7,6},{8,9},{9,8},{10,11... | collective-permute-start | bytes 2359304 | tf_op jit(solution)/shard_map/ppermute | solution.py:770
  340.6 26.8 %collective-permute-start.38 = (bf16[2,2,5,48,384]{4,3,2,1,0:T(8,128)(2,1)}, bf16[2,2,5,48,384]{4,3,2,1,0:T(8,128)(2,1)}, u32[]{:S(2)}, u32[]{:S(2)}) collective-permute-start(bf16[2,2,5,48,384]{4,3,2,1,0:T(8,128)(2,1)} %pad_maximum_fusion), channel_id=1, source_target_pairs={{0,4},{2,6},{4,0},{6,2},{8,12},{10,14},{12,8},{14,10},{16,20},{18,... | collective-permute-start | bytes 2211848 | tf_op jit(solution)/shard_map/ppermute | solution.py:766
  341.9 25.4 %collective-permute-start.39 = (bf16[2,2,5,48,384]{4,3,2,1,0:T(8,128)(2,1)}, bf16[2,2,5,48,384]{4,3,2,1,0:T(8,128)(2,1)}, u32[]{:S(2)}, u32[]{:S(2)}) collective-permute-start(bf16[2,2,5,48,384]{4,3,2,1,0:T(8,128)(2,1)} %pad_maximum_fusion.1), channel_id=1, source_target_pairs={{0,1},{1,0},{2,3},{3,2},{4,5},{5,4},{6,7},{7,6},{8,9},{9,8},{10,11... | collective-permute-start | bytes 2211848 | tf_op jit(solution)/shard_map/ppermute | solution.py:770
  369.0 12.5 %collective-permute-start.41 = (bf16[2,5,48,384]{3,2,1,0:T(8,128)(2,1)S(1)}, bf16[2,5,48,384]{3,2,1,0:T(8,128)(2,1)S(1)}, u32[]{:S(2)}, u32[]{:S(2)}) collective-permute-start(bf16[2,5,48,384]{3,2,1,0:T(8,128)(2,1)S(1)} %get-tuple-element.270), channel_id=1, source_target_pairs={{0,4},{2,6},{4,0},{6,2},{8,12},{10,14},{12,8},{14,10},{16,20},{18,... | collective-permute-start | bytes 1105928 | tf_op jit(solution)/shard_map/ppermute | solution.py:766
  381.5 19.6 %collective-permute-start.43 = (bf16[2,2,2,2,3,48,384]{6,5,4,3,2,1,0:T(8,128)(2,1)}, bf16[2,2,2,2,3,48,384]{6,5,4,3,2,1,0:T(8,128)(2,1)S(1)}, u32[]{:S(2)}, u32[]{:S(2)}) collective-permute-start(bf16[2,2,2,2,3,48,384]{6,5,4,3,2,1,0:T(8,128)(2,1)} %get-tuple-element.213), channel_id=1, source_target_pairs={{0,2},{2,0},{4,6},{6,4},{8,10},{10,8},{12,14},{14,12},{16,18},{18,... | collective-permute-start | bytes 5308424 | tf_op jit(solution)/shard_map/ppermute | solution.py:766
  388.7 12.3 %collective-permute-start.42 = (bf16[2,5,48,384]{3,2,1,0:T(8,128)(2,1)S(1)}, bf16[2,5,48,384]{3,2,1,0:T(8,128)(2,1)S(1)}, u32[]{:S(2)}, u32[]{:S(2)}) collective-permute-start(bf16[2,5,48,384]{3,2,1,0:T(8,128)(2,1)S(1)} %fusion.5), channel_id=1, source_target_pairs={{0,8},{2,10},{4,12},{6,14},{8,0},{10,2},{12,4},{14,6},{16,24},{18,... | collective-permute-start | bytes 1105928 | tf_op jit(solution)/shard_map/ppermute | solution.py:766
  402.1 14.5 %collective-permute-start.46 = (bf16[2,2,3,48,384]{4,3,2,1,0:T(8,128)(2,1)S(1)}, bf16[2,2,3,48,384]{4,3,2,1,0:T(8,128)(2,1)S(1)}, u32[]{:S(2)}, u32[]{:S(2)}) collective-permute-start(bf16[2,2,3,48,384]{4,3,2,1,0:T(8,128)(2,1)S(1)} %pad_maximum_fusion.3), channel_id=1, source_target_pairs={{0,4},{2,6},{4,0},{6,2},{8,12},{10,14},{12,8},{14,10},{16,20},{18,... | collective-permute-start | bytes 1327112 | tf_op jit(solution)/shard_map/ppermute | solution.py:766
  402.8 13.9 %collective-permute-start.47 = (bf16[2,2,3,48,384]{4,3,2,1,0:T(8,128)(2,1)S(1)}, bf16[2,2,3,48,384]{4,3,2,1,0:T(8,128)(2,1)S(1)}, u32[]{:S(2)}, u32[]{:S(2)}) collective-permute-start(bf16[2,2,3,48,384]{4,3,2,1,0:T(8,128)(2,1)S(1)} %pad_maximum_fusion.4), channel_id=1, source_target_pairs={{0,1},{1,0},{2,3},{3,2},{4,5},{5,4},{6,7},{7,6},{8,9},{9,8},{10,11... | collective-permute-start | bytes 1327112 | tf_op jit(solution)/shard_map/ppermute | solution.py:770
  408.0 30.7 %collective-permute-start.44 = (bf16[512,768]{1,0:T(8,128)(2,1)S(1)}, bf16[512,768]{1,0:T(8,128)(2,1)S(1)}, u32[]{:S(2)}, u32[]{:S(2)}) collective-permute-start(bf16[512,768]{1,0:T(8,128)(2,1)S(1)} %constant_dynamic-slice_fusion), channel_id=1, source_target_pairs={{0,1},{1,0},{2,3},{3,2},{4,5},{5,4},{6,7},{7,6},{8,9},{9,8},{10,11... | collective-permute-start | bytes 2359304 | tf_op jit(solution)/shard_map/ppermute | solution.py:770
  419.1 17.3 %collective-permute-start.49 = (bf16[2,3,48,384]{3,2,1,0:T(8,128)(2,1)S(1)}, bf16[2,3,48,384]{3,2,1,0:T(8,128)(2,1)S(1)}, u32[]{:S(2)}, u32[]{:S(2)}) collective-permute-start(bf16[2,3,48,384]{3,2,1,0:T(8,128)(2,1)S(1)} %get-tuple-element.277), channel_id=1, source_target_pairs={{0,1},{1,0},{2,3},{3,2},{4,5},{5,4},{6,7},{7,6},{8,9},{9,8},{10,11... | collective-permute-start | bytes 663560 | tf_op jit(solution)/shard_map/ppermute | solution.py:770
  (75 other events, 864.6 us)
Sparse Core Ops, SparseCore 0:
  11.5 83.7 all-gather.2
  241.4 152.0 reduce-scatter.1

commit v3 on v1

v3 whole, which is shorter than its diff:
```python
import functools
import jax
import jax.numpy as jnp
import numpy as np
from jax import lax
from jax.experimental import pallas as pl
from jax.experimental.pallas import tpu as pltpu
from jax.sharding import PartitionSpec as P

DH = 64
NB = 32
REACH = 128
ROW = 1024
LANES = 128
QB = 256
masked_score = -1000000000.0
BF = jnp.bfloat16
F32 = jnp.float32
FORWARD_MB = 56
BACKWARD_MB = 56
PROJECT_MB = 56
MIDDLE_MB = 56
FEED_MB = 60
CROSS_BACK_MB = 56
WEIGHTS_MB = 56
SELF_BACK_MB = 56


def params(megabytes):
    return pltpu.CompilerParams(vmem_limit_bytes=megabytes * 1024 * 1024, dimension_semantics=("arbitrary",))


def dot_t(a, b):
    return lax.dot_general(a, b, (((1,), (1,)), ((), ())), preferred_element_type=F32)


def dot_n(a, b):
    return lax.dot_general(a, b, (((1,), (0,)), ((), ())), preferred_element_type=F32)


def dot_tn(a, b):
    return lax.dot_general(a, b, (((0,), (0,)), ((), ())), preferred_element_type=F32)


def split_three(x):
    top = x.astype(BF)
    rest = x - top.astype(F32)
    mid = rest.astype(BF)
    low = (rest - mid.astype(F32)).astype(BF)
    return top.astype(F32), mid.astype(F32), low.astype(F32)


def place_three(x, slot, other):
    top, mid, low = split_three(x)
    return jnp.where(slot == 4, top, jnp.where(slot == 5, mid, jnp.where(slot == 6, low, other)))


def lane_slots(shape):
    lane = lax.broadcasted_iota(jnp.int32, shape, 1)
    return lane, lane % DH


def make_extras(ids_ref, bounds_ref, causal, extra_q, extra_k):
    me = ids_ref[1]
    shape = extra_q.shape
    _, slot = lane_slots(shape)
    rows = lax.broadcasted_iota(jnp.int32, shape, 0)
    if causal:
        first = bounds_ref[me, 0]
        second = first + bounds_ref[me, 1]
        third = second + bounds_ref[me, 2]
        seg = (
            (rows >= first).astype(jnp.int32)
            + (rows >= second).astype(jnp.int32)
            + (rows >= third).astype(jnp.int32)
        )
        own = jnp.where(slot == seg, 1.0, 0.0)
        barred = jnp.where((slot < 4) & (slot != seg), masked_score, 0.0)
    else:
        own = jnp.where(slot == 0, 1.0, 0.0)
        barred = jnp.where((slot == 0) & (rows >= bounds_ref[me]), masked_score, 0.0)
    extra_q[...] = jnp.where(slot == 7, 1.0, own).astype(BF)
    extra_k[...] = jnp.where((slot >= 4) & (slot <= 6), 1.0, barred).astype(BF)


def band_square(band_ref, head):
    wide = jnp.broadcast_to(band_ref[head : head + 1, :], (LANES, 3 * LANES))
    rolled = pltpu.roll(wide, 0, 1, stride=1, stride_axis=0)
    return rolled[:, LANES : 2 * LANES], rolled[:, :LANES]


def add_band(scores, first, near, side):
    above = jnp.full((LANES, LANES), masked_score, F32)
    corner = jnp.concatenate([side, jnp.zeros((LANES, LANES), F32)], axis=0)
    left = jnp.concatenate([near, side], axis=0)
    right = jnp.concatenate([above, near], axis=0)
    pieces = []
    if first > 0:
        pieces.append(scores[:, : first - LANES])
        pieces.append(scores[:, first - LANES : first] + corner)
    pieces.append(scores[:, first : first + LANES] + left)
    pieces.append(scores[:, first + LANES :] + right)
    return jnp.concatenate(pieces, axis=1)


def forward_kernel(causal, extra, ids_ref, bounds_ref, band_ref, q_ref, k_ref, v_ref, *rest):
    o_ref, qa_ref, extra_q, extra_k = rest[extra:]
    length = q_ref.shape[0]

    @pl.when(pl.program_id(0) == 0)
    def _():
        make_extras(ids_ref, bounds_ref, causal, extra_q, extra_k)

    lane, slot = lane_slots((QB, LANES))
    full_lane, full_slot = lane_slots((length, LANES))
    ones = jnp.where(full_slot == 0, 1.0, 0.0).astype(BF)
    keys, values, bands = [], [], []
    for head in range(2):
        mine = (full_lane < DH) == (head == 0)
        keys.append(jnp.where(mine, k_ref[...], extra_k[...]))
        values.append(jnp.where(mine, v_ref[...], ones))
        if causal:
            bands.append(band_square(band_ref, head))

    def scores_of(block, head):
        first = block * QB
        count = first + QB if causal else length
        mine_block = (lane < DH) == (head == 0)
        queries = jnp.where(mine_block, q_ref[first : first + QB, :], extra_q[first : first + QB, :])
        return queries, dot_t(queries, keys[head][:count])

    todo = [(block, head) for block in range(length // QB) for head in range(2)]
    ahead = [scores_of(*item) for item in todo[:2]]
    for at, (block, head) in enumerate(todo):
        first = block * QB
        span = slice(first, first + QB)
        queries, scores = ahead.pop(0)
        if at + 2 < len(todo):
            ahead.append(scores_of(*todo[at + 2]))
        if causal:
            scores = add_band(scores, first, *bands[head])
        top = jnp.max(scores, axis=1, keepdims=True)
        weights = jnp.exp(scores - top).astype(BF)
        mixed = dot_n(weights, values[head][: weights.shape[1]])
        spare_column = DH if head == 0 else 0
        total = mixed[:, spare_column : spare_column + 1]
        mixed = mixed * (1.0 / total)
        if head == 0:
            kept = mixed
        else:
            o_ref[span, :] = jnp.where(lane < DH, kept, mixed).astype(BF)
        spare = place_three(-(top + jnp.log(total)), slot, queries.astype(F32))
        qa_ref[head, span, :] = jnp.where((lane < DH) == (head == 0), queries, spare.astype(BF))


def backward_kernel(causal, packed, extra, ids_ref, bounds_ref, band_ref, qa_ref, k_ref, v_ref, g_ref, o_ref, *rest):
    if causal:
        rest = rest[:2] + rest[2 + extra :]
        near_ref, normed_ref, grad_ref, bias_ref = rest[:4]
        wgrads = rest[4:-7]
        extra_q, extra_k, dk_acc, dv_acc, near_acc, side_acc, left = rest[-7:]
    else:
        grad_ref, extra_q, extra_k, dk_acc, dv_acc = rest[-5:]
    length = k_ref.shape[0]

    @pl.when(pl.program_id(0) == 0)
    def _():
        make_extras(ids_ref, bounds_ref, causal, extra_q, extra_k)
        if causal:
            put_turned(packed, ids_ref, left, slice(None), normed_ref[...])

    if causal:
        bias_ref[...] = jnp.zeros_like(bias_ref)

    lane, slot = lane_slots((QB, LANES))
    full_lane, full_slot = lane_slots((length, LANES))
    spare_v = jnp.where((full_slot >= 4) & (full_slot <= 6), 1.0, 0.0).astype(BF)
    for head in range(2):
        mine = (full_lane < DH) == (head == 0)
        mine_block = (lane < DH) == (head == 0)
        keys = jnp.where(mine, k_ref[...], extra_k[...])
        values = jnp.where(mine, v_ref[...], spare_v)
        if causal:
            near, side = band_square(band_ref, head)
            near, side = near.T, side.T
            near_only = jnp.full((LANES, LANES), masked_score, F32)
            near_acc[...] = jnp.zeros_like(near_acc)
            side_acc[...] = jnp.zeros_like(side_acc)
        dk_acc[...] = jnp.zeros_like(dk_acc)
        dv_acc[...] = jnp.zeros_like(dv_acc)
        for block in range(length // QB):
            first = block * QB
            count = first + QB if causal else length
            span = slice(first, first + QB)
            queries = qa_ref[head, span, :]
            upstream = g_ref[span, :]
            inner = jnp.sum(
                jnp.where(mine_block, upstream.astype(F32) * o_ref[span, :].astype(F32), 0.0), axis=1, keepdims=True
            )
            spare = place_three(-inner, slot, jnp.zeros((QB, LANES), F32))
            grads = jnp.where(mine_block, upstream, spare.astype(BF))
            scores = dot_t(keys[:count], queries)
            if causal:
                corner = jnp.concatenate([side, jnp.zeros((LANES, LANES), F32)], axis=1)
                upper = jnp.concatenate([near, side], axis=1)
                lower = jnp.concatenate([near_only, near], axis=1)
                pieces = []
                if block > 0:
                    if first > LANES:
                        pieces.append(scores[: first - LANES])
                    pieces.append(scores[first - LANES : first] + corner)
                pieces.append(scores[first : first + LANES] + upper)
                pieces.append(scores[first + LANES :] + lower)
                scores = jnp.concatenate(pieces, axis=0)
            probs = jnp.exp(scores)
            lifted = dot_t(values[:count], grads)
            score_grads = (probs * lifted).astype(BF)
            dv_acc[:count, :] += dot_n(probs.astype(BF), grads)
            dk_acc[:count, :] += dot_n(score_grads, queries)
            dq = dot_tn(score_grads, keys[:count])
            if causal:
                near_acc[...] += score_grads[first : first + LANES, :LANES].astype(F32)
                near_acc[...] += score_grads[first + LANES :, LANES:].astype(F32)
                side_acc[...] += score_grads[first : first + LANES, LANES:].astype(F32)
                if block > 0:
                    side_acc[...] += score_grads[first - LANES : first, :LANES].astype(F32)
            if head == 0:
                grad_ref[0, span, :] = dq.astype(BF)
            else:
                grad_ref[0, span, :] = jnp.where(lane < DH, grad_ref[0, span, :], dq.astype(BF))
        if head == 0:
            grad_ref[1] = dk_acc[...].astype(BF)
            grad_ref[2] = dv_acc[...].astype(BF)
        else:
            grad_ref[1] = jnp.where(full_lane < DH, grad_ref[1], dk_acc[...].astype(BF))
            grad_ref[2] = jnp.where(full_lane < DH, grad_ref[2], dv_acc[...].astype(BF))
        if causal:
            square = jnp.concatenate([side_acc[...], near_acc[...]], axis=0)
            wide = jnp.concatenate([square, jnp.zeros((2 * LANES, 2 * LANES), F32)], axis=1)
            half = LANES
            while half:
                wide = wide[:half] + pltpu.roll(wide[half:], 3 * LANES - half, 1)
                half //= 2
            diag = wide[:, 2 * LANES :]
            ones_column = jnp.where((full_lane % DH == 7) & ~mine, dk_acc[...], 0.0)
            whole = jnp.sum(ones_column, axis=0, keepdims=True)
            table = lax.dot_general(
                diag, near_ref[...], (((1,), (0,)), ((), ())),
                precision=lax.Precision.HIGHEST, preferred_element_type=F32,
            )
            last = jnp.sum(whole, axis=1, keepdims=True) - jnp.sum(table, axis=1, keepdims=True)
            at_last = lax.broadcasted_iota(jnp.int32, table.shape, 1) == NB - 1
            bias_ref[0, head : head + 1, :] = jnp.where(at_last, last, table)
    if causal:
        right = jnp.concatenate([grad_ref[n] for n in range(3)], axis=1)
        grads = dot_n(left[...], right).astype(BF)
        middle_row = grads.shape[0] // 2
        for n in range(3):
            part = grads[:, n * LANES : (n + 1) * LANES]
            if packed:
                shape = wgrads[0].shape[:3] + wgrads[0].shape[4:]
                wgrads[0][:, :, :, n] = part[:middle_row].reshape(shape)
                wgrads[1][:, :, :, n] = part[middle_row:].reshape(shape)
            else:
                wgrads[0][n] = part


def attention_forward(causal, ids, bounds, band, q, k, v, cols, start=0, stop=None, into=()):
    rows = q[0].shape[0]
    pairs = (cols // LANES if stop is None else stop) - start

    def spec(offset):
        return pl.BlockSpec((rows, LANES), lambda p, ids: (0, p + offset + start))

    n = rows * rows * pairs * 2
    return call(
        functools.partial(forward_kernel, causal, len(into)), "attention_forward", FORWARD_MB, pairs,
        [
            pl.BlockSpec(memory_space=pltpu.SMEM),
            pl.BlockSpec((None, 2, 3 * LANES), lambda p, ids: (p + start, 0, 0)),
            spec(q[1]), spec(k[1]), spec(v[1]),
        ] + [anywhere()] * len(into),
        [
            (spec(0), (rows, cols), BF),
            (pl.BlockSpec((2, rows, LANES), lambda p, ids: (p + start, 0, 0)), (2 * cols // LANES, rows, LANES), BF),
        ],
        [pltpu.VMEM((rows, LANES), BF)] * 2,
        n * 256 * 4 // (2 if causal else 1), rows * cols * 16,
        {6: 0, 7: 1} if into else {},
    )(ids, bounds, band, q[0], k[0], v[0], *into)


def cross_backward(ids, bounds, band, qa, k, v, g, o, start, stop, into=()):
    rows, cols = g.shape

    def spec(offset):
        return pl.BlockSpec((rows, LANES), lambda p, ids: (0, p + start + offset))

    n = rows * rows * (stop - start) * 2
    return call(
        functools.partial(backward_kernel, False, False, 0), "cross_backward", BACKWARD_MB, stop - start,
        [
            pl.BlockSpec(memory_space=pltpu.SMEM),
            pl.BlockSpec((None, 2, 3 * LANES), lambda p, ids: (p + start, 0, 0)),
            pl.BlockSpec((2, rows, LANES), lambda p, ids: (p + start, 0, 0)),
            spec(k[1]), spec(v[1]), spec(0), spec(0),
        ] + [anywhere()] * len(into),
        [(pl.BlockSpec((3, rows, LANES), lambda p, ids: (0, 0, p + start)), (3, rows, cols), BF)],
        [pltpu.VMEM((rows, LANES), BF)] * 2 + [pltpu.VMEM((rows, LANES), F32)] * 2,
        n * 256 * 10, rows * cols * 20,
        {8: 0} if into else {},
    )(ids, bounds, band, qa, k[0], v[0], g, o, *into)[0]


def self_backward(side, packed, ids, bounds, band, qa, k, v, g, o, normed, start=0, stop=None, into=()):
    rows, cols = g.shape
    pairs = cols // LANES // 2
    stop = pairs if stop is None else stop
    depth = normed.shape[1] >> BITS

    def at(p, ids):
        return p + start + pairs * jnp.bitwise_xor(ids[1], side)

    def spec(offset):
        return pl.BlockSpec((rows, LANES), lambda p, ids: (0, at(p, ids) + offset))

    n = rows * rows * (stop - start) * 2
    if packed:
        block = pl.BlockSpec((2, 2, 2, 3, depth, LANES), lambda p, ids: (0, 0, 0, 0, 0, p + start))
        wgrads = [(block, (2, 2, 2, 3, depth, cols // 2), BF)] * 2
    else:
        block = pl.BlockSpec((3, normed.shape[1], LANES), lambda p, ids: (0, 0, p + start))
        wgrads = [(block, (3, normed.shape[1], cols // 2), BF)]
    return call(
        functools.partial(backward_kernel, True, packed, len(into)), "self_backward", BACKWARD_MB, stop - start,
        [
            pl.BlockSpec(memory_space=pltpu.SMEM),
            pl.BlockSpec((None, 2, 3 * LANES), lambda p, ids: (at(p, ids), 0, 0)),
            pl.BlockSpec((2, rows, LANES), lambda p, ids: (at(p, ids), 0, 0)),
            spec(k[1]), spec(v[1]), spec(0), spec(0),
            held((LANES, LANES)), held(normed.shape),
        ] + [anywhere()] * len(into),
        [
            (pl.BlockSpec((3, rows, LANES), lambda p, ids: (0, 0, p + start)), (3, rows, cols // 2), BF),
            (pl.BlockSpec((1, 8, LANES), lambda p, ids: (at(p, ids), 0, 0)), (2 * pairs, 8, LANES), F32),
        ] + wgrads,
        [pltpu.VMEM((rows, LANES), BF)] * 2 + [pltpu.VMEM((rows, LANES), F32)] * 2
        + [pltpu.VMEM((LANES, LANES), F32)] * 2 + [pltpu.VMEM((normed.shape[1], rows), BF)],
        n * 256 * 8, rows * cols * 20,
        {10 + i: i for i in range(len(into))},
    )(ids, bounds, band, qa, k[0], v[0], g, o, jnp.asarray(near_buckets()), normed, *into)


def near_buckets():
    buckets = bucket_table(LANES, NB, REACH)
    columns = np.arange(LANES)[None, :]
    return ((buckets[:, None] == columns) & (columns < NB - 1)).astype(np.float32)


def bucket_table(length, buckets, reach):
    offsets = np.arange(length)
    exact_part = buckets // 2
    scaled = np.log(np.maximum(offsets, 1) / exact_part) / np.log(reach / exact_part) * (buckets - exact_part)
    far_bucket = np.minimum(exact_part + np.floor(scaled).astype(np.int64), buckets - 1)
    return np.where(offsets < exact_part, offsets, far_bucket).astype(np.int32)


def bias_band(rel_table):
    distance = LANES - np.arange(3 * LANES)
    buckets = bucket_table(LANES + 1, NB, REACH)
    onehot = np.zeros((3 * LANES, NB), np.float32)
    shift = np.zeros((3 * LANES,), np.float32)
    for at, far in enumerate(distance):
        if 0 <= far < LANES:
            onehot[at, buckets[far]] = 1.0
        elif -LANES < far < 0:
            shift[at] = masked_score
    relative = rel_table - rel_table[NB - 1 :]
    band = jnp.dot(jnp.asarray(onehot), relative, precision=lax.Precision.HIGHEST) + shift[:, None]
    return band.T.reshape(-1, 2, 3 * LANES)


epsilon = 1e-06
TB = 256
BITS = 4


def rms(values, gain):
    inverse = lax.rsqrt(jnp.mean(values * values, axis=-1, keepdims=True) + epsilon)
    return (values * inverse * gain).astype(BF), inverse


def rms_back(values, inverse, gain, upstream):
    weighted = upstream * gain
    inner_mean = jnp.mean(weighted * values, axis=-1, keepdims=True)
    grad_values = inverse * weighted - values * (inverse * inverse * inverse * inner_mean)
    return grad_values, jnp.sum(upstream * values * inverse, axis=0, keepdims=True)


def cost(flops, moved):
    return pl.CostEstimate(flops=flops, bytes_accessed=moved, transcendentals=0)


def turn(s, ids, blocks):
    return ((1 - ids[1]) * (blocks // 2) + jnp.minimum(s, blocks - 1)) % blocks


def row_spec(blocks, width, *lead):
    zeros = (0,) * len(lead)
    return pl.BlockSpec(lead + (TB, width), lambda s, ids: zeros + (turn(s, ids, blocks), 0))


def kept_spec(blocks, width):
    half = blocks // 2
    return pl.BlockSpec((None, TB, width), lambda s, ids: (ids[1], jnp.clip(s - half, 0, half - 1), 0))


def own_spec(blocks, width):
    half = blocks // 2
    return pl.BlockSpec((TB, width), lambda s, ids: (jnp.clip(s - half, 0, half - 1), 0))


def other_spec(blocks, width):
    return pl.BlockSpec((TB, width), lambda s, ids: (jnp.minimum(s, blocks // 2 - 1), 0))


def held(shape):
    zeros = (0,) * len(shape)
    return pl.BlockSpec(shape, lambda s, ids: zeros, pipeline_mode=pl.Buffered(1))


def anywhere():
    return pl.BlockSpec(memory_space=pl.ANY)


def call(kernel, name, megabytes, grid, in_specs, outs, scratch, flops, moved, aliases=None):
    return pl.pallas_call(
        kernel,
        grid_spec=pltpu.PrefetchScalarGridSpec(
            num_scalar_prefetch=1,
            grid=(grid,),
            in_specs=in_specs,
            out_specs=[o[0] for o in outs],
            scratch_shapes=scratch,
        ),
        out_shape=[jax.ShapeDtypeStruct(o[1], o[2]) for o in outs],
        input_output_aliases=aliases or {},
        compiler_params=params(megabytes),
        cost_estimate=cost(flops, moved),
        name=name,
    )


def chosen(step, blocks, came_ref, kept_ref):
    return jnp.where(step < blocks // 2, came_ref[...], kept_ref[...])


def share(step, blocks, values, own_ref, other_ref):
    @pl.when(step < blocks // 2)
    def _():
        other_ref[...] = values.astype(BF)

    @pl.when(step >= blocks // 2)
    def _():
        own_ref[...] = values


def gather_table():
    near = [((0, 0, 0),), ((0, 1, 0),), ((1, 0, 0), (1, 1, 0)), ((0, 0, 1),), ((1, 0, 1),), ((0, 1, 1), (1, 1, 1))]
    table = []
    for c in range(2):
        for places in near:
            entries = []
            for at, (y, x, z0) in enumerate(places):
                for z1 in range(2):
                    entries.append(((at, z1) if len(places) > 1 else (z1,), (y, x, z0, z1, c), 0))
            table.append(entries)
    return table


def wide_table():
    pairs = [(a, b) for a in range(2) for b in range(2)]
    table = []
    for c in range(2):
        for y in range(2):
            table.append([((z0, z1, x), (y, x, z0, z1, c), 0) for x in range(2) for z0, z1 in pairs])
    for c in range(2):
        for z0 in range(2):
            table.append([((z1, y, x), (y, x, z0, z1, c), 1) for x in range(2) for z1, y in pairs])
    return table


def copy_pieces(ids_ref, pieces, table, place, w_ref, sem):
    if len(pieces) == 1:
        pltpu.make_async_copy(pieces[0], w_ref, sem).start()
    else:
        mine = ids_ref[2]
        rows = pieces[0].shape[-2]

        def copy(flip):
            for piece, entries in zip(pieces, table):
                for at, (y, x, z0, z1, c), part in entries:
                    block = jnp.bitwise_xor(mine, 8 * z1 + 4 * z0 + 2 * y + c)
                    span = pl.ds(pl.multiple_of(block * rows, 16), rows)
                    pltpu.make_async_copy(piece.at[at], place(span, x ^ flip, part), sem).start()

        @pl.when(ids_ref[1] == 0)
        def _():
            copy(0)

        @pl.when(ids_ref[1] == 1)
        def _():
            copy(1)

    pltpu.make_async_copy(w_ref, w_ref, sem).wait()


def natural_place(w_ref, cols):
    return lambda span, x, part: w_ref.at[:, span, x * cols : (x + 1) * cols]


def put_turned(packed, ids_ref, target, span, values):
    turned = values.T
    if not packed:
        target[:, span] = turned
        return
    depth = turned.shape[0] >> BITS
    for block in range(1 << BITS):
        reverse = int(format(block, "04b")[::-1], 2)
        at = jnp.bitwise_xor(ids_ref[0], reverse) * depth
        target[pl.ds(pl.multiple_of(at, 16), depth), span] = turned[block * depth : (block + 1) * depth]


def put_grads(packed, ids_ref, n, grads, outs):
    if not packed:
        outs[0][n] = grads
        return
    keep_ref, send_ref = outs
    rows, cols = keep_ref.shape[-2:]
    middle = grads.shape[0] // 2

    def store(flip):
        for x in range(2):
            first = cols * (x ^ flip)
            for target, part in ((keep_ref, grads[:middle]), (send_ref, grads[middle:])):
                block = part[:, first : first + cols].reshape(2, 2, 2, rows, cols)
                target[:, x, :, :, n] = block

    @pl.when(ids_ref[1] == 0)
    def _():
        store(0)

    @pl.when(ids_ref[1] == 1)
    def _():
        store(1)


def grads_out(packed, n, width):
    if not packed:
        shape = (n, width, width)
        return [(held(shape), shape, BF)]
    shape = (2, 2, 2, 2, n, width >> BITS, width // 2)
    return [(held(shape), shape, BF)] * 2


def project_kernel(blocks, pieces, ids_ref, gain_ref, came_ref, kept_ref, *refs):
    w_in = refs[:pieces]
    normed_ref, out_ref, w_ref, sem = refs[pieces:]
    step = pl.program_id(0)

    @pl.when(step == 0)
    def _():
        copy_pieces(ids_ref, w_in, gather_table(), natural_place(w_ref, w_in[0].shape[-1]), w_ref, sem)

    normed, _ = rms(chosen(step, blocks, came_ref, kept_ref).astype(F32), gain_ref[0:1, :])
    normed_ref[...] = normed
    width = normed.shape[1]
    for s in range(3):
        out_ref[:, s * width : (s + 1) * width] = dot_n(normed, w_ref[s]).astype(BF)


def project(ids, gain, came, kept, pieces):
    _, half, width = kept.shape
    rows = 2 * half
    blocks = rows // TB
    full = (3, width, width)
    return call(
        functools.partial(project_kernel, blocks, len(pieces)), "project", PROJECT_MB, blocks,
        [held((3, width)), other_spec(blocks, width), kept_spec(blocks, width)] + [anywhere()] * len(pieces),
        [
            (row_spec(blocks, width), (rows, width), BF),
            (row_spec(blocks, 3 * width), (rows, 3 * width), BF),
            (held(full), full, BF),
        ],
        [pltpu.SemaphoreType.DMA],
        6 * rows * width * width, 10 * rows * width + 6 * width * width,
    )(ids, gain, came, kept, *pieces)


def middle_kernel(blocks, pieces, ids_ref, gain_ref, came_ref, kept_ref, mixed_ref, mem_came_ref, mem_kept_ref, *refs):
    w_in = refs[:pieces]
    resid_ref, normed_ref, q_ref, k_ref, v_ref, w_ref, sem = refs[pieces:]
    step = pl.program_id(0)

    @pl.when(step == 0)
    def _():
        copy_pieces(ids_ref, w_in, gather_table(), natural_place(w_ref, w_in[0].shape[-1]), w_ref, sem)

    resid = chosen(step, blocks, came_ref, kept_ref).astype(F32) + dot_t(mixed_ref[...], w_ref[0])
    resid_ref[...] = resid
    normed, _ = rms(resid, gain_ref[1:2, :])
    normed_ref[...] = normed
    q_ref[...] = dot_n(normed, w_ref[1]).astype(BF)
    memory = chosen(step, blocks, mem_came_ref, mem_kept_ref)
    k_ref[...] = dot_n(memory, w_ref[2]).astype(BF)
    v_ref[...] = dot_n(memory, w_ref[3]).astype(BF)


def middle(ids, gain, came, kept, mixed, mem_came, mem_kept, pieces):
    rows, width = mixed.shape
    blocks = rows // TB
    full = (5, width, width)
    spec = row_spec(blocks, width)
    pair = [other_spec(blocks, width), kept_spec(blocks, width)]
    return call(
        functools.partial(middle_kernel, blocks, len(pieces)), "middle", MIDDLE_MB, blocks,
        [held((3, width))] + pair + [spec] + pair + [anywhere()] * len(pieces),
        [(spec, (rows, width), F32)] + [(spec, (rows, width), BF)] * 4 + [(held(full), full, BF)],
        [pltpu.SemaphoreType.DMA],
        8 * rows * width * width, 20 * rows * width + 10 * width * width,
    )(ids, gain, came, kept, mixed, mem_came, mem_kept, *pieces)


def feed_kernel(blocks, pieces, packed, ids_ref, docs_ref, gain_ref, resid_ref, mixed_ref, cot_came_ref, cot_kept_ref,
                wo_ref, *refs):
    w_in = refs[:pieces]
    refs = refs[pieces:]
    own_ref, other_ref, grad_ref, gmix_ref, gain_grad_ref = refs[:5]
    wgrads = refs[5:-7]
    w_ref, normed_t, branch_t, hidden_s, gate_s, up_s, sem = refs[-7:]
    step = pl.program_id(0)
    me = ids_ref[1]
    width = resid_ref.shape[1]

    def weight(which, x):
        return w_ref[x, which]

    @pl.when(step == 0)
    def _():
        cols = w_in[0].shape[-1]
        copy_pieces(
            ids_ref, w_in, wide_table(),
            lambda span, x, part: w_ref.at[x, :, span, cols * part : cols if part == 0 else None], w_ref, sem,
        )
        gain_grad_ref[...] = jnp.zeros_like(gain_grad_ref)

    @pl.when(step < blocks)
    def _():
        first = pl.multiple_of(turn(step, ids_ref, blocks) * TB, TB)
        span = pl.ds(first, TB)
        resid = resid_ref[...] + dot_t(mixed_ref[...], wo_ref[...])
        normed, inverse = rms(resid, gain_ref[2:3, :])
        slots = first + lax.broadcasted_iota(jnp.int32, (TB, 1), 0)
        padding = slots >= docs_ref[me, 0] + docs_ref[me, 1] + docs_ref[me, 2]
        grad_four = jnp.where(padding, 0.0, chosen(step, blocks, cot_came_ref, cot_kept_ref).astype(F32))
        branch = grad_four.astype(BF)
        put_turned(packed, ids_ref, normed_t, span, normed)
        put_turned(packed, ids_ref, branch_t, span, branch)
        total = resid
        upstream = jnp.zeros((TB, width), F32)
        for x in range(2):
            gate = dot_n(normed, weight(0, x))
            up = dot_n(normed, weight(1, x))
            lifted = dot_n(branch, weight(2, x))
            square = gate * gate
            inner = jnp.tanh(gate * (0.7978845608028654 + 0.035677408136300125 * square))
            half_up = 0.5 + 0.5 * inner
            activated = gate * half_up
            slope = half_up + (0.5 * gate) * (1.0 - inner * inner) * (
                0.7978845608028654 + 0.10703222440890037 * square
            )
            hidden = (activated * up).astype(BF)
            gate_grad = (lifted * up * slope).astype(BF)
            up_grad = (lifted * activated).astype(BF)
            hidden_s[x, span, :] = hidden
            gate_s[x, span, :] = gate_grad
            up_s[x, span, :] = up_grad
            total = total + dot_t(hidden, weight(2, x))
            upstream = upstream + dot_t(gate_grad, weight(0, x)) + dot_t(up_grad, weight(1, x))
        share(step, blocks, jnp.where(padding, 0.0, total), own_ref, other_ref)
        grad_resid, gain_grad = rms_back(resid, inverse, gain_ref[2:3, :], upstream)
        grad = grad_four + grad_resid
        grad_ref[...] = grad
        gain_grad_ref[...] += gain_grad
        gmix_ref[...] = dot_n(grad.astype(BF), wo_ref[...]).astype(BF)

    for which, (left, right) in enumerate(((normed_t, gate_s), (normed_t, up_s), (branch_t, hidden_s))):
        for x in range(2):

            @pl.when(step == blocks + 2 * which + x)
            def _():
                if packed:
                    grads = dot_n(left[...], right[jnp.bitwise_xor(x, me)]).astype(BF)
                    middle_row = grads.shape[0] // 2
                    wgrads[0][...] = grads[:middle_row].reshape(wgrads[0].shape)
                    wgrads[1][...] = grads[middle_row:].reshape(wgrads[1].shape)
                else:
                    wgrads[0][...] = dot_n(left[...], right[x]).astype(BF)


def feed(packed, ids, docs, gain, resid, mixed, cot_came, cot_kept, w_mid, pieces):
    rows, width = resid.shape
    half = pieces[0].shape[-1] if len(pieces) == 1 else pieces[0].shape[-1] + pieces[-1].shape[-1]
    blocks = rows // TB
    spec = row_spec(blocks, width)

    def at(s):
        late = jnp.maximum(s - blocks, 0)
        return late // 2, late % 2

    if packed:
        depth = width >> BITS
        block = pl.BlockSpec((2, None, 2, 2, None, depth, half), lambda s, ids: (0, at(s)[1], 0, 0, at(s)[0], 0, 0))
        wgrads = [(block, (2, 2, 2, 2, 3, depth, half), BF)] * 2
    else:
        block = pl.BlockSpec((None, None, width, half), lambda s, ids: (at(s)[1], at(s)[0], 0, 0))
        wgrads = [(block, (2, 3, width, half), BF)]
    return call(
        functools.partial(feed_kernel, blocks, len(pieces), packed), "feed", FEED_MB, blocks + 6,
        [pl.BlockSpec(memory_space=pltpu.SMEM), held((3, width)), spec, spec, other_spec(blocks, width),
         kept_spec(blocks, width),
         pl.BlockSpec((None, width, width), lambda s, ids: (4, 0, 0), pipeline_mode=pl.Buffered(1))]
        + [anywhere()] * len(pieces),
        [
            (own_spec(blocks, width), (rows // 2, width), F32),
            (other_spec(blocks, width), (rows // 2, width), BF),
            (spec, (rows, width), F32),
            (spec, (rows, width), BF),
            (held((1, width)), (1, width), F32),
        ] + wgrads,
        [pltpu.VMEM((2, 3, width, half), BF)] + [pltpu.VMEM((width, rows), BF)] * 2
        + [pltpu.VMEM((2, rows, half), BF)] * 3 + [pltpu.SemaphoreType.DMA],
        36 * rows * width * half, 24 * rows * width + 24 * width * half,
    )(ids, docs, gain, resid, mixed, cot_came, cot_kept, w_mid, *pieces)


def cross_back_kernel(blocks, packed, ids_ref, gain_ref, d_ref, resid_ref, normed_ref, mem_came_ref, mem_kept_ref,
                      grad_ref, mixed_cross_ref, mixed_self_ref, w_ref, *outs):
    grad_two_ref, gmix_ref, gmem_own_ref, gmem_other_ref, gain_grad_ref = outs[:5]
    wgrads = outs[5:-2]
    lefts, rights = outs[-2:]
    step = pl.program_id(0)

    @pl.when(step == 0)
    def _():
        gain_grad_ref[...] = jnp.zeros_like(gain_grad_ref)

    @pl.when(step < blocks)
    def _():
        span = pl.ds(pl.multiple_of(turn(step, ids_ref, blocks) * TB, TB), TB)
        resid = resid_ref[...]
        inverse = lax.rsqrt(jnp.mean(resid * resid, axis=-1, keepdims=True) + epsilon)
        grad_resid, gain_grad = rms_back(resid, inverse, gain_ref[1:2, :], dot_t(d_ref[0], w_ref[1]))
        gain_grad_ref[...] += gain_grad
        grad_three = grad_ref[...]
        grad_two = grad_three + grad_resid
        grad_two_ref[...] = grad_two
        branch = grad_two.astype(BF)
        gmix_ref[...] = dot_n(branch, w_ref[0]).astype(BF)
        gmem = dot_t(d_ref[1], w_ref[2]) + dot_t(d_ref[2], w_ref[3])
        share(step, blocks, gmem, gmem_own_ref, gmem_other_ref)
        memory = chosen(step, blocks, mem_came_ref, mem_kept_ref)
        for n, values in enumerate((branch, normed_ref[...], memory, grad_three.astype(BF))):
            put_turned(packed, ids_ref, lefts.at[n], span, values)
        rights[0, span, :] = mixed_self_ref[...]
        rights[1, span, :] = d_ref[0]
        rights[2, span, :] = d_ref[1]
        rights[3, span, :] = d_ref[2]
        rights[4, span, :] = mixed_cross_ref[...]

    for n, left in enumerate((0, 1, 2, 2, 3)):

        @pl.when(step == blocks + n)
        def _():
            put_grads(packed, ids_ref, n, dot_n(lefts[left], rights[n]).astype(BF), wgrads)


def cross_back(packed, ids, gain, d, resid, normed, mem_came, mem_kept, grad, mixed_cross, mixed_self, w):
    rows, width = resid.shape
    blocks = rows // TB
    spec = row_spec(blocks, width)
    return call(
        functools.partial(cross_back_kernel, blocks, packed), "cross_back", CROSS_BACK_MB, blocks + 5,
        [held((3, width)), row_spec(blocks, width, 3), spec, spec, other_spec(blocks, width), kept_spec(blocks, width),
         spec, spec, spec, held(w.shape)],
        [
            (spec, (rows, width), F32),
            (spec, (rows, width), BF),
            (own_spec(blocks, width), (rows // 2, width), F32),
            (other_spec(blocks, width), (rows // 2, width), BF),
            (held((1, width)), (1, width), F32),
        ] + grads_out(packed, 5, width),
        [pltpu.VMEM((4, width, rows), BF), pltpu.VMEM((5, rows, width), BF)],
        18 * rows * width * width, 36 * rows * width + 20 * width * width,
    )(ids, gain, d, resid, normed, mem_came, mem_kept, grad, mixed_cross, mixed_self, w)


def self_back_kernel(blocks, ids_ref, gain_ref, ours_ref, theirs_ref, came_ref, kept_ref, grad_ref, w_ref,
                     own_ref, other_ref, gain_grad_ref):
    step = pl.program_id(0)

    @pl.when(step == 0)
    def _():
        gain_grad_ref[...] = jnp.zeros_like(gain_grad_ref)

    values = chosen(step, blocks, came_ref, kept_ref).astype(F32)
    inverse = lax.rsqrt(jnp.mean(values * values, axis=-1, keepdims=True) + epsilon)
    upstream = jnp.zeros(values.shape, F32)
    for n in range(3):
        ours, theirs = ours_ref[n], theirs_ref[n]
        first = jnp.where(ids_ref[1] == 0, ours, theirs)
        second = jnp.where(ids_ref[1] == 0, theirs, ours)
        upstream = upstream + dot_t(jnp.concatenate([first, second], axis=1), w_ref[n])
    grad_values, gain_grad = rms_back(values, inverse, gain_ref[0:1, :], upstream)
    gain_grad_ref[...] += gain_grad
    share(step, blocks, grad_ref[...] + grad_values, own_ref, other_ref)


def self_back(ids, gain, ours, theirs, came, kept, grad, w):
    rows, width = grad.shape
    blocks = rows // TB
    part = row_spec(blocks, width // 2, 3)
    return call(
        functools.partial(self_back_kernel, blocks), "self_back", SELF_BACK_MB, blocks,
        [held((3, width)), part, part, other_spec(blocks, width), kept_spec(blocks, width),
         row_spec(blocks, width), held(w.shape)],
        [
            (own_spec(blocks, width), (rows // 2, width), F32),
            (other_spec(blocks, width), (rows // 2, width), BF),
            (held((1, width)), (1, width), F32),
        ],
        [],
        6 * rows * width * width, 20 * rows * width + 6 * width * width,
    )(ids, gain, ours, theirs, came, kept, grad, w)


def flip_bit(values, bit):
    size = lax.axis_size("dp")
    return lax.ppermute(values, "dp", [(i, i ^ (1 << bit)) for i in range(size)])


def flip_mp(values):
    return lax.ppermute(values, "mp", [(0, 1), (1, 0)])


class Steps:
    def send(self, *parts):
        self.sent = [part[0] for part in parts]
        self.bits = [part[1] for part in parts]

    def launch(self):
        self.state = [flip_mp(a) if bit is None else flip_bit(a, bit) for a, bit in zip(self.sent, self.bits)]


def begin(value, *steps):
    value, sent = lax.optimization_barrier((value, [s.sent for s in steps]))
    for step, arrays in zip(steps, sent):
        step.sent = arrays
        step.launch()
    return value


def hold(value, *steps):
    value, states = lax.optimization_barrier((value, [s.state for s in steps]))
    for step, state in zip(steps, states):
        step.state = state
    return value


class Swap(Steps):
    def __init__(self, sent):
        self.send((sent, None))


class Gather(Steps):
    def __init__(self, shard):
        self.shard = shard
        self.low_c = None
        self.send((shard, 3))

    def second(self):
        self.low = jnp.stack([self.shard, self.state[0]])
        self.send((self.low, 2))

    def third(self):
        (self.high,) = self.state
        self.send((self.low, None), (self.high, 1))

    def fourth(self):
        self.low_x, self.high_y = self.state
        self.send((jnp.stack([self.low, self.low_x]), 1), (jnp.stack([self.high, self.high_y]), None))

    def over_cores(self):
        self.low_c = flip_bit(self.low, 0)
        self.high_c = flip_bit(self.high, 0)

    def pieces(self):
        low_y, high_x = self.state
        if self.low_c is None:
            self.over_cores()
        return [
            self.low, self.low_x, low_y, self.high, self.high_y, high_x,
            self.low_c, flip_bit(self.low_x, 0), flip_bit(low_y, 0),
            self.high_c, flip_bit(self.high_y, 0), flip_bit(high_x, 0),
        ]


class WideGather(Steps):
    def __init__(self, proj, out):
        self.shard = jnp.concatenate([proj, out])
        self.send((proj, None), (out, None))

    def split(self):
        both = jnp.stack([self.shard, jnp.concatenate(self.state)])
        cut = both.shape[-1] * 5 // 8
        return WidePart(both[..., :cut], 3), WidePart(both[..., cut:], 1)


class WidePart(Steps):
    def __init__(self, near, bit):
        self.near = near
        self.send((near, bit))

    def flip(self, bit):
        self.near = jnp.stack([self.near, self.state[0]])
        self.send((self.near, bit))

    def pieces(self):
        near = [self.near, self.state[0]]
        return near + [flip_bit(piece, 0) for piece in near]


class Scatter(Steps):
    def __init__(self, keep, send):
        self.keep = keep
        self.send((send, 0))

    def own(self, *at):
        return self.keep[at].astype(F32) + self.came[at].astype(F32)

    def second(self):
        (self.came,) = self.state
        every = slice(None)
        self.send((self.own(1, every, 0).astype(BF), 1), (self.own(every, 1, 1).astype(BF), None))

    def third(self):
        low_y, high_x = self.state
        self.kept = (low_y, high_x)
        self.send(
            ((self.own(0, 1, 0) + low_y[1].astype(F32)).astype(BF), None),
            ((self.own(1, 0, 1) + high_x[1].astype(F32)).astype(BF), 1),
        )

    def fourth(self):
        low_y, high_x = self.kept
        low_x, high_y = self.state
        high = self.own(0, 0, 1) + high_x[0].astype(F32) + high_y.astype(F32)
        self.kept = self.own(0, 0, 0) + low_y[0].astype(F32) + low_x.astype(F32)
        self.send((high.astype(BF), 2))

    def fifth(self):
        self.kept = self.kept + self.state[0].astype(F32)
        self.send((self.kept[1].astype(BF), 3))

    def total(self):
        return self.kept[0] + self.state[0].astype(F32)


class SideScatter(Steps):
    def __init__(self, keep, send):
        self.kept = keep
        self.send((send, 0))

    def take(self):
        self.kept = self.kept.astype(F32) + self.state[0].astype(F32)

    def flip(self, bit):
        self.take()
        self.send((self.kept[1].astype(BF), bit))
        self.kept = self.kept[0]

    def across(self):
        self.take()
        self.send((self.kept.astype(BF), None))


def gather_whole(shard):
    n, rows, cols = shard.shape
    dp = lax.axis_size("dp")
    mp = lax.axis_size("mp")
    pieces = lax.all_gather(shard, ("dp", "mp"), axis=0).reshape(dp, mp, n, rows, cols)
    return pieces.transpose(2, 0, 3, 1, 4).reshape(n, dp * rows, mp * cols)


def scatter_whole(grads):
    dp = lax.axis_size("dp")
    mp = lax.axis_size("mp")
    n, rows, cols = grads.shape
    pieces = grads.reshape(n, dp, rows // dp, mp, cols // mp).transpose(1, 3, 0, 2, 4)
    pieces = pieces.reshape((dp * mp,) + pieces.shape[2:])
    return lax.psum_scatter(pieces, ("dp", "mp"), scatter_dimension=0, tiled=True)[0].astype(F32)


class Sum(Steps):
    def __init__(self, values, bit):
        self.values = values
        self.send((values, bit))

    def flip(self, bit):
        self.take()
        self.send((self.values, bit))

    def take(self):
        self.values = self.values + self.state[0]


def other_row(pair_rows, me):
    return lax.dynamic_index_in_dim(pair_rows, 1 - me, 0, False)


def both_halves(own, came, me):
    came = came.astype(F32)
    return jnp.where(me == 0, jnp.stack([own, came]), jnp.stack([came, own]))


def per_device(
    tokens,
    memory,
    doc_lengths,
    mem_lengths,
    norm_gains,
    rel_table,
    self_proj,
    self_out,
    cross_proj,
    cross_out,
    ffn_proj,
    ffn_out,
    cotangent,
):
    me = lax.axis_index("mp")
    dp = lax.axis_size("dp")
    width = tokens.shape[2]
    packed = dp == 1 << BITS and lax.axis_size("mp") == 2
    place = lax.axis_index("dp")
    reverse = sum(((place >> i) & 1) << (BITS - 1 - i) for i in range(BITS))
    ids = jnp.stack([reverse, me, place]).astype(jnp.int32)
    band = bias_band(rel_table)
    pairs = width // LANES
    x_swap = Swap(other_row(tokens, me))
    shard_mid = jnp.concatenate([self_out.T[None], cross_proj, cross_out.T[None]])
    mem_swap = Swap(other_row(memory, me))

    if packed:
        w_one = Gather(self_proj)
        w_ffn = WideGather(ffn_proj, ffn_out.T[None])
        w_one.launch()
        x_swap.launch()
        shard_mid, w_ffn.sent, mem_swap.sent, ids, band, cotangent = hold(
            (shard_mid, w_ffn.sent, mem_swap.sent, ids, band, cotangent), w_one
        )
        w_one.second()
        cot_swap = Swap(other_row(cotangent, me))
        begin((), w_one, w_ffn)
        shard_mid, cot_swap.sent = hold((shard_mid, cot_swap.sent), w_one)
        w_two = Gather(shard_mid)
        w_one.third()
        begin((), w_one, w_two)
        hold((), w_one, x_swap, w_two)
        w_one.fourth()
        w_two.second()
        begin((), w_one, w_two)
        w_one.over_cores()
        hold((), w_one, w_two, w_ffn)
        left, right = w_ffn.split()
        w_self = w_one.pieces()
        w_two.third()
        w_self = begin(w_self, w_two, left, right, mem_swap)
    else:
        cot_swap = Swap(other_row(cotangent, me))
        begin((), x_swap, mem_swap, cot_swap)
        w_self = [gather_whole(self_proj)]
        w_mid = [gather_whole(shard_mid)]
        w_ffn = gather_whole(jnp.concatenate([ffn_proj, ffn_out.T[None]]))
        w_ffn = [w_ffn.reshape(3, width, 2, -1).transpose(2, 0, 1, 3)]
    x = (x_swap.state[0], tokens)
    normed_one, qkv, w_self = project(ids, norm_gains, *x, w_self)
    parts = ((qkv, 0), (qkv, pairs), (qkv, 2 * pairs))
    self_args = (True, ids, doc_lengths, band)
    if packed:
        mixed = attention_forward(*self_args, *parts, width, 0, pairs // 2)
        mixed = hold(mixed, w_two, left, right)
        w_two.fourth()
        left.flip(2)
        mixed = begin(mixed, w_two, left)
        w_two.over_cores()
        mixed_self, qa_self = attention_forward(*self_args, *parts, width, pairs // 2, pairs, mixed)
        mixed_self = hold(mixed_self, mem_swap, w_two, left)
        w_mid = w_two.pieces()
        left.flip(1)
        right.flip(3)
        mixed_self, w_mid = begin((mixed_self, w_mid), left, right, cot_swap)
    else:
        mixed_self, qa_self = attention_forward(*self_args, *parts, width)
    mem = (mem_swap.state[0], memory)
    resid_two, normed_two, q_cross, k_cross, v_cross, w_mid = middle(ids, norm_gains, *x, mixed_self, *mem, w_mid)
    cross_args = (False, ids, mem_lengths, band)
    if packed:
        q_cross = hold(q_cross, right)
        right.flip(2)
        q_cross = begin(q_cross, right)
    parts = ((q_cross, 0), (k_cross, 0), (v_cross, 0))
    if packed:
        mixed = attention_forward(*cross_args, *parts, width, 0, pairs - 1)
        mixed = hold(mixed, left, right, cot_swap)
        w_ffn = left.pieces() + right.pieces()
        mixed_cross, qa_cross = attention_forward(*cross_args, *parts, width, pairs - 1, pairs, mixed)
    else:
        mixed_cross, qa_cross = attention_forward(*cross_args, *parts, width)
    output, output_sent, grad_three, grad_mixed, gain_three, *ffn_grads = feed(
        packed, ids, doc_lengths, norm_gains, resid_two, mixed_cross, cot_swap.state[0], cotangent, w_mid, w_ffn
    )
    out_swap = Swap(output_sent)
    cross_args = cross_args[1:]
    parts = (qa_cross, (k_cross, 0), (v_cross, 0))
    if packed:
        ffn = Scatter(*ffn_grads)
        grad_mixed = begin(grad_mixed, out_swap, ffn)
        grads = cross_backward(*cross_args, *parts, grad_mixed, mixed_cross, 0, 2)
        grads = hold(grads, ffn)
        ffn.second()
        grads, grad_mixed = begin((grads, grad_mixed), ffn)
        grads_cross = cross_backward(*cross_args, *parts, grad_mixed, mixed_cross, 2, pairs, (grads,))
        grads_cross = hold(grads_cross, ffn)
        ffn.third()
        grads_cross = begin(grads_cross, ffn)
    else:
        begin((), out_swap)
        grads_cross = cross_backward(*cross_args, *parts, grad_mixed, mixed_cross, 0, pairs)
    grads_cross = hold(grads_cross, out_swap)
    grad_two, grad_mixed, gmem, gmem_sent, gain_two, *mid_grads = cross_back(
        packed, ids, norm_gains, grads_cross, resid_two, normed_two, *mem, grad_three, mixed_cross, mixed_self, w_mid
    )
    gmem_swap = Swap(gmem_sent)
    parts = (qa_self, (qkv, pairs), (qkv, 2 * pairs))
    more = (mixed_self, normed_one)
    if packed:
        mid = Scatter(*mid_grads)
        hold((), ffn)
        ffn.fourth()
        grad_mixed = begin(grad_mixed, mid, gmem_swap, ffn)
        results = self_backward(1, packed, *self_args[1:], *parts, grad_mixed, *more, 0, 1)
        results = hold(results, mid)
        mid.second()
        results, grad_mixed = begin((results, grad_mixed), mid)
        d_theirs, table_theirs, *grads_theirs = self_backward(
            1, packed, *self_args[1:], *parts, grad_mixed, *more, 1, None, results
        )
        d_theirs, grads_theirs, grad_mixed = hold((d_theirs, grads_theirs, grad_mixed), mid, ffn)
        theirs = SideScatter(*grads_theirs)
        theirs.launch()
        mid.third()
        ffn.fifth()
        mid.sent, ffn.sent = hold((mid.sent, ffn.sent), theirs)
        theirs.flip(1)
        grad_mixed = begin(grad_mixed, mid, theirs, ffn)
        d_ours, table_ours, *grads_ours = self_backward(0, packed, *self_args[1:], *parts, grad_mixed, *more)
        d_ours, grads_ours = hold((d_ours, grads_ours), mid, theirs, gmem_swap, ffn)
        ours = SideScatter(*grads_ours)
        ours.launch()
        theirs.flip(2)
        mid.fourth()
        theirs.sent, mid.sent = hold((theirs.sent, mid.sent), ours)
        ours.flip(1)
        d_ours = begin(d_ours, ours, theirs, mid)
    else:
        begin((), gmem_swap)
        d_theirs, table_theirs, *grads_theirs = self_backward(1, packed, *self_args[1:], *parts, grad_mixed, *more)
        d_ours, table_ours, *grads_ours = self_backward(0, packed, *self_args[1:], *parts, grad_mixed, *more)
    grad_x, grad_x_sent, gain_one = self_back(ids, norm_gains, d_ours, d_theirs, *x, grad_two, w_self)
    grad_x_swap = Swap(grad_x_sent)
    half_of = (jnp.arange(pairs, dtype=jnp.int32) >= pairs // 2).astype(jnp.int32)[:, None, None]
    if packed:
        grad_x_swap.sent, gain_one, table_ours, table_theirs = hold(
            (grad_x_swap.sent, gain_one, table_ours, table_theirs), mid, ours, theirs
        )
        ours.flip(2)
        theirs.flip(3)
        mid.fifth()
        gain_one, table_ours, table_theirs = begin(
            (gain_one, table_ours, table_theirs), grad_x_swap, ours, theirs, mid
        )
    table = jnp.where(half_of == me, table_ours, table_theirs).reshape(-1, width)
    small = jnp.concatenate([gain_one, gain_two, gain_three, table])
    if packed:
        small = Sum(small, 0)
        small.launch()
        small.flip(None)
        small.launch()
        small.flip(1)
        small.launch()
        hold((), mid, ours, theirs, small)
        small.flip(2)
        small.launch()
        ours.flip(3)
        theirs.across()
        begin((), ours, theirs)
        small.flip(3)
        small.launch()
        ffn_grads = ffn.total()
        mid_grads = mid.total()
        ours.take()
        self_grads = ours.kept + theirs.state[0].astype(F32)
        small.take()
        small = small.values
    else:
        begin((), grad_x_swap)
        ffn_grads = scatter_whole(ffn_grads[0].transpose(1, 2, 0, 3).reshape(3, width, -1))
        mid_grads = scatter_whole(mid_grads[0])
        self_grads = scatter_whole(
            jnp.where(
                me == 0,
                jnp.concatenate([grads_ours[0], grads_theirs[0]], axis=2),
                jnp.concatenate([grads_theirs[0], grads_ours[0]], axis=2),
            )
        )
        small = lax.psum(small, ("dp", "mp"))
    table = small[3:].reshape(pairs, -1, LANES)[:, :2, :NB].reshape(2 * pairs, NB).T
    output = both_halves(output, out_swap.state[0], me)
    grad_memory = both_halves(gmem, gmem_swap.state[0], me)
    grad_tokens = both_halves(grad_x, grad_x_swap.state[0], me)
    return (
        output,
        grad_tokens,
        grad_memory,
        small[:3],
        table,
        self_grads,
        mid_grads[0].T,
        mid_grads[1:4],
        mid_grads[4].T,
        ffn_grads[:2],
        ffn_grads[2].T,
    )


def solution(mesh):
    rows = P("dp", "mp", None)
    proj = P(None, "dp", "mp")
    out = P("mp", "dp")
    return jax.shard_map(
        per_device,
        mesh=mesh,
        in_specs=(rows, rows, P("dp", None), P("dp"), P(), P(), proj, out, proj, out, proj, out, rows),
        out_specs=(rows, rows, rows, P(), P(), proj, out, proj, out, proj, out),
        check_vma=False,
    )
```

time: 809 us -> 433 us (0.54)
  waiting for transfers between devices: 219 us -> 58.6 us
  matrix products: 152 us -> 0.35 us
  local copies, waits for them, and re-layouts: 144 us -> 20.2 us
  Pallas kernels: 132 us -> 249 us
  blocking collectives: 75.3 us -> 0 us
  starting transfers between devices: 8.43 us -> 63.2 us
  other arithmetic: 56.6 us -> 35.5 us
  between operations: 15.7 us -> 1.99 us
    dot_general x34 -> x0, matrix products: 152 us -> none  [the longest x33 152 us: mm(): lax.dot_general(a, b, ((dims[0], dims[1]), ((), ())), preferred_element_t...]
    reduce_scatter x3 -> x0, waiting for transfers between devices: 120 us -> none  [scatter_grads(): lax.psum_scatter(pieces, ('dp', 'mp'), scatter_dimension=0, tiled=True)[0]]
    pallas_call x4 -> x14, Pallas kernels: 132 us -> 249 us  [the longest x1 50.7 us: feed(): call(functools.partial(feed_kernel, blocks, len(pieces), packed), 'feed',...]
    all_gather x3 -> x0, waiting for transfers between devices: 86.8 us -> none  [gather_weights(): pieces = lax.all_gather(shard, ('dp', 'mp'), axis=0)]
    psum x1 -> x0, blocking collectives: 75.3 us -> none  [per_device(): lax.psum((jnp.stack([gain_one, gain_two, gain_three]), table_gradient(sum...]
    ppermute x6 -> x70, starting transfers between devices: 8.19 us -> 63.2 us  [the longest x52 43.8 us: flip_bit(): return lax.ppermute(values, 'dp', [(i, i ^ 1 << bit) for i in range(size)])]
    another operation x15 -> x0, local copies, waits for them, and re-layouts: 48.5 us -> none  [the longest x6 19.1 us: per_device(): jnp.stack([grad_self_out, tn(normed_two, grads_cross[0], BF), tn(memory_r...]
    ppermute x6 -> x70, waiting for transfers between devices: 11.1 us -> 58.6 us  [the longest x52 45 us: flip_bit(): return lax.ppermute(values, 'dp', [(i, i ^ 1 << bit) for i in range(size)])]
  transfers between devices with their start and end apart: 12 -> 70, of which waited for: 5 -> 19; matrix products, arithmetic and copies ran while one was open for 33% -> 9% of each run, Pallas kernels for 8% -> 46%
where the time goes in v3:
time: 433 us; the launch traced here: 429 us
  Pallas kernels  249 us (58%)
  starting transfers between devices  63.2 us (15%)
  waiting for transfers between devices  58.6 us (14%)
  other arithmetic  35.5 us (8%)
  local copies, waits for them, and re-layouts  20.2 us (5%)
    pallas_call x1, Pallas kernels, feed(): call(functools.partial(feed_kernel, blocks, len(pieces), packed), 'feed',...  50.7 us
    pallas_call x3, Pallas kernels, self_backward(): call(functools.partial(backward_kernel, True, packed, len(into)), 'self_b...  47.5 us
    pallas_call x4, Pallas kernels, attention_forward(): call(functools.partial(forward_kernel, causal, len(into)), 'attention_for...  45.5 us
    ppermute x52, waiting for transfers between devices, flip_bit(): return lax.ppermute(values, 'dp', [(i, i ^ 1 << bit) for i in range(size)])  45 us
    ppermute x52, starting transfers between devices, flip_bit(): return lax.ppermute(values, 'dp', [(i, i ^ 1 << bit) for i in range(size)])  43.8 us
    pallas_call x2, Pallas kernels, cross_backward(): call(functools.partial(backward_kernel, False, False, 0), 'cross_backward...  41.5 us
    pallas_call x1, Pallas kernels, cross_back(): call(functools.partial(cross_back_kernel, blocks, packed), 'cross_back',...  28.8 us
    ppermute x18, starting transfers between devices, flip_mp(): return lax.ppermute(values, 'mp', [(0, 1), (1, 0)])  19.4 us
  transfers between devices with their start and end apart: 70, of which 19 were waited for; matrix products, arithmetic and copies ran while one was open for 9% of the time, Pallas kernels for 46%

profile of v3, /device:TPU:0, one launch (start us, length us, event | category | flops | bytes accessed | tf_op | source)
XLA Modules:
  0.0 429.2 jit_solution(6687357123713527135)
XLA Ops:
  0.7 4.1 collective-permute-start
  13.5 3.8 collective-permute-done.1.refs_3_
  20.0 3.3 collective-permute-start.5
  23.3 7.7 %collective-permute-done.5 = bf16[5,48,384]{2,1,0:T(8,128)(2,1)S(1)} collective-permute-done((bf16[5,48,384]{2,1,0:T(8,128)(2,1)S(1)}, bf16[5,48,384]{2,1,0:T(8,128)(2,1)S(1)}, u32[]{:S(2)}, u32[]{:S(2)}) %collective-permute-start.5) | collective-permute-done | bytes 184352 | tf_op jit(solution)/shard_map/ppermute | solution.py:849
  36.8 12.2 %collective-permute-done.10 = bf16[1,48,1024]{2,1,0:T(8,128)(2,1)S(1)} collective-permute-done((bf16[1,48,1024]{2,1,0:T(8,128)(2,1)S(1)}, bf16[1,48,1024]{2,1,0:T(8,128)(2,1)S(1)}, u32[]{:S(2)}, u32[]{:S(2)}) %collective-permute-start.10) | collective-permute-done | bytes 98336 | tf_op jit(solution)/shard_map/ppermute | solution.py:853
  56.9 10.4 %project.1 = (bf16[1024,768]{1,0:T(8,128)(2,1)}, bf16[1024,2304]{1,0:T(8,128)(2,1)}, bf16[3,768,768]{2,1,0:T(8,128)(2,1)}) custom-call(s32[3]{0:T(128)} %pad_add_fusion.ids_ref, f32[3,768]{1,0:T(4,128)} %gain_ref.9, bf16[512,768]{1,0:T(8,128)(2,1)} %copy-done.20, bf16[2,512,768]{2,1,0:T(8,128)(2,1)} %kept_ref.5, bf16[2,3,48,384]{3,2,1,0:T(8,128)(2,1)} %copy-done.30, ...), custom_call_target="tpu_custom_call" | custom-call | flops 3623878656 | bytes 11403264 | tf_op jit(solution)/shard_map/project/pallas_call | solution.py:587
  67.3 10.7 %attention_forward.4 = (bf16[1024,768]{1,0:T(8,128)(2,1)}, bf16[12,1024,128]{2,1,0:T(8,128)(2,1)}) custom-call(s32[3]{0:T(128)} %pad_add_fusion.ids_ref, s32[2,3]{1,0:T(2,128)} %bounds_ref.17, f32[6,2,384]{2,1,0:T(2,128)} %reshape.105.band_ref, bf16[1024,2304]{1,0:T(8,128)(2,1)} %get-tuple-element.270.q_ref.k_ref.v_ref, ...), custom_call_target="tpu_custom_call" | custom-call | flops 3221225472 | bytes 12582912 | tf_op jit(solution)/shard_map/attention_forward/pallas_call | solution.py:276
  82.1 5.0 %collective-permute-start.24 = (bf16[2,2,3,48,640]{4,3,2,1,0:T(8,128)(2,1)S(1)}, bf16[2,2,3,48,640]{4,3,2,1,0:T(8,128)(2,1)S(1)}, u32[]{:S(2)}, u32[]{:S(2)}) collective-permute-start(bf16[2,2,3,48,640]{4,3,2,1,0:T(8,128)(2,1)S(1)} %get-tuple-element.288), channel_id=1, source_target_pairs={{0,8},{2,10},{4,12},{6,14},{8,0},{10,2},{12,4},{14,6},{16,24},{18,... | collective-permute-start | bytes 2211848 | tf_op jit(solution)/shard_map/ppermute | solution.py:849
  87.1 10.7 %attention_forward.5 = (bf16[1024,768]{1,0:T(8,128)(2,1)}, bf16[12,1024,128]{2,1,0:T(8,128)(2,1)}) custom-call(s32[3]{0:T(128)} %pad_add_fusion.ids_ref, s32[2,3]{1,0:T(2,128)} %bounds_ref.17, f32[6,2,384]{2,1,0:T(2,128)} %reshape.105.band_ref, ...), custom_call_target="tpu_custom_call", output_to_operand_aliasing={{0}: (6, {}), {1}: (7, {})} | custom-call | flops 3221225472 | bytes 12582912 | tf_op jit(solution)/shard_map/attention_forward/pallas_call | solution.py:276
  99.0 3.0 collective-permute-done.24
  110.3 14.3 %middle.1 = (f32[1024,768]{1,0:T(8,128)}, bf16[1024,768]{1,0:T(8,128)(2,1)}, bf16[1024,768]{1,0:T(8,128)(2,1)}, bf16[1024,768]{1,0:T(8,128)(2,1)}, bf16[1024,768...) custom-call(s32[3]{0:T(128)} %pad_add_fusion.ids_ref, f32[3,768]{1,0:T(4,128)} %gain_ref.9, bf16[512,768]{1,0:T(8,128)(2,1)} %copy-done.20, ...), custom_call_target="tpu_custom_call" | custom-call | flops 4831838208 | bytes 21626880 | tf_op jit(solution)/shard_map/middle/pallas_call | solution.py:625
  124.6 6.0 %collective-permute-done.31 = bf16[2,2,3,48,384]{4,3,2,1,0:T(8,128)(2,1)S(1)} collective-permute-done((bf16[2,2,3,48,384]{4,3,2,1,0:T(8,128)(2,1)S(1)}, bf16[2,2,3,48,384]{4,3,2,1,0:T(8,128)(2,1)S(1)}, u32[]{:S(2)}, u32[]{:S(2)}) %collective-permute-start.31) | collective-permute-done | bytes 442400 | tf_op jit(solution)/shard_map/ppermute | solution.py:849
  130.7 18.3 %attention_forward.6 = (bf16[1024,768]{1,0:T(8,128)(2,1)}, bf16[12,1024,128]{2,1,0:T(8,128)(2,1)}) custom-call(s32[3]{0:T(128)} %pad_add_fusion.ids_ref, s32[2]{0:T(128)} %bounds_ref.14, f32[6,2,384]{2,1,0:T(2,128)} %reshape.105.band_ref, bf16[1024,768]{1,0:T(8,128)(2,1)} %get-tuple-element.314.q_ref, bf16[1024,768]{1,0:T(8,128)(2,1)} %get-tuple-element.315.k_ref, ...), custom_call_target="tpu_custom_call" | custom-call | flops 10737418240 | bytes 12582912 | tf_op jit(solution)/shard_map/attention_forward/pallas_call | solution.py:276
  149.1 2.5 collective-permute-done.33.refs_5_
  153.0 5.8 %attention_forward.7 = (bf16[1024,768]{1,0:T(8,128)(2,1)}, bf16[12,1024,128]{2,1,0:T(8,128)(2,1)}) custom-call(s32[3]{0:T(128)} %pad_add_fusion.ids_ref, s32[2]{0:T(128)} %bounds_ref.14, f32[6,2,384]{2,1,0:T(2,128)} %reshape.105.band_ref, bf16[1024,768]{1,0:T(8,128)(2,1)} %get-tuple-element.314.q_ref, ...), custom_call_target="tpu_custom_call", output_to_operand_aliasing={{0}: (6, {}), {1}: (7, {})} | custom-call | flops 2147483648 | bytes 12582912 | tf_op jit(solution)/shard_map/attention_forward/pallas_call | solution.py:276
  160.7 50.7 %feed.1 = (f32[512,768]{1,0:T(8,128)}, bf16[512,768]{1,0:T(8,128)(2,1)}, f32[1024,768]{1,0:T(8,128)}, bf16[1024,768]{1,0:T(8,128)(2,1)}, f32[1,768]{1,0:T(1,128)...) custom-call(s32[3]{0:T(128)} %pad_add_fusion.ids_ref, s32[2,3]{1,0:T(2,128)} %bounds_ref.17, ...), custom_call_target="tpu_custom_call" | custom-call | flops 28991029248 | bytes 37748736 | tf_op jit(solution)/shard_map/feed/pallas_call | solution.py:728
  213.6 15.2 %cross_backward.2.rest_0_ = bf16[3,1024,768]{2,1,0:T(8,128)(2,1)} custom-call(s32[3]{0:T(128)} %pad_add_fusion.ids_ref, s32[2]{0:T(128)} %bounds_ref.14, f32[6,2,384]{2,1,0:T(2,128)} %reshape.105.band_ref, bf16[12,1024,128]{2,1,0:T(8,128)(2,1)} %get-tuple-element.330.qa_ref, bf16[1024,768]{1,0:T(8,128)(2,1)} %get-tuple-element.315.k_ref, ...), custom_call_target="tpu_custom_call" | custom-call | flops 10737418240 | bytes 15728640 | tf_op jit(solution)/shard_map/cross_backward/pallas_call | solution.py:300
  230.6 2.8 fusion
  234.4 26.3 %cross_backward.3.d_ref = bf16[3,1024,768]{2,1,0:T(8,128)(2,1)} custom-call(s32[3]{0:T(128)} %pad_add_fusion.ids_ref, s32[2]{0:T(128)} %bounds_ref.14, f32[6,2,384]{2,1,0:T(2,128)} %reshape.105.band_ref, bf16[12,1024,128]{2,1,0:T(8,128)(2,1)} %get-tuple-element.330.qa_ref, ...), custom_call_target="tpu_custom_call", output_to_operand_aliasing={{}: (8, {})} | custom-call | flops 21474836480 | bytes 15728640 | tf_op jit(solution)/shard_map/cross_backward/pallas_call | solution.py:300
  261.3 2.4 fusion.6
  266.3 28.8 %cross_back.1 = (f32[1024,768]{1,0:T(8,128)}, bf16[1024,768]{1,0:T(8,128)(2,1)}, f32[512,768]{1,0:T(8,128)}, bf16[512,768]{1,0:T(8,128)(2,1)}, f32[1,768]{1,0:T(...) custom-call(s32[3]{0:T(128)} %pad_add_fusion.ids_ref, ...), custom_call_target="tpu_custom_call" | custom-call | flops 10871635968 | bytes 40108032 | tf_op jit(solution)/shard_map/cross_back/pallas_call | solution.py:792
  295.1 2.5 fusion.5
  297.9 9.3 %self_backward.3 = (bf16[3,1024,384]{2,1,0:T(8,128)(2,1)}, f32[6,8,128]{2,1,0:T(8,128)}, bf16[2,2,2,3,48,384]{5,4,3,2,1,0:T(8,128)(2,1)}, bf16[2,2,2,3,48,384]{5,4,3,2,1,0:T(8,128)(2,1)}) custom-call(s32[3]{0:T(128)} %pad_add_fusion.ids_ref, s32[2,3]{1,0:T(2,128)} %bounds_ref.17, f32[6,2,384]{2,1,0:T(2,128)} %reshape.105.band_ref, ...), custom_call_target="tpu_custom_call" | custom-call | flops 4294967296 | bytes 15728640 | tf_op jit(solution)/shard_map/self_backward/pallas_call | solution.py:334
  310.4 16.2 %self_backward.4 = (bf16[3,1024,384]{2,1,0:T(8,128)(2,1)}, f32[6,8,128]{2,1,0:T(8,128)}, bf16[2,2,2,3,48,384]{5,4,3,2,1,0:T(8,128)(2,1)}, bf16[2,2,2,3,48,384]{5,4,3,2,1,0:T(8,128)(2,1)}) custom-call(s32[3]{0:T(128)} %pad_add_fusion.ids_ref, s32[2,3]{1,0:T(2,128)} %bounds_ref.17, ...), custom_call_target="tpu_custom_call", output_to_operand_aliasing={{0}: (10, {}), {1}: (11, {}), {2}: (12, {}), {3}: (13, {})} | custom-call | flops 8589934592 | bytes 15728640 | tf_op jit(solution)/shard_map/self_backward/pallas_call | solution.py:334
  331.8 2.2 fusion.16
  340.7 22.0 %self_backward.5 = (bf16[3,1024,384]{2,1,0:T(8,128)(2,1)}, f32[6,8,128]{2,1,0:T(8,128)}, bf16[2,2,2,3,48,384]{5,4,3,2,1,0:T(8,128)(2,1)}, bf16[2,2,2,3,48,384]{5,4,3,2,1,0:T(8,128)(2,1)}) custom-call(s32[3]{0:T(128)} %pad_add_fusion.ids_ref, s32[2,3]{1,0:T(2,128)} %bounds_ref.17, f32[6,2,384]{2,1,0:T(2,128)} %reshape.105.band_ref, ...), custom_call_target="tpu_custom_call" | custom-call | flops 12884901888 | bytes 15728640 | tf_op jit(solution)/shard_map/self_backward/pallas_call | solution.py:334
  372.9 10.6 %self_back.1 = (f32[512,768]{1,0:T(8,128)}, bf16[512,768]{1,0:T(8,128)(2,1)}, f32[1,768]{1,0:T(1,128)}) custom-call(s32[3]{0:T(128)} %pad_add_fusion.ids_ref, f32[3,768]{1,0:T(4,128)} %gain_ref.9, bf16[3,1024,384]{2,1,0:T(8,128)(2,1)} %get-tuple-element.411.ours_ref, bf16[3,1024,384]{2,1,0:T(8,128)(2,1)} %get-tuple-element.412.theirs_ref, ...), custom_call_target="tpu_custom_call" | custom-call | flops 3623878656 | bytes 19267584 | tf_op jit(solution)/shard_map/self_back/pallas_call | solution.py:833
  391.7 5.8 %maximum_select_fusion = (f32[2,512,768]{2,1,0:T(8,128)}, f32[2,512,768]{2,1,0:T(8,128)}) fusion(f32[1,512,768]{2,1,0:T(8,128)S(1)} %bitcast_convert_fusion.2, f32[1,512,768]{2,1,0:T(8,128)} %bitcast.174, pred[]{:T(512)S(6)} %eq.16, f32[1,512,768]{2,1,0:T(8,128)} %bitcast.175, f32[1,512,768]{2,1,0:T(8,128)S(1)} %bitcast_convert_fusion), kind=kLoop, calls=%fused_computation | loop fusion | flops 4718592 | bytes 12582913 | tf_op jit(solution)/shard_map/jit(_where)/select_n | solution.py:1033
  398.9 2.2 collective-permute-start.62
  406.0 9.1 %collective-permute-done.64 = bf16[3,48,384]{2,1,0:T(8,128)(2,1)S(1)} collective-permute-done((bf16[3,48,384]{2,1,0:T(8,128)(2,1)S(1)}, bf16[3,48,384]{2,1,0:T(8,128)(2,1)S(1)}, u32[]{:S(2)}, u32[]{:S(2)}) %collective-permute-start.64) | collective-permute-done | bytes 110624 | tf_op jit(solution)/shard_map/ppermute | solution.py:849
  415.4 2.5 collective-permute-start.68
  421.5 3.5 collective-permute-done.67
  (329 shorter events, 97.2 us)
Async XLA Ops:
  6.0 25.0 %collective-permute-start.4 = (bf16[512,768]{1,0:T(8,128)(2,1)S(1)}, bf16[512,768]{1,0:T(8,128)(2,1)S(1)}, u32[]{:S(2)}, u32[]{:S(2)}) collective-permute-start(bf16[512,768]{1,0:T(8,128)(2,1)S(1)} %dynamic-slice_bitcast_fusion), channel_id=1, source_target_pairs={{0,1},{1,0},{2,3},{3,2},{4,5},{5,4},{6,7},{7,6},{8,9},{9,8},{10,11... | collective-permute-start | bytes 2359304 | tf_op jit(solution)/shard_map/ppermute | solution.py:853
  31.2 18.4 %collective-permute-start.6 = (bf16[2,2,3,48,384]{4,3,2,1,0:T(8,128)(2,1)S(1)}, bf16[2,2,3,48,384]{4,3,2,1,0:T(8,128)(2,1)S(1)}, u32[]{:S(2)}, u32[]{:S(2)}) collective-permute-start(bf16[2,2,3,48,384]{4,3,2,1,0:T(8,128)(2,1)S(1)} %pad_maximum_fusion.5), channel_id=1, source_target_pairs={{0,4},{2,6},{4,0},{6,2},{8,12},{10,14},{12,8},{14,10},{16,20},{18,... | collective-permute-start | bytes 1327112 | tf_op jit(solution)/shard_map/ppermute | solution.py:849
  31.8 17.8 %collective-permute-start.7 = (bf16[2,2,3,48,384]{4,3,2,1,0:T(8,128)(2,1)S(1)}, bf16[2,2,3,48,384]{4,3,2,1,0:T(8,128)(2,1)S(1)}, u32[]{:S(2)}, u32[]{:S(2)}) collective-permute-start(bf16[2,2,3,48,384]{4,3,2,1,0:T(8,128)(2,1)S(1)} %pad_maximum_fusion.6), channel_id=1, source_target_pairs={{0,1},{1,0},{2,3},{3,2},{4,5},{5,4},{6,7},{7,6},{8,9},{9,8},{10,11... | collective-permute-start | bytes 1327112 | tf_op jit(solution)/shard_map/ppermute | solution.py:853
  52.7 25.3 %collective-permute-start.17 = (bf16[2,5,48,384]{3,2,1,0:T(8,128)(2,1)S(1)}, bf16[2,5,48,384]{3,2,1,0:T(8,128)(2,1)S(1)}, u32[]{:S(2)}, u32[]{:S(2)}) collective-permute-start(bf16[2,5,48,384]{3,2,1,0:T(8,128)(2,1)S(1)} %get-tuple-element.297.refs_0_), channel_id=1, source_target_pairs={{0,1},{1,0},{2,3},{3,2},{4,5},{5,4},{6,7},{7,6},{8,9},{9,8},{10,11... | collective-permute-start | bytes 1105928 | tf_op jit(solution)/shard_map/ppermute | solution.py:853
  53.7 24.3 %collective-permute-start.18 = (bf16[2,5,48,384]{3,2,1,0:T(8,128)(2,1)}, bf16[2,5,48,384]{3,2,1,0:T(8,128)(2,1)}, u32[]{:S(2)}, u32[]{:S(2)}) collective-permute-start(bf16[2,5,48,384]{3,2,1,0:T(8,128)(2,1)} %collective-permute-done.8.refs_3_), channel_id=1, source_target_pairs={{0,4},{2,6},{4,0},{6,2},{8,12},{10,14},{12,8},{14,10},{16,20},{18,... | collective-permute-start | bytes 1105928 | tf_op jit(solution)/shard_map/ppermute | solution.py:849
  54.8 23.2 %collective-permute-start.19 = (bf16[2,3,48,640]{3,2,1,0:T(8,128)(2,1)S(1)}, bf16[2,3,48,640]{3,2,1,0:T(8,128)(2,1)S(1)}, u32[]{:S(2)}, u32[]{:S(2)}) collective-permute-start(bf16[2,3,48,640]{3,2,1,0:T(8,128)(2,1)S(1)} %fusion.23), channel_id=1, source_target_pairs={{0,16},{2,18},{4,20},{6,22},{8,24},{10,26},{12,28},{14,30},{16,0},... | collective-permute-start | bytes 1105928 | tf_op jit(solution)/shard_map/ppermute | solution.py:849
  54.8 23.1 %collective-permute-start.20 = (bf16[2,3,48,384]{3,2,1,0:T(8,128)(2,1)S(1)}, bf16[2,3,48,384]{3,2,1,0:T(8,128)(2,1)S(1)}, u32[]{:S(2)}, u32[]{:S(2)}) collective-permute-start(bf16[2,3,48,384]{3,2,1,0:T(8,128)(2,1)S(1)} %pad_maximum_fusion.9), channel_id=1, source_target_pairs={{0,4},{2,6},{4,0},{6,2},{8,12},{10,14},{12,8},{14,10},{16,20},{18,... | collective-permute-start | bytes 663560 | tf_op jit(solution)/shard_map/ppermute | solution.py:849
  56.1 41.7 %collective-permute-start.21 = (bf16[512,768]{1,0:T(8,128)(2,1)S(1)}, bf16[512,768]{1,0:T(8,128)(2,1)}, u32[]{:S(2)}, u32[]{:S(2)}) collective-permute-start(bf16[512,768]{1,0:T(8,128)(2,1)S(1)} %dynamic-slice_bitcast_fusion.2), channel_id=1, source_target_pairs={{0,1},{1,0},{2,3},{3,2},{4,5},{5,4},{6,7},{7,6},{8,9},{9,8},{10,11... | collective-permute-start | bytes 2359304 | tf_op jit(solution)/shard_map/ppermute | solution.py:853
  80.1 17.7 %collective-permute-start.22 = (bf16[2,2,5,48,384]{4,3,2,1,0:T(8,128)(2,1)S(1)}, bf16[2,2,5,48,384]{4,3,2,1,0:T(8,128)(2,1)}, u32[]{:S(2)}, u32[]{:S(2)}) collective-permute-start(bf16[2,2,5,48,384]{4,3,2,1,0:T(8,128)(2,1)S(1)} %pad_maximum_fusion.2), channel_id=1, source_target_pairs={{0,4},{2,6},{4,0},{6,2},{8,12},{10,14},{12,8},{14,10},{16,20},{18,... | collective-permute-start | bytes 2211848 | tf_op jit(solution)/shard_map/ppermute | solution.py:849
  81.7 17.3 %collective-permute-start.23 = (bf16[2,2,5,48,384]{4,3,2,1,0:T(8,128)(2,1)S(1)}, bf16[2,2,5,48,384]{4,3,2,1,0:T(8,128)(2,1)}, u32[]{:S(2)}, u32[]{:S(2)}) collective-permute-start(bf16[2,2,5,48,384]{4,3,2,1,0:T(8,128)(2,1)S(1)} %pad_maximum_fusion.3), channel_id=1, source_target_pairs={{0,1},{1,0},{2,3},{3,2},{4,5},{5,4},{6,7},{7,6},{8,9},{9,8},{10,11... | collective-permute-start | bytes 2211848 | tf_op jit(solution)/shard_map/ppermute | solution.py:853
  82.1 19.8 %collective-permute-start.24 = (bf16[2,2,3,48,640]{4,3,2,1,0:T(8,128)(2,1)S(1)}, bf16[2,2,3,48,640]{4,3,2,1,0:T(8,128)(2,1)S(1)}, u32[]{:S(2)}, u32[]{:S(2)}) collective-permute-start(bf16[2,2,3,48,640]{4,3,2,1,0:T(8,128)(2,1)S(1)} %get-tuple-element.288), channel_id=1, source_target_pairs={{0,8},{2,10},{4,12},{6,14},{8,0},{10,2},{12,4},{14,6},{16,24},{18,... | collective-permute-start | bytes 2211848 | tf_op jit(solution)/shard_map/ppermute | solution.py:849
  106.1 52.7 %collective-permute-start.35 = (bf16[2,2,2,3,48,640]{5,4,3,2,1,0:T(8,128)(2,1)S(1)}, bf16[2,2,2,3,48,640]{5,4,3,2,1,0:T(8,128)(2,1)S(1)}, u32[]{:S(2)}, u32[]{:S(2)}) collective-permute-start(bf16[2,2,2,3,48,640]{5,4,3,2,1,0:T(8,128)(2,1)S(1)} %pad_maximum_fusion.refs_0_), channel_id=1, source_target_pairs={{0,2},{2,0},{4,6},{6,4},{8,10},{10,8},{12,14},{14,12},{16,18},{18,... | collective-permute-start | bytes 4423688 | tf_op jit(solution)/shard_map/ppermute | solution.py:849
  107.9 22.6 %collective-permute-start.31 = (bf16[2,2,3,48,384]{4,3,2,1,0:T(8,128)(2,1)S(1)}, bf16[2,2,3,48,384]{4,3,2,1,0:T(8,128)(2,1)S(1)}, u32[]{:S(2)}, u32[]{:S(2)}) collective-permute-start(bf16[2,2,3,48,384]{4,3,2,1,0:T(8,128)(2,1)S(1)} %get-tuple-element.311), channel_id=1, source_target_pairs={{0,16},{2,18},{4,20},{6,22},{8,24},{10,26},{12,28},{14,30},{16,0},... | collective-permute-start | bytes 1327112 | tf_op jit(solution)/shard_map/ppermute | solution.py:849
  108.2 43.4 %collective-permute-start.32 = (bf16[2,2,2,3,48,640]{5,4,3,2,1,0:T(8,128)(2,1)S(1)}, bf16[2,2,2,3,48,640]{5,4,3,2,1,0:T(8,128)(2,1)S(1)}, u32[]{:S(2)}, u32[]{:S(2)}) collective-permute-start(bf16[2,2,2,3,48,640]{5,4,3,2,1,0:T(8,128)(2,1)S(1)} %pad_maximum_fusion.refs_0_), channel_id=1, source_target_pairs={{0,4},{2,6},{4,0},{6,2},{8,12},{10,14},{12,8},{14,10},{16,20},{18,... | collective-permute-start | bytes 4423688 | tf_op jit(solution)/shard_map/ppermute | solution.py:849
  108.8 40.3 %collective-permute-start.34 = (bf16[512,768]{1,0:T(8,128)(2,1)S(1)}, bf16[512,768]{1,0:T(8,128)(2,1)}, u32[]{:S(2)}, u32[]{:S(2)}) collective-permute-start(bf16[512,768]{1,0:T(8,128)(2,1)S(1)} %dynamic-slice_bitcast_fusion.1), channel_id=1, source_target_pairs={{0,1},{1,0},{2,3},{3,2},{4,5},{5,4},{6,7},{7,6},{8,9},{9,8},{10,11... | collective-permute-start | bytes 2359304 | tf_op jit(solution)/shard_map/ppermute | solution.py:853
  130.7 20.9 %collective-permute-start.33 = (bf16[2,2,2,3,48,384]{5,4,3,2,1,0:T(8,128)(2,1)S(1)}, bf16[2,2,2,3,48,384]{5,4,3,2,1,0:T(8,128)(2,1)S(1)}, u32[]{:S(2)}, u32[]{:S(2)}) collective-permute-start(bf16[2,2,2,3,48,384]{5,4,3,2,1,0:T(8,128)(2,1)S(1)} %pad_maximum_fusion.1.refs_4_), channel_id=1, source_target_pairs={{0,8},{2,10},{4,12},{6,14},{8,0},{10,2},{12,4},{14,6},{16,24},{18,... | collective-permute-start | bytes 2654216 | tf_op jit(solution)/shard_map/ppermute | solution.py:849
  211.5 17.4 %collective-permute-start.39 = (bf16[2,2,2,2,3,48,1024]{6,5,4,3,2,1,0:T(8,128)(2,1)}, bf16[2,2,2,2,3,48,1024]{6,5,4,3,2,1,0:T(8,128)(2,1)}, u32[]{:S(2)}, u32[]{:S(2)}) collective-permute-start(bf16[2,2,2,2,3,48,1024]{6,5,4,3,2,1,0:T(8,128)(2,1)} %get-tuple-element.335), channel_id=1, source_target_pairs={{0,2},{2,0},{4,6},{6,4},{8,10},{10,8},{12,14},{14,12},{16,18},{18,... | collective-permute-start | bytes 14155784 | tf_op jit(solution)/shard_map/ppermute | solution.py:849
  212.1 54.2 %collective-permute-start.42 = (bf16[512,768]{1,0:T(8,128)(2,1)}, bf16[512,768]{1,0:T(8,128)(2,1)}, u32[]{:S(2)}, u32[]{:S(2)}) collective-permute-start(bf16[512,768]{1,0:T(8,128)(2,1)} %get-tuple-element.347), channel_id=1, source_target_pairs={{0,1},{1,0},{2,3},{3,2},{4,5},{5,4},{6,7},{7,6},{8,9},{9,8},{10,11... | collective-permute-start | bytes 2359304 | tf_op jit(solution)/shard_map/ppermute | solution.py:853
  233.4 27.9 %collective-permute-start.40 = (bf16[2,2,3,48,1024]{4,3,2,1,0:T(8,128)(2,1)}, bf16[2,2,3,48,1024]{4,3,2,1,0:T(8,128)(2,1)S(1)}, u32[]{:S(2)}, u32[]{:S(2)}) collective-permute-start(bf16[2,2,3,48,1024]{4,3,2,1,0:T(8,128)(2,1)} %fusion), channel_id=1, source_target_pairs={{0,4},{2,6},{4,0},{6,2},{8,12},{10,14},{12,8},{14,10},{16,20},{18,... | collective-permute-start | bytes 3538952 | tf_op jit(solution)/shard_map/ppermute | solution.py:849
  233.9 27.4 %collective-permute-start.41 = (bf16[2,2,3,48,1024]{4,3,2,1,0:T(8,128)(2,1)S(1)}, bf16[2,2,3,48,1024]{4,3,2,1,0:T(8,128)(2,1)S(1)}, u32[]{:S(2)}, u32[]{:S(2)}) collective-permute-start(bf16[2,2,3,48,1024]{4,3,2,1,0:T(8,128)(2,1)S(1)} %fusion.1), channel_id=1, source_target_pairs={{0,1},{1,0},{2,3},{3,2},{4,5},{5,4},{6,7},{7,6},{8,9},{9,8},{10,11... | collective-permute-start | bytes 3538952 | tf_op jit(solution)/shard_map/ppermute | solution.py:853
  263.7 31.3 %collective-permute-start.43 = (bf16[2,3,48,1024]{3,2,1,0:T(8,128)(2,1)S(1)}, bf16[2,3,48,1024]{3,2,1,0:T(8,128)(2,1)S(1)}, u32[]{:S(2)}, u32[]{:S(2)}) collective-permute-start(bf16[2,3,48,1024]{3,2,1,0:T(8,128)(2,1)S(1)} %get-tuple-element.356), channel_id=1, source_target_pairs={{0,1},{1,0},{2,3},{3,2},{4,5},{5,4},{6,7},{7,6},{8,9},{9,8},{10,11... | collective-permute-start | bytes 1769480 | tf_op jit(solution)/shard_map/ppermute | solution.py:853
  264.7 30.3 %collective-permute-start.44 = (bf16[2,3,48,1024]{3,2,1,0:T(8,128)(2,1)S(1)}, bf16[2,3,48,1024]{3,2,1,0:T(8,128)(2,1)S(1)}, u32[]{:S(2)}, u32[]{:S(2)}) collective-permute-start(bf16[2,3,48,1024]{3,2,1,0:T(8,128)(2,1)S(1)} %get-tuple-element.357), channel_id=1, source_target_pairs={{0,4},{2,6},{4,0},{6,2},{8,12},{10,14},{12,8},{14,10},{16,20},{18,... | collective-permute-start | bytes 1769480 | tf_op jit(solution)/shard_map/ppermute | solution.py:849
  297.6 29.0 %collective-permute-start.48 = (bf16[2,3,48,1024]{3,2,1,0:T(8,128)(2,1)}, bf16[2,3,48,1024]{3,2,1,0:T(8,128)(2,1)}, u32[]{:S(2)}, u32[]{:S(2)}) collective-permute-start(bf16[2,3,48,1024]{3,2,1,0:T(8,128)(2,1)} %fusion.5), channel_id=1, source_target_pairs={{0,8},{2,10},{4,12},{6,14},{8,0},{10,2},{12,4},{14,6},{16,24},{18,... | collective-permute-start | bytes 1769480 | tf_op jit(solution)/shard_map/ppermute | solution.py:849
  308.9 18.7 %collective-permute-start.46 = (bf16[2,2,5,48,384]{4,3,2,1,0:T(8,128)(2,1)S(1)}, bf16[2,2,5,48,384]{4,3,2,1,0:T(8,128)(2,1)}, u32[]{:S(2)}, u32[]{:S(2)}) collective-permute-start(bf16[2,2,5,48,384]{4,3,2,1,0:T(8,128)(2,1)S(1)} %fusion.10), channel_id=1, source_target_pairs={{0,4},{2,6},{4,0},{6,2},{8,12},{10,14},{12,8},{14,10},{16,20},{18,... | collective-permute-start | bytes 2211848 | tf_op jit(solution)/shard_map/ppermute | solution.py:849
  309.3 18.4 %collective-permute-start.47 = (bf16[2,2,5,48,384]{4,3,2,1,0:T(8,128)(2,1)S(1)}, bf16[2,2,5,48,384]{4,3,2,1,0:T(8,128)(2,1)}, u32[]{:S(2)}, u32[]{:S(2)}) collective-permute-start(bf16[2,2,5,48,384]{4,3,2,1,0:T(8,128)(2,1)S(1)} %fusion.11), channel_id=1, source_target_pairs={{0,1},{1,0},{2,3},{3,2},{4,5},{5,4},{6,7},{7,6},{8,9},{9,8},{10,11... | collective-permute-start | bytes 2211848 | tf_op jit(solution)/shard_map/ppermute | solution.py:853
  327.8 34.9 %collective-permute-start.53 = (bf16[512,768]{1,0:T(8,128)(2,1)}, bf16[512,768]{1,0:T(8,128)(2,1)}, u32[]{:S(2)}, u32[]{:S(2)}) collective-permute-start(bf16[512,768]{1,0:T(8,128)(2,1)} %get-tuple-element.401), channel_id=1, source_target_pairs={{0,1},{1,0},{2,3},{3,2},{4,5},{5,4},{6,7},{7,6},{8,9},{9,8},{10,11... | collective-permute-start | bytes 2359304 | tf_op jit(solution)/shard_map/ppermute | solution.py:853
  335.5 27.3 %collective-permute-start.52 = (bf16[2,2,3,48,384]{4,3,2,1,0:T(8,128)(2,1)S(1)}, bf16[2,2,3,48,384]{4,3,2,1,0:T(8,128)(2,1)S(1)}, u32[]{:S(2)}, u32[]{:S(2)}) collective-permute-start(bf16[2,2,3,48,384]{4,3,2,1,0:T(8,128)(2,1)S(1)} %fusion.19), channel_id=1, source_target_pairs={{0,4},{2,6},{4,0},{6,2},{8,12},{10,14},{12,8},{14,10},{16,20},{18,... | collective-permute-start | bytes 1327112 | tf_op jit(solution)/shard_map/ppermute | solution.py:849
  336.8 25.9 %collective-permute-start.50 = (bf16[2,5,48,384]{3,2,1,0:T(8,128)(2,1)}, bf16[2,5,48,384]{3,2,1,0:T(8,128)(2,1)S(1)}, u32[]{:S(2)}, u32[]{:S(2)}) collective-permute-start(bf16[2,5,48,384]{3,2,1,0:T(8,128)(2,1)} %get-tuple-element.398), channel_id=1, source_target_pairs={{0,1},{1,0},{2,3},{3,2},{4,5},{5,4},{6,7},{7,6},{8,9},{9,8},{10,11... | collective-permute-start | bytes 1105928 | tf_op jit(solution)/shard_map/ppermute | solution.py:853
  338.1 24.7 %collective-permute-start.51 = (bf16[2,5,48,384]{3,2,1,0:T(8,128)(2,1)}, bf16[2,5,48,384]{3,2,1,0:T(8,128)(2,1)S(1)}, u32[]{:S(2)}, u32[]{:S(2)}) collective-permute-start(bf16[2,5,48,384]{3,2,1,0:T(8,128)(2,1)} %get-tuple-element.399), channel_id=1, source_target_pairs={{0,4},{2,6},{4,0},{6,2},{8,12},{10,14},{12,8},{14,10},{16,20},{18,... | collective-permute-start | bytes 1105928 | tf_op jit(solution)/shard_map/ppermute | solution.py:849
  338.6 24.2 %collective-permute-start.54 = (bf16[3,48,1024]{2,1,0:T(8,128)(2,1)}, bf16[3,48,1024]{2,1,0:T(8,128)(2,1)S(1)}, u32[]{:S(2)}, u32[]{:S(2)}) collective-permute-start(bf16[3,48,1024]{2,1,0:T(8,128)(2,1)} %fusion.25), channel_id=1, source_target_pairs={{0,16},{2,18},{4,20},{6,22},{8,24},{10,26},{12,28},{14,30},{16,0},... | collective-permute-start | bytes 884744 | tf_op jit(solution)/shard_map/ppermute | solution.py:849
  368.0 17.3 %collective-permute-start.57 = (bf16[2,2,3,48,384]{4,3,2,1,0:T(8,128)(2,1)}, bf16[2,2,3,48,384]{4,3,2,1,0:T(8,128)(2,1)}, u32[]{:S(2)}, u32[]{:S(2)}) collective-permute-start(bf16[2,2,3,48,384]{4,3,2,1,0:T(8,128)(2,1)} %fusion.20), channel_id=1, source_target_pairs={{0,4},{2,6},{4,0},{6,2},{8,12},{10,14},{12,8},{14,10},{16,20},{18,... | collective-permute-start | bytes 1327112 | tf_op jit(solution)/shard_map/ppermute | solution.py:849
  404.1 22.8 %collective-permute-start.59 = (bf16[512,768]{1,0:T(8,128)(2,1)}, bf16[512,768]{1,0:T(8,128)(2,1)S(1)}, u32[]{:S(2)}, u32[]{:S(2)}) collective-permute-start(bf16[512,768]{1,0:T(8,128)(2,1)} %get-tuple-element.431), channel_id=1, source_target_pairs={{0,1},{1,0},{2,3},{3,2},{4,5},{5,4},{6,7},{7,6},{8,9},{9,8},{10,11... | collective-permute-start | bytes 2359304 | tf_op jit(solution)/shard_map/ppermute | solution.py:853
  (104 other events, 912.3 us)

commit v4 on v3

--- a/solution.py
+++ b/solution.py
@@ -16,9 +16,10 @@
 masked_score = -1000000000.0
 BF = jnp.bfloat16
 F32 = jnp.float32
-FORWARD_MB = 56
+SELF_FORWARD_MB = 20
+CROSS_FORWARD_MB = 56
 BACKWARD_MB = 56
-PROJECT_MB = 56
+PROJECT_MB = 20
 MIDDLE_MB = 56
 FEED_MB = 60
 CROSS_BACK_MB = 56
@@ -274,7 +275,7 @@
 
     n = rows * rows * pairs * 2
     return call(
-        functools.partial(forward_kernel, causal, len(into)), "attention_forward", FORWARD_MB, pairs,
+        functools.partial(forward_kernel, causal, len(into)), "attention_forward", SELF_FORWARD_MB if causal else CROSS_FORWARD_MB, pairs,
         [
             pl.BlockSpec(memory_space=pltpu.SMEM),
             pl.BlockSpec((None, 2, 3 * LANES), lambda p, ids: (p + start, 0, 0)),
@@ -492,31 +493,40 @@
 
 def copy_pieces(ids_ref, pieces, table, place, w_ref, sem):
     if len(pieces) == 1:
-        pltpu.make_async_copy(pieces[0], w_ref, sem).start()
-    else:
-        mine = ids_ref[2]
-        rows = pieces[0].shape[-2]
-
-        def copy(flip):
+        for x in range(sem.shape[0]):
+            part = pieces[0].at[x] if sem.shape[0] > 1 else pieces[0]
+            target = w_ref.at[x] if sem.shape[0] > 1 else w_ref
+            pltpu.make_async_copy(part, target, sem.at[x]).start()
+        return
+    mine = ids_ref[2]
+    rows = pieces[0].shape[-2]
+
+    def copy(flip):
+        for first in range(2):
             for piece, entries in zip(pieces, table):
                 for at, (y, x, z0, z1, c), part in entries:
+                    if x ^ flip != first:
+                        continue
                     block = jnp.bitwise_xor(mine, 8 * z1 + 4 * z0 + 2 * y + c)
                     span = pl.ds(pl.multiple_of(block * rows, 16), rows)
-                    pltpu.make_async_copy(piece.at[at], place(span, x ^ flip, part), sem).start()
-
-        @pl.when(ids_ref[1] == 0)
-        def _():
-            copy(0)
-
-        @pl.when(ids_ref[1] == 1)
-        def _():
-            copy(1)
-
+                    target, done = place(span, x ^ flip, part)
+                    pltpu.make_async_copy(piece.at[at], target, done).start()
+
+    @pl.when(ids_ref[1] == 0)
+    def _():
+        copy(0)
+
+    @pl.when(ids_ref[1] == 1)
+    def _():
+        copy(1)
+
+
+def wait_pieces(w_ref, sem):
     pltpu.make_async_copy(w_ref, w_ref, sem).wait()
 
 
-def natural_place(w_ref, cols):
-    return lambda span, x, part: w_ref.at[:, span, x * cols : (x + 1) * cols]
+def natural_place(w_ref, cols, sem):
+    return lambda span, x, part: (w_ref.at[:, span, x * cols : (x + 1) * cols], sem.at[0])
 
 
 def put_turned(packed, ids_ref, target, span, values):
@@ -570,7 +580,8 @@
 
     @pl.when(step == 0)
     def _():
-        copy_pieces(ids_ref, w_in, gather_table(), natural_place(w_ref, w_in[0].shape[-1]), w_ref, sem)
+        copy_pieces(ids_ref, w_in, gather_table(), natural_place(w_ref, w_in[0].shape[-1], sem), w_ref, sem)
+        wait_pieces(w_ref, sem.at[0])
 
     normed, _ = rms(chosen(step, blocks, came_ref, kept_ref).astype(F32), gain_ref[0:1, :])
     normed_ref[...] = normed
@@ -592,7 +603,7 @@
             (row_spec(blocks, 3 * width), (rows, 3 * width), BF),
             (held(full), full, BF),
         ],
-        [pltpu.SemaphoreType.DMA],
+        [pltpu.SemaphoreType.DMA((1,))],
         6 * rows * width * width, 10 * rows * width + 6 * width * width,
     )(ids, gain, came, kept, *pieces)
 
@@ -604,7 +615,8 @@
 
     @pl.when(step == 0)
     def _():
-        copy_pieces(ids_ref, w_in, gather_table(), natural_place(w_ref, w_in[0].shape[-1]), w_ref, sem)
+        copy_pieces(ids_ref, w_in, gather_table(), natural_place(w_ref, w_in[0].shape[-1], sem), w_ref, sem)
+        wait_pieces(w_ref, sem.at[0])
 
     resid = chosen(step, blocks, came_ref, kept_ref).astype(F32) + dot_t(mixed_ref[...], w_ref[0])
     resid_ref[...] = resid
@@ -626,7 +638,7 @@
         functools.partial(middle_kernel, blocks, len(pieces)), "middle", MIDDLE_MB, blocks,
         [held((3, width))] + pair + [spec] + pair + [anywhere()] * len(pieces),
         [(spec, (rows, width), F32)] + [(spec, (rows, width), BF)] * 4 + [(held(full), full, BF)],
-        [pltpu.SemaphoreType.DMA],
+        [pltpu.SemaphoreType.DMA((1,))],
         8 * rows * width * width, 20 * rows * width + 10 * width * width,
     )(ids, gain, came, kept, mixed, mem_came, mem_kept, *pieces)
 
@@ -650,7 +662,7 @@
         cols = w_in[0].shape[-1]
         copy_pieces(
             ids_ref, w_in, wide_table(),
-            lambda span, x, part: w_ref.at[x, :, span, cols * part : cols if part == 0 else None], w_ref, sem,
+            lambda span, x, part: (w_ref.at[x, :, span, cols * part : cols if part == 0 else None], sem.at[x]), w_ref, sem,
         )
         gain_grad_ref[...] = jnp.zeros_like(gain_grad_ref)
 
@@ -669,6 +681,11 @@
         total = resid
         upstream = jnp.zeros((TB, width), F32)
         for x in range(2):
+
+            @pl.when(step == 0)
+            def _():
+                wait_pieces(w_ref.at[x], sem.at[x])
+
             gate = dot_n(normed, weight(0, x))
             up = dot_n(normed, weight(1, x))
             lifted = dot_n(branch, weight(2, x))
@@ -739,7 +756,7 @@
             (held((1, width)), (1, width), F32),
         ] + wgrads,
         [pltpu.VMEM((2, 3, width, half), BF)] + [pltpu.VMEM((width, rows), BF)] * 2
-        + [pltpu.VMEM((2, rows, half), BF)] * 3 + [pltpu.SemaphoreType.DMA],
+        + [pltpu.VMEM((2, rows, half), BF)] * 3 + [pltpu.SemaphoreType.DMA((2,))],
         36 * rows * width * half, 24 * rows * width + 24 * width * half,
     )(ids, docs, gain, resid, mixed, cot_came, cot_kept, w_mid, *pieces)
 
@@ -984,8 +1001,10 @@
     def take(self):
         self.kept = self.kept.astype(F32) + self.state[0].astype(F32)
 
-    def flip(self, bit):
+    def flip(self, bit, more=None):
         self.take()
+        if more is not None:
+            self.kept = self.kept + more.astype(F32)
         self.send((self.kept[1].astype(BF), bit))
         self.kept = self.kept[0]
 
@@ -1071,21 +1090,19 @@
         )
         w_one.second()
         cot_swap = Swap(other_row(cotangent, me))
-        begin((), w_one, w_ffn)
+        begin((), w_one)
         shard_mid, cot_swap.sent = hold((shard_mid, cot_swap.sent), w_one)
         w_two = Gather(shard_mid)
         w_one.third()
         begin((), w_one, w_two)
-        hold((), w_one, x_swap, w_two)
+        hold((), w_one, x_swap)
         w_one.fourth()
+        begin((), w_one)
+        w_one.over_cores()
+        hold((), w_one, w_two)
+        w_self = w_one.pieces()
         w_two.second()
-        begin((), w_one, w_two)
-        w_one.over_cores()
-        hold((), w_one, w_two, w_ffn)
-        left, right = w_ffn.split()
-        w_self = w_one.pieces()
-        w_two.third()
-        w_self = begin(w_self, w_two, left, right, mem_swap)
+        w_self = begin(w_self, w_two, w_ffn)
     else:
         cot_swap = Swap(other_row(cotangent, me))
         begin((), x_swap, mem_swap, cot_swap)
@@ -1095,6 +1112,11 @@
         w_ffn = [w_ffn.reshape(3, width, 2, -1).transpose(2, 0, 1, 3)]
     x = (x_swap.state[0], tokens)
     normed_one, qkv, w_self = project(ids, norm_gains, *x, w_self)
+    if packed:
+        qkv = hold(qkv, w_two, w_ffn)
+        w_two.third()
+        left, right = w_ffn.split()
+        qkv = begin(qkv, w_two, left, right, mem_swap)
     parts = ((qkv, 0), (qkv, pairs), (qkv, 2 * pairs))
     self_args = (True, ids, doc_lengths, band)
     if packed:
@@ -1178,7 +1200,7 @@
         d_ours, grads_ours = hold((d_ours, grads_ours), mid, theirs, gmem_swap, ffn)
         ours = SideScatter(*grads_ours)
         ours.launch()
-        theirs.flip(2)
+        theirs.across()
         mid.fourth()
         theirs.sent, mid.sent = hold((theirs.sent, mid.sent), ours)
         ours.flip(1)
@@ -1194,33 +1216,35 @@
         grad_x_swap.sent, gain_one, table_ours, table_theirs = hold(
             (grad_x_swap.sent, gain_one, table_ours, table_theirs), mid, ours, theirs
         )
-        ours.flip(2)
-        theirs.flip(3)
+        ours.flip(2, theirs.state[0])
         mid.fifth()
         gain_one, table_ours, table_theirs = begin(
-            (gain_one, table_ours, table_theirs), grad_x_swap, ours, theirs, mid
+            (gain_one, table_ours, table_theirs), grad_x_swap, ours, mid
         )
     table = jnp.where(half_of == me, table_ours, table_theirs).reshape(-1, width)
     small = jnp.concatenate([gain_one, gain_two, gain_three, table])
     if packed:
         small = Sum(small, 0)
         small.launch()
-        small.flip(None)
-        small.launch()
+        output, out_swap.state, gmem, gmem_swap.state, ffn.state = hold(
+            (output, out_swap.state, gmem, gmem_swap.state, ffn.state), small
+        )
         small.flip(1)
         small.launch()
-        hold((), mid, ours, theirs, small)
+        hold((), ours, small)
         small.flip(2)
+        ours.flip(3)
+        begin((), small, ours)
+        hold((), small, mid)
+        small.flip(3)
         small.launch()
-        ours.flip(3)
-        theirs.across()
-        begin((), ours, theirs)
-        small.flip(3)
+        hold((), small, grad_x_swap)
+        small.flip(None)
         small.launch()
         ffn_grads = ffn.total()
         mid_grads = mid.total()
         ours.take()
-        self_grads = ours.kept + theirs.state[0].astype(F32)
+        self_grads = ours.kept
         small.take()
         small = small.values
     else:

time: 433 us -> 411 us (0.949)
  starting transfers between devices: 63.2 us -> 52.4 us
  Pallas kernels: 249 us -> 242 us
  local copies, waits for them, and re-layouts: 20.2 us -> 14 us
  waiting for transfers between devices: 58.6 us -> 64.6 us
    ppermute x52 -> x50, starting transfers between devices: 43.8 us -> 34.3 us  [flip_bit(): return lax.ppermute(values, 'dp', [(i, i ^ 1 << bit) for i in range(size)])]
    ppermute x52 -> x50, waiting for transfers between devices: 45 us -> 48.4 us  [flip_bit(): return lax.ppermute(values, 'dp', [(i, i ^ 1 << bit) for i in range(size)])]
  transfers between devices with their start and end apart: 70 -> 68, of which waited for: 19 -> 24; matrix products, arithmetic and copies ran while one was open for 9% -> 9% of each run, Pallas kernels for 46% -> 47%
where the time goes in v4:
time: 411 us; the launch traced here: 408 us
  Pallas kernels  242 us (59%)
  waiting for transfers between devices  64.6 us (16%)
  starting transfers between devices  52.4 us (13%)
  other arithmetic  31.8 us (8%)
  local copies, waits for them, and re-layouts  14 us (3%)
    pallas_call x1, Pallas kernels, feed(): call(functools.partial(feed_kernel, blocks, len(pieces), packed), 'feed',...  49.9 us
    ppermute x50, waiting for transfers between devices, flip_bit(): return lax.ppermute(values, 'dp', [(i, i ^ 1 << bit) for i in range(size)])  48.4 us
    pallas_call x3, Pallas kernels, self_backward(): call(functools.partial(backward_kernel, True, packed, len(into)), 'self_b...  47.5 us
    pallas_call x4, Pallas kernels, attention_forward(): call(functools.partial(forward_kernel, causal, len(into)), 'attention_for...  42.9 us
    pallas_call x2, Pallas kernels, cross_backward(): call(functools.partial(backward_kernel, False, False, 0), 'cross_backward...  41.5 us
    ppermute x50, starting transfers between devices, flip_bit(): return lax.ppermute(values, 'dp', [(i, i ^ 1 << bit) for i in range(size)])  34.3 us
    pallas_call x1, Pallas kernels, cross_back(): call(functools.partial(cross_back_kernel, blocks, packed), 'cross_back',...  28.8 us
    ppermute x18, starting transfers between devices, flip_mp(): return lax.ppermute(values, 'mp', [(0, 1), (1, 0)])  18.1 us
  transfers between devices with their start and end apart: 68, of which 24 were waited for; matrix products, arithmetic and copies ran while one was open for 9% of the time, Pallas kernels for 47%

profile of v4, /device:TPU:0, one launch (start us, length us, event | category | flops | bytes accessed | tf_op | source)
XLA Modules:
  0.0 407.6 jit_solution(12356666558617262810)
XLA Ops:
  0.7 4.1 %collective-permute-start = (bf16[3,48,384]{2,1,0:T(8,128)(2,1)}, bf16[3,48,384]{2,1,0:T(8,128)(2,1)}, u32[]{:S(2)}, u32[]{:S(2)}) collective-permute-start(bf16[3,48,384]{2,1,0:T(8,128)(2,1)} %param.24), channel_id=1, source_target_pairs={{0,16},{2,18},{4,20},{6,22},{8,24},{10,26},{12,28},{14,30},{16,0},... | collective-permute-start | bytes 331784 | tf_op jit(solution)/shard_map/ppermute | solution.py:866
  7.6 2.1 dynamic-slice_bitcast_fusion.2
  14.7 4.1 collective-permute-done.1.refs_3_
  21.0 8.8 %collective-permute-done.2.refs_1_ = bf16[2,3,48,384]{3,2,1,0:T(8,128)(2,1)S(1)} collective-permute-done((bf16[2,3,48,384]{3,2,1,0:T(8,128)(2,1)S(1)}, bf16[2,3,48,384]{3,2,1,0:T(8,128)(2,1)S(1)}, u32[]{:S(2)}, u32[]{:S(2)}) %collective-permute-start.2) | collective-permute-done | bytes 221216 | tf_op jit(solution)/shard_map/ppermute | solution.py:870
  33.4 9.1 %collective-permute-done.7 = bf16[5,48,384]{2,1,0:T(8,128)(2,1)S(1)} collective-permute-done((bf16[5,48,384]{2,1,0:T(8,128)(2,1)S(1)}, bf16[5,48,384]{2,1,0:T(8,128)(2,1)S(1)}, u32[]{:S(2)}, u32[]{:S(2)}) %collective-permute-start.7) | collective-permute-done | bytes 184352 | tf_op jit(solution)/shard_map/ppermute | solution.py:866
  49.1 6.5 %project.1 = (bf16[1024,768]{1,0:T(8,128)(2,1)S(1)}, bf16[1024,2304]{1,0:T(8,128)(2,1)S(1)}, bf16[3,768,768]{2,1,0:T(8,128)(2,1)S(1)}) custom-call(s32[3]{0:T(128)S(1)} %pad_add_fusion.ids_ref, f32[3,768]{1,0:T(4,128)S(1)} %copy-done.9, bf16[512,768]{1,0:T(8,128)(2,1)S(1)} %collective-permute-done.4.came_ref, bf16[2,512,768]{2,1,0:T(8,128)(2,1)S(1)} %copy-done.4, ...), custom_call_target="tpu_custom_call" | custom-call | flops 3623878656 | bytes 11403264 | tf_op jit(solution)/shard_map/project/pallas_call | solution.py:598
  60.9 9.5 %attention_forward.4 = (bf16[1024,768]{1,0:T(8,128)(2,1)S(1)}, bf16[12,1024,128]{2,1,0:T(8,128)(2,1)S(1)}) custom-call(s32[3]{0:T(128)S(1)} %pad_add_fusion.ids_ref, s32[2,3]{1,0:T(2,128)S(1)} %copy-done.10, f32[6,2,384]{2,1,0:T(2,128)S(1)} %reshape.103.band_ref, bf16[1024,2304]{1,0:T(8,128)(2,1)S(1)} %get-tuple-element.279.q_ref.k_ref.v_ref, ...), custom_call_target="tpu_custom_call" | custom-call | flops 3221225472 | bytes 12582912 | tf_op jit(solution)/shard_map/attention_forward/pallas_call | solution.py:277
  71.9 4.3 %collective-permute-done.19 = bf16[2,3,48,640]{3,2,1,0:T(8,128)(2,1)S(1)} collective-permute-done((bf16[2,3,48,640]{3,2,1,0:T(8,128)(2,1)S(1)}, bf16[2,3,48,640]{3,2,1,0:T(8,128)(2,1)S(1)}, u32[]{:S(2)}, u32[]{:S(2)}) %collective-permute-start.19) | collective-permute-done | bytes 368672 | tf_op jit(solution)/shard_map/ppermute | solution.py:866
  79.2 9.5 %attention_forward.5 = (bf16[1024,768]{1,0:T(8,128)(2,1)S(1)}, bf16[12,1024,128]{2,1,0:T(8,128)(2,1)S(1)}) custom-call(s32[3]{0:T(128)S(1)} %pad_add_fusion.ids_ref, s32[2,3]{1,0:T(2,128)S(1)} %copy-done.10, f32[6,2,384]{2,1,0:T(2,128)S(1)} %reshape.103.band_ref, ...), custom_call_target="tpu_custom_call", output_to_operand_aliasing={{0}: (6, {}), {1}: (7, {})} | custom-call | flops 3221225472 | bytes 12582912 | tf_op jit(solution)/shard_map/attention_forward/pallas_call | solution.py:277
  88.8 5.1 %collective-permute-done.22.refs_2_ = bf16[2,2,5,48,384]{4,3,2,1,0:T(8,128)(2,1)S(1)} collective-permute-done((bf16[2,2,5,48,384]{4,3,2,1,0:T(8,128)(2,1)S(1)}, bf16[2,2,5,48,384]{4,3,2,1,0:T(8,128)(2,1)S(1)}, u32[]{:S(2)}, u32[]{:S(2)}) %collective-permute-start.22) | collective-permute-done | bytes 737312 | tf_op jit(solution)/shard_map/ppermute | solution.py:866
  93.9 5.3 %collective-permute-done.23.refs_5_ = bf16[2,2,5,48,384]{4,3,2,1,0:T(8,128)(2,1)S(1)} collective-permute-done((bf16[2,2,5,48,384]{4,3,2,1,0:T(8,128)(2,1)S(1)}, bf16[2,2,5,48,384]{4,3,2,1,0:T(8,128)(2,1)S(1)}, u32[]{:S(2)}, u32[]{:S(2)}) %collective-permute-start.23) | collective-permute-done | bytes 737312 | tf_op jit(solution)/shard_map/ppermute | solution.py:870
  106.2 14.5 %middle.1 = (f32[1024,768]{1,0:T(8,128)}, bf16[1024,768]{1,0:T(8,128)(2,1)}, bf16[1024,768]{1,0:T(8,128)(2,1)}, bf16[1024,768]{1,0:T(8,128)(2,1)}, bf16[1024,768...) custom-call(s32[3]{0:T(128)} %copy-done.8, f32[3,768]{1,0:T(4,128)} %gain_ref.9, bf16[512,768]{1,0:T(8,128)(2,1)} %copy-done.6, ...), custom_call_target="tpu_custom_call" | custom-call | flops 4831838208 | bytes 21626880 | tf_op jit(solution)/shard_map/middle/pallas_call | solution.py:637
  120.7 6.1 %collective-permute-done.31 = bf16[2,2,3,48,384]{4,3,2,1,0:T(8,128)(2,1)S(1)} collective-permute-done((bf16[2,2,3,48,384]{4,3,2,1,0:T(8,128)(2,1)S(1)}, bf16[2,2,3,48,384]{4,3,2,1,0:T(8,128)(2,1)S(1)}, u32[]{:S(2)}, u32[]{:S(2)}) %collective-permute-start.31) | collective-permute-done | bytes 442400 | tf_op jit(solution)/shard_map/ppermute | solution.py:866
  127.0 18.1 %attention_forward.6 = (bf16[1024,768]{1,0:T(8,128)(2,1)}, bf16[12,1024,128]{2,1,0:T(8,128)(2,1)}) custom-call(s32[3]{0:T(128)} %copy-done.8, s32[2]{0:T(128)} %bounds_ref.14, f32[6,2,384]{2,1,0:T(2,128)} %copy-done.7, bf16[1024,768]{1,0:T(8,128)(2,1)} %get-tuple-element.323.q_ref, bf16[1024,768]{1,0:T(8,128)(2,1)} %get-tuple-element.324.k_ref, ...), custom_call_target="tpu_custom_call" | custom-call | flops 10737418240 | bytes 12582912 | tf_op jit(solution)/shard_map/attention_forward/pallas_call | solution.py:277
  145.1 3.0 collective-permute-done.33.refs_5_
  148.8 5.8 %attention_forward.7 = (bf16[1024,768]{1,0:T(8,128)(2,1)}, bf16[12,1024,128]{2,1,0:T(8,128)(2,1)}) custom-call(s32[3]{0:T(128)} %copy-done.8, s32[2]{0:T(128)} %bounds_ref.14, f32[6,2,384]{2,1,0:T(2,128)} %copy-done.7, bf16[1024,768]{1,0:T(8,128)(2,1)} %get-tuple-element.323.q_ref, ...), custom_call_target="tpu_custom_call", output_to_operand_aliasing={{0}: (6, {}), {1}: (7, {})} | custom-call | flops 2147483648 | bytes 12582912 | tf_op jit(solution)/shard_map/attention_forward/pallas_call | solution.py:277
  156.2 49.9 %feed.1 = (f32[512,768]{1,0:T(8,128)}, bf16[512,768]{1,0:T(8,128)(2,1)}, f32[1024,768]{1,0:T(8,128)}, bf16[1024,768]{1,0:T(8,128)(2,1)}, f32[1,768]{1,0:T(1,128)...) custom-call(s32[3]{0:T(128)} %copy-done.8, s32[2,3]{1,0:T(2,128)} %bounds_ref.17, ...), custom_call_target="tpu_custom_call" | custom-call | flops 28991029248 | bytes 37748736 | tf_op jit(solution)/shard_map/feed/pallas_call | solution.py:745
  207.3 15.2 %cross_backward.2.rest_0_ = bf16[3,1024,768]{2,1,0:T(8,128)(2,1)} custom-call(s32[3]{0:T(128)} %copy-done.8, s32[2]{0:T(128)} %bounds_ref.14, f32[6,2,384]{2,1,0:T(2,128)} %copy-done.7, bf16[12,1024,128]{2,1,0:T(8,128)(2,1)} %get-tuple-element.339.qa_ref, bf16[1024,768]{1,0:T(8,128)(2,1)} %get-tuple-element.324.k_ref, ...), custom_call_target="tpu_custom_call" | custom-call | flops 10737418240 | bytes 15728640 | tf_op jit(solution)/shard_map/cross_backward/pallas_call | solution.py:301
  224.3 2.8 fusion
  228.9 26.3 %cross_backward.3.d_ref = bf16[3,1024,768]{2,1,0:T(8,128)(2,1)} custom-call(s32[3]{0:T(128)} %copy-done.8, s32[2]{0:T(128)} %bounds_ref.14, f32[6,2,384]{2,1,0:T(2,128)} %copy-done.7, bf16[12,1024,128]{2,1,0:T(8,128)(2,1)} %get-tuple-element.339.qa_ref, bf16[1024,768]{1,0:T(8,128)(2,1)} %get-tuple-element.324.k_ref, ...), custom_call_target="tpu_custom_call", output_to_operand_aliasing={{}: (8, {})} | custom-call | flops 21474836480 | bytes 15728640 | tf_op jit(solution)/shard_map/cross_backward/pallas_call | solution.py:301
  255.3 2.4 fusion.6
  260.0 28.8 %cross_back.1 = (f32[1024,768]{1,0:T(8,128)}, bf16[1024,768]{1,0:T(8,128)(2,1)}, f32[512,768]{1,0:T(8,128)}, bf16[512,768]{1,0:T(8,128)(2,1)}, f32[1,768]{1,0:T(...) custom-call(s32[3]{0:T(128)} %copy-done.8, f32[3,768]{1,0:T(4,128)} %gain_ref.9, ...), custom_call_target="tpu_custom_call" | custom-call | flops 10871635968 | bytes 40108032 | tf_op jit(solution)/shard_map/cross_back/pallas_call | solution.py:809
  288.9 2.6 fusion.5
  291.7 9.3 %self_backward.3 = (bf16[3,1024,384]{2,1,0:T(8,128)(2,1)}, f32[6,8,128]{2,1,0:T(8,128)}, bf16[2,2,2,3,48,384]{5,4,3,2,1,0:T(8,128)(2,1)}, bf16[2,2,2,3,48,384]{5,4,3,2,1,0:T(8,128)(2,1)}) custom-call(s32[3]{0:T(128)} %copy-done.8, s32[2,3]{1,0:T(2,128)} %bounds_ref.17, f32[6,2,384]{2,1,0:T(2,128)} %copy-done.7, bf16[12,1024,128]{2,1,0:T(8,128)(2,1)} %copy-done.1, ...), custom_call_target="tpu_custom_call" | custom-call | flops 4294967296 | bytes 15728640 | tf_op jit(solution)/shard_map/self_backward/pallas_call | solution.py:335
  301.0 2.2 fusion.13
  303.3 2.2 fusion.12
  307.3 16.2 %self_backward.4 = (bf16[3,1024,384]{2,1,0:T(8,128)(2,1)}, f32[6,8,128]{2,1,0:T(8,128)}, bf16[2,2,2,3,48,384]{5,4,3,2,1,0:T(8,128)(2,1)}, bf16[2,2,2,3,48,384]{5,4,3,2,1,0:T(8,128)(2,1)}) custom-call(s32[3]{0:T(128)} %copy-done.8, s32[2,3]{1,0:T(2,128)} %bounds_ref.17, ...), custom_call_target="tpu_custom_call", output_to_operand_aliasing={{0}: (10, {}), {1}: (11, {}), {2}: (12, {}), {3}: (13, {})} | custom-call | flops 8589934592 | bytes 15728640 | tf_op jit(solution)/shard_map/self_backward/pallas_call | solution.py:335
  336.0 22.0 %self_backward.5 = (bf16[3,1024,384]{2,1,0:T(8,128)(2,1)}, f32[6,8,128]{2,1,0:T(8,128)}, bf16[2,2,2,3,48,384]{5,4,3,2,1,0:T(8,128)(2,1)}, bf16[2,2,2,3,48,384]{5,4,3,2,1,0:T(8,128)(2,1)}) custom-call(s32[3]{0:T(128)} %copy-done.8, s32[2,3]{1,0:T(2,128)} %bounds_ref.17, f32[6,2,384]{2,1,0:T(2,128)} %copy-done.7, bf16[12,1024,128]{2,1,0:T(8,128)(2,1)} %copy-done.1, ...), custom_call_target="tpu_custom_call" | custom-call | flops 12884901888 | bytes 15728640 | tf_op jit(solution)/shard_map/self_backward/pallas_call | solution.py:335
  363.9 10.8 %self_back.1 = (f32[512,768]{1,0:T(8,128)}, bf16[512,768]{1,0:T(8,128)(2,1)}, f32[1,768]{1,0:T(1,128)}) custom-call(s32[3]{0:T(128)} %copy-done.8, f32[3,768]{1,0:T(4,128)} %gain_ref.9, bf16[3,1024,384]{2,1,0:T(8,128)(2,1)} %get-tuple-element.423.ours_ref, bf16[3,1024,384]{2,1,0:T(8,128)(2,1)} %get-tuple-element.424.theirs_ref, bf16[512,768]{1,0:T(8,128)(2,1)} %copy-done.6, ...), custom_call_target="tpu_custom_call" | custom-call | flops 3623878656 | bytes 19267584 | tf_op jit(solution)/shard_map/self_back/pallas_call | solution.py:850
  385.7 3.3 collective-permute-done.60
  391.8 2.4 collective-permute-start.67
  396.1 5.1 %collective-permute-done.67 = bf16[3,48,384]{2,1,0:T(8,128)(2,1)S(1)} collective-permute-done((bf16[3,48,384]{2,1,0:T(8,128)(2,1)S(1)}, bf16[3,48,384]{2,1,0:T(8,128)(2,1)S(1)}, u32[]{:S(2)}, u32[]{:S(2)}) %collective-permute-start.67) | collective-permute-done | bytes 110624 | tf_op jit(solution)/shard_map/ppermute | solution.py:866
  (311 shorter events, 88.3 us)
Async XLA Ops:
  6.0 23.8 %collective-permute-start.4 = (bf16[512,768]{1,0:T(8,128)(2,1)S(1)}, bf16[512,768]{1,0:T(8,128)(2,1)S(1)}, u32[]{:S(2)}, u32[]{:S(2)}) collective-permute-start(bf16[512,768]{1,0:T(8,128)(2,1)S(1)} %dynamic-slice_bitcast_fusion), channel_id=1, source_target_pairs={{0,1},{1,0},{2,3},{3,2},{4,5},{5,4},{6,7},{7,6},{8,9},{9,8},{10,11... | collective-permute-start | bytes 2359304 | tf_op jit(solution)/shard_map/ppermute | solution.py:870
  56.6 15.3 %collective-permute-start.17 = (bf16[2,5,48,384]{3,2,1,0:T(8,128)(2,1)S(1)}, bf16[2,5,48,384]{3,2,1,0:T(8,128)(2,1)S(1)}, u32[]{:S(2)}, u32[]{:S(2)}) collective-permute-start(bf16[2,5,48,384]{3,2,1,0:T(8,128)(2,1)S(1)} %get-tuple-element.306.refs_0_), channel_id=1, source_target_pairs={{0,1},{1,0},{2,3},{3,2},{4,5},{5,4},{6,7},{7,6},{8,9},{9,8},{10,11... | collective-permute-start | bytes 1105928 | tf_op jit(solution)/shard_map/ppermute | solution.py:870
  57.7 14.3 %collective-permute-start.18 = (bf16[2,5,48,384]{3,2,1,0:T(8,128)(2,1)S(1)}, bf16[2,5,48,384]{3,2,1,0:T(8,128)(2,1)S(1)}, u32[]{:S(2)}, u32[]{:S(2)}) collective-permute-start(bf16[2,5,48,384]{3,2,1,0:T(8,128)(2,1)S(1)} %collective-permute-done.14.refs_3_), channel_id=1, source_target_pairs={{0,4},{2,6},{4,0},{6,2},{8,12},{10,14},{12,8},{14,10},{16,20},{18,... | collective-permute-start | bytes 1105928 | tf_op jit(solution)/shard_map/ppermute | solution.py:866
  58.2 18.0 %collective-permute-start.19 = (bf16[2,3,48,640]{3,2,1,0:T(8,128)(2,1)S(1)}, bf16[2,3,48,640]{3,2,1,0:T(8,128)(2,1)S(1)}, u32[]{:S(2)}, u32[]{:S(2)}) collective-permute-start(bf16[2,3,48,640]{3,2,1,0:T(8,128)(2,1)S(1)} %fusion.24), channel_id=1, source_target_pairs={{0,16},{2,18},{4,20},{6,22},{8,24},{10,26},{12,28},{14,30},{16,0},... | collective-permute-start | bytes 1105928 | tf_op jit(solution)/shard_map/ppermute | solution.py:866
  58.6 13.4 %collective-permute-start.20 = (bf16[2,3,48,384]{3,2,1,0:T(8,128)(2,1)S(1)}, bf16[2,3,48,384]{3,2,1,0:T(8,128)(2,1)S(1)}, u32[]{:S(2)}, u32[]{:S(2)}) collective-permute-start(bf16[2,3,48,384]{3,2,1,0:T(8,128)(2,1)S(1)} %pad_maximum_fusion.9), channel_id=1, source_target_pairs={{0,4},{2,6},{4,0},{6,2},{8,12},{10,14},{12,8},{14,10},{16,20},{18,... | collective-permute-start | bytes 663560 | tf_op jit(solution)/shard_map/ppermute | solution.py:866
  60.1 28.7 %collective-permute-start.21 = (bf16[512,768]{1,0:T(8,128)(2,1)}, bf16[512,768]{1,0:T(8,128)(2,1)S(1)}, u32[]{:S(2)}, u32[]{:S(2)}) collective-permute-start(bf16[512,768]{1,0:T(8,128)(2,1)} %dynamic-slice_bitcast_fusion.2), channel_id=1, source_target_pairs={{0,1},{1,0},{2,3},{3,2},{4,5},{5,4},{6,7},{7,6},{8,9},{9,8},{10,11... | collective-permute-start | bytes 2359304 | tf_op jit(solution)/shard_map/ppermute | solution.py:870
  76.5 17.4 %collective-permute-start.22 = (bf16[2,2,5,48,384]{4,3,2,1,0:T(8,128)(2,1)S(1)}, bf16[2,2,5,48,384]{4,3,2,1,0:T(8,128)(2,1)S(1)}, u32[]{:S(2)}, u32[]{:S(2)}) collective-permute-start(bf16[2,2,5,48,384]{4,3,2,1,0:T(8,128)(2,1)S(1)} %pad_maximum_fusion.2), channel_id=1, source_target_pairs={{0,4},{2,6},{4,0},{6,2},{8,12},{10,14},{12,8},{14,10},{16,20},{18,... | collective-permute-start | bytes 2211848 | tf_op jit(solution)/shard_map/ppermute | solution.py:866
  78.1 21.1 %collective-permute-start.23 = (bf16[2,2,5,48,384]{4,3,2,1,0:T(8,128)(2,1)S(1)}, bf16[2,2,5,48,384]{4,3,2,1,0:T(8,128)(2,1)S(1)}, u32[]{:S(2)}, u32[]{:S(2)}) collective-permute-start(bf16[2,2,5,48,384]{4,3,2,1,0:T(8,128)(2,1)S(1)} %pad_maximum_fusion.3), channel_id=1, source_target_pairs={{0,1},{1,0},{2,3},{3,2},{4,5},{5,4},{6,7},{7,6},{8,9},{9,8},{10,11... | collective-permute-start | bytes 2211848 | tf_op jit(solution)/shard_map/ppermute | solution.py:870
  79.2 20.0 %collective-permute-start.24 = (bf16[2,2,3,48,640]{4,3,2,1,0:T(8,128)(2,1)S(1)}, bf16[2,2,3,48,640]{4,3,2,1,0:T(8,128)(2,1)S(1)}, u32[]{:S(2)}, u32[]{:S(2)}) collective-permute-start(bf16[2,2,3,48,640]{4,3,2,1,0:T(8,128)(2,1)S(1)} %get-tuple-element.297), channel_id=1, source_target_pairs={{0,8},{2,10},{4,12},{6,14},{8,0},{10,2},{12,4},{14,6},{16,24},{18,... | collective-permute-start | bytes 2211848 | tf_op jit(solution)/shard_map/ppermute | solution.py:866
  79.2 21.0 %collective-permute-start.25 = (bf16[2,5,48,384]{3,2,1,0:T(8,128)(2,1)S(1)}, bf16[2,5,48,384]{3,2,1,0:T(8,128)(2,1)S(1)}, u32[]{:S(2)}, u32[]{:S(2)}) collective-permute-start(bf16[2,5,48,384]{3,2,1,0:T(8,128)(2,1)S(1)} %get-tuple-element.306.refs_0_), channel_id=1, source_target_pairs={{0,2},{2,0},{4,6},{6,4},{8,10},{10,8},{12,14},{14,12},{16,18},{18,... | collective-permute-start | bytes 1105928 | tf_op jit(solution)/shard_map/ppermute | solution.py:866
  103.0 51.6 %collective-permute-start.35 = (bf16[2,2,2,3,48,640]{5,4,3,2,1,0:T(8,128)(2,1)S(1)}, bf16[2,2,2,3,48,640]{5,4,3,2,1,0:T(8,128)(2,1)S(1)}, u32[]{:S(2)}, u32[]{:S(2)}) collective-permute-start(bf16[2,2,2,3,48,640]{5,4,3,2,1,0:T(8,128)(2,1)S(1)} %pad_maximum_fusion.refs_0_), channel_id=1, source_target_pairs={{0,2},{2,0},{4,6},{6,4},{8,10},{10,8},{12,14},{14,12},{16,18},{18,... | collective-permute-start | bytes 4423688 | tf_op jit(solution)/shard_map/ppermute | solution.py:866
  104.2 22.6 %collective-permute-start.31 = (bf16[2,2,3,48,384]{4,3,2,1,0:T(8,128)(2,1)S(1)}, bf16[2,2,3,48,384]{4,3,2,1,0:T(8,128)(2,1)S(1)}, u32[]{:S(2)}, u32[]{:S(2)}) collective-permute-start(bf16[2,2,3,48,384]{4,3,2,1,0:T(8,128)(2,1)S(1)} %get-tuple-element.320), channel_id=1, source_target_pairs={{0,16},{2,18},{4,20},{6,22},{8,24},{10,26},{12,28},{14,30},{16,0},... | collective-permute-start | bytes 1327112 | tf_op jit(solution)/shard_map/ppermute | solution.py:866
  104.6 43.5 %collective-permute-start.32 = (bf16[2,2,2,3,48,640]{5,4,3,2,1,0:T(8,128)(2,1)S(1)}, bf16[2,2,2,3,48,640]{5,4,3,2,1,0:T(8,128)(2,1)S(1)}, u32[]{:S(2)}, u32[]{:S(2)}) collective-permute-start(bf16[2,2,2,3,48,640]{5,4,3,2,1,0:T(8,128)(2,1)S(1)} %pad_maximum_fusion.refs_0_), channel_id=1, source_target_pairs={{0,4},{2,6},{4,0},{6,2},{8,12},{10,14},{12,8},{14,10},{16,20},{18,... | collective-permute-start | bytes 4423688 | tf_op jit(solution)/shard_map/ppermute | solution.py:866
  105.3 39.8 %collective-permute-start.34 = (bf16[512,768]{1,0:T(8,128)(2,1)}, bf16[512,768]{1,0:T(8,128)(2,1)}, u32[]{:S(2)}, u32[]{:S(2)}) collective-permute-start(bf16[512,768]{1,0:T(8,128)(2,1)} %dynamic-slice_bitcast_fusion.1), channel_id=1, source_target_pairs={{0,1},{1,0},{2,3},{3,2},{4,5},{5,4},{6,7},{7,6},{8,9},{9,8},{10,11... | collective-permute-start | bytes 2359304 | tf_op jit(solution)/shard_map/ppermute | solution.py:870
  126.9 21.2 %collective-permute-start.33 = (bf16[2,2,2,3,48,384]{5,4,3,2,1,0:T(8,128)(2,1)S(1)}, bf16[2,2,2,3,48,384]{5,4,3,2,1,0:T(8,128)(2,1)S(1)}, u32[]{:S(2)}, u32[]{:S(2)}) collective-permute-start(bf16[2,2,2,3,48,384]{5,4,3,2,1,0:T(8,128)(2,1)S(1)} %pad_maximum_fusion.1.refs_4_), channel_id=1, source_target_pairs={{0,8},{2,10},{4,12},{6,14},{8,0},{10,2},{12,4},{14,6},{16,24},{18,... | collective-permute-start | bytes 2654216 | tf_op jit(solution)/shard_map/ppermute | solution.py:866
  206.1 16.4 %collective-permute-start.39 = (bf16[2,2,2,2,3,48,1024]{6,5,4,3,2,1,0:T(8,128)(2,1)}, bf16[2,2,2,2,3,48,1024]{6,5,4,3,2,1,0:T(8,128)(2,1)}, u32[]{:S(2)}, u32[]{:S(2)}) collective-permute-start(bf16[2,2,2,2,3,48,1024]{6,5,4,3,2,1,0:T(8,128)(2,1)} %get-tuple-element.344), channel_id=1, source_target_pairs={{0,2},{2,0},{4,6},{6,4},{8,10},{10,8},{12,14},{14,12},{16,18},{18,... | collective-permute-start | bytes 14155784 | tf_op jit(solution)/shard_map/ppermute | solution.py:866
  206.6 53.4 %collective-permute-start.42 = (bf16[512,768]{1,0:T(8,128)(2,1)}, bf16[512,768]{1,0:T(8,128)(2,1)}, u32[]{:S(2)}, u32[]{:S(2)}) collective-permute-start(bf16[512,768]{1,0:T(8,128)(2,1)} %get-tuple-element.356), channel_id=1, source_target_pairs={{0,1},{1,0},{2,3},{3,2},{4,5},{5,4},{6,7},{7,6},{8,9},{9,8},{10,11... | collective-permute-start | bytes 2359304 | tf_op jit(solution)/shard_map/ppermute | solution.py:870
  227.1 28.2 %collective-permute-start.40 = (bf16[2,2,3,48,1024]{4,3,2,1,0:T(8,128)(2,1)}, bf16[2,2,3,48,1024]{4,3,2,1,0:T(8,128)(2,1)S(1)}, u32[]{:S(2)}, u32[]{:S(2)}) collective-permute-start(bf16[2,2,3,48,1024]{4,3,2,1,0:T(8,128)(2,1)} %fusion), channel_id=1, source_target_pairs={{0,4},{2,6},{4,0},{6,2},{8,12},{10,14},{12,8},{14,10},{16,20},{18,... | collective-permute-start | bytes 3538952 | tf_op jit(solution)/shard_map/ppermute | solution.py:866
  227.6 27.7 %collective-permute-start.41 = (bf16[2,2,3,48,1024]{4,3,2,1,0:T(8,128)(2,1)S(1)}, bf16[2,2,3,48,1024]{4,3,2,1,0:T(8,128)(2,1)S(1)}, u32[]{:S(2)}, u32[]{:S(2)}) collective-permute-start(bf16[2,2,3,48,1024]{4,3,2,1,0:T(8,128)(2,1)S(1)} %fusion.1), channel_id=1, source_target_pairs={{0,1},{1,0},{2,3},{3,2},{4,5},{5,4},{6,7},{7,6},{8,9},{9,8},{10,11... | collective-permute-start | bytes 3538952 | tf_op jit(solution)/shard_map/ppermute | solution.py:870
  257.7 31.1 %collective-permute-start.43 = (bf16[2,3,48,1024]{3,2,1,0:T(8,128)(2,1)S(1)}, bf16[2,3,48,1024]{3,2,1,0:T(8,128)(2,1)S(1)}, u32[]{:S(2)}, u32[]{:S(2)}) collective-permute-start(bf16[2,3,48,1024]{3,2,1,0:T(8,128)(2,1)S(1)} %get-tuple-element.366), channel_id=1, source_target_pairs={{0,1},{1,0},{2,3},{3,2},{4,5},{5,4},{6,7},{7,6},{8,9},{9,8},{10,11... | collective-permute-start | bytes 1769480 | tf_op jit(solution)/shard_map/ppermute | solution.py:870
  258.8 30.0 %collective-permute-start.44 = (bf16[2,3,48,1024]{3,2,1,0:T(8,128)(2,1)S(1)}, bf16[2,3,48,1024]{3,2,1,0:T(8,128)(2,1)S(1)}, u32[]{:S(2)}, u32[]{:S(2)}) collective-permute-start(bf16[2,3,48,1024]{3,2,1,0:T(8,128)(2,1)S(1)} %get-tuple-element.367), channel_id=1, source_target_pairs={{0,4},{2,6},{4,0},{6,2},{8,12},{10,14},{12,8},{14,10},{16,20},{18,... | collective-permute-start | bytes 1769480 | tf_op jit(solution)/shard_map/ppermute | solution.py:866
  291.4 32.1 %collective-permute-start.48 = (bf16[2,3,48,1024]{3,2,1,0:T(8,128)(2,1)}, bf16[2,3,48,1024]{3,2,1,0:T(8,128)(2,1)}, u32[]{:S(2)}, u32[]{:S(2)}) collective-permute-start(bf16[2,3,48,1024]{3,2,1,0:T(8,128)(2,1)} %fusion.5), channel_id=1, source_target_pairs={{0,8},{2,10},{4,12},{6,14},{8,0},{10,2},{12,4},{14,6},{16,24},{18,... | collective-permute-start | bytes 1769480 | tf_op jit(solution)/shard_map/ppermute | solution.py:866
  305.4 18.8 %collective-permute-start.46 = (bf16[2,2,5,48,384]{4,3,2,1,0:T(8,128)(2,1)}, bf16[2,2,5,48,384]{4,3,2,1,0:T(8,128)(2,1)S(1)}, u32[]{:S(2)}, u32[]{:S(2)}) collective-permute-start(bf16[2,2,5,48,384]{4,3,2,1,0:T(8,128)(2,1)} %fusion.12), channel_id=1, source_target_pairs={{0,4},{2,6},{4,0},{6,2},{8,12},{10,14},{12,8},{14,10},{16,20},{18,... | collective-permute-start | bytes 2211848 | tf_op jit(solution)/shard_map/ppermute | solution.py:866
  306.3 18.6 %collective-permute-start.47 = (bf16[2,2,5,48,384]{4,3,2,1,0:T(8,128)(2,1)}, bf16[2,2,5,48,384]{4,3,2,1,0:T(8,128)(2,1)S(1)}, u32[]{:S(2)}, u32[]{:S(2)}) collective-permute-start(bf16[2,2,5,48,384]{4,3,2,1,0:T(8,128)(2,1)} %fusion.13), channel_id=1, source_target_pairs={{0,1},{1,0},{2,3},{3,2},{4,5},{5,4},{6,7},{7,6},{8,9},{9,8},{10,11... | collective-permute-start | bytes 2211848 | tf_op jit(solution)/shard_map/ppermute | solution.py:870
  325.7 32.2 %collective-permute-start.53 = (bf16[512,768]{1,0:T(8,128)(2,1)}, bf16[512,768]{1,0:T(8,128)(2,1)S(1)}, u32[]{:S(2)}, u32[]{:S(2)}) collective-permute-start(bf16[512,768]{1,0:T(8,128)(2,1)} %get-tuple-element.411), channel_id=1, source_target_pairs={{0,1},{1,0},{2,3},{3,2},{4,5},{5,4},{6,7},{7,6},{8,9},{9,8},{10,11... | collective-permute-start | bytes 2359304 | tf_op jit(solution)/shard_map/ppermute | solution.py:870
  330.9 27.2 %collective-permute-start.52 = (bf16[2,2,3,48,384]{4,3,2,1,0:T(8,128)(2,1)S(1)}, bf16[2,2,3,48,384]{4,3,2,1,0:T(8,128)(2,1)S(1)}, u32[]{:S(2)}, u32[]{:S(2)}) collective-permute-start(bf16[2,2,3,48,384]{4,3,2,1,0:T(8,128)(2,1)S(1)} %fusion.21), channel_id=1, source_target_pairs={{0,4},{2,6},{4,0},{6,2},{8,12},{10,14},{12,8},{14,10},{16,20},{18,... | collective-permute-start | bytes 1327112 | tf_op jit(solution)/shard_map/ppermute | solution.py:866
  332.4 25.6 %collective-permute-start.50 = (bf16[2,5,48,384]{3,2,1,0:T(8,128)(2,1)S(1)}, bf16[2,5,48,384]{3,2,1,0:T(8,128)(2,1)S(1)}, u32[]{:S(2)}, u32[]{:S(2)}) collective-permute-start(bf16[2,5,48,384]{3,2,1,0:T(8,128)(2,1)S(1)} %get-tuple-element.408), channel_id=1, source_target_pairs={{0,1},{1,0},{2,3},{3,2},{4,5},{5,4},{6,7},{7,6},{8,9},{9,8},{10,11... | collective-permute-start | bytes 1105928 | tf_op jit(solution)/shard_map/ppermute | solution.py:870
  333.1 24.9 %collective-permute-start.51 = (bf16[2,5,48,384]{3,2,1,0:T(8,128)(2,1)S(1)}, bf16[2,5,48,384]{3,2,1,0:T(8,128)(2,1)S(1)}, u32[]{:S(2)}, u32[]{:S(2)}) collective-permute-start(bf16[2,5,48,384]{3,2,1,0:T(8,128)(2,1)S(1)} %get-tuple-element.409), channel_id=1, source_target_pairs={{0,4},{2,6},{4,0},{6,2},{8,12},{10,14},{12,8},{14,10},{16,20},{18,... | collective-permute-start | bytes 1105928 | tf_op jit(solution)/shard_map/ppermute | solution.py:866
  334.0 24.0 %collective-permute-start.54 = (bf16[3,48,1024]{2,1,0:T(8,128)(2,1)S(1)}, bf16[3,48,1024]{2,1,0:T(8,128)(2,1)S(1)}, u32[]{:S(2)}, u32[]{:S(2)}) collective-permute-start(bf16[3,48,1024]{2,1,0:T(8,128)(2,1)S(1)} %fusion.26), channel_id=1, source_target_pairs={{0,16},{2,18},{4,20},{6,22},{8,24},{10,26},{12,28},{14,30},{16,0},... | collective-permute-start | bytes 884744 | tf_op jit(solution)/shard_map/ppermute | solution.py:866
  361.0 13.7 %collective-permute-start.57 = (bf16[2,2,3,48,384]{4,3,2,1,0:T(8,128)(2,1)S(1)}, bf16[2,2,3,48,384]{4,3,2,1,0:T(8,128)(2,1)S(1)}, u32[]{:S(2)}, u32[]{:S(2)}) collective-permute-start(bf16[2,2,3,48,384]{4,3,2,1,0:T(8,128)(2,1)S(1)} %fusion.22), channel_id=1, source_target_pairs={{0,4},{2,6},{4,0},{6,2},{8,12},{10,14},{12,8},{14,10},{16,20},{18,... | collective-permute-start | bytes 1327112 | tf_op jit(solution)/shard_map/ppermute | solution.py:866
  379.0 15.2 %collective-permute-start.63 = (bf16[5,48,384]{2,1,0:T(8,128)(2,1)}, bf16[5,48,384]{2,1,0:T(8,128)(2,1)S(1)}, u32[]{:S(2)}, u32[]{:S(2)}) collective-permute-start(bf16[5,48,384]{2,1,0:T(8,128)(2,1)} %fusion.29), channel_id=1, source_target_pairs={{0,16},{2,18},{4,20},{6,22},{8,24},{10,26},{12,28},{14,30},{16,0},... | collective-permute-start | bytes 552968 | tf_op jit(solution)/shard_map/ppermute | solution.py:866
  379.9 22.1 %collective-permute-start.65 = (bf16[512,768]{1,0:T(8,128)(2,1)}, bf16[512,768]{1,0:T(8,128)(2,1)S(1)}, u32[]{:S(2)}, u32[]{:S(2)}) collective-permute-start(bf16[512,768]{1,0:T(8,128)(2,1)} %get-tuple-element.457), channel_id=1, source_target_pairs={{0,1},{1,0},{2,3},{3,2},{4,5},{5,4},{6,7},{7,6},{8,9},{9,8},{10,11... | collective-permute-start | bytes 2359304 | tf_op jit(solution)/shard_map/ppermute | solution.py:870
  (97 other events, 1014.7 us)

commit v5 on v4

--- a/solution.py
+++ b/solution.py
@@ -157,9 +157,9 @@
 def backward_kernel(causal, packed, extra, ids_ref, bounds_ref, band_ref, qa_ref, k_ref, v_ref, g_ref, o_ref, *rest):
     if causal:
         rest = rest[:2] + rest[2 + extra :]
-        near_ref, normed_ref, grad_ref, bias_ref = rest[:4]
-        wgrads = rest[4:-7]
-        extra_q, extra_k, dk_acc, dv_acc, near_acc, side_acc, left = rest[-7:]
+        near_ref, left, grad_ref, bias_ref = rest[:4]
+        wgrads = rest[4:-6]
+        extra_q, extra_k, dk_acc, dv_acc, near_acc, side_acc = rest[-6:]
     else:
         grad_ref, extra_q, extra_k, dk_acc, dv_acc = rest[-5:]
     length = k_ref.shape[0]
@@ -167,15 +167,11 @@
     @pl.when(pl.program_id(0) == 0)
     def _():
         make_extras(ids_ref, bounds_ref, causal, extra_q, extra_k)
-        if causal:
-            put_turned(packed, ids_ref, left, slice(None), normed_ref[...])
-
-    if causal:
-        bias_ref[...] = jnp.zeros_like(bias_ref)
 
     lane, slot = lane_slots((QB, LANES))
     full_lane, full_slot = lane_slots((length, LANES))
     spare_v = jnp.where((full_slot >= 4) & (full_slot <= 6), 1.0, 0.0).astype(BF)
+    squares, wholes = [], []
     for head in range(2):
         mine = (full_lane < DH) == (head == 0)
         mine_block = (lane < DH) == (head == 0)
@@ -183,12 +179,10 @@
         values = jnp.where(mine, v_ref[...], spare_v)
         if causal:
             near, side = band_square(band_ref, head)
-            near, side = near.T, side.T
-            near_only = jnp.full((LANES, LANES), masked_score, F32)
             near_acc[...] = jnp.zeros_like(near_acc)
             side_acc[...] = jnp.zeros_like(side_acc)
-        dk_acc[...] = jnp.zeros_like(dk_acc)
-        dv_acc[...] = jnp.zeros_like(dv_acc)
+        dk_acc[head] = jnp.zeros(dk_acc.shape[1:], F32)
+        dv_acc[head] = jnp.zeros(dv_acc.shape[1:], F32)
         for block in range(length // QB):
             first = block * QB
             count = first + QB if causal else length
@@ -200,58 +194,47 @@
             )
             spare = place_three(-inner, slot, jnp.zeros((QB, LANES), F32))
             grads = jnp.where(mine_block, upstream, spare.astype(BF))
-            scores = dot_t(keys[:count], queries)
+            scores = dot_t(queries, keys[:count])
             if causal:
-                corner = jnp.concatenate([side, jnp.zeros((LANES, LANES), F32)], axis=1)
-                upper = jnp.concatenate([near, side], axis=1)
-                lower = jnp.concatenate([near_only, near], axis=1)
-                pieces = []
+                scores = add_band(scores, first, near, side)
+            probs = jnp.exp(scores)
+            lifted = dot_t(grads, values[:count])
+            score_grads = (probs * lifted).astype(BF)
+            dv_acc[head, :, :count] += dot_n(grads.T, probs.astype(BF))
+            dk_acc[head, :, :count] += dot_n(queries.T, score_grads)
+            dq = dot_n(score_grads, keys[:count]).astype(BF)
+            if causal:
+                near_acc[...] += score_grads[:LANES, first : first + LANES].astype(F32)
+                near_acc[...] += score_grads[LANES:, first + LANES :].astype(F32)
+                side_acc[...] += score_grads[LANES:, first : first + LANES].astype(F32)
                 if block > 0:
-                    if first > LANES:
-                        pieces.append(scores[: first - LANES])
-                    pieces.append(scores[first - LANES : first] + corner)
-                pieces.append(scores[first : first + LANES] + upper)
-                pieces.append(scores[first + LANES :] + lower)
-                scores = jnp.concatenate(pieces, axis=0)
-            probs = jnp.exp(scores)
-            lifted = dot_t(values[:count], grads)
-            score_grads = (probs * lifted).astype(BF)
-            dv_acc[:count, :] += dot_n(probs.astype(BF), grads)
-            dk_acc[:count, :] += dot_n(score_grads, queries)
-            dq = dot_tn(score_grads, keys[:count])
-            if causal:
-                near_acc[...] += score_grads[first : first + LANES, :LANES].astype(F32)
-                near_acc[...] += score_grads[first + LANES :, LANES:].astype(F32)
-                side_acc[...] += score_grads[first : first + LANES, LANES:].astype(F32)
-                if block > 0:
-                    side_acc[...] += score_grads[first - LANES : first, :LANES].astype(F32)
+                    side_acc[...] += score_grads[:LANES, first - LANES : first].astype(F32)
             if head == 0:
-                grad_ref[0, span, :] = dq.astype(BF)
+                grad_ref[0, span, :] = dq
             else:
-                grad_ref[0, span, :] = jnp.where(lane < DH, grad_ref[0, span, :], dq.astype(BF))
-        if head == 0:
-            grad_ref[1] = dk_acc[...].astype(BF)
-            grad_ref[2] = dv_acc[...].astype(BF)
-        else:
-            grad_ref[1] = jnp.where(full_lane < DH, grad_ref[1], dk_acc[...].astype(BF))
-            grad_ref[2] = jnp.where(full_lane < DH, grad_ref[2], dv_acc[...].astype(BF))
+                grad_ref[0, span, :] = jnp.where(lane < DH, grad_ref[0, span, :], dq)
         if causal:
-            square = jnp.concatenate([side_acc[...], near_acc[...]], axis=0)
-            wide = jnp.concatenate([square, jnp.zeros((2 * LANES, 2 * LANES), F32)], axis=1)
-            half = LANES
-            while half:
-                wide = wide[:half] + pltpu.roll(wide[half:], 3 * LANES - half, 1)
-                half //= 2
-            diag = wide[:, 2 * LANES :]
-            ones_column = jnp.where((full_lane % DH == 7) & ~mine, dk_acc[...], 0.0)
-            whole = jnp.sum(ones_column, axis=0, keepdims=True)
-            table = lax.dot_general(
-                diag, near_ref[...], (((1,), (0,)), ((), ())),
-                precision=lax.Precision.HIGHEST, preferred_element_type=F32,
-            )
-            last = jnp.sum(whole, axis=1, keepdims=True) - jnp.sum(table, axis=1, keepdims=True)
-            at_last = lax.broadcasted_iota(jnp.int32, table.shape, 1) == NB - 1
-            bias_ref[0, head : head + 1, :] = jnp.where(at_last, last, table)
+            squares.append(jnp.concatenate([side_acc[...], near_acc[...]], axis=1))
+            ones_row = DH + 7 if head == 0 else 7
+            wholes.append(jnp.sum(dk_acc[head, ones_row : ones_row + 1, :], axis=1, keepdims=True))
+    upper = lax.broadcasted_iota(jnp.int32, (LANES, length), 0) < DH
+    grad_ref[1] = jnp.where(upper, dk_acc[0], dk_acc[1]).astype(BF).T
+    grad_ref[2] = jnp.where(upper, dv_acc[0], dv_acc[1]).astype(BF).T
+    if causal:
+        wide = jnp.concatenate([jnp.stack(squares), jnp.zeros((2, LANES, LANES), F32)], axis=2)
+        half = LANES // 2
+        while half:
+            wide = wide[:, :half] + pltpu.roll(wide[:, half:], 3 * LANES - half, 2)
+            half //= 2
+        diag = jnp.concatenate([wide[0], wide[1], jnp.zeros((6, 3 * LANES), F32)], axis=0)[:, : 2 * LANES]
+        table = lax.dot_general(
+            diag, near_ref[...], (((1,), (0,)), ((), ())),
+            precision=lax.Precision.HIGHEST, preferred_element_type=F32,
+        )
+        whole = jnp.concatenate(wholes + [jnp.zeros((6, 1), F32)], axis=0)
+        last = whole - jnp.sum(table, axis=1, keepdims=True)
+        at_last = lax.broadcasted_iota(jnp.int32, table.shape, 1) == NB - 1
+        bias_ref[0] = jnp.where(at_last, last, table)
     if causal:
         right = jnp.concatenate([grad_ref[n] for n in range(3)], axis=1)
         grads = dot_n(left[...], right).astype(BF)
@@ -307,17 +290,17 @@
             spec(k[1]), spec(v[1]), spec(0), spec(0),
         ] + [anywhere()] * len(into),
         [(pl.BlockSpec((3, rows, LANES), lambda p, ids: (0, 0, p + start)), (3, rows, cols), BF)],
-        [pltpu.VMEM((rows, LANES), BF)] * 2 + [pltpu.VMEM((rows, LANES), F32)] * 2,
+        [pltpu.VMEM((rows, LANES), BF)] * 2 + [pltpu.VMEM((2, LANES, rows), F32)] * 2,
         n * 256 * 10, rows * cols * 20,
         {8: 0} if into else {},
     )(ids, bounds, band, qa, k[0], v[0], g, o, *into)[0]
 
 
-def self_backward(side, packed, ids, bounds, band, qa, k, v, g, o, normed, start=0, stop=None, into=()):
+def self_backward(side, packed, ids, bounds, band, qa, k, v, g, o, normed_t, start=0, stop=None, into=()):
     rows, cols = g.shape
     pairs = cols // LANES // 2
     stop = pairs if stop is None else stop
-    depth = normed.shape[1] >> BITS
+    depth = normed_t.shape[0] >> BITS
 
     def at(p, ids):
         return p + start + pairs * jnp.bitwise_xor(ids[1], side)
@@ -330,8 +313,8 @@
         block = pl.BlockSpec((2, 2, 2, 3, depth, LANES), lambda p, ids: (0, 0, 0, 0, 0, p + start))
         wgrads = [(block, (2, 2, 2, 3, depth, cols // 2), BF)] * 2
     else:
-        block = pl.BlockSpec((3, normed.shape[1], LANES), lambda p, ids: (0, 0, p + start))
-        wgrads = [(block, (3, normed.shape[1], cols // 2), BF)]
+        block = pl.BlockSpec((3, normed_t.shape[0], LANES), lambda p, ids: (0, 0, p + start))
+        wgrads = [(block, (3, normed_t.shape[0], cols // 2), BF)]
     return call(
         functools.partial(backward_kernel, True, packed, len(into)), "self_backward", BACKWARD_MB, stop - start,
         [
@@ -339,23 +322,26 @@
             pl.BlockSpec((None, 2, 3 * LANES), lambda p, ids: (at(p, ids), 0, 0)),
             pl.BlockSpec((2, rows, LANES), lambda p, ids: (at(p, ids), 0, 0)),
             spec(k[1]), spec(v[1]), spec(0), spec(0),
-            held((LANES, LANES)), held(normed.shape),
+            held((2 * LANES, LANES)), held(normed_t.shape),
         ] + [anywhere()] * len(into),
         [
             (pl.BlockSpec((3, rows, LANES), lambda p, ids: (0, 0, p + start)), (3, rows, cols // 2), BF),
             (pl.BlockSpec((1, 8, LANES), lambda p, ids: (at(p, ids), 0, 0)), (2 * pairs, 8, LANES), F32),
         ] + wgrads,
-        [pltpu.VMEM((rows, LANES), BF)] * 2 + [pltpu.VMEM((rows, LANES), F32)] * 2
-        + [pltpu.VMEM((LANES, LANES), F32)] * 2 + [pltpu.VMEM((normed.shape[1], rows), BF)],
+        [pltpu.VMEM((rows, LANES), BF)] * 2 + [pltpu.VMEM((2, LANES, rows), F32)] * 2
+        + [pltpu.VMEM((LANES, LANES), F32)] * 2,
         n * 256 * 8, rows * cols * 20,
         {10 + i: i for i in range(len(into))},
-    )(ids, bounds, band, qa, k[0], v[0], g, o, jnp.asarray(near_buckets()), normed, *into)
+    )(ids, bounds, band, qa, k[0], v[0], g, o, jnp.asarray(near_buckets()), normed_t, *into)
 
 
 def near_buckets():
     buckets = bucket_table(LANES, NB, REACH)
-    columns = np.arange(LANES)[None, :]
-    return ((buckets[:, None] == columns) & (columns < NB - 1)).astype(np.float32)
+    table = np.zeros((2 * LANES, LANES), np.float32)
+    for distance in range(LANES):
+        if buckets[distance] < NB - 1:
+            table[LANES - distance, buckets[distance]] = 1.0
+    return table
 
 
 def bucket_table(length, buckets, reach):
@@ -404,6 +390,10 @@
 
 def turn(s, ids, blocks):
     return ((1 - ids[1]) * (blocks // 2) + jnp.minimum(s, blocks - 1)) % blocks
+
+
+def row_span(s, ids, blocks):
+    return pl.ds(pl.multiple_of(turn(s, ids, blocks) * TB, TB), TB)
 
 
 def row_spec(blocks, width, *lead):
@@ -541,9 +531,9 @@
         target[pl.ds(pl.multiple_of(at, 16), depth), span] = turned[block * depth : (block + 1) * depth]
 
 
-def put_grads(packed, ids_ref, n, grads, outs):
+def put_grads(packed, ids_ref, grads, outs):
     if not packed:
-        outs[0][n] = grads
+        outs[0][...] = grads
         return
     keep_ref, send_ref = outs
     rows, cols = keep_ref.shape[-2:]
@@ -553,8 +543,7 @@
         for x in range(2):
             first = cols * (x ^ flip)
             for target, part in ((keep_ref, grads[:middle]), (send_ref, grads[middle:])):
-                block = part[:, first : first + cols].reshape(2, 2, 2, rows, cols)
-                target[:, x, :, :, n] = block
+                target[:, x] = part[:, first : first + cols].reshape(2, 2, 2, rows, cols)
 
     @pl.when(ids_ref[1] == 0)
     def _():
@@ -565,17 +554,20 @@
         store(1)
 
 
-def grads_out(packed, n, width):
+def grads_out(packed, n, width, first):
+    def at(s):
+        return jnp.maximum(s - first, 0)
+
     if not packed:
-        shape = (n, width, width)
-        return [(held(shape), shape, BF)]
-    shape = (2, 2, 2, 2, n, width >> BITS, width // 2)
-    return [(held(shape), shape, BF)] * 2
-
-
-def project_kernel(blocks, pieces, ids_ref, gain_ref, came_ref, kept_ref, *refs):
+        return [(pl.BlockSpec((None, width, width), lambda s, ids: (at(s), 0, 0)), (n, width, width), BF)]
+    rows, cols = width >> BITS, width // 2
+    block = pl.BlockSpec((2, 2, 2, 2, None, rows, cols), lambda s, ids: (0, 0, 0, 0, at(s), 0, 0))
+    return [(block, (2, 2, 2, 2, n, rows, cols), BF)] * 2
+
+
+def project_kernel(blocks, pieces, packed, ids_ref, gain_ref, came_ref, kept_ref, *refs):
     w_in = refs[:pieces]
-    normed_ref, out_ref, w_ref, sem = refs[pieces:]
+    turned_ref, out_ref, w_ref, sem = refs[pieces:]
     step = pl.program_id(0)
 
     @pl.when(step == 0)
@@ -584,22 +576,22 @@
         wait_pieces(w_ref, sem.at[0])
 
     normed, _ = rms(chosen(step, blocks, came_ref, kept_ref).astype(F32), gain_ref[0:1, :])
-    normed_ref[...] = normed
+    put_turned(packed, ids_ref, turned_ref, row_span(step, ids_ref, blocks), normed)
     width = normed.shape[1]
     for s in range(3):
         out_ref[:, s * width : (s + 1) * width] = dot_n(normed, w_ref[s]).astype(BF)
 
 
-def project(ids, gain, came, kept, pieces):
+def project(packed, ids, gain, came, kept, pieces):
     _, half, width = kept.shape
     rows = 2 * half
     blocks = rows // TB
     full = (3, width, width)
     return call(
-        functools.partial(project_kernel, blocks, len(pieces)), "project", PROJECT_MB, blocks,
+        functools.partial(project_kernel, blocks, len(pieces), packed), "project", PROJECT_MB, blocks,
         [held((3, width)), other_spec(blocks, width), kept_spec(blocks, width)] + [anywhere()] * len(pieces),
         [
-            (row_spec(blocks, width), (rows, width), BF),
+            (held((width, rows)), (width, rows), BF),
             (row_spec(blocks, 3 * width), (rows, 3 * width), BF),
             (held(full), full, BF),
         ],
@@ -608,9 +600,9 @@
     )(ids, gain, came, kept, *pieces)
 
 
-def middle_kernel(blocks, pieces, ids_ref, gain_ref, came_ref, kept_ref, mixed_ref, mem_came_ref, mem_kept_ref, *refs):
+def middle_kernel(blocks, pieces, packed, ids_ref, gain_ref, came_ref, kept_ref, mixed_ref, mem_came_ref, mem_kept_ref, *refs):
     w_in = refs[:pieces]
-    resid_ref, normed_ref, q_ref, k_ref, v_ref, w_ref, sem = refs[pieces:]
+    resid_ref, turned_ref, mem_turned_ref, q_ref, k_ref, v_ref, w_ref, sem = refs[pieces:]
     step = pl.program_id(0)
 
     @pl.when(step == 0)
@@ -621,23 +613,26 @@
     resid = chosen(step, blocks, came_ref, kept_ref).astype(F32) + dot_t(mixed_ref[...], w_ref[0])
     resid_ref[...] = resid
     normed, _ = rms(resid, gain_ref[1:2, :])
-    normed_ref[...] = normed
+    span = row_span(step, ids_ref, blocks)
+    put_turned(packed, ids_ref, turned_ref, span, normed)
     q_ref[...] = dot_n(normed, w_ref[1]).astype(BF)
     memory = chosen(step, blocks, mem_came_ref, mem_kept_ref)
+    put_turned(packed, ids_ref, mem_turned_ref, span, memory)
     k_ref[...] = dot_n(memory, w_ref[2]).astype(BF)
     v_ref[...] = dot_n(memory, w_ref[3]).astype(BF)
 
 
-def middle(ids, gain, came, kept, mixed, mem_came, mem_kept, pieces):
+def middle(packed, ids, gain, came, kept, mixed, mem_came, mem_kept, pieces):
     rows, width = mixed.shape
     blocks = rows // TB
     full = (5, width, width)
     spec = row_spec(blocks, width)
     pair = [other_spec(blocks, width), kept_spec(blocks, width)]
     return call(
-        functools.partial(middle_kernel, blocks, len(pieces)), "middle", MIDDLE_MB, blocks,
+        functools.partial(middle_kernel, blocks, len(pieces), packed), "middle", MIDDLE_MB, blocks,
         [held((3, width))] + pair + [spec] + pair + [anywhere()] * len(pieces),
-        [(spec, (rows, width), F32)] + [(spec, (rows, width), BF)] * 4 + [(held(full), full, BF)],
+        [(spec, (rows, width), F32)] + [(held((width, rows)), (width, rows), BF)] * 2
+        + [(spec, (rows, width), BF)] * 3 + [(held(full), full, BF)],
         [pltpu.SemaphoreType.DMA((1,))],
         8 * rows * width * width, 20 * rows * width + 10 * width * width,
     )(ids, gain, came, kept, mixed, mem_came, mem_kept, *pieces)
@@ -761,8 +756,8 @@
     )(ids, docs, gain, resid, mixed, cot_came, cot_kept, w_mid, *pieces)
 
 
-def cross_back_kernel(blocks, packed, ids_ref, gain_ref, d_ref, resid_ref, normed_ref, mem_came_ref, mem_kept_ref,
-                      grad_ref, mixed_cross_ref, mixed_self_ref, w_ref, *outs):
+def cross_back_kernel(blocks, packed, ids_ref, gain_ref, d_ref, resid_ref, normed_t, mem_t, grad_ref,
+                       mixed_cross_ref, mixed_self_ref, w_ref, *outs):
     grad_two_ref, gmix_ref, gmem_own_ref, gmem_other_ref, gain_grad_ref = outs[:5]
     wgrads = outs[5:-2]
     lefts, rights = outs[-2:]
@@ -786,29 +781,28 @@
         gmix_ref[...] = dot_n(branch, w_ref[0]).astype(BF)
         gmem = dot_t(d_ref[1], w_ref[2]) + dot_t(d_ref[2], w_ref[3])
         share(step, blocks, gmem, gmem_own_ref, gmem_other_ref)
-        memory = chosen(step, blocks, mem_came_ref, mem_kept_ref)
-        for n, values in enumerate((branch, normed_ref[...], memory, grad_three.astype(BF))):
-            put_turned(packed, ids_ref, lefts.at[n], span, values)
+        put_turned(packed, ids_ref, lefts.at[0], span, branch)
+        put_turned(packed, ids_ref, lefts.at[1], span, grad_three.astype(BF))
         rights[0, span, :] = mixed_self_ref[...]
         rights[1, span, :] = d_ref[0]
         rights[2, span, :] = d_ref[1]
         rights[3, span, :] = d_ref[2]
         rights[4, span, :] = mixed_cross_ref[...]
 
-    for n, left in enumerate((0, 1, 2, 2, 3)):
+    for n, left in enumerate((lefts.at[0], normed_t, mem_t, mem_t, lefts.at[1])):
 
         @pl.when(step == blocks + n)
         def _():
-            put_grads(packed, ids_ref, n, dot_n(lefts[left], rights[n]).astype(BF), wgrads)
-
-
-def cross_back(packed, ids, gain, d, resid, normed, mem_came, mem_kept, grad, mixed_cross, mixed_self, w):
+            put_grads(packed, ids_ref, dot_n(left[...], rights[n]).astype(BF), wgrads)
+
+
+def cross_back(packed, ids, gain, d, resid, normed_t, mem_t, grad, mixed_cross, mixed_self, w):
     rows, width = resid.shape
     blocks = rows // TB
     spec = row_spec(blocks, width)
     return call(
         functools.partial(cross_back_kernel, blocks, packed), "cross_back", CROSS_BACK_MB, blocks + 5,
-        [held((3, width)), row_spec(blocks, width, 3), spec, spec, other_spec(blocks, width), kept_spec(blocks, width),
+        [held((3, width)), row_spec(blocks, width, 3), spec, held((width, rows)), held((width, rows)),
          spec, spec, spec, held(w.shape)],
         [
             (spec, (rows, width), F32),
@@ -816,10 +810,10 @@
             (own_spec(blocks, width), (rows // 2, width), F32),
             (other_spec(blocks, width), (rows // 2, width), BF),
             (held((1, width)), (1, width), F32),
-        ] + grads_out(packed, 5, width),
-        [pltpu.VMEM((4, width, rows), BF), pltpu.VMEM((5, rows, width), BF)],
+        ] + grads_out(packed, 5, width, blocks),
+        [pltpu.VMEM((2, width, rows), BF), pltpu.VMEM((5, rows, width), BF)],
         18 * rows * width * width, 36 * rows * width + 20 * width * width,
-    )(ids, gain, d, resid, normed, mem_came, mem_kept, grad, mixed_cross, mixed_self, w)
+    )(ids, gain, d, resid, normed_t, mem_t, grad, mixed_cross, mixed_self, w)
 
 
 def self_back_kernel(blocks, ids_ref, gain_ref, ours_ref, theirs_ref, came_ref, kept_ref, grad_ref, w_ref,
@@ -967,8 +961,9 @@
 
     def second(self):
         (self.came,) = self.state
-        every = slice(None)
-        self.send((self.own(1, every, 0).astype(BF), 1), (self.own(every, 1, 1).astype(BF), None))
+        low = self.keep[1, :, 0] + self.came[1, :, 0]
+        high = self.keep[:, 1, 1] + self.came[:, 1, 1]
+        self.send((low, 1), (high, None))
 
     def third(self):
         low_y, high_x = self.state
@@ -1111,7 +1106,7 @@
         w_ffn = gather_whole(jnp.concatenate([ffn_proj, ffn_out.T[None]]))
         w_ffn = [w_ffn.reshape(3, width, 2, -1).transpose(2, 0, 1, 3)]
     x = (x_swap.state[0], tokens)
-    normed_one, qkv, w_self = project(ids, norm_gains, *x, w_self)
+    normed_one_t, qkv, w_self = project(packed, ids, norm_gains, *x, w_self)
     if packed:
         qkv = hold(qkv, w_two, w_ffn)
         w_two.third()
@@ -1135,7 +1130,9 @@
     else:
         mixed_self, qa_self = attention_forward(*self_args, *parts, width)
     mem = (mem_swap.state[0], memory)
-    resid_two, normed_two, q_cross, k_cross, v_cross, w_mid = middle(ids, norm_gains, *x, mixed_self, *mem, w_mid)
+    resid_two, normed_two_t, mem_t, q_cross, k_cross, v_cross, w_mid = middle(
+        packed, ids, norm_gains, *x, mixed_self, *mem, w_mid
+    )
     cross_args = (False, ids, mem_lengths, band)
     if packed:
         q_cross = hold(q_cross, right)
@@ -1158,11 +1155,11 @@
     if packed:
         ffn = Scatter(*ffn_grads)
         grad_mixed = begin(grad_mixed, out_swap, ffn)
-        grads = cross_backward(*cross_args, *parts, grad_mixed, mixed_cross, 0, 2)
+        grads = cross_backward(*cross_args, *parts, grad_mixed, mixed_cross, 0, 1)
         grads = hold(grads, ffn)
         ffn.second()
         grads, grad_mixed = begin((grads, grad_mixed), ffn)
-        grads_cross = cross_backward(*cross_args, *parts, grad_mixed, mixed_cross, 2, pairs, (grads,))
+        grads_cross = cross_backward(*cross_args, *parts, grad_mixed, mixed_cross, 1, pairs, (grads,))
         grads_cross = hold(grads_cross, ffn)
         ffn.third()
         grads_cross = begin(grads_cross, ffn)
@@ -1171,11 +1168,11 @@
         grads_cross = cross_backward(*cross_args, *parts, grad_mixed, mixed_cross, 0, pairs)
     grads_cross = hold(grads_cross, out_swap)
     grad_two, grad_mixed, gmem, gmem_sent, gain_two, *mid_grads = cross_back(
-        packed, ids, norm_gains, grads_cross, resid_two, normed_two, *mem, grad_three, mixed_cross, mixed_self, w_mid
+        packed, ids, norm_gains, grads_cross, resid_two, normed_two_t, mem_t, grad_three, mixed_cross, mixed_self, w_mid
     )
     gmem_swap = Swap(gmem_sent)
     parts = (qa_self, (qkv, pairs), (qkv, 2 * pairs))
-    more = (mixed_self, normed_one)
+    more = (mixed_self, normed_one_t)
     if packed:
         mid = Scatter(*mid_grads)
         hold((), ffn)
@@ -1229,9 +1226,13 @@
         output, out_swap.state, gmem, gmem_swap.state, ffn.state = hold(
             (output, out_swap.state, gmem, gmem_swap.state, ffn.state), small
         )
+        output = both_halves(output, out_swap.state[0], me)
+        grad_memory = both_halves(gmem, gmem_swap.state[0], me)
+        ffn_grads = ffn.total()
+        ffn_grads = (ffn_grads[:2], ffn_grads[2].T)
         small.flip(1)
         small.launch()
-        hold((), ours, small)
+        output, grad_memory, ffn_grads = hold((output, grad_memory, ffn_grads), ours, small)
         small.flip(2)
         ours.flip(3)
         begin((), small, ours)
@@ -1241,7 +1242,6 @@
         hold((), small, grad_x_swap)
         small.flip(None)
         small.launch()
-        ffn_grads = ffn.total()
         mid_grads = mid.total()
         ours.take()
         self_grads = ours.kept
@@ -1249,7 +1249,10 @@
         small = small.values
     else:
         begin((), grad_x_swap)
+        output = both_halves(output, out_swap.state[0], me)
+        grad_memory = both_halves(gmem, gmem_swap.state[0], me)
         ffn_grads = scatter_whole(ffn_grads[0].transpose(1, 2, 0, 3).reshape(3, width, -1))
+        ffn_grads = (ffn_grads[:2], ffn_grads[2].T)
         mid_grads = scatter_whole(mid_grads[0])
         self_grads = scatter_whole(
             jnp.where(
@@ -1260,8 +1263,6 @@
         )
         small = lax.psum(small, ("dp", "mp"))
     table = small[3:].reshape(pairs, -1, LANES)[:, :2, :NB].reshape(2 * pairs, NB).T
-    output = both_halves(output, out_swap.state[0], me)
-    grad_memory = both_halves(gmem, gmem_swap.state[0], me)
     grad_tokens = both_halves(grad_x, grad_x_swap.state[0], me)
     return (
         output,
@@ -1273,8 +1274,7 @@
         mid_grads[0].T,
         mid_grads[1:4],
         mid_grads[4].T,
-        ffn_grads[:2],
-        ffn_grads[2].T,
+        *ffn_grads,
     )
 
 

time: 411 us -> 398 us (0.968)
  Pallas kernels: 242 us -> 233 us
    convert_element_type x4 -> x0, other arithmetic: 8.98 us -> none  [the longest x2 5 us: second(): self.own(1, every, 0).astype(BF)]
    add x0 -> x4, other arithmetic: none -> 8.91 us  [the longest x2 4.97 us: second(): low = self.keep[1, :, 0] + self.came[1, :, 0]]
    pallas_call x3, Pallas kernels: 47.5 us -> 42.5 us  [self_backward(): call(functools.partial(backward_kernel, True, packed, len(into)), 'self_b...]
    ppermute x50, waiting for transfers between devices: 48.4 us -> 43.6 us  [flip_bit(): return lax.ppermute(values, 'dp', [(i, i ^ 1 << bit) for i in range(size)])]
    pallas_call x2, Pallas kernels: 41.5 us -> 36.8 us  [cross_backward(): call(functools.partial(backward_kernel, False, False, 0), 'cross_backward...]
  transfers between devices with their start and end apart: 68 -> 68, of which waited for: 24 -> 25; matrix products, arithmetic and copies ran while one was open for 9% -> 9% of each run, Pallas kernels for 47% -> 46%
where the time goes in v5:
time: 398 us; the launch traced here: 395 us
  Pallas kernels  233 us (59%)
  waiting for transfers between devices  60.8 us (15%)
  starting transfers between devices  54.4 us (14%)
  other arithmetic  30.6 us (8%)
  local copies, waits for them, and re-layouts  14.3 us (4%)
    pallas_call x1, Pallas kernels, feed(): call(functools.partial(feed_kernel, blocks, len(pieces), packed), 'feed',...  49.9 us
    ppermute x50, waiting for transfers between devices, flip_bit(): return lax.ppermute(values, 'dp', [(i, i ^ 1 << bit) for i in range(size)])  43.6 us
    pallas_call x4, Pallas kernels, attention_forward(): call(functools.partial(forward_kernel, causal, len(into)), 'attention_for...  42.9 us
    pallas_call x3, Pallas kernels, self_backward(): call(functools.partial(backward_kernel, True, packed, len(into)), 'self_b...  42.5 us
    pallas_call x2, Pallas kernels, cross_backward(): call(functools.partial(backward_kernel, False, False, 0), 'cross_backward...  36.8 us
    ppermute x50, starting transfers between devices, flip_bit(): return lax.ppermute(values, 'dp', [(i, i ^ 1 << bit) for i in range(size)])  35 us
    pallas_call x1, Pallas kernels, cross_back(): call(functools.partial(cross_back_kernel, blocks, packed), 'cross_back',...  26.6 us
    ppermute x18, starting transfers between devices, flip_mp(): return lax.ppermute(values, 'mp', [(0, 1), (1, 0)])  19.4 us
  transfers between devices with their start and end apart: 68, of which 25 were waited for; matrix products, arithmetic and copies ran while one was open for 9% of the time, Pallas kernels for 46%

profile of v5, /device:TPU:0, one launch (start us, length us, event | category | flops | bytes accessed | tf_op | source)
XLA Modules:
  0.0 395.3 jit_solution(8413380241994350821)
XLA Ops:
  0.7 4.1 %collective-permute-start = (bf16[3,48,384]{2,1,0:T(8,128)(2,1)}, bf16[3,48,384]{2,1,0:T(8,128)(2,1)}, u32[]{:S(2)}, u32[]{:S(2)}) collective-permute-start(bf16[3,48,384]{2,1,0:T(8,128)(2,1)} %param.24), channel_id=1, source_target_pairs={{0,16},{2,18},{4,20},{6,22},{8,24},{10,26},{12,28},{14,30},{16,0},... | collective-permute-start | bytes 331784 | tf_op jit(solution)/shard_map/ppermute | solution.py:860
  12.3 2.1 dynamic-slice_bitcast_fusion.1
  14.4 3.8 collective-permute-done.1.refs_3_
  21.0 8.8 %collective-permute-done.2.refs_1_ = bf16[2,3,48,384]{3,2,1,0:T(8,128)(2,1)S(1)} collective-permute-done((bf16[2,3,48,384]{3,2,1,0:T(8,128)(2,1)S(1)}, bf16[2,3,48,384]{3,2,1,0:T(8,128)(2,1)S(1)}, u32[]{:S(2)}, u32[]{:S(2)}) %collective-permute-start.2) | collective-permute-done | bytes 221216 | tf_op jit(solution)/shard_map/ppermute | solution.py:864
  33.5 9.0 %collective-permute-done.7 = bf16[5,48,384]{2,1,0:T(8,128)(2,1)S(1)} collective-permute-done((bf16[5,48,384]{2,1,0:T(8,128)(2,1)S(1)}, bf16[5,48,384]{2,1,0:T(8,128)(2,1)S(1)}, u32[]{:S(2)}, u32[]{:S(2)}) %collective-permute-start.7) | collective-permute-done | bytes 184352 | tf_op jit(solution)/shard_map/ppermute | solution.py:860
  49.1 6.5 %project.1 = (bf16[768,1024]{1,0:T(8,128)(2,1)S(1)}, bf16[1024,2304]{1,0:T(8,128)(2,1)S(1)}, bf16[3,768,768]{2,1,0:T(8,128)(2,1)S(1)}) custom-call(s32[3]{0:T(128)S(1)} %pad_add_fusion.ids_ref, f32[3,768]{1,0:T(4,128)S(1)} %copy-done.9, bf16[512,768]{1,0:T(8,128)(2,1)S(1)} %collective-permute-done.4.came_ref, bf16[2,512,768]{2,1,0:T(8,128)(2,1)S(1)} %copy-done.4, ...), custom_call_target="tpu_custom_call" | custom-call | flops 3623878656 | bytes 11403264 | tf_op jit(solution)/shard_map/project/pallas_call | solution.py:590
  60.8 9.5 %attention_forward.4 = (bf16[1024,768]{1,0:T(8,128)(2,1)S(1)}, bf16[12,1024,128]{2,1,0:T(8,128)(2,1)S(1)}) custom-call(s32[3]{0:T(128)S(1)} %pad_add_fusion.ids_ref, s32[2,3]{1,0:T(2,128)S(1)} %copy-done.10, f32[6,2,384]{2,1,0:T(2,128)S(1)} %reshape.91.band_ref, bf16[1024,2304]{1,0:T(8,128)(2,1)S(1)} %get-tuple-element.284.q_ref.k_ref.v_ref, ...), custom_call_target="tpu_custom_call" | custom-call | flops 3221225472 | bytes 12582912 | tf_op jit(solution)/shard_map/attention_forward/pallas_call | solution.py:260
  71.9 4.3 %collective-permute-done.19 = bf16[2,3,48,640]{3,2,1,0:T(8,128)(2,1)S(1)} collective-permute-done((bf16[2,3,48,640]{3,2,1,0:T(8,128)(2,1)S(1)}, bf16[2,3,48,640]{3,2,1,0:T(8,128)(2,1)S(1)}, u32[]{:S(2)}, u32[]{:S(2)}) %collective-permute-start.19) | collective-permute-done | bytes 368672 | tf_op jit(solution)/shard_map/ppermute | solution.py:860
  79.2 9.5 %attention_forward.5 = (bf16[1024,768]{1,0:T(8,128)(2,1)S(1)}, bf16[12,1024,128]{2,1,0:T(8,128)(2,1)S(1)}) custom-call(s32[3]{0:T(128)S(1)} %pad_add_fusion.ids_ref, s32[2,3]{1,0:T(2,128)S(1)} %copy-done.10, f32[6,2,384]{2,1,0:T(2,128)S(1)} %reshape.91.band_ref, ...), custom_call_target="tpu_custom_call", output_to_operand_aliasing={{0}: (6, {}), {1}: (7, {})} | custom-call | flops 3221225472 | bytes 12582912 | tf_op jit(solution)/shard_map/attention_forward/pallas_call | solution.py:260
  88.8 5.1 %collective-permute-done.22.refs_2_ = bf16[2,2,5,48,384]{4,3,2,1,0:T(8,128)(2,1)S(1)} collective-permute-done((bf16[2,2,5,48,384]{4,3,2,1,0:T(8,128)(2,1)S(1)}, bf16[2,2,5,48,384]{4,3,2,1,0:T(8,128)(2,1)S(1)}, u32[]{:S(2)}, u32[]{:S(2)}) %collective-permute-start.22) | collective-permute-done | bytes 737312 | tf_op jit(solution)/shard_map/ppermute | solution.py:860
  93.9 5.3 %collective-permute-done.23.refs_5_ = bf16[2,2,5,48,384]{4,3,2,1,0:T(8,128)(2,1)S(1)} collective-permute-done((bf16[2,2,5,48,384]{4,3,2,1,0:T(8,128)(2,1)S(1)}, bf16[2,2,5,48,384]{4,3,2,1,0:T(8,128)(2,1)S(1)}, u32[]{:S(2)}, u32[]{:S(2)}) %collective-permute-start.23) | collective-permute-done | bytes 737312 | tf_op jit(solution)/shard_map/ppermute | solution.py:864
  101.0 2.0 collective-permute-done.28.refs_9_
  106.3 16.7 %middle.1 = (f32[1024,768]{1,0:T(8,128)}, bf16[768,1024]{1,0:T(8,128)(2,1)}, bf16[768,1024]{1,0:T(8,128)(2,1)}, bf16[1024,768]{1,0:T(8,128)(2,1)}, bf16[1024,768...) custom-call(s32[3]{0:T(128)} %copy-done.8, f32[3,768]{1,0:T(4,128)} %gain_ref.9, ...), custom_call_target="tpu_custom_call" | custom-call | flops 4831838208 | bytes 21626880 | tf_op jit(solution)/shard_map/middle/pallas_call | solution.py:631
  123.0 3.8 collective-permute-done.31
  127.0 18.1 %attention_forward.6 = (bf16[1024,768]{1,0:T(8,128)(2,1)}, bf16[12,1024,128]{2,1,0:T(8,128)(2,1)}) custom-call(s32[3]{0:T(128)} %copy-done.8, s32[2]{0:T(128)} %bounds_ref.14, f32[6,2,384]{2,1,0:T(2,128)} %copy-done.7, bf16[1024,768]{1,0:T(8,128)(2,1)} %get-tuple-element.328.q_ref, bf16[1024,768]{1,0:T(8,128)(2,1)} %get-tuple-element.329.k_ref, ...), custom_call_target="tpu_custom_call" | custom-call | flops 10737418240 | bytes 12582912 | tf_op jit(solution)/shard_map/attention_forward/pallas_call | solution.py:260
  145.1 3.0 collective-permute-done.33.refs_5_
  148.8 5.8 %attention_forward.7 = (bf16[1024,768]{1,0:T(8,128)(2,1)}, bf16[12,1024,128]{2,1,0:T(8,128)(2,1)}) custom-call(s32[3]{0:T(128)} %copy-done.8, s32[2]{0:T(128)} %bounds_ref.14, f32[6,2,384]{2,1,0:T(2,128)} %copy-done.7, bf16[1024,768]{1,0:T(8,128)(2,1)} %get-tuple-element.328.q_ref, ...), custom_call_target="tpu_custom_call", output_to_operand_aliasing={{0}: (6, {}), {1}: (7, {})} | custom-call | flops 2147483648 | bytes 12582912 | tf_op jit(solution)/shard_map/attention_forward/pallas_call | solution.py:260
  156.2 49.9 %feed.1 = (f32[512,768]{1,0:T(8,128)}, bf16[512,768]{1,0:T(8,128)(2,1)}, f32[1024,768]{1,0:T(8,128)}, bf16[1024,768]{1,0:T(8,128)(2,1)}, f32[1,768]{1,0:T(1,128)...) custom-call(s32[3]{0:T(128)} %copy-done.8, s32[2,3]{1,0:T(2,128)} %bounds_ref.17, ...), custom_call_target="tpu_custom_call" | custom-call | flops 28991029248 | bytes 37748736 | tf_op jit(solution)/shard_map/feed/pallas_call | solution.py:740
  207.4 8.6 %cross_backward.2.rest_0_ = bf16[3,1024,768]{2,1,0:T(8,128)(2,1)} custom-call(s32[3]{0:T(128)} %copy-done.8, s32[2]{0:T(128)} %bounds_ref.14, f32[6,2,384]{2,1,0:T(2,128)} %copy-done.7, bf16[12,1024,128]{2,1,0:T(8,128)(2,1)} %get-tuple-element.344.qa_ref, bf16[1024,768]{1,0:T(8,128)(2,1)} %get-tuple-element.329.k_ref, ...), custom_call_target="tpu_custom_call" | custom-call | flops 5368709120 | bytes 15728640 | tf_op jit(solution)/shard_map/cross_backward/pallas_call | solution.py:284
  217.7 2.8 fusion.1
  222.4 28.2 %cross_backward.3.d_ref = bf16[3,1024,768]{2,1,0:T(8,128)(2,1)} custom-call(s32[3]{0:T(128)} %copy-done.8, s32[2]{0:T(128)} %bounds_ref.14, f32[6,2,384]{2,1,0:T(2,128)} %copy-done.7, bf16[12,1024,128]{2,1,0:T(8,128)(2,1)} %get-tuple-element.344.qa_ref, bf16[1024,768]{1,0:T(8,128)(2,1)} %get-tuple-element.329.k_ref, ...), custom_call_target="tpu_custom_call", output_to_operand_aliasing={{}: (8, {})} | custom-call | flops 26843545600 | bytes 15728640 | tf_op jit(solution)/shard_map/cross_backward/pallas_call | solution.py:284
  255.3 26.6 %cross_back.1 = (f32[1024,768]{1,0:T(8,128)}, bf16[1024,768]{1,0:T(8,128)(2,1)}, f32[512,768]{1,0:T(8,128)}, bf16[512,768]{1,0:T(8,128)(2,1)}, f32[1,768]{1,0:T(...) custom-call(s32[3]{0:T(128)} %copy-done.8, f32[3,768]{1,0:T(4,128)} %gain_ref.9, ...), custom_call_target="tpu_custom_call" | custom-call | flops 10871635968 | bytes 40108032 | tf_op jit(solution)/shard_map/cross_back/pallas_call | solution.py:803
  282.0 2.5 fusion.5
  284.8 8.8 %self_backward.3 = (bf16[3,1024,384]{2,1,0:T(8,128)(2,1)}, f32[6,8,128]{2,1,0:T(8,128)}, bf16[2,2,2,3,48,384]{5,4,3,2,1,0:T(8,128)(2,1)}, bf16[2,2,2,3,48,384]{5,4,3,2,1,0:T(8,128)(2,1)}) custom-call(s32[3]{0:T(128)} %copy-done.8, s32[2,3]{1,0:T(2,128)} %bounds_ref.17, f32[6,2,384]{2,1,0:T(2,128)} %copy-done.7, bf16[12,1024,128]{2,1,0:T(8,128)(2,1)} %copy-done.1, ...), custom_call_target="tpu_custom_call" | custom-call | flops 4294967296 | bytes 15728640 | tf_op jit(solution)/shard_map/self_backward/pallas_call | solution.py:318
  293.6 2.2 fusion.12
  295.8 2.2 fusion.13
  300.4 14.4 %self_backward.4 = (bf16[3,1024,384]{2,1,0:T(8,128)(2,1)}, f32[6,8,128]{2,1,0:T(8,128)}, bf16[2,2,2,3,48,384]{5,4,3,2,1,0:T(8,128)(2,1)}, bf16[2,2,2,3,48,384]{5,4,3,2,1,0:T(8,128)(2,1)}) custom-call(s32[3]{0:T(128)} %copy-done.8, s32[2,3]{1,0:T(2,128)} %bounds_ref.17, ...), custom_call_target="tpu_custom_call", output_to_operand_aliasing={{0}: (10, {}), {1}: (11, {}), {2}: (12, {}), {3}: (13, {})} | custom-call | flops 8589934592 | bytes 15728640 | tf_op jit(solution)/shard_map/self_backward/pallas_call | solution.py:318
  326.8 2.2 collective-permute-start.54
  329.0 19.3 %self_backward.5 = (bf16[3,1024,384]{2,1,0:T(8,128)(2,1)}, f32[6,8,128]{2,1,0:T(8,128)}, bf16[2,2,2,3,48,384]{5,4,3,2,1,0:T(8,128)(2,1)}, bf16[2,2,2,3,48,384]{5,4,3,2,1,0:T(8,128)(2,1)}) custom-call(s32[3]{0:T(128)} %copy-done.8, s32[2,3]{1,0:T(2,128)} %bounds_ref.17, f32[6,2,384]{2,1,0:T(2,128)} %copy-done.7, bf16[12,1024,128]{2,1,0:T(8,128)(2,1)} %copy-done.1, ...), custom_call_target="tpu_custom_call" | custom-call | flops 12884901888 | bytes 15728640 | tf_op jit(solution)/shard_map/self_backward/pallas_call | solution.py:318
  353.5 10.8 %self_back.1 = (f32[512,768]{1,0:T(8,128)}, bf16[512,768]{1,0:T(8,128)(2,1)}, f32[1,768]{1,0:T(1,128)}) custom-call(s32[3]{0:T(128)} %copy-done.8, f32[3,768]{1,0:T(4,128)} %gain_ref.9, bf16[3,1024,384]{2,1,0:T(8,128)(2,1)} %get-tuple-element.429.ours_ref, bf16[3,1024,384]{2,1,0:T(8,128)(2,1)} %get-tuple-element.430.theirs_ref, bf16[512,768]{1,0:T(8,128)(2,1)} %copy-done.6, ...), custom_call_target="tpu_custom_call" | custom-call | flops 3623878656 | bytes 19267584 | tf_op jit(solution)/shard_map/self_back/pallas_call | solution.py:844
  384.5 2.3 collective-permute-start.64
  386.8 2.1 collective-permute-done.67
  (313 shorter events, 92.8 us)
Async XLA Ops:
  6.0 23.8 %collective-permute-start.4 = (bf16[512,768]{1,0:T(8,128)(2,1)S(1)}, bf16[512,768]{1,0:T(8,128)(2,1)S(1)}, u32[]{:S(2)}, u32[]{:S(2)}) collective-permute-start(bf16[512,768]{1,0:T(8,128)(2,1)S(1)} %dynamic-slice_bitcast_fusion), channel_id=1, source_target_pairs={{0,1},{1,0},{2,3},{3,2},{4,5},{5,4},{6,7},{7,6},{8,9},{9,8},{10,11... | collective-permute-start | bytes 2359304 | tf_op jit(solution)/shard_map/ppermute | solution.py:864
  29.9 12.6 %collective-permute-start.5 = (bf16[2,2,3,48,384]{4,3,2,1,0:T(8,128)(2,1)S(1)}, bf16[2,2,3,48,384]{4,3,2,1,0:T(8,128)(2,1)S(1)}, u32[]{:S(2)}, u32[]{:S(2)}) collective-permute-start(bf16[2,2,3,48,384]{4,3,2,1,0:T(8,128)(2,1)S(1)} %pad_maximum_fusion.5), channel_id=1, source_target_pairs={{0,4},{2,6},{4,0},{6,2},{8,12},{10,14},{12,8},{14,10},{16,20},{18,... | collective-permute-start | bytes 1327112 | tf_op jit(solution)/shard_map/ppermute | solution.py:860
  56.6 15.3 %collective-permute-start.17 = (bf16[2,5,48,384]{3,2,1,0:T(8,128)(2,1)S(1)}, bf16[2,5,48,384]{3,2,1,0:T(8,128)(2,1)S(1)}, u32[]{:S(2)}, u32[]{:S(2)}) collective-permute-start(bf16[2,5,48,384]{3,2,1,0:T(8,128)(2,1)S(1)} %get-tuple-element.311.refs_0_), channel_id=1, source_target_pairs={{0,1},{1,0},{2,3},{3,2},{4,5},{5,4},{6,7},{7,6},{8,9},{9,8},{10,11... | collective-permute-start | bytes 1105928 | tf_op jit(solution)/shard_map/ppermute | solution.py:864
  57.7 14.3 %collective-permute-start.18 = (bf16[2,5,48,384]{3,2,1,0:T(8,128)(2,1)S(1)}, bf16[2,5,48,384]{3,2,1,0:T(8,128)(2,1)S(1)}, u32[]{:S(2)}, u32[]{:S(2)}) collective-permute-start(bf16[2,5,48,384]{3,2,1,0:T(8,128)(2,1)S(1)} %collective-permute-done.14.refs_3_), channel_id=1, source_target_pairs={{0,4},{2,6},{4,0},{6,2},{8,12},{10,14},{12,8},{14,10},{16,20},{18,... | collective-permute-start | bytes 1105928 | tf_op jit(solution)/shard_map/ppermute | solution.py:860
  58.2 18.0 %collective-permute-start.19 = (bf16[2,3,48,640]{3,2,1,0:T(8,128)(2,1)S(1)}, bf16[2,3,48,640]{3,2,1,0:T(8,128)(2,1)S(1)}, u32[]{:S(2)}, u32[]{:S(2)}) collective-permute-start(bf16[2,3,48,640]{3,2,1,0:T(8,128)(2,1)S(1)} %fusion.24), channel_id=1, source_target_pairs={{0,16},{2,18},{4,20},{6,22},{8,24},{10,26},{12,28},{14,30},{16,0},... | collective-permute-start | bytes 1105928 | tf_op jit(solution)/shard_map/ppermute | solution.py:860
  58.5 13.5 %collective-permute-start.20 = (bf16[2,3,48,384]{3,2,1,0:T(8,128)(2,1)S(1)}, bf16[2,3,48,384]{3,2,1,0:T(8,128)(2,1)S(1)}, u32[]{:S(2)}, u32[]{:S(2)}) collective-permute-start(bf16[2,3,48,384]{3,2,1,0:T(8,128)(2,1)S(1)} %pad_maximum_fusion.9), channel_id=1, source_target_pairs={{0,4},{2,6},{4,0},{6,2},{8,12},{10,14},{12,8},{14,10},{16,20},{18,... | collective-permute-start | bytes 663560 | tf_op jit(solution)/shard_map/ppermute | solution.py:860
  60.0 28.8 %collective-permute-start.21 = (bf16[512,768]{1,0:T(8,128)(2,1)}, bf16[512,768]{1,0:T(8,128)(2,1)S(1)}, u32[]{:S(2)}, u32[]{:S(2)}) collective-permute-start(bf16[512,768]{1,0:T(8,128)(2,1)} %dynamic-slice_bitcast_fusion.2), channel_id=1, source_target_pairs={{0,1},{1,0},{2,3},{3,2},{4,5},{5,4},{6,7},{7,6},{8,9},{9,8},{10,11... | collective-permute-start | bytes 2359304 | tf_op jit(solution)/shard_map/ppermute | solution.py:864
  76.5 17.4 %collective-permute-start.22 = (bf16[2,2,5,48,384]{4,3,2,1,0:T(8,128)(2,1)S(1)}, bf16[2,2,5,48,384]{4,3,2,1,0:T(8,128)(2,1)S(1)}, u32[]{:S(2)}, u32[]{:S(2)}) collective-permute-start(bf16[2,2,5,48,384]{4,3,2,1,0:T(8,128)(2,1)S(1)} %pad_maximum_fusion.2), channel_id=1, source_target_pairs={{0,4},{2,6},{4,0},{6,2},{8,12},{10,14},{12,8},{14,10},{16,20},{18,... | collective-permute-start | bytes 2211848 | tf_op jit(solution)/shard_map/ppermute | solution.py:860
  78.1 21.1 %collective-permute-start.23 = (bf16[2,2,5,48,384]{4,3,2,1,0:T(8,128)(2,1)S(1)}, bf16[2,2,5,48,384]{4,3,2,1,0:T(8,128)(2,1)S(1)}, u32[]{:S(2)}, u32[]{:S(2)}) collective-permute-start(bf16[2,2,5,48,384]{4,3,2,1,0:T(8,128)(2,1)S(1)} %pad_maximum_fusion.3), channel_id=1, source_target_pairs={{0,1},{1,0},{2,3},{3,2},{4,5},{5,4},{6,7},{7,6},{8,9},{9,8},{10,11... | collective-permute-start | bytes 2211848 | tf_op jit(solution)/shard_map/ppermute | solution.py:864
  79.2 20.0 %collective-permute-start.24 = (bf16[2,2,3,48,640]{4,3,2,1,0:T(8,128)(2,1)S(1)}, bf16[2,2,3,48,640]{4,3,2,1,0:T(8,128)(2,1)S(1)}, u32[]{:S(2)}, u32[]{:S(2)}) collective-permute-start(bf16[2,2,3,48,640]{4,3,2,1,0:T(8,128)(2,1)S(1)} %get-tuple-element.302), channel_id=1, source_target_pairs={{0,8},{2,10},{4,12},{6,14},{8,0},{10,2},{12,4},{14,6},{16,24},{18,... | collective-permute-start | bytes 2211848 | tf_op jit(solution)/shard_map/ppermute | solution.py:860
  79.2 21.0 %collective-permute-start.25 = (bf16[2,5,48,384]{3,2,1,0:T(8,128)(2,1)S(1)}, bf16[2,5,48,384]{3,2,1,0:T(8,128)(2,1)S(1)}, u32[]{:S(2)}, u32[]{:S(2)}) collective-permute-start(bf16[2,5,48,384]{3,2,1,0:T(8,128)(2,1)S(1)} %get-tuple-element.311.refs_0_), channel_id=1, source_target_pairs={{0,2},{2,0},{4,6},{6,4},{8,10},{10,8},{12,14},{14,12},{16,18},{18,... | collective-permute-start | bytes 1105928 | tf_op jit(solution)/shard_map/ppermute | solution.py:860
  103.0 51.6 %collective-permute-start.35 = (bf16[2,2,2,3,48,640]{5,4,3,2,1,0:T(8,128)(2,1)S(1)}, bf16[2,2,2,3,48,640]{5,4,3,2,1,0:T(8,128)(2,1)S(1)}, u32[]{:S(2)}, u32[]{:S(2)}) collective-permute-start(bf16[2,2,2,3,48,640]{5,4,3,2,1,0:T(8,128)(2,1)S(1)} %pad_maximum_fusion.refs_0_), channel_id=1, source_target_pairs={{0,2},{2,0},{4,6},{6,4},{8,10},{10,8},{12,14},{14,12},{16,18},{18,... | collective-permute-start | bytes 4423688 | tf_op jit(solution)/shard_map/ppermute | solution.py:860
  104.2 22.6 %collective-permute-start.31 = (bf16[2,2,3,48,384]{4,3,2,1,0:T(8,128)(2,1)S(1)}, bf16[2,2,3,48,384]{4,3,2,1,0:T(8,128)(2,1)S(1)}, u32[]{:S(2)}, u32[]{:S(2)}) collective-permute-start(bf16[2,2,3,48,384]{4,3,2,1,0:T(8,128)(2,1)S(1)} %get-tuple-element.325), channel_id=1, source_target_pairs={{0,16},{2,18},{4,20},{6,22},{8,24},{10,26},{12,28},{14,30},{16,0},... | collective-permute-start | bytes 1327112 | tf_op jit(solution)/shard_map/ppermute | solution.py:860
  104.5 43.6 %collective-permute-start.32 = (bf16[2,2,2,3,48,640]{5,4,3,2,1,0:T(8,128)(2,1)S(1)}, bf16[2,2,2,3,48,640]{5,4,3,2,1,0:T(8,128)(2,1)S(1)}, u32[]{:S(2)}, u32[]{:S(2)}) collective-permute-start(bf16[2,2,2,3,48,640]{5,4,3,2,1,0:T(8,128)(2,1)S(1)} %pad_maximum_fusion.refs_0_), channel_id=1, source_target_pairs={{0,4},{2,6},{4,0},{6,2},{8,12},{10,14},{12,8},{14,10},{16,20},{18,... | collective-permute-start | bytes 4423688 | tf_op jit(solution)/shard_map/ppermute | solution.py:860
  105.3 39.8 %collective-permute-start.34 = (bf16[512,768]{1,0:T(8,128)(2,1)}, bf16[512,768]{1,0:T(8,128)(2,1)}, u32[]{:S(2)}, u32[]{:S(2)}) collective-permute-start(bf16[512,768]{1,0:T(8,128)(2,1)} %dynamic-slice_bitcast_fusion.1), channel_id=1, source_target_pairs={{0,1},{1,0},{2,3},{3,2},{4,5},{5,4},{6,7},{7,6},{8,9},{9,8},{10,11... | collective-permute-start | bytes 2359304 | tf_op jit(solution)/shard_map/ppermute | solution.py:864
  126.9 21.2 %collective-permute-start.33 = (bf16[2,2,2,3,48,384]{5,4,3,2,1,0:T(8,128)(2,1)S(1)}, bf16[2,2,2,3,48,384]{5,4,3,2,1,0:T(8,128)(2,1)S(1)}, u32[]{:S(2)}, u32[]{:S(2)}) collective-permute-start(bf16[2,2,2,3,48,384]{5,4,3,2,1,0:T(8,128)(2,1)S(1)} %pad_maximum_fusion.1.refs_4_), channel_id=1, source_target_pairs={{0,8},{2,10},{4,12},{6,14},{8,0},{10,2},{12,4},{14,6},{16,24},{18,... | collective-permute-start | bytes 2654216 | tf_op jit(solution)/shard_map/ppermute | solution.py:860
  206.7 48.6 %collective-permute-start.42 = (bf16[512,768]{1,0:T(8,128)(2,1)}, bf16[512,768]{1,0:T(8,128)(2,1)}, u32[]{:S(2)}, u32[]{:S(2)}) collective-permute-start(bf16[512,768]{1,0:T(8,128)(2,1)} %get-tuple-element.361), channel_id=1, source_target_pairs={{0,1},{1,0},{2,3},{3,2},{4,5},{5,4},{6,7},{7,6},{8,9},{9,8},{10,11... | collective-permute-start | bytes 2359304 | tf_op jit(solution)/shard_map/ppermute | solution.py:864
  220.5 30.0 %collective-permute-start.40 = (bf16[2,2,3,48,1024]{4,3,2,1,0:T(8,128)(2,1)}, bf16[2,2,3,48,1024]{4,3,2,1,0:T(8,128)(2,1)S(1)}, u32[]{:S(2)}, u32[]{:S(2)}) collective-permute-start(bf16[2,2,3,48,1024]{4,3,2,1,0:T(8,128)(2,1)} %fusion.1), channel_id=1, source_target_pairs={{0,4},{2,6},{4,0},{6,2},{8,12},{10,14},{12,8},{14,10},{16,20},{18,... | collective-permute-start | bytes 3538952 | tf_op jit(solution)/shard_map/ppermute | solution.py:860
  221.1 30.6 %collective-permute-start.41 = (bf16[2,2,3,48,1024]{4,3,2,1,0:T(8,128)(2,1)S(1)}, bf16[2,2,3,48,1024]{4,3,2,1,0:T(8,128)(2,1)S(1)}, u32[]{:S(2)}, u32[]{:S(2)}) collective-permute-start(bf16[2,2,3,48,1024]{4,3,2,1,0:T(8,128)(2,1)S(1)} %fusion), channel_id=1, source_target_pairs={{0,1},{1,0},{2,3},{3,2},{4,5},{5,4},{6,7},{7,6},{8,9},{9,8},{10,11... | collective-permute-start | bytes 3538952 | tf_op jit(solution)/shard_map/ppermute | solution.py:864
  253.7 28.2 %collective-permute-start.43 = (bf16[2,3,48,1024]{3,2,1,0:T(8,128)(2,1)S(1)}, bf16[2,3,48,1024]{3,2,1,0:T(8,128)(2,1)S(1)}, u32[]{:S(2)}, u32[]{:S(2)}) collective-permute-start(bf16[2,3,48,1024]{3,2,1,0:T(8,128)(2,1)S(1)} %get-tuple-element.372), channel_id=1, source_target_pairs={{0,1},{1,0},{2,3},{3,2},{4,5},{5,4},{6,7},{7,6},{8,9},{9,8},{10,11... | collective-permute-start | bytes 1769480 | tf_op jit(solution)/shard_map/ppermute | solution.py:864
  254.5 27.5 %collective-permute-start.44 = (bf16[2,3,48,1024]{3,2,1,0:T(8,128)(2,1)S(1)}, bf16[2,3,48,1024]{3,2,1,0:T(8,128)(2,1)S(1)}, u32[]{:S(2)}, u32[]{:S(2)}) collective-permute-start(bf16[2,3,48,1024]{3,2,1,0:T(8,128)(2,1)S(1)} %get-tuple-element.373), channel_id=1, source_target_pairs={{0,4},{2,6},{4,0},{6,2},{8,12},{10,14},{12,8},{14,10},{16,20},{18,... | collective-permute-start | bytes 1769480 | tf_op jit(solution)/shard_map/ppermute | solution.py:860
  284.5 30.3 %collective-permute-start.48 = (bf16[2,3,48,1024]{3,2,1,0:T(8,128)(2,1)}, bf16[2,3,48,1024]{3,2,1,0:T(8,128)(2,1)}, u32[]{:S(2)}, u32[]{:S(2)}) collective-permute-start(bf16[2,3,48,1024]{3,2,1,0:T(8,128)(2,1)} %fusion.5), channel_id=1, source_target_pairs={{0,8},{2,10},{4,12},{6,14},{8,0},{10,2},{12,4},{14,6},{16,24},{18,... | collective-permute-start | bytes 1769480 | tf_op jit(solution)/shard_map/ppermute | solution.py:860
  298.0 18.8 %collective-permute-start.46 = (bf16[2,2,5,48,384]{4,3,2,1,0:T(8,128)(2,1)}, bf16[2,2,5,48,384]{4,3,2,1,0:T(8,128)(2,1)S(1)}, u32[]{:S(2)}, u32[]{:S(2)}) collective-permute-start(bf16[2,2,5,48,384]{4,3,2,1,0:T(8,128)(2,1)} %fusion.13), channel_id=1, source_target_pairs={{0,4},{2,6},{4,0},{6,2},{8,12},{10,14},{12,8},{14,10},{16,20},{18,... | collective-permute-start | bytes 2211848 | tf_op jit(solution)/shard_map/ppermute | solution.py:860
  299.1 18.5 %collective-permute-start.47 = (bf16[2,2,5,48,384]{4,3,2,1,0:T(8,128)(2,1)}, bf16[2,2,5,48,384]{4,3,2,1,0:T(8,128)(2,1)S(1)}, u32[]{:S(2)}, u32[]{:S(2)}) collective-permute-start(bf16[2,2,5,48,384]{4,3,2,1,0:T(8,128)(2,1)} %fusion.12), channel_id=1, source_target_pairs={{0,1},{1,0},{2,3},{3,2},{4,5},{5,4},{6,7},{7,6},{8,9},{9,8},{10,11... | collective-permute-start | bytes 2211848 | tf_op jit(solution)/shard_map/ppermute | solution.py:864
  318.5 29.8 %collective-permute-start.53 = (bf16[512,768]{1,0:T(8,128)(2,1)}, bf16[512,768]{1,0:T(8,128)(2,1)S(1)}, u32[]{:S(2)}, u32[]{:S(2)}) collective-permute-start(bf16[512,768]{1,0:T(8,128)(2,1)} %get-tuple-element.417), channel_id=1, source_target_pairs={{0,1},{1,0},{2,3},{3,2},{4,5},{5,4},{6,7},{7,6},{8,9},{9,8},{10,11... | collective-permute-start | bytes 2359304 | tf_op jit(solution)/shard_map/ppermute | solution.py:864
  323.9 24.4 %collective-permute-start.52 = (bf16[2,2,3,48,384]{4,3,2,1,0:T(8,128)(2,1)S(1)}, bf16[2,2,3,48,384]{4,3,2,1,0:T(8,128)(2,1)S(1)}, u32[]{:S(2)}, u32[]{:S(2)}) collective-permute-start(bf16[2,2,3,48,384]{4,3,2,1,0:T(8,128)(2,1)S(1)} %fusion.21), channel_id=1, source_target_pairs={{0,4},{2,6},{4,0},{6,2},{8,12},{10,14},{12,8},{14,10},{16,20},{18,... | collective-permute-start | bytes 1327112 | tf_op jit(solution)/shard_map/ppermute | solution.py:860
  324.8 23.5 %collective-permute-start.50 = (bf16[2,5,48,384]{3,2,1,0:T(8,128)(2,1)S(1)}, bf16[2,5,48,384]{3,2,1,0:T(8,128)(2,1)S(1)}, u32[]{:S(2)}, u32[]{:S(2)}) collective-permute-start(bf16[2,5,48,384]{3,2,1,0:T(8,128)(2,1)S(1)} %get-tuple-element.414), channel_id=1, source_target_pairs={{0,1},{1,0},{2,3},{3,2},{4,5},{5,4},{6,7},{7,6},{8,9},{9,8},{10,11... | collective-permute-start | bytes 1105928 | tf_op jit(solution)/shard_map/ppermute | solution.py:864
  325.6 22.8 %collective-permute-start.51 = (bf16[2,5,48,384]{3,2,1,0:T(8,128)(2,1)S(1)}, bf16[2,5,48,384]{3,2,1,0:T(8,128)(2,1)S(1)}, u32[]{:S(2)}, u32[]{:S(2)}) collective-permute-start(bf16[2,5,48,384]{3,2,1,0:T(8,128)(2,1)S(1)} %get-tuple-element.415), channel_id=1, source_target_pairs={{0,4},{2,6},{4,0},{6,2},{8,12},{10,14},{12,8},{14,10},{16,20},{18,... | collective-permute-start | bytes 1105928 | tf_op jit(solution)/shard_map/ppermute | solution.py:860
  326.8 21.6 %collective-permute-start.54 = (bf16[3,48,1024]{2,1,0:T(8,128)(2,1)S(1)}, bf16[3,48,1024]{2,1,0:T(8,128)(2,1)S(1)}, u32[]{:S(2)}, u32[]{:S(2)}) collective-permute-start(bf16[3,48,1024]{2,1,0:T(8,128)(2,1)S(1)} %fusion.26), channel_id=1, source_target_pairs={{0,16},{2,18},{4,20},{6,22},{8,24},{10,26},{12,28},{14,30},{16,0},... | collective-permute-start | bytes 884744 | tf_op jit(solution)/shard_map/ppermute | solution.py:860
  351.3 13.0 %collective-permute-start.57 = (bf16[2,2,3,48,384]{4,3,2,1,0:T(8,128)(2,1)S(1)}, bf16[2,2,3,48,384]{4,3,2,1,0:T(8,128)(2,1)S(1)}, u32[]{:S(2)}, u32[]{:S(2)}) collective-permute-start(bf16[2,2,3,48,384]{4,3,2,1,0:T(8,128)(2,1)S(1)} %fusion.22), channel_id=1, source_target_pairs={{0,4},{2,6},{4,0},{6,2},{8,12},{10,14},{12,8},{14,10},{16,20},{18,... | collective-permute-start | bytes 1327112 | tf_op jit(solution)/shard_map/ppermute | solution.py:860
  368.7 12.7 %collective-permute-start.63 = (bf16[5,48,384]{2,1,0:T(8,128)(2,1)}, bf16[5,48,384]{2,1,0:T(8,128)(2,1)S(1)}, u32[]{:S(2)}, u32[]{:S(2)}) collective-permute-start(bf16[5,48,384]{2,1,0:T(8,128)(2,1)} %fusion.29), channel_id=1, source_target_pairs={{0,16},{2,18},{4,20},{6,22},{8,24},{10,26},{12,28},{14,30},{16,0},... | collective-permute-start | bytes 552968 | tf_op jit(solution)/shard_map/ppermute | solution.py:860
  369.7 19.9 %collective-permute-start.65 = (bf16[512,768]{1,0:T(8,128)(2,1)}, bf16[512,768]{1,0:T(8,128)(2,1)S(1)}, u32[]{:S(2)}, u32[]{:S(2)}) collective-permute-start(bf16[512,768]{1,0:T(8,128)(2,1)} %get-tuple-element.467), channel_id=1, source_target_pairs={{0,1},{1,0},{2,3},{3,2},{4,5},{5,4},{6,7},{7,6},{8,9},{9,8},{10,11... | collective-permute-start | bytes 2359304 | tf_op jit(solution)/shard_map/ppermute | solution.py:864
  (98 other events, 1011.2 us)

commit v6 on v5

--- a/solution.py
+++ b/solution.py
@@ -17,8 +17,8 @@
 BF = jnp.bfloat16
 F32 = jnp.float32
 SELF_FORWARD_MB = 20
-CROSS_FORWARD_MB = 56
-BACKWARD_MB = 56
+CROSS_FORWARD_MB = 48
+BACKWARD_MB = 48
 PROJECT_MB = 20
 MIDDLE_MB = 56
 FEED_MB = 60

time: 398 us -> 398 us (level)
  other arithmetic: 30.6 us -> 25 us
  local copies, waits for them, and re-layouts: 14.3 us -> 19.9 us
  waiting for transfers between devices: 60.8 us -> 65.3 us
  Pallas kernels: 233 us -> 229 us
    unnamed x124 -> x148, local copies, waits for them, and re-layouts: 5.01 us -> 10.3 us
  transfers between devices with their start and end apart: 68 -> 68, of which waited for: 25 -> 27; matrix products, arithmetic and copies ran while one was open for 9% -> 7% of each run, Pallas kernels for 46% -> 45%
where the time goes in v6:
time: 398 us; the launch traced here: 395 us
  Pallas kernels  229 us (58%)
  waiting for transfers between devices  65.3 us (16%)
  starting transfers between devices  53.4 us (13%)
  other arithmetic  25 us (6%)
  local copies, waits for them, and re-layouts  19.9 us (5%)
    pallas_call x1, Pallas kernels, feed(): call(functools.partial(feed_kernel, blocks, len(pieces), packed), 'feed',...  50.2 us
    ppermute x50, waiting for transfers between devices, flip_bit(): return lax.ppermute(values, 'dp', [(i, i ^ 1 << bit) for i in range(size)])  46 us
    pallas_call x4, Pallas kernels, attention_forward(): call(functools.partial(forward_kernel, causal, len(into)), 'attention_for...  42.7 us
    pallas_call x3, Pallas kernels, self_backward(): call(functools.partial(backward_kernel, True, packed, len(into)), 'self_b...  39.6 us
    pallas_call x2, Pallas kernels, cross_backward(): call(functools.partial(backward_kernel, False, False, 0), 'cross_backward...  36.2 us
    ppermute x50, starting transfers between devices, flip_bit(): return lax.ppermute(values, 'dp', [(i, i ^ 1 << bit) for i in range(size)])  33.9 us
    pallas_call x1, Pallas kernels, cross_back(): call(functools.partial(cross_back_kernel, blocks, packed), 'cross_back',...  26.6 us
    ppermute x18, starting transfers between devices, flip_mp(): return lax.ppermute(values, 'mp', [(0, 1), (1, 0)])  19.5 us
  transfers between devices with their start and end apart: 68, of which 27 were waited for; matrix products, arithmetic and copies ran while one was open for 7% of the time, Pallas kernels for 45%

profile of v6, /device:TPU:0, one launch (start us, length us, event | category | flops | bytes accessed | tf_op | source)
XLA Modules:
  0.0 395.2 jit_solution(13662199193583518050)
XLA Ops:
  0.7 4.1 %collective-permute-start = (bf16[3,48,384]{2,1,0:T(8,128)(2,1)}, bf16[3,48,384]{2,1,0:T(8,128)(2,1)S(1)}, u32[]{:S(2)}, u32[]{:S(2)}) collective-permute-start(bf16[3,48,384]{2,1,0:T(8,128)(2,1)} %param.24), channel_id=1, source_target_pairs={{0,16},{2,18},{4,20},{6,22},{8,24},{10,26},{12,28},{14,30},{16,0},... | collective-permute-start | bytes 331784 | tf_op jit(solution)/shard_map/ppermute | solution.py:860
  12.6 4.6 %collective-permute-done.1.refs_3_ = bf16[2,3,48,384]{3,2,1,0:T(8,128)(2,1)S(1)} collective-permute-done((bf16[2,3,48,384]{3,2,1,0:T(8,128)(2,1)S(1)}, bf16[2,3,48,384]{3,2,1,0:T(8,128)(2,1)S(1)}, u32[]{:S(2)}, u32[]{:S(2)}) %collective-permute-start.1) | collective-permute-done | bytes 221216 | tf_op jit(solution)/shard_map/ppermute | solution.py:860
  20.0 9.8 %collective-permute-done.2.refs_1_ = bf16[2,3,48,384]{3,2,1,0:T(8,128)(2,1)S(1)} collective-permute-done((bf16[2,3,48,384]{3,2,1,0:T(8,128)(2,1)S(1)}, bf16[2,3,48,384]{3,2,1,0:T(8,128)(2,1)S(1)}, u32[]{:S(2)}, u32[]{:S(2)}) %collective-permute-start.2) | collective-permute-done | bytes 221216 | tf_op jit(solution)/shard_map/ppermute | solution.py:864
  33.4 9.1 %collective-permute-done.7 = bf16[5,48,384]{2,1,0:T(8,128)(2,1)S(1)} collective-permute-done((bf16[5,48,384]{2,1,0:T(8,128)(2,1)S(1)}, bf16[5,48,384]{2,1,0:T(8,128)(2,1)S(1)}, u32[]{:S(2)}, u32[]{:S(2)}) %collective-permute-start.7) | collective-permute-done | bytes 184352 | tf_op jit(solution)/shard_map/ppermute | solution.py:860
  49.1 6.6 %project.1 = (bf16[768,1024]{1,0:T(8,128)(2,1)S(1)}, bf16[1024,2304]{1,0:T(8,128)(2,1)S(1)}, bf16[3,768,768]{2,1,0:T(8,128)(2,1)S(1)}) custom-call(s32[3]{0:T(128)S(1)} %pad_add_fusion.ids_ref, f32[3,768]{1,0:T(4,128)S(1)} %copy-done.18, bf16[512,768]{1,0:T(8,128)(2,1)S(1)} %collective-permute-done.4.came_ref, bf16[2,512,768]{2,1,0:T(8,128)(2,1)S(1)} %copy-done.5, ...), custom_call_target="tpu_custom_call" | custom-call | flops 3623878656 | bytes 11403264 | tf_op jit(solution)/shard_map/project/pallas_call | solution.py:590
  60.9 9.5 %attention_forward.4 = (bf16[1024,768]{1,0:T(8,128)(2,1)S(1)}, bf16[12,1024,128]{2,1,0:T(8,128)(2,1)S(1)}) custom-call(s32[3]{0:T(128)S(1)} %pad_add_fusion.ids_ref, s32[2,3]{1,0:T(2,128)S(1)} %copy-done.19, f32[6,2,384]{2,1,0:T(2,128)S(1)} %reshape.91.band_ref, bf16[1024,2304]{1,0:T(8,128)(2,1)S(1)} %get-tuple-element.284.q_ref.k_ref.v_ref, ...), custom_call_target="tpu_custom_call" | custom-call | flops 3221225472 | bytes 12582912 | tf_op jit(solution)/shard_map/attention_forward/pallas_call | solution.py:260
  72.0 4.3 %collective-permute-done.19 = bf16[2,3,48,640]{3,2,1,0:T(8,128)(2,1)S(1)} collective-permute-done((bf16[2,3,48,640]{3,2,1,0:T(8,128)(2,1)S(1)}, bf16[2,3,48,640]{3,2,1,0:T(8,128)(2,1)S(1)}, u32[]{:S(2)}, u32[]{:S(2)}) %collective-permute-start.19) | collective-permute-done | bytes 368672 | tf_op jit(solution)/shard_map/ppermute | solution.py:860
  79.2 9.5 %attention_forward.5 = (bf16[1024,768]{1,0:T(8,128)(2,1)S(1)}, bf16[12,1024,128]{2,1,0:T(8,128)(2,1)S(1)}) custom-call(s32[3]{0:T(128)S(1)} %pad_add_fusion.ids_ref, s32[2,3]{1,0:T(2,128)S(1)} %copy-done.19, f32[6,2,384]{2,1,0:T(2,128)S(1)} %reshape.91.band_ref, ...), custom_call_target="tpu_custom_call", output_to_operand_aliasing={{0}: (6, {}), {1}: (7, {})} | custom-call | flops 3221225472 | bytes 12582912 | tf_op jit(solution)/shard_map/attention_forward/pallas_call | solution.py:260
  88.8 5.2 %collective-permute-done.22.refs_2_ = bf16[2,2,5,48,384]{4,3,2,1,0:T(8,128)(2,1)S(1)} collective-permute-done((bf16[2,2,5,48,384]{4,3,2,1,0:T(8,128)(2,1)S(1)}, bf16[2,2,5,48,384]{4,3,2,1,0:T(8,128)(2,1)S(1)}, u32[]{:S(2)}, u32[]{:S(2)}) %collective-permute-start.22) | collective-permute-done | bytes 737312 | tf_op jit(solution)/shard_map/ppermute | solution.py:860
  93.9 5.3 %collective-permute-done.23.refs_5_ = bf16[2,2,5,48,384]{4,3,2,1,0:T(8,128)(2,1)S(1)} collective-permute-done((bf16[2,2,5,48,384]{4,3,2,1,0:T(8,128)(2,1)S(1)}, bf16[2,2,5,48,384]{4,3,2,1,0:T(8,128)(2,1)S(1)}, u32[]{:S(2)}, u32[]{:S(2)}) %collective-permute-start.23) | collective-permute-done | bytes 737312 | tf_op jit(solution)/shard_map/ppermute | solution.py:864
  101.2 1.8 collective-permute-done.28.refs_9_
  106.8 16.6 %middle.1 = (f32[1024,768]{1,0:T(8,128)}, bf16[768,1024]{1,0:T(8,128)(2,1)}, bf16[768,1024]{1,0:T(8,128)(2,1)}, bf16[1024,768]{1,0:T(8,128)(2,1)}, bf16[1024,768...) custom-call(s32[3]{0:T(128)} %copy-done.14, f32[3,768]{1,0:T(4,128)} %gain_ref.9, ...), custom_call_target="tpu_custom_call" | custom-call | flops 4831838208 | bytes 21626880 | tf_op jit(solution)/shard_map/middle/pallas_call | solution.py:631
  123.5 3.4 collective-permute-done.31
  128.7 18.2 %attention_forward.6 = (bf16[1024,768]{1,0:T(8,128)(2,1)S(1)}, bf16[12,1024,128]{2,1,0:T(8,128)(2,1)}) custom-call(s32[3]{0:T(128)S(1)} %copy-done.15, s32[2]{0:T(128)S(1)} %copy-done.21, f32[6,2,384]{2,1,0:T(2,128)S(1)} %reshape.91.band_ref, bf16[1024,768]{1,0:T(8,128)(2,1)S(1)} %copy-done.10, bf16[1024,768]{1,0:T(8,128)(2,1)S(1)} %copy-done.8, ...), custom_call_target="tpu_custom_call" | custom-call | flops 10737418240 | bytes 12582912 | tf_op jit(solution)/shard_map/attention_forward/pallas_call | solution.py:260
  148.8 5.6 %attention_forward.7 = (bf16[1024,768]{1,0:T(8,128)(2,1)S(1)}, bf16[12,1024,128]{2,1,0:T(8,128)(2,1)}) custom-call(s32[3]{0:T(128)S(1)} %copy-done.15, s32[2]{0:T(128)S(1)} %copy-done.21, f32[6,2,384]{2,1,0:T(2,128)S(1)} %reshape.91.band_ref, bf16[1024,768]{1,0:T(8,128)(2,1)S(1)} %copy-done.10, ...), custom_call_target="tpu_custom_call", output_to_operand_aliasing={{0}: (6, {}), {1}: (7, {})} | custom-call | flops 2147483648 | bytes 12582912 | tf_op jit(solution)/shard_map/attention_forward/pallas_call | solution.py:260
  157.4 50.2 %feed.1 = (f32[512,768]{1,0:T(8,128)}, bf16[512,768]{1,0:T(8,128)(2,1)}, f32[1024,768]{1,0:T(8,128)}, bf16[1024,768]{1,0:T(8,128)(2,1)}, f32[1,768]{1,0:T(1,128)...) custom-call(s32[3]{0:T(128)} %copy-done.14, s32[2,3]{1,0:T(2,128)} %bounds_ref.17, ...), custom_call_target="tpu_custom_call" | custom-call | flops 28991029248 | bytes 37748736 | tf_op jit(solution)/shard_map/feed/pallas_call | solution.py:740
  210.1 7.9 %cross_backward.2.rest_0_ = bf16[3,1024,768]{2,1,0:T(8,128)(2,1)} custom-call(s32[3]{0:T(128)S(1)} %copy-done.16, s32[2]{0:T(128)S(1)} %copy-done.21, f32[6,2,384]{2,1,0:T(2,128)S(1)} %reshape.91.band_ref, bf16[12,1024,128]{2,1,0:T(8,128)(2,1)} %get-tuple-element.344.qa_ref, bf16[1024,768]{1,0:T(8,128)(2,1)S(1)} %copy-done.8, ...), custom_call_target="tpu_custom_call" | custom-call | flops 5368709120 | bytes 15728640 | tf_op jit(solution)/shard_map/cross_backward/pallas_call | solution.py:284
  218.1 1.8 fusion
  223.3 28.2 %cross_backward.3.d_ref = bf16[3,1024,768]{2,1,0:T(8,128)(2,1)} custom-call(s32[3]{0:T(128)S(1)} %copy-done.16, s32[2]{0:T(128)S(1)} %copy-done.21, f32[6,2,384]{2,1,0:T(2,128)S(1)} %reshape.91.band_ref, bf16[12,1024,128]{2,1,0:T(8,128)(2,1)} %get-tuple-element.344.qa_ref, bf16[1024,768]{1,0:T(8,128)(2,1)S(1)} %copy-done.8, ...), custom_call_target="tpu_custom_call", output_to_operand_aliasing={{}: (8, {})} | custom-call | flops 26843545600 | bytes 15728640 | tf_op jit(solution)/shard_map/cross_backward/pallas_call | solution.py:284
  253.2 1.8 fusion.6
  256.3 26.6 %cross_back.1 = (f32[1024,768]{1,0:T(8,128)}, bf16[1024,768]{1,0:T(8,128)(2,1)}, f32[512,768]{1,0:T(8,128)}, bf16[512,768]{1,0:T(8,128)(2,1)}, f32[1,768]{1,0:T(...) custom-call(s32[3]{0:T(128)} %copy-done.14, f32[3,768]{1,0:T(4,128)} %gain_ref.9, ...), custom_call_target="tpu_custom_call" | custom-call | flops 10871635968 | bytes 40108032 | tf_op jit(solution)/shard_map/cross_back/pallas_call | solution.py:803
  283.0 2.9 fusion.5
  288.9 7.8 %self_backward.3 = (bf16[3,1024,384]{2,1,0:T(8,128)(2,1)}, f32[6,8,128]{2,1,0:T(8,128)S(1)}, bf16[2,2,2,3,48,384]{5,4,3,2,1,0:T(8,128)(2,1)S(1)}, bf16[2,2,2,3,48,384]{5,4,3,2,1,0:T(8,128)(2,1)S(1)}) custom-call(s32[3]{0:T(128)S(1)} %copy-done.17, s32[2,3]{1,0:T(2,128)S(1)} %copy-done.20, f32[6,2,384]{2,1,0:T(2,128)S(1)} %reshape.91.band_ref, ...), custom_call_target="tpu_custom_call" | custom-call | flops 4294967296 | bytes 15728640 | tf_op jit(solution)/shard_map/self_backward/pallas_call | solution.py:318
  299.8 13.4 %self_backward.4 = (bf16[3,1024,384]{2,1,0:T(8,128)(2,1)}, f32[6,8,128]{2,1,0:T(8,128)S(1)}, bf16[2,2,2,3,48,384]{5,4,3,2,1,0:T(8,128)(2,1)S(1)}, bf16[2,2,2,3,48,384]{5,4,3,2,1,0:T(8,128)(2,1)S(1)}) custom-call(s32[3]{0:T(128)S(1)} %copy-done.17, ...), custom_call_target="tpu_custom_call", output_to_operand_aliasing={{0}: (10, {}), {1}: (11, {}), {2}: (12, {}), {3}: (13, {})} | custom-call | flops 8589934592 | bytes 15728640 | tf_op jit(solution)/shard_map/self_backward/pallas_call | solution.py:318
  313.2 2.7 collective-permute-done.46
  318.1 2.0 fusion.3
  326.4 18.4 %self_backward.5 = (bf16[3,1024,384]{2,1,0:T(8,128)(2,1)}, f32[6,8,128]{2,1,0:T(8,128)S(1)}, bf16[2,2,2,3,48,384]{5,4,3,2,1,0:T(8,128)(2,1)S(1)}, bf16[2,2,2,3,48,384]{5,4,3,2,1,0:T(8,128)(2,1)S(1)}) custom-call(s32[3]{0:T(128)S(1)} %copy-done.17, s32[2,3]{1,0:T(2,128)S(1)} %copy-done.20, f32[6,2,384]{2,1,0:T(2,128)S(1)} %reshape.91.band_ref, ...), custom_call_target="tpu_custom_call" | custom-call | flops 12884901888 | bytes 15728640 | tf_op jit(solution)/shard_map/self_backward/pallas_call | solution.py:318
  350.3 10.8 %self_back.1 = (f32[512,768]{1,0:T(8,128)}, bf16[512,768]{1,0:T(8,128)(2,1)}, f32[1,768]{1,0:T(1,128)}) custom-call(s32[3]{0:T(128)} %copy-done.14, f32[3,768]{1,0:T(4,128)} %gain_ref.9, bf16[3,1024,384]{2,1,0:T(8,128)(2,1)} %get-tuple-element.429.ours_ref, bf16[3,1024,384]{2,1,0:T(8,128)(2,1)} %get-tuple-element.430.theirs_ref, ...), custom_call_target="tpu_custom_call" | custom-call | flops 3623878656 | bytes 19267584 | tf_op jit(solution)/shard_map/self_back/pallas_call | solution.py:844
  373.3 1.9 maximum_select_fusion.1
  375.4 1.9 maximum_select_fusion
  380.0 2.9 collective-permute-done.62
  391.0 1.9 maximum_select_fusion.2
  (337 shorter events, 96.6 us)
Async XLA Ops:
  6.0 23.8 %collective-permute-start.4 = (bf16[512,768]{1,0:T(8,128)(2,1)S(1)}, bf16[512,768]{1,0:T(8,128)(2,1)S(1)}, u32[]{:S(2)}, u32[]{:S(2)}) collective-permute-start(bf16[512,768]{1,0:T(8,128)(2,1)S(1)} %dynamic-slice_bitcast_fusion), channel_id=1, source_target_pairs={{0,1},{1,0},{2,3},{3,2},{4,5},{5,4},{6,7},{7,6},{8,9},{9,8},{10,11... | collective-permute-start | bytes 2359304 | tf_op jit(solution)/shard_map/ppermute | solution.py:864
  56.7 15.3 %collective-permute-start.17 = (bf16[2,5,48,384]{3,2,1,0:T(8,128)(2,1)S(1)}, bf16[2,5,48,384]{3,2,1,0:T(8,128)(2,1)S(1)}, u32[]{:S(2)}, u32[]{:S(2)}) collective-permute-start(bf16[2,5,48,384]{3,2,1,0:T(8,128)(2,1)S(1)} %get-tuple-element.311.refs_0_), channel_id=1, source_target_pairs={{0,1},{1,0},{2,3},{3,2},{4,5},{5,4},{6,7},{7,6},{8,9},{9,8},{10,11... | collective-permute-start | bytes 1105928 | tf_op jit(solution)/shard_map/ppermute | solution.py:864
  57.7 14.3 %collective-permute-start.18 = (bf16[2,5,48,384]{3,2,1,0:T(8,128)(2,1)S(1)}, bf16[2,5,48,384]{3,2,1,0:T(8,128)(2,1)S(1)}, u32[]{:S(2)}, u32[]{:S(2)}) collective-permute-start(bf16[2,5,48,384]{3,2,1,0:T(8,128)(2,1)S(1)} %collective-permute-done.14.refs_3_), channel_id=1, source_target_pairs={{0,4},{2,6},{4,0},{6,2},{8,12},{10,14},{12,8},{14,10},{16,20},{18,... | collective-permute-start | bytes 1105928 | tf_op jit(solution)/shard_map/ppermute | solution.py:860
  58.2 18.0 %collective-permute-start.19 = (bf16[2,3,48,640]{3,2,1,0:T(8,128)(2,1)S(1)}, bf16[2,3,48,640]{3,2,1,0:T(8,128)(2,1)S(1)}, u32[]{:S(2)}, u32[]{:S(2)}) collective-permute-start(bf16[2,3,48,640]{3,2,1,0:T(8,128)(2,1)S(1)} %fusion.24), channel_id=1, source_target_pairs={{0,16},{2,18},{4,20},{6,22},{8,24},{10,26},{12,28},{14,30},{16,0},... | collective-permute-start | bytes 1105928 | tf_op jit(solution)/shard_map/ppermute | solution.py:860
  58.5 13.4 %collective-permute-start.20 = (bf16[2,3,48,384]{3,2,1,0:T(8,128)(2,1)S(1)}, bf16[2,3,48,384]{3,2,1,0:T(8,128)(2,1)S(1)}, u32[]{:S(2)}, u32[]{:S(2)}) collective-permute-start(bf16[2,3,48,384]{3,2,1,0:T(8,128)(2,1)S(1)} %pad_maximum_fusion.9), channel_id=1, source_target_pairs={{0,4},{2,6},{4,0},{6,2},{8,12},{10,14},{12,8},{14,10},{16,20},{18,... | collective-permute-start | bytes 663560 | tf_op jit(solution)/shard_map/ppermute | solution.py:860
  60.1 28.7 %collective-permute-start.21 = (bf16[512,768]{1,0:T(8,128)(2,1)S(1)}, bf16[512,768]{1,0:T(8,128)(2,1)S(1)}, u32[]{:S(2)}, u32[]{:S(2)}) collective-permute-start(bf16[512,768]{1,0:T(8,128)(2,1)S(1)} %dynamic-slice_bitcast_fusion.2), channel_id=1, source_target_pairs={{0,1},{1,0},{2,3},{3,2},{4,5},{5,4},{6,7},{7,6},{8,9},{9,8},{10,11... | collective-permute-start | bytes 2359304 | tf_op jit(solution)/shard_map/ppermute | solution.py:864
  76.5 17.4 %collective-permute-start.22 = (bf16[2,2,5,48,384]{4,3,2,1,0:T(8,128)(2,1)S(1)}, bf16[2,2,5,48,384]{4,3,2,1,0:T(8,128)(2,1)S(1)}, u32[]{:S(2)}, u32[]{:S(2)}) collective-permute-start(bf16[2,2,5,48,384]{4,3,2,1,0:T(8,128)(2,1)S(1)} %pad_maximum_fusion.2), channel_id=1, source_target_pairs={{0,4},{2,6},{4,0},{6,2},{8,12},{10,14},{12,8},{14,10},{16,20},{18,... | collective-permute-start | bytes 2211848 | tf_op jit(solution)/shard_map/ppermute | solution.py:860
  78.1 21.1 %collective-permute-start.23 = (bf16[2,2,5,48,384]{4,3,2,1,0:T(8,128)(2,1)S(1)}, bf16[2,2,5,48,384]{4,3,2,1,0:T(8,128)(2,1)S(1)}, u32[]{:S(2)}, u32[]{:S(2)}) collective-permute-start(bf16[2,2,5,48,384]{4,3,2,1,0:T(8,128)(2,1)S(1)} %pad_maximum_fusion.3), channel_id=1, source_target_pairs={{0,1},{1,0},{2,3},{3,2},{4,5},{5,4},{6,7},{7,6},{8,9},{9,8},{10,11... | collective-permute-start | bytes 2211848 | tf_op jit(solution)/shard_map/ppermute | solution.py:864
  79.2 20.0 %collective-permute-start.24 = (bf16[2,2,3,48,640]{4,3,2,1,0:T(8,128)(2,1)S(1)}, bf16[2,2,3,48,640]{4,3,2,1,0:T(8,128)(2,1)S(1)}, u32[]{:S(2)}, u32[]{:S(2)}) collective-permute-start(bf16[2,2,3,48,640]{4,3,2,1,0:T(8,128)(2,1)S(1)} %get-tuple-element.302), channel_id=1, source_target_pairs={{0,8},{2,10},{4,12},{6,14},{8,0},{10,2},{12,4},{14,6},{16,24},{18,... | collective-permute-start | bytes 2211848 | tf_op jit(solution)/shard_map/ppermute | solution.py:860
  79.2 21.0 %collective-permute-start.25 = (bf16[2,5,48,384]{3,2,1,0:T(8,128)(2,1)S(1)}, bf16[2,5,48,384]{3,2,1,0:T(8,128)(2,1)S(1)}, u32[]{:S(2)}, u32[]{:S(2)}) collective-permute-start(bf16[2,5,48,384]{3,2,1,0:T(8,128)(2,1)S(1)} %get-tuple-element.311.refs_0_), channel_id=1, source_target_pairs={{0,2},{2,0},{4,6},{6,4},{8,10},{10,8},{12,14},{14,12},{16,18},{18,... | collective-permute-start | bytes 1105928 | tf_op jit(solution)/shard_map/ppermute | solution.py:860
  103.0 52.6 %collective-permute-start.35 = (bf16[2,2,2,3,48,640]{5,4,3,2,1,0:T(8,128)(2,1)S(1)}, bf16[2,2,2,3,48,640]{5,4,3,2,1,0:T(8,128)(2,1)}, u32[]{:S(2)}, u32[]{:S(2)}) collective-permute-start(bf16[2,2,2,3,48,640]{5,4,3,2,1,0:T(8,128)(2,1)S(1)} %pad_maximum_fusion.refs_0_), channel_id=1, source_target_pairs={{0,2},{2,0},{4,6},{6,4},{8,10},{10,8},{12,14},{14,12},{16,18},{18,... | collective-permute-start | bytes 4423688 | tf_op jit(solution)/shard_map/ppermute | solution.py:860
  104.3 22.6 %collective-permute-start.31 = (bf16[2,2,3,48,384]{4,3,2,1,0:T(8,128)(2,1)S(1)}, bf16[2,2,3,48,384]{4,3,2,1,0:T(8,128)(2,1)S(1)}, u32[]{:S(2)}, u32[]{:S(2)}) collective-permute-start(bf16[2,2,3,48,384]{4,3,2,1,0:T(8,128)(2,1)S(1)} %get-tuple-element.325), channel_id=1, source_target_pairs={{0,16},{2,18},{4,20},{6,22},{8,24},{10,26},{12,28},{14,30},{16,0},... | collective-permute-start | bytes 1327112 | tf_op jit(solution)/shard_map/ppermute | solution.py:860
  105.3 42.9 %collective-permute-start.32 = (bf16[2,2,2,3,48,640]{5,4,3,2,1,0:T(8,128)(2,1)S(1)}, bf16[2,2,2,3,48,640]{5,4,3,2,1,0:T(8,128)(2,1)}, u32[]{:S(2)}, u32[]{:S(2)}) collective-permute-start(bf16[2,2,2,3,48,640]{5,4,3,2,1,0:T(8,128)(2,1)S(1)} %pad_maximum_fusion.refs_0_), channel_id=1, source_target_pairs={{0,4},{2,6},{4,0},{6,2},{8,12},{10,14},{12,8},{14,10},{16,20},{18,... | collective-permute-start | bytes 4423688 | tf_op jit(solution)/shard_map/ppermute | solution.py:860
  105.8 41.0 %collective-permute-start.34 = (bf16[512,768]{1,0:T(8,128)(2,1)S(1)}, bf16[512,768]{1,0:T(8,128)(2,1)S(1)}, u32[]{:S(2)}, u32[]{:S(2)}) collective-permute-start(bf16[512,768]{1,0:T(8,128)(2,1)S(1)} %dynamic-slice_bitcast_fusion.1), channel_id=1, source_target_pairs={{0,1},{1,0},{2,3},{3,2},{4,5},{5,4},{6,7},{7,6},{8,9},{9,8},{10,11... | collective-permute-start | bytes 2359304 | tf_op jit(solution)/shard_map/ppermute | solution.py:864
  127.0 21.2 %collective-permute-start.33 = (bf16[2,2,2,3,48,384]{5,4,3,2,1,0:T(8,128)(2,1)S(1)}, bf16[2,2,2,3,48,384]{5,4,3,2,1,0:T(8,128)(2,1)S(1)}, u32[]{:S(2)}, u32[]{:S(2)}) collective-permute-start(bf16[2,2,2,3,48,384]{5,4,3,2,1,0:T(8,128)(2,1)S(1)} %pad_maximum_fusion.1.refs_4_), channel_id=1, source_target_pairs={{0,8},{2,10},{4,12},{6,14},{8,0},{10,2},{12,4},{14,6},{16,24},{18,... | collective-permute-start | bytes 2654216 | tf_op jit(solution)/shard_map/ppermute | solution.py:860
  208.0 48.2 %collective-permute-start.42 = (bf16[512,768]{1,0:T(8,128)(2,1)}, bf16[512,768]{1,0:T(8,128)(2,1)S(1)}, u32[]{:S(2)}, u32[]{:S(2)}) collective-permute-start(bf16[512,768]{1,0:T(8,128)(2,1)} %get-tuple-element.361), channel_id=1, source_target_pairs={{0,1},{1,0},{2,3},{3,2},{4,5},{5,4},{6,7},{7,6},{8,9},{9,8},{10,11... | collective-permute-start | bytes 2359304 | tf_op jit(solution)/shard_map/ppermute | solution.py:864
  221.4 30.1 %collective-permute-start.40 = (bf16[2,2,3,48,1024]{4,3,2,1,0:T(8,128)(2,1)}, bf16[2,2,3,48,1024]{4,3,2,1,0:T(8,128)(2,1)S(1)}, u32[]{:S(2)}, u32[]{:S(2)}) collective-permute-start(bf16[2,2,3,48,1024]{4,3,2,1,0:T(8,128)(2,1)} %fusion.1), channel_id=1, source_target_pairs={{0,4},{2,6},{4,0},{6,2},{8,12},{10,14},{12,8},{14,10},{16,20},{18,... | collective-permute-start | bytes 3538952 | tf_op jit(solution)/shard_map/ppermute | solution.py:860
  222.0 31.2 %collective-permute-start.41 = (bf16[2,2,3,48,1024]{4,3,2,1,0:T(8,128)(2,1)}, bf16[2,2,3,48,1024]{4,3,2,1,0:T(8,128)(2,1)}, u32[]{:S(2)}, u32[]{:S(2)}) collective-permute-start(bf16[2,2,3,48,1024]{4,3,2,1,0:T(8,128)(2,1)} %fusion), channel_id=1, source_target_pairs={{0,1},{1,0},{2,3},{3,2},{4,5},{5,4},{6,7},{7,6},{8,9},{9,8},{10,11... | collective-permute-start | bytes 3538952 | tf_op jit(solution)/shard_map/ppermute | solution.py:864
  255.0 28.0 %collective-permute-start.43 = (bf16[2,3,48,1024]{3,2,1,0:T(8,128)(2,1)S(1)}, bf16[2,3,48,1024]{3,2,1,0:T(8,128)(2,1)S(1)}, u32[]{:S(2)}, u32[]{:S(2)}) collective-permute-start(bf16[2,3,48,1024]{3,2,1,0:T(8,128)(2,1)S(1)} %get-tuple-element.372), channel_id=1, source_target_pairs={{0,1},{1,0},{2,3},{3,2},{4,5},{5,4},{6,7},{7,6},{8,9},{9,8},{10,11... | collective-permute-start | bytes 1769480 | tf_op jit(solution)/shard_map/ppermute | solution.py:864
  255.8 27.2 %collective-permute-start.44 = (bf16[2,3,48,1024]{3,2,1,0:T(8,128)(2,1)S(1)}, bf16[2,3,48,1024]{3,2,1,0:T(8,128)(2,1)S(1)}, u32[]{:S(2)}, u32[]{:S(2)}) collective-permute-start(bf16[2,3,48,1024]{3,2,1,0:T(8,128)(2,1)S(1)} %get-tuple-element.373), channel_id=1, source_target_pairs={{0,4},{2,6},{4,0},{6,2},{8,12},{10,14},{12,8},{14,10},{16,20},{18,... | collective-permute-start | bytes 1769480 | tf_op jit(solution)/shard_map/ppermute | solution.py:860
  285.9 27.2 %collective-permute-start.48 = (bf16[2,3,48,1024]{3,2,1,0:T(8,128)(2,1)}, bf16[2,3,48,1024]{3,2,1,0:T(8,128)(2,1)}, u32[]{:S(2)}, u32[]{:S(2)}) collective-permute-start(bf16[2,3,48,1024]{3,2,1,0:T(8,128)(2,1)} %fusion.5), channel_id=1, source_target_pairs={{0,8},{2,10},{4,12},{6,14},{8,0},{10,2},{12,4},{14,6},{16,24},{18,... | collective-permute-start | bytes 1769480 | tf_op jit(solution)/shard_map/ppermute | solution.py:860
  297.2 18.7 %collective-permute-start.46 = (bf16[2,2,5,48,384]{4,3,2,1,0:T(8,128)(2,1)S(1)}, bf16[2,2,5,48,384]{4,3,2,1,0:T(8,128)(2,1)S(1)}, u32[]{:S(2)}, u32[]{:S(2)}) collective-permute-start(bf16[2,2,5,48,384]{4,3,2,1,0:T(8,128)(2,1)S(1)} %fusion.13), channel_id=1, source_target_pairs={{0,4},{2,6},{4,0},{6,2},{8,12},{10,14},{12,8},{14,10},{16,20},{18,... | collective-permute-start | bytes 2211848 | tf_op jit(solution)/shard_map/ppermute | solution.py:860
  298.8 18.3 %collective-permute-start.47 = (bf16[2,2,5,48,384]{4,3,2,1,0:T(8,128)(2,1)S(1)}, bf16[2,2,5,48,384]{4,3,2,1,0:T(8,128)(2,1)S(1)}, u32[]{:S(2)}, u32[]{:S(2)}) collective-permute-start(bf16[2,2,5,48,384]{4,3,2,1,0:T(8,128)(2,1)S(1)} %fusion.12), channel_id=1, source_target_pairs={{0,1},{1,0},{2,3},{3,2},{4,5},{5,4},{6,7},{7,6},{8,9},{9,8},{10,11... | collective-permute-start | bytes 2211848 | tf_op jit(solution)/shard_map/ppermute | solution.py:864
  317.1 27.7 %collective-permute-start.53 = (bf16[512,768]{1,0:T(8,128)(2,1)}, bf16[512,768]{1,0:T(8,128)(2,1)S(1)}, u32[]{:S(2)}, u32[]{:S(2)}) collective-permute-start(bf16[512,768]{1,0:T(8,128)(2,1)} %get-tuple-element.417), channel_id=1, source_target_pairs={{0,1},{1,0},{2,3},{3,2},{4,5},{5,4},{6,7},{7,6},{8,9},{9,8},{10,11... | collective-permute-start | bytes 2359304 | tf_op jit(solution)/shard_map/ppermute | solution.py:864
  322.4 22.9 %collective-permute-start.52 = (bf16[2,2,3,48,384]{4,3,2,1,0:T(8,128)(2,1)}, bf16[2,2,3,48,384]{4,3,2,1,0:T(8,128)(2,1)S(1)}, u32[]{:S(2)}, u32[]{:S(2)}) collective-permute-start(bf16[2,2,3,48,384]{4,3,2,1,0:T(8,128)(2,1)} %fusion.21), channel_id=1, source_target_pairs={{0,4},{2,6},{4,0},{6,2},{8,12},{10,14},{12,8},{14,10},{16,20},{18,... | collective-permute-start | bytes 1327112 | tf_op jit(solution)/shard_map/ppermute | solution.py:860
  322.9 22.4 %collective-permute-start.50 = (bf16[2,5,48,384]{3,2,1,0:T(8,128)(2,1)}, bf16[2,5,48,384]{3,2,1,0:T(8,128)(2,1)}, u32[]{:S(2)}, u32[]{:S(2)}) collective-permute-start(bf16[2,5,48,384]{3,2,1,0:T(8,128)(2,1)} %get-tuple-element.414), channel_id=1, source_target_pairs={{0,1},{1,0},{2,3},{3,2},{4,5},{5,4},{6,7},{7,6},{8,9},{9,8},{10,11... | collective-permute-start | bytes 1105928 | tf_op jit(solution)/shard_map/ppermute | solution.py:864
  323.9 21.4 %collective-permute-start.51 = (bf16[2,5,48,384]{3,2,1,0:T(8,128)(2,1)}, bf16[2,5,48,384]{3,2,1,0:T(8,128)(2,1)}, u32[]{:S(2)}, u32[]{:S(2)}) collective-permute-start(bf16[2,5,48,384]{3,2,1,0:T(8,128)(2,1)} %get-tuple-element.415), channel_id=1, source_target_pairs={{0,4},{2,6},{4,0},{6,2},{8,12},{10,14},{12,8},{14,10},{16,20},{18,... | collective-permute-start | bytes 1105928 | tf_op jit(solution)/shard_map/ppermute | solution.py:860
  325.4 19.4 %collective-permute-start.54 = (bf16[3,48,1024]{2,1,0:T(8,128)(2,1)S(1)}, bf16[3,48,1024]{2,1,0:T(8,128)(2,1)S(1)}, u32[]{:S(2)}, u32[]{:S(2)}) collective-permute-start(bf16[3,48,1024]{2,1,0:T(8,128)(2,1)S(1)} %fusion.26), channel_id=1, source_target_pairs={{0,16},{2,18},{4,20},{6,22},{8,24},{10,26},{12,28},{14,30},{16,0},... | collective-permute-start | bytes 884744 | tf_op jit(solution)/shard_map/ppermute | solution.py:860
  348.0 13.1 %collective-permute-start.57 = (bf16[2,2,3,48,384]{4,3,2,1,0:T(8,128)(2,1)S(1)}, bf16[2,2,3,48,384]{4,3,2,1,0:T(8,128)(2,1)S(1)}, u32[]{:S(2)}, u32[]{:S(2)}) collective-permute-start(bf16[2,2,3,48,384]{4,3,2,1,0:T(8,128)(2,1)S(1)} %fusion.22), channel_id=1, source_target_pairs={{0,4},{2,6},{4,0},{6,2},{8,12},{10,14},{12,8},{14,10},{16,20},{18,... | collective-permute-start | bytes 1327112 | tf_op jit(solution)/shard_map/ppermute | solution.py:860
  364.9 13.1 %collective-permute-start.60 = (bf16[2,3,48,384]{3,2,1,0:T(8,128)(2,1)S(1)}, bf16[2,3,48,384]{3,2,1,0:T(8,128)(2,1)S(1)}, u32[]{:S(2)}, u32[]{:S(2)}) collective-permute-start(bf16[2,3,48,384]{3,2,1,0:T(8,128)(2,1)S(1)} %fusion.27), channel_id=1, source_target_pairs={{0,8},{2,10},{4,12},{6,14},{8,0},{10,2},{12,4},{14,6},{16,24},{18,... | collective-permute-start | bytes 663560 | tf_op jit(solution)/shard_map/ppermute | solution.py:860
  366.2 13.8 %collective-permute-start.63 = (bf16[5,48,384]{2,1,0:T(8,128)(2,1)S(1)}, bf16[5,48,384]{2,1,0:T(8,128)(2,1)S(1)}, u32[]{:S(2)}, u32[]{:S(2)}) collective-permute-start(bf16[5,48,384]{2,1,0:T(8,128)(2,1)S(1)} %fusion.29), channel_id=1, source_target_pairs={{0,16},{2,18},{4,20},{6,22},{8,24},{10,26},{12,28},{14,30},{16,0},... | collective-permute-start | bytes 552968 | tf_op jit(solution)/shard_map/ppermute | solution.py:860
  367.7 21.8 %collective-permute-start.65 = (bf16[512,768]{1,0:T(8,128)(2,1)}, bf16[512,768]{1,0:T(8,128)(2,1)S(1)}, u32[]{:S(2)}, u32[]{:S(2)}) collective-permute-start(bf16[512,768]{1,0:T(8,128)(2,1)} %get-tuple-element.467), channel_id=1, source_target_pairs={{0,1},{1,0},{2,3},{3,2},{4,5},{5,4},{6,7},{7,6},{8,9},{9,8},{10,11... | collective-permute-start | bytes 2359304 | tf_op jit(solution)/shard_map/ppermute | solution.py:864
  (110 other events, 1228.7 us)
